TPU v7x, 32 devices: a whole 2x2x4 slice. The times are simulated.
32 devices in a mesh: grp: 2 (over y), code: 4 (over z), rep: 4 (over x, core).
Axes of the slice: x: 2, y: 2, z: 4, core: 2. Of those that a mesh axis runs over, the one named last changes fastest.
Arguments:
- state_slab: float32 [8, 4, 128, 512], P(('grp', 'rep'), 'code'), parts along dimension 0, may hold values from -6 to 6
- previous_slab: float32 [8, 4, 128, 512], P(('grp', 'rep'), 'code'), parts along dimension 0, may hold values from -6 to 6
- previous_parity: float32 [8, 128, 2048], P(('grp', 'rep'), 'code'), parts along dimension 0, may hold values from -6 to 6
- generator: float32 [4, 4], replicated, as said below
- failed_ids: int32 [8, 2], P(('grp', 'rep')), parts along dimension 0, may hold values from 0 to 3, as said below
Outputs:
- new_parity: float32 [8, 128, 2048], P(('grp', 'rep'), 'code'), parts along dimension 0
- restored_state: float32 [8, 4, 128, 512], P(('grp', 'rep'), 'code'), parts along dimension 0
There are 2 independent parts, one for each index of `grp`. A program takes and returns all parts, laid end to end along the dimension named above; an argument that names none is the same for every part. Nothing has to cross between parts.
Inputs may be any that keep to these rules, and one draw needn't show every extreme that they name: generator has first row all ones; for any two columns at cyclic distance at least 1 the Gram determinant of those columns is at least 2. `failed_ids`: the two failed members of a stripe differ, and their cyclic distance along the stripe is at least 1.
All inputs are finite; a program needn't handle non-finite values.
Results may differ from a plain program's by a relative error of at most 0.00007.
Values sent between devices are 32-bit elements; how exact they have to be, the bound alone decides.
No kernel may reach another device: no remote copies, remote signals or barrier semaphores. Data moves between devices by JAX's collectives and lax.ppermute only.
A program may use at most 64 MiB of HBM per device.

v0:
```python
import jax
import jax.numpy as jnp
from jax import lax
from jax.sharding import PartitionSpec as P


def solve_weights(failed_columns):
    col_first = failed_columns[..., 0]
    col_second = failed_columns[..., 1]
    gram_first = jnp.sum(col_first * col_first, axis=-1, keepdims=True)
    gram_cross = jnp.sum(col_first * col_second, axis=-1, keepdims=True)
    gram_second = jnp.sum(col_second * col_second, axis=-1, keepdims=True)
    determinant = gram_first * gram_second - gram_cross * gram_cross
    solve_first = (gram_second * col_first - gram_cross * col_second) / determinant
    solve_second = (gram_first * col_second - gram_cross * col_first) / determinant
    return jnp.stack([solve_first, solve_second], axis=-2)


def local(state_slab, previous_slab, previous_parity, generator, failed_ids):
    highest_setting = lax.Precision.HIGHEST
    position = lax.axis_index("code")
    code_count = lax.axis_size("code")
    slab_rows = state_slab.shape[2]
    row_span_width = state_slab.shape[3]
    parity_row_block = generator.shape[0]
    member_own_rows = slab_rows // code_count
    current = state_slab[0, 0]
    earlier = previous_slab[0, 0]
    column_ids = jnp.arange(generator.shape[1], dtype=jnp.int32)
    own_pick = (column_ids == position).astype(jnp.float32)
    own_column = jnp.dot(generator, own_pick, precision=highest_setting)
    failed_one = failed_ids[0, 0]
    failed_two = failed_ids[0, 1]
    own_alive = ((position != failed_one) & (position != failed_two)).astype(jnp.float32)
    failed_pick = (column_ids[None, :] == failed_ids[0][:, None]).astype(jnp.float32)
    failed_columns = jnp.dot(generator, failed_pick.T, precision=highest_setting)
    weights = solve_weights(failed_columns)

    def scaled(member_slab, coefficients, count_rows):
        product = member_slab[:, None, :] * coefficients[None, :, None]
        return product.reshape(count_rows, coefficients.shape[0] * row_span_width)

    new_parity = lax.psum_scatter(
        scaled(current, own_column, member_own_rows * lax.axis_size("code")),
        "code",
        scatter_dimension=0,
        tiled=True,
    )
    surviving_members = lax.psum_scatter(
        scaled(earlier, own_column * own_alive, member_own_rows * lax.axis_size("code")),
        "code",
        scatter_dimension=0,
        tiled=True,
    )
    leftover_term = (previous_parity[0] - surviving_members).reshape(
        member_own_rows, parity_row_block, row_span_width
    )
    rebuilt = jnp.einsum("kj,xjy->xky", weights, leftover_term, precision=highest_setting)
    gathered = lax.all_gather(rebuilt, "code", axis=0, tiled=True)
    restored_state = jnp.where(
        position == failed_one,
        gathered[:, 0],
        jnp.where(position == failed_two, gathered[:, 1], earlier),
    )
    return (new_parity[None], restored_state[None, None])


def solution(mesh):
    placed = (
        P(("grp", "rep"), "code", None, None),
        P(("grp", "rep"), "code", None, None),
        P(("grp", "rep"), "code", None),
        P(),
        P(("grp", "rep"), None),
    )
    return jax.shard_map(
        local,
        mesh=mesh,
        in_specs=placed,
        out_specs=(P(("grp", "rep"), "code", None), P(("grp", "rep"), "code", None, None)),
        check_vma=False,
    )
```

profile of v0, /device:TPU:0, one launch (start us, length us, event | category | flops | bytes accessed | tf_op | source)
XLA Modules:
  0.0 82.1 jit_solution(17402171914403249692)
XLA Ops:
  7.2 0.0 copy-start
  7.2 0.0 reduce-scatter.5.cloned.1.call-start
  7.2 0.0 copy-start.4
  7.2 0.6 copy-done.4
  7.9 0.6 fusion.10
  9.8 0.0 copy-done
  9.8 0.1 broadcast_multiply_fusion.2
  9.9 0.1 broadcast_bitcast_fusion
  10.0 1.1 %mul.140 = f32[128,4,512]{2,1,0:T(4,128)S(1)} broadcast(f32[128,512]{1,0:T(8,128)} %bitcast.51), dimensions={0,2} | broadcast | bytes 1310720 | tf_op jit(solution)/shard_map/mul | solution.py:40
  11.2 0.3 copy.13
  11.5 1.1 %broadcast_multiply_fusion = f32[128,2048]{1,0:T(8,128)} fusion(f32[128,2048]{1,0:T(8,128)S(1)} %bitcast.49, f32[2048]{0:T(1024)S(1)} %bitcast.53), kind=kLoop, calls=%fused_computation.3 | loop fusion | flops 262144 | bytes 2105344 | tf_op jit(solution)/shard_map/mul | solution.py:40
  12.7 0.0 copy-start.2
  12.7 0.0 reduce-scatter.5.cloned.1.call-update
  12.7 0.0 reduce-scatter.3.cloned.1.call-start
  12.7 0.9 %copy-done.2 = f32[1,1,128,512]{3,2,1,0:T(8,128)S(1)} copy-done((f32[1,1,128,512]{3,2,1,0:T(8,128)S(1)}, f32[1,1,128,512]{3,2,1,0:T(8,128)}, u32[]{:S(2)}) %copy-start.2) | copy-done | bytes 262168
  13.6 0.2 mul.133
  13.8 0.3 copy.11
  14.1 1.1 %broadcast_multiply_fusion.1 = f32[128,2048]{1,0:T(8,128)} fusion(f32[128,2048]{1,0:T(8,128)S(1)} %bitcast.50, f32[2048]{0:T(1024)S(1)} %bitcast.54), kind=kLoop, calls=%fused_computation.4 | loop fusion | flops 262144 | bytes 2105344 | tf_op jit(solution)/shard_map/mul | solution.py:40
  15.2 0.0 copy-start.3
  15.2 0.0 reduce-scatter.3.cloned.1.call-update
  16.6 0.2 convolution_bitcast_fusion.1
  16.8 0.7 multiply_reduce_fusion.1
  20.0 1.9 %divide_bitcast_fusion.1 = (f32[1,4]{1,0:T(1,128)S(1)}, f32[1,4]{1,0:T(1,128)S(1)}) fusion(f32[]{:T(128)S(6)} %sub.31, f32[]{:T(128)} %get-tuple-element.6, f32[]{:T(128)} %get-tuple-element.8, f32[4,2]{0,1:T(2,128)S(1)} %convolution_bitcast_fusion.1, f32[]{:T(128)} %get-tuple-element.7), kind=kLoop, calls=%fused_computation.20 | loop fusion | flops 32 | bytes 80 | tf_op jit(solution)/shard_map/div | solution.py:14
  22.0 20.7 %reduce-scatter.5.cloned.1.call-done = f32[32,2048]{1,0:T(8,128)} async-done(((f32[128,2048]{1,0:T(8,128)}), f32[32,2048]{1,0:T(8,128)}) %reduce-scatter.5.cloned.1.call-update) | async-done | bytes 262160 | tf_op jit(solution)/shard_map/reduce_scatter | solution.py:49
  42.7 0.0 copy-done.3
  42.7 1.0 %bitcast_subtract_fusion = f32[32,2048]{1,0:T(8,128)S(1)} fusion(f32[32,2048]{1,0:T(8,128)} %reduce-scatter.5.cloned.1.call-done, f32[1,32,2048]{2,1,0:T(8,128)S(1)} %copy-done.3), kind=kLoop, calls=%fused_computation.9 | loop fusion | flops 65536 | bytes 786432 | tf_op jit(solution)/shard_map/sub | solution.py:55
  43.7 0.2 reshape.96
  43.8 0.6 convolution_bitcast_fusion
  44.4 0.0 copy-start.1
  44.4 19.5 %all_gather.3 = f32[128,2,512]{2,1,0:T(2,128)S(1)} all-gather(f32[32,2,512]{2,1,0:T(2,128)S(1)} %convolution_bitcast_fusion), channel_id=1, replica_groups=mesh['grp'=2,'code'=4,'rep'=4] {'code'}, dimensions={0}, use_global_device_ids=true | all-gather | bytes 655360 | tf_op jit(solution)/shard_map/all_gather | solution.py:59
  63.9 0.0 copy-done.1
  63.9 0.4 broadcast_select_fusion.1
  64.4 0.7 copy.10
  65.1 10.2 %reduce-scatter.3.cloned.1.call-done = f32[32,2048]{1,0:T(8,128)} async-done(((f32[128,2048]{1,0:T(8,128)}), f32[32,2048]{1,0:T(8,128)}) %reduce-scatter.3.cloned.1.call-update) | async-done | bytes 262160 | tf_op jit(solution)/shard_map/reduce_scatter | solution.py:43
  (2 shorter events, 0.0 us)
Async XLA Ops:
  7.2 2.7 %copy-start = (f32[4,4]{1,0:T(4,128)S(1)}, f32[4,4]{1,0:T(4,128)}, u32[]{:S(2)}) copy-start(f32[4,4]{1,0:T(4,128)} %param.8) | copy-start | bytes 196
  7.2 35.5 %reduce-scatter.5.cloned.1.call-start = ((), (), s32[]{:S(2)}) async-start(), calls=%async_computation.3 | async-start | bytes 1310720 | tf_op jit(solution)/shard_map/reduce_scatter | solution.py:49
  7.2 0.7 copy-start.4
  12.7 0.9 %copy-start.2 = (f32[1,1,128,512]{3,2,1,0:T(8,128)S(1)}, f32[1,1,128,512]{3,2,1,0:T(8,128)}, u32[]{:S(2)}) copy-start(f32[1,1,128,512]{3,2,1,0:T(8,128)} %param.5) | copy-start | bytes 786436
  12.7 62.6 %reduce-scatter.3.cloned.1.call-start = ((), (), s32[]{:S(2)}) async-start(), calls=%async_computation.2 | async-start | bytes 1310720 | tf_op jit(solution)/shard_map/reduce_scatter | solution.py:43
  15.2 27.4 %copy-start.3 = (f32[1,32,2048]{2,1,0:T(8,128)S(1)}, f32[1,32,2048]{2,1,0:T(8,128)}, u32[]{:S(2)}) copy-start(f32[1,32,2048]{2,1,0:T(8,128)} %param.7) | copy-start | bytes 786436
  44.4 19.5 %copy-start.1 = (f32[1,1,128,512]{3,2,1,0:T(8,128)S(1)}, f32[1,1,128,512]{3,2,1,0:T(8,128)}, u32[]{:S(2)}) copy-start(f32[1,1,128,512]{3,2,1,0:T(8,128)} %param.6) | copy-start | bytes 786436
Sparse Core Ops, SparseCore 0:
  12.8 29.8 reduce-scatter.4
  45.6 29.6 reduce-scatter.2
where the time goes:
time: 82.5 us; the launch traced here: 82.1 us
  waiting for transfers between devices  31 us (38%)
  blocking collectives  19.5 us (24%)
  between operations  19.4 us (24%)
  other arithmetic  6.25 us (8%)
  local copies, waits for them, and re-layouts  5.11 us (6%)
  matrix products  0.87 us (1%)
    reduce_scatter x1, waiting for transfers between devices, local(): lax.psum_scatter(scaled(earlier, own_column * own_alive, member_own_rows...  20.7 us
    all_gather x1, blocking collectives, local(): gathered = lax.all_gather(rebuilt, 'code', axis=0, tiled=True)  19.5 us
    reduce_scatter x1, waiting for transfers between devices, local(): lax.psum_scatter(scaled(current, own_column, member_own_rows * lax.axis_s...  10.2 us
    unnamed x16, local copies, waits for them, and re-layouts  3.02 us
    mul x2, other arithmetic, scaled(): product = member_slab[:, None, :] * coefficients[None, :, None]  2.21 us
    div x1, other arithmetic, solve_weights(): (gram_second * col_first - gram_cross * col_second) / determinant  1.9 us
  transfers between devices with their start and end apart: 2, of which 2 were waited for; matrix products, arithmetic and copies ran while one was open for 9% of the time, Pallas kernels for 0%

commit v1 on v0

v1 whole, which is shorter than its diff:
```python
import jax
import jax.numpy as jnp
from jax import lax
from jax.sharding import PartitionSpec as P


def local(state_slab, previous_slab, previous_parity, generator, failed_ids):
    position = lax.axis_index("code")
    code_count = lax.axis_size("code")
    slab_rows, width = state_slab.shape[2:]
    spans = generator.shape[0]
    own_rows = slab_rows // code_count
    earlier = previous_slab[0, 0]
    blocks = (code_count, own_rows, width)
    earlier_rows = lax.all_to_all(earlier.reshape(blocks), "code", 0, 0, tiled=True)
    current_rows = lax.all_to_all(state_slab.reshape(blocks), "code", 0, 0, tiled=True)

    column_ids = jnp.arange(code_count, dtype=jnp.int32)
    failed_one = failed_ids[0, 0]
    failed_two = failed_ids[0, 1]
    alive = ((column_ids != failed_one) & (column_ids != failed_two)).astype(jnp.float32)
    col_first = jnp.sum(jnp.where(column_ids == failed_one, generator, 0.0), axis=1)
    col_second = jnp.sum(jnp.where(column_ids == failed_two, generator, 0.0), axis=1)
    gram_first = jnp.sum(col_first * col_first)
    gram_cross = jnp.sum(col_first * col_second)
    gram_second = jnp.sum(col_second * col_second)
    determinant = gram_first * gram_second - gram_cross * gram_cross
    solve_first = (gram_second * col_first - gram_cross * col_second) / determinant
    solve_second = (gram_first * col_second - gram_cross * col_first) / determinant

    parity = previous_parity[0]
    leftover = [
        parity[:, j * width : (j + 1) * width]
        - jnp.sum((generator[j] * alive)[:, None, None] * earlier_rows, axis=0)
        for j in range(spans)
    ]
    rebuilt_first = sum(solve_first[j] * leftover[j] for j in range(spans))
    rebuilt_second = sum(solve_second[j] * leftover[j] for j in range(spans))
    outgoing = jnp.where(
        (column_ids == failed_one)[:, None, None], rebuilt_first[None], rebuilt_second[None]
    )
    incoming = lax.all_to_all(outgoing, "code", 0, 0, tiled=True)
    lost = (position == failed_one) | (position == failed_two)
    restored_state = jnp.where(lost, incoming.reshape(slab_rows, width), earlier)
    new_parity = jnp.concatenate(
        [jnp.sum(generator[j][:, None, None] * current_rows, axis=0) for j in range(spans)], axis=1
    )
    return (new_parity[None], restored_state[None, None])


def solution(mesh):
    placed = (
        P(("grp", "rep"), "code", None, None),
        P(("grp", "rep"), "code", None, None),
        P(("grp", "rep"), "code", None),
        P(),
        P(("grp", "rep"), None),
    )
    return jax.shard_map(
        local,
        mesh=mesh,
        in_specs=placed,
        out_specs=(P(("grp", "rep"), "code", None), P(("grp", "rep"), "code", None, None)),
        check_vma=False,
    )
```

time: 82.5 us -> 43.8 us (0.53)
  waiting for transfers between devices: 31 us -> 7.26 us
  blocking collectives: 19.5 us -> 0 us
  starting transfers between devices: 0.08 us -> 15 us
  between operations: 19.4 us -> 4.56 us
  other arithmetic: 6.25 us -> 12.9 us
  local copies, waits for them, and re-layouts: 5.11 us -> 3.48 us
  matrix products: 0.87 us -> 0 us
    reduce_scatter x2 -> x0, waiting for transfers between devices: 30.9 us -> none  [the longest x1 20.7 us: local(): lax.psum_scatter(scaled(earlier, own_column * own_alive, member_own_rows...]
    all_gather x1 -> x0, blocking collectives: 19.5 us -> none  [local(): gathered = lax.all_gather(rebuilt, 'code', axis=0, tiled=True)]
    all_to_all x0 -> x3, starting transfers between devices: none -> 15 us  [the longest x1 6.33 us: local(): lax.all_to_all(earlier.reshape(blocks), 'code', 0, 0, tiled=True)]
    all_to_all x0 -> x3, waiting for transfers between devices: none -> 7.26 us  [the longest x1 5.72 us: local(): incoming = lax.all_to_all(outgoing, 'code', 0, 0, tiled=True)]
    add x0 -> x2, other arithmetic: none -> 5.02 us  [the longest x1 2.51 us: local(): rebuilt_first = sum((solve_first[j] * leftover[j] for j in range(spans)))]
    unnamed x16 -> x8, local copies, waits for them, and re-layouts: 3.02 us -> 1.5 us
    slice x1 -> x3, local copies, waits for them, and re-layouts: 0.59 us -> 1.98 us  [the longest x1 0.67 us: local(): rebuilt_first = sum((solve_first[j] * leftover[j] for j in range(spans)))]
    eq x0 -> x1, other arithmetic: none -> 1.34 us  [local(): column_ids == failed_two]
  transfers between devices with their start and end apart: 2 -> 3, of which waited for: 2 -> 2; matrix products, arithmetic and copies ran while one was open for 9% -> 33% of each run, Pallas kernels for 0% -> 0%
where the time goes in v1:
time: 43.8 us; the launch traced here: 43.2 us
  starting transfers between devices  15 us (34%)
  other arithmetic  12.9 us (29%)
  waiting for transfers between devices  7.26 us (17%)
  between operations  4.56 us (10%)
  local copies, waits for them, and re-layouts  3.48 us (8%)
    all_to_all x1, starting transfers between devices, local(): lax.all_to_all(earlier.reshape(blocks), 'code', 0, 0, tiled=True)  6.33 us
    all_to_all x1, waiting for transfers between devices, local(): incoming = lax.all_to_all(outgoing, 'code', 0, 0, tiled=True)  5.72 us
    all_to_all x1, starting transfers between devices, local(): lax.all_to_all(state_slab.reshape(blocks), 'code', 0, 0, tiled=True)  5.1 us
    all_to_all x1, starting transfers between devices, local(): incoming = lax.all_to_all(outgoing, 'code', 0, 0, tiled=True)  3.56 us
    add x1, other arithmetic, local(): rebuilt_first = sum((solve_first[j] * leftover[j] for j in range(spans)))  2.51 us
    add x1, other arithmetic, local(): rebuilt_second = sum((solve_second[j] * leftover[j] for j in range(spans)))  2.51 us
    div x1, other arithmetic, local(): (gram_second * col_first - gram_cross * col_second) / determinant  1.84 us
    all_to_all x1, waiting for transfers between devices, local(): lax.all_to_all(state_slab.reshape(blocks), 'code', 0, 0, tiled=True)  1.54 us
  transfers between devices with their start and end apart: 3, of which 2 were waited for; matrix products, arithmetic and copies ran while one was open for 33% of the time, Pallas kernels for 0%

profile of v1, /device:TPU:0, one launch (start us, length us, event | category | flops | bytes accessed | tf_op | source)
XLA Modules:
  0.0 43.2 jit_solution(1851161629403154057)
XLA Ops:
  0.6 0.0 copy-start.3
  0.6 6.3 %all-to-all-start.1 = ((f32[4,32,512]{2,1,0:T(8,128)}), f32[4,32,512]{2,1,0:T(8,128)S(1)}, u32[]{:S(2)}, u32[]{:S(2)}) async-start(f32[4,32,512]{2,1,0:T(8,128)} %bitcast.34), calls=%async_computation.1 | async-start | bytes 524288 | tf_op jit(solution)/shard_map/all_to_all | solution.py:15
  7.0 0.0 copy-done.3
  7.0 0.7 %fusion.2 = (s32[1,1]{1,0:T(1,128)}, s32[1,1]{1,0:T(1,128)}) fusion(s32[1,2]{1,0:T(1,128)S(1)} %copy-done.3), kind=kLoop, calls=%fused_computation.37 | loop fusion | bytes 16 | tf_op jit(solution)/shard_map/slice | solution.py:19
  7.6 1.3 %iota_compare_fusion = (pred[4]{0:T(512)(128)(4,1)S(1)}, pred[4]{0:T(512)(128)(4,1)S(1)}) fusion(s32[]{:T(128)} %bitcast.7, s32[]{:T(128)} %bitcast.6), kind=kLoop, calls=%fused_computation.25 | loop fusion | flops 8 | bytes 16 | tf_op jit(solution)/shard_map/eq | solution.py:23
  9.0 0.0 copy-start.2
  9.0 0.7 %copy-done.2 = f32[4,4]{1,0:T(4,128)S(1)} copy-done((f32[4,4]{1,0:T(4,128)S(1)}, f32[4,4]{1,0:T(4,128)}, u32[]{:S(2)}) %copy-start.2) | copy-done | bytes 88
  9.7 0.1 select_reduce_fusion.1
  9.8 0.6 %multiply_reduce_fusion.9 = (f32[]{:T(128)}, f32[]{:T(128)}, f32[]{:T(128)}) fusion(f32[4]{0:T(128)S(1)} %get-tuple-element.11, f32[4]{0:T(128)S(1)} %get-tuple-element.10), kind=kLoop, calls=%fused_computation.23 | loop fusion | flops 21 | bytes 44 | tf_op jit(solution)/shard_map/reduce_sum | solution.py:25
  12.9 1.8 %subtract_divide_fusion.1 = (f32[4]{0:T(128)S(1)}, f32[4]{0:T(128)S(1)}) fusion(f32[4]{0:T(128)S(1)} %get-tuple-element.10, f32[4]{0:T(128)S(1)} %get-tuple-element.11, f32[]{:T(128)S(6)} %sub.22, f32[]{:T(128)} %get-tuple-element.12, f32[]{:T(128)} %get-tuple-element.13, f32[]{:T(128)} %get-tuple-element.14), kind=kLoop, calls=%fused_computation.22 | loop fusion | flops 32 | bytes 80 | tf_op jit(solution)/shard_map/div | solution.py:28
  14.8 0.7 %fusion = (f32[1]{0:T(128)}, f32[1]{0:T(128)}, f32[1]{0:T(128)}, f32[1]{0:T(128)}) fusion(f32[4]{0:T(128)S(1)} %get-tuple-element.24), kind=kLoop, calls=%fused_computation.35 | loop fusion | bytes 32 | tf_op jit(solution)/shard_map/slice | solution.py:37
  15.5 0.6 %fusion.1 = (f32[1]{0:T(128)}, f32[1]{0:T(128)}, f32[1]{0:T(128)}, f32[1]{0:T(128)}) fusion(f32[4]{0:T(128)S(1)} %get-tuple-element.25), kind=kLoop, calls=%fused_computation.36 | loop fusion | bytes 32 | tf_op jit(solution)/shard_map/slice | solution.py:38
  16.1 1.3 %broadcast_select_fusion.5 = (f32[4]{0:T(128)S(1)}, pred[4]{0:T(512)(128)(4,1)S(1)}) fusion(f32[4,4]{1,0:T(4,128)S(1)} %copy-done.2, s32[]{:T(128)} %bitcast.7, s32[]{:T(128)} %bitcast.6), kind=kLoop, calls=%fused_computation.34 | loop fusion | flops 16 | bytes 44 | tf_op jit(solution)/shard_map/mul | solution.py:34
  17.5 0.0 all-to-all-done.1
  17.5 5.1 %all-to-all-start = ((f32[4,32,512]{2,1,0:T(8,128)}), f32[4,32,512]{2,1,0:T(8,128)S(1)}, u32[]{:S(2)}, u32[]{:S(2)}) async-start(f32[4,32,512]{2,1,0:T(8,128)} %bitcast.1), calls=%async_computation | async-start | bytes 524288 | tf_op jit(solution)/shard_map/all_to_all | solution.py:16
  22.6 0.0 copy-start
  22.6 0.1 multiply_reduce_fusion
  22.7 0.8 %copy-done = f32[1,32,2048]{2,1,0:T(8,128)S(1)} copy-done((f32[1,32,2048]{2,1,0:T(8,128)S(1)}, f32[1,32,2048]{2,1,0:T(8,128)}, u32[]{:S(2)}) %copy-start) | copy-done | bytes 262168
  23.5 2.5 %multiply_add_fusion.1 = f32[32,512]{1,0:T(8,128)S(1)} fusion(f32[]{:T(128)} %bitcast.13, f32[]{:T(128)} %bitcast.12, f32[]{:T(128)} %bitcast.11, f32[]{:T(128)} %bitcast.8, f32[32,512]{1,0:T(8,128)S(1)} %get-tuple-element.5, f32[32,2048]{1,0:T(8,128)S(1)} %bitcast.32, f32[32,512]{1,0:T(8,128)S(1)} %get-tuple-element.4, f32[32,512]{1,0:T(8,128)S(1)} %get-tuple-element.3, ...), kind=kLoop, calls=%fused_computation.16 | loop fusion | flops 180224 | bytes 589840 | tf_op jit(solution)/shard_map/add | solution.py:37
  26.1 2.5 %multiply_add_fusion = f32[32,512]{1,0:T(8,128)S(1)} fusion(f32[]{:T(128)} %bitcast.17, f32[]{:T(128)} %bitcast.16, f32[]{:T(128)} %bitcast.15, f32[]{:T(128)} %bitcast.14, f32[32,512]{1,0:T(8,128)S(1)} %get-tuple-element.5, f32[32,2048]{1,0:T(8,128)S(1)} %bitcast.33, f32[32,512]{1,0:T(8,128)S(1)} %get-tuple-element.4, f32[32,512]{1,0:T(8,128)S(1)} %get-tuple-element.3, ...), kind=kLoop, calls=%fused_computation.15 | loop fusion | flops 180224 | bytes 589840 | tf_op jit(solution)/shard_map/add | solution.py:38
  28.6 0.8 %broadcast_select_fusion = f32[4,32,512]{2,1,0:T(8,128)} fusion(f32[32,512]{1,0:T(8,128)S(1)} %multiply_add_fusion, f32[32,512]{1,0:T(8,128)S(1)} %multiply_add_fusion.1, pred[4]{0:T(512)(128)(4,1)S(1)} %get-tuple-element.37), kind=kLoop, calls=%fused_computation.9 | loop fusion | flops 65536 | bytes 393220 | tf_op jit(solution)/shard_map/jit(_where)/select_n | solution.py:39
  29.4 1.5 %all-to-all-done = f32[4,32,512]{2,1,0:T(8,128)S(1)} async-done(((f32[4,32,512]{2,1,0:T(8,128)}), f32[4,32,512]{2,1,0:T(8,128)S(1)}, u32[]{:S(2)}, u32[]{:S(2)}) %all-to-all-start) | async-done | bytes 262176 | tf_op jit(solution)/shard_map/all_to_all | solution.py:16
  30.9 3.6 %all-to-all-start.2 = ((f32[4,32,512]{2,1,0:T(8,128)}), f32[4,32,512]{2,1,0:T(8,128)S(1)}, u32[]{:S(2)}, u32[]{:S(2)}) async-start(f32[4,32,512]{2,1,0:T(8,128)} %broadcast_select_fusion), calls=%async_computation.2 | async-start | bytes 524288 | tf_op jit(solution)/shard_map/all_to_all | solution.py:42
  35.8 0.1 multiply_reduce_fusion.7
  36.0 0.0 copy-start.1
  36.0 0.7 %maximum_bitcast_fusion = f32[1,32,2048]{2,1,0:T(8,128)} fusion(f32[32,512]{1,0:T(8,128)S(1)} %get-tuple-element.7, f32[32,512]{1,0:T(8,128)S(1)} %get-tuple-element.8, f32[32,512]{1,0:T(8,128)S(1)} %get-tuple-element.9, f32[32,512]{1,0:T(8,128)S(1)} %get-tuple-element.6), kind=kLoop, calls=%fused_computation | loop fusion | flops 196608 | bytes 524288 | tf_op jit(solution)/shard_map/broadcast_in_dim | solution.py:48
  36.7 5.7 %all-to-all-done.2 = f32[4,32,512]{2,1,0:T(8,128)S(1)} async-done(((f32[4,32,512]{2,1,0:T(8,128)}), f32[4,32,512]{2,1,0:T(8,128)S(1)}, u32[]{:S(2)}, u32[]{:S(2)}) %all-to-all-start.2) | async-done | bytes 262176 | tf_op jit(solution)/shard_map/all_to_all | solution.py:42
  42.4 0.0 copy-done.1
  42.4 0.7 %broadcast_select_fusion.1 = f32[1,1,128,512]{3,2,1,0:T(8,128)} fusion(f32[1,1,128,512]{3,2,1,0:T(8,128)S(1)} %bitcast.35, f32[1,1,128,512]{3,2,1,0:T(8,128)S(1)} %copy-done.1, pred[]{:T(512)S(6)} %or.3), kind=kLoop, calls=%fused_computation.10 | loop fusion | flops 65536 | bytes 786433 | tf_op jit(solution)/shard_map/jit(_where)/select_n | solution.py:44
  (2 shorter events, 0.0 us)
Async XLA Ops:
  0.6 6.3 %copy-start.3 = (s32[1,2]{1,0:T(1,128)S(1)}, s32[1,2]{1,0:T(1,128)}, u32[]{:S(2)}) copy-start(s32[1,2]{1,0:T(1,128)} %param.9) | copy-start | bytes 28
  0.6 16.8 %all-to-all-start.1 = ((f32[4,32,512]{2,1,0:T(8,128)}), f32[4,32,512]{2,1,0:T(8,128)S(1)}, u32[]{:S(2)}, u32[]{:S(2)}) async-start(f32[4,32,512]{2,1,0:T(8,128)} %bitcast.34), calls=%async_computation.1 | async-start | bytes 524288 | tf_op jit(solution)/shard_map/all_to_all | solution.py:15
  9.0 0.7 %copy-start.2 = (f32[4,4]{1,0:T(4,128)S(1)}, f32[4,4]{1,0:T(4,128)}, u32[]{:S(2)}) copy-start(f32[4,4]{1,0:T(4,128)} %param.8) | copy-start | bytes 196
  17.5 13.4 %all-to-all-start = ((f32[4,32,512]{2,1,0:T(8,128)}), f32[4,32,512]{2,1,0:T(8,128)S(1)}, u32[]{:S(2)}, u32[]{:S(2)}) async-start(f32[4,32,512]{2,1,0:T(8,128)} %bitcast.1), calls=%async_computation | async-start | bytes 524288 | tf_op jit(solution)/shard_map/all_to_all | solution.py:16
  22.6 0.9 %copy-start = (f32[1,32,2048]{2,1,0:T(8,128)S(1)}, f32[1,32,2048]{2,1,0:T(8,128)}, u32[]{:S(2)}) copy-start(f32[1,32,2048]{2,1,0:T(8,128)} %param.7) | copy-start | bytes 786436
  30.9 11.5 %all-to-all-start.2 = ((f32[4,32,512]{2,1,0:T(8,128)}), f32[4,32,512]{2,1,0:T(8,128)S(1)}, u32[]{:S(2)}, u32[]{:S(2)}) async-start(f32[4,32,512]{2,1,0:T(8,128)} %broadcast_select_fusion), calls=%async_computation.2 | async-start | bytes 524288 | tf_op jit(solution)/shard_map/all_to_all | solution.py:42
  36.0 6.5 %copy-start.1 = (f32[1,1,128,512]{3,2,1,0:T(8,128)S(1)}, f32[1,1,128,512]{3,2,1,0:T(8,128)}, u32[]{:S(2)}) copy-start(f32[1,1,128,512]{3,2,1,0:T(8,128)} %param.6) | copy-start | bytes 786436

commit v2 on v1

v2 whole, which is shorter than its diff:
```python
import jax
import jax.numpy as jnp
from jax import lax
from jax.experimental import pallas as pl
from jax.experimental.pallas import tpu as pltpu
from jax.sharding import PartitionSpec as P

IN_VMEM = pl.BlockSpec(memory_space=pltpu.VMEM)
IN_SMEM = pl.BlockSpec(memory_space=pltpu.SMEM)


def cost(arrays, outs, flops):
    total = sum(x.size * x.dtype.itemsize for x in arrays) + sum(4 * o.size for o in outs)
    return pl.CostEstimate(flops=flops, bytes_accessed=total, transcendentals=0)


def plan_kernel(ids_ref, generator_ref, parity_ref, base_ref, solve_ref, generator_rows_ref):
    spans, members = generator_ref.shape
    width = base_ref.shape[2]
    first, second = ids_ref[0, 0], ids_ref[0, 1]
    col_first = [generator_ref[j, first] for j in range(spans)]
    col_second = [generator_ref[j, second] for j in range(spans)]
    gram_first = sum(x * x for x in col_first)
    gram_cross = sum(x * y for x, y in zip(col_first, col_second))
    gram_second = sum(y * y for y in col_second)
    determinant = gram_first * gram_second - gram_cross * gram_cross

    def spread(value):
        return jnp.full((1, width), value, jnp.float32)

    over = spread(determinant)
    weights = [
        [spread(gram_second * x - gram_cross * y) / over for x, y in zip(col_first, col_second)],
        [spread(gram_first * y - gram_cross * x) / over for x, y in zip(col_first, col_second)],
    ]
    for k in range(2):
        base_ref[k] = sum(
            weights[k][j] * parity_ref[:, j * width : (j + 1) * width] for j in range(spans)
        )
    for c in range(members):
        alive = jnp.logical_and(first != c, second != c)
        for k in range(2):
            row = sum(
                weights[k][j] * jnp.where(alive, generator_ref[j, c], 0.0) for j in range(spans)
            )
            solve_ref[k * members + c : k * members + c + 1, :] = row
        for j in range(spans):
            generator_rows_ref[j * members + c : j * members + c + 1, :] = spread(
                generator_ref[j, c]
            )


def rebuild_kernel(ids_ref, base_ref, solve_ref, rows_ref, out_ref):
    members = rows_ref.shape[0]
    first, second = ids_ref[0, 0], ids_ref[0, 1]
    for k, target in enumerate((first, second)):
        total = base_ref[k]
        for c in range(members):
            i = k * members + c
            total = total - solve_ref[i : i + 1, :] * rows_ref[c]
        out_ref[target] = total


def parity_kernel(generator_rows_ref, rows_ref, out_ref):
    members, _, width = rows_ref.shape
    for j in range(generator_rows_ref.shape[0] // members):
        total = None
        for c in range(members):
            i = j * members + c
            term = generator_rows_ref[i : i + 1, :] * rows_ref[c]
            total = term if total is None else total + term
        out_ref[:, j * width : (j + 1) * width] = total


def call(kernel, specs, outs, args, flops):
    return pl.pallas_call(
        kernel,
        in_specs=specs,
        out_specs=jax.tree.map(lambda _: IN_VMEM, outs),
        out_shape=outs,
        cost_estimate=cost(args, jax.tree.leaves(outs), flops),
    )(*args)


def local(state_slab, previous_slab, previous_parity, generator, failed_ids):
    position = lax.axis_index("code")
    members = lax.axis_size("code")
    slab_rows, width = state_slab.shape[2:]
    spans = generator.shape[0]
    own_rows = slab_rows // members
    earlier = previous_slab[0, 0]
    blocks = (members, own_rows, width)

    def floats(*shape):
        return jax.ShapeDtypeStruct(shape, jnp.float32)

    earlier_rows = lax.all_to_all(earlier.reshape(blocks), "code", 0, 0, tiled=True)
    current_rows = lax.all_to_all(state_slab.reshape(blocks), "code", 0, 0, tiled=True)
    base, solve_rows, generator_rows = call(
        plan_kernel,
        [IN_SMEM, IN_SMEM, IN_VMEM],
        (floats(2, own_rows, width), floats(2 * members, width), floats(spans * members, width)),
        (failed_ids, generator, previous_parity[0]),
        4 * spans * own_rows * width,
    )
    outgoing = call(
        rebuild_kernel,
        [IN_SMEM, IN_VMEM, IN_VMEM, IN_VMEM],
        floats(*blocks),
        (failed_ids, base, solve_rows, earlier_rows),
        4 * slab_rows * width,
    )
    incoming = lax.all_to_all(outgoing, "code", 0, 0, tiled=True)
    new_parity = call(
        parity_kernel,
        [IN_VMEM, IN_VMEM],
        floats(own_rows, spans * width),
        (generator_rows, current_rows),
        2 * spans * slab_rows * width,
    )
    lost = (position == failed_ids[0, 0]) | (position == failed_ids[0, 1])
    restored_state = jnp.where(lost, incoming.reshape(slab_rows, width), earlier)
    return (new_parity[None], restored_state[None, None])


def solution(mesh):
    placed = (
        P(("grp", "rep"), "code", None, None),
        P(("grp", "rep"), "code", None, None),
        P(("grp", "rep"), "code", None),
        P(),
        P(("grp", "rep"), None),
    )
    return jax.shard_map(
        local,
        mesh=mesh,
        in_specs=placed,
        out_specs=(P(("grp", "rep"), "code", None), P(("grp", "rep"), "code", None, None)),
        check_vma=False,
    )
```

time: 43.8 us -> 38.6 us (0.88)
  blocking collectives: 0 us -> 15.3 us
  other arithmetic: 12.9 us -> 0.74 us
  starting transfers between devices: 15 us -> 6.81 us
  Pallas kernels: 0 us -> 5.27 us
  between operations: 4.56 us -> 1.96 us
  local copies, waits for them, and re-layouts: 3.48 us -> 1.24 us
    all_to_all x0 -> x1, blocking collectives: none -> 15.3 us  [local(): lax.all_to_all(earlier.reshape(blocks), 'code', 0, 0, tiled=True)]
    all_to_all x1 -> x0, starting transfers between devices: 6.33 us -> none  [local(): lax.all_to_all(earlier.reshape(blocks), 'code', 0, 0, tiled=True)]
    pallas_call x0 -> x3, Pallas kernels: none -> 5.27 us  [call(): pl.pallas_call(kernel, in_specs=specs, out_specs=jax.tree.map(lambda _: I...]
    add x2 -> x0, other arithmetic: 5.02 us -> none  [the longest x1 2.51 us: local(): rebuilt_first = sum((solve_first[j] * leftover[j] for j in range(spans)))]
    all_to_all x1, waiting for transfers between devices: 5.72 us -> 2.41 us  [local(): incoming = lax.all_to_all(outgoing, 'code', 0, 0, tiled=True)]
    all_to_all x1, waiting for transfers between devices: 1.54 us -> 4.43 us  [local(): lax.all_to_all(state_slab.reshape(blocks), 'code', 0, 0, tiled=True)]
    div x1 -> x0, other arithmetic: 1.84 us -> none  [local(): (gram_second * col_first - gram_cross * col_second) / determinant]
    all_to_all x1, starting transfers between devices: 5.1 us -> 3.41 us  [local(): lax.all_to_all(state_slab.reshape(blocks), 'code', 0, 0, tiled=True)]
  transfers between devices with their start and end apart: 3 -> 2, of which waited for: 2 -> 2; matrix products, arithmetic and copies ran while one was open for 33% -> 2% of each run, Pallas kernels for 0% -> 14%
where the time goes in v2:
time: 38.6 us; the launch traced here: 38.2 us
  blocking collectives  15.3 us (40%)
  waiting for transfers between devices  6.83 us (18%)
  starting transfers between devices  6.81 us (18%)
  Pallas kernels  5.27 us (14%)
  between operations  1.96 us (5%)
  local copies, waits for them, and re-layouts  1.24 us (3%)
  other arithmetic  0.74 us (2%)
    all_to_all x1, blocking collectives, local(): lax.all_to_all(earlier.reshape(blocks), 'code', 0, 0, tiled=True)  15.3 us
    pallas_call x3, Pallas kernels, call(): pl.pallas_call(kernel, in_specs=specs, out_specs=jax.tree.map(lambda _: I...  5.27 us
    all_to_all x1, waiting for transfers between devices, local(): lax.all_to_all(state_slab.reshape(blocks), 'code', 0, 0, tiled=True)  4.43 us
    all_to_all x1, starting transfers between devices, local(): lax.all_to_all(state_slab.reshape(blocks), 'code', 0, 0, tiled=True)  3.41 us
    all_to_all x1, starting transfers between devices, local(): incoming = lax.all_to_all(outgoing, 'code', 0, 0, tiled=True)  3.4 us
    all_to_all x1, waiting for transfers between devices, local(): incoming = lax.all_to_all(outgoing, 'code', 0, 0, tiled=True)  2.41 us
  transfers between devices with their start and end apart: 2, of which 2 were waited for; matrix products, arithmetic and copies ran while one was open for 2% of the time, Pallas kernels for 14%

profile of v2, /device:TPU:0, one launch (start us, length us, event | category | flops | bytes accessed | tf_op | source)
XLA Modules:
  0.0 38.2 jit_solution(4011496571602444439)
XLA Ops:
  0.6 15.3 %all_to_all.15.rows_ref = f32[4,32,512]{2,1,0:T(8,128)} all-to-all(f32[4,32,512]{2,1,0:T(8,128)} %bitcast.7), channel_id=1, replica_groups=mesh['grp'=2,'code'=4,'rep'=4] {'code'}, dimensions={0} | all-to-all | bytes 524288 | tf_op jit(solution)/shard_map/all_to_all | solution.py:97
  15.9 3.4 %all-to-all-start = ((f32[4,32,512]{2,1,0:T(8,128)}), f32[4,32,512]{2,1,0:T(8,128)S(1)}, u32[]{:S(2)}, u32[]{:S(2)}) async-start(f32[4,32,512]{2,1,0:T(8,128)} %bitcast.1), calls=%async_computation | async-start | bytes 524288 | tf_op jit(solution)/shard_map/all_to_all | solution.py:98
  19.4 1.7 %shard_map.68 = (f32[2,32,512]{2,1,0:T(8,128)}, f32[8,512]{1,0:T(8,128)}, f32[16,512]{1,0:T(8,128)}) custom-call(s32[1,2]{1,0:T(1,128)} %ids_ref.3, f32[4,4]{1,0:T(4,128)} %generator_ref.1, f32[32,2048]{1,0:T(8,128)} %bitcast.9), custom_call_target="tpu_custom_call" | custom-call | flops 262144 | bytes 442440 | tf_op jit(solution)/shard_map/pallas_call | solution.py:76
  21.1 1.8 %shard_map.70 = f32[4,32,512]{2,1,0:T(8,128)} custom-call(s32[1,2]{1,0:T(1,128)} %ids_ref.3, f32[2,32,512]{2,1,0:T(8,128)} %get-tuple-element.6.base_ref, f32[8,512]{1,0:T(8,128)} %get-tuple-element.7.solve_ref, f32[4,32,512]{2,1,0:T(8,128)} %all_to_all.15.rows_ref), custom_call_target="tpu_custom_call" | custom-call | flops 262144 | bytes 671752 | tf_op jit(solution)/shard_map/pallas_call | solution.py:76
  22.8 4.4 %all-to-all-done.rows_ref = f32[4,32,512]{2,1,0:T(8,128)S(1)} async-done(((f32[4,32,512]{2,1,0:T(8,128)}), f32[4,32,512]{2,1,0:T(8,128)S(1)}, u32[]{:S(2)}, u32[]{:S(2)}) %all-to-all-start) | async-done | bytes 262176 | tf_op jit(solution)/shard_map/all_to_all | solution.py:98
  27.3 0.0 copy-start
  27.3 3.4 %all-to-all-start.2 = ((f32[4,32,512]{2,1,0:T(8,128)}), f32[4,32,512]{2,1,0:T(8,128)S(1)}, u32[]{:S(2)}, u32[]{:S(2)}) async-start(f32[4,32,512]{2,1,0:T(8,128)} %shard_map.70), calls=%async_computation.2 | async-start | bytes 524288 | tf_op jit(solution)/shard_map/all_to_all | solution.py:113
  30.7 0.0 copy-done
  30.7 0.0 copy-start.2
  30.7 0.6 %copy-done.2 = s32[1,2]{1,0:T(1,128)S(1)} copy-done((s32[1,2]{1,0:T(1,128)S(1)}, s32[1,2]{1,0:T(1,128)}, u32[]{:S(2)}) %copy-start.2) | copy-done | bytes 32
  31.4 0.6 %fusion = (s32[1,1]{1,0:T(1,128)}, s32[1,1]{1,0:T(1,128)}) fusion(s32[1,2]{1,0:T(1,128)S(1)} %copy-done.2), kind=kLoop, calls=%fused_computation.1 | loop fusion | bytes 16 | tf_op jit(solution)/shard_map/slice | solution.py:121
  33.2 0.0 copy-start.1
  33.2 1.8 %shard_map.69 = f32[32,2048]{1,0:T(8,128)} custom-call(f32[16,512]{1,0:T(8,128)} %get-tuple-element.5.generator_rows_ref, f32[4,32,512]{2,1,0:T(8,128)} %copy-done), custom_call_target="tpu_custom_call" | custom-call | flops 524288 | bytes 557056 | tf_op jit(solution)/shard_map/pallas_call | solution.py:76
  35.0 2.4 %all-to-all-done.2 = f32[4,32,512]{2,1,0:T(8,128)S(1)} async-done(((f32[4,32,512]{2,1,0:T(8,128)}), f32[4,32,512]{2,1,0:T(8,128)S(1)}, u32[]{:S(2)}, u32[]{:S(2)}) %all-to-all-start.2) | async-done | bytes 262176 | tf_op jit(solution)/shard_map/all_to_all | solution.py:113
  37.4 0.0 copy-done.1
  37.4 0.7 %broadcast_select_fusion = f32[1,1,128,512]{3,2,1,0:T(8,128)} fusion(f32[1,1,128,512]{3,2,1,0:T(8,128)S(1)} %bitcast.8, f32[1,1,128,512]{3,2,1,0:T(8,128)S(1)} %copy-done.1, pred[]{:T(512)S(6)} %or.3), kind=kLoop, calls=%fused_computation | loop fusion | flops 65536 | bytes 786433 | tf_op jit(solution)/shard_map/jit(_where)/select_n | solution.py:122
Async XLA Ops:
  15.9 11.3 %all-to-all-start = ((f32[4,32,512]{2,1,0:T(8,128)}), f32[4,32,512]{2,1,0:T(8,128)S(1)}, u32[]{:S(2)}, u32[]{:S(2)}) async-start(f32[4,32,512]{2,1,0:T(8,128)} %bitcast.1), calls=%async_computation | async-start | bytes 524288 | tf_op jit(solution)/shard_map/all_to_all | solution.py:98
  27.3 3.4 %copy-start = (f32[4,32,512]{2,1,0:T(8,128)}, f32[4,32,512]{2,1,0:T(8,128)S(1)}, u32[]{:S(2)}) copy-start(f32[4,32,512]{2,1,0:T(8,128)S(1)} %all-to-all-done.rows_ref) | copy-start | bytes 786436
  27.3 10.2 %all-to-all-start.2 = ((f32[4,32,512]{2,1,0:T(8,128)}), f32[4,32,512]{2,1,0:T(8,128)S(1)}, u32[]{:S(2)}, u32[]{:S(2)}) async-start(f32[4,32,512]{2,1,0:T(8,128)} %shard_map.70), calls=%async_computation.2 | async-start | bytes 524288 | tf_op jit(solution)/shard_map/all_to_all | solution.py:113
  30.7 0.7 %copy-start.2 = (s32[1,2]{1,0:T(1,128)S(1)}, s32[1,2]{1,0:T(1,128)}, u32[]{:S(2)}) copy-start(s32[1,2]{1,0:T(1,128)} %ids_ref.3) | copy-start | bytes 28
  33.2 4.2 %copy-start.1 = (f32[1,1,128,512]{3,2,1,0:T(8,128)S(1)}, f32[1,1,128,512]{3,2,1,0:T(8,128)}, u32[]{:S(2)}) copy-start(f32[1,1,128,512]{3,2,1,0:T(8,128)} %param.6) | copy-start | bytes 786436

commit v3 on v2

v3 whole, which is shorter than its diff:
```python
import jax
import jax.numpy as jnp
from jax import lax
from jax.experimental import pallas as pl
from jax.experimental.pallas import tpu as pltpu
from jax.sharding import PartitionSpec as P

IN_VMEM = pl.BlockSpec(memory_space=pltpu.VMEM)
IN_SMEM = pl.BlockSpec(memory_space=pltpu.SMEM)
ANYWHERE = pl.BlockSpec(memory_space=pl.ANY)

DIRECT_MEMBERS = 8


def wrap(index, members):
    return lax.rem(index + 2 * members, members)


def plan_kernel(ids_ref, generator_ref, parity_ref, base_ref, solve_ref, generator_rows_ref):
    spans, members = generator_ref.shape
    width = base_ref.shape[2]
    first, second = ids_ref[0, 0], ids_ref[0, 1]
    col_first = [generator_ref[j, first] for j in range(spans)]
    col_second = [generator_ref[j, second] for j in range(spans)]
    gram_first = sum(x * x for x in col_first)
    gram_cross = sum(x * y for x, y in zip(col_first, col_second))
    gram_second = sum(y * y for y in col_second)
    determinant = gram_first * gram_second - gram_cross * gram_cross

    def spread(value):
        return jnp.full((1, width), value, jnp.float32)

    over = spread(determinant)
    weights = [
        [spread(gram_second * x - gram_cross * y) / over for x, y in zip(col_first, col_second)],
        [spread(gram_first * y - gram_cross * x) / over for x, y in zip(col_first, col_second)],
    ]
    for k in range(2):
        base_ref[k] = sum(
            weights[k][j] * parity_ref[:, j * width : (j + 1) * width] for j in range(spans)
        )
    for c in range(members):
        alive = jnp.logical_and(first != c, second != c)
        for k in range(2):
            row = sum(
                weights[k][j] * jnp.where(alive, generator_ref[j, c], 0.0) for j in range(spans)
            )
            solve_ref[k * members + c : k * members + c + 1, :] = row
        for j in range(spans):
            generator_rows_ref[j * members + c : j * members + c + 1, :] = spread(
                generator_ref[j, c]
            )


def weigh(coefficient_ref, start, rows):
    total = None
    for member, block in rows:
        term = coefficient_ref[pl.ds(start + member, 1), :] * block
        total = term if total is None else total + term
    return total


def whole_rows(rows_ref):
    return [(c, rows_ref[c]) for c in range(rows_ref.shape[0])]


def shifted_rows(own_ref, refs):
    members = len(refs) + 1
    me = lax.axis_index("code")
    rows = [(me, own_ref[me])]
    return rows + [(wrap(me - s, members), ref[...]) for s, ref in enumerate(refs, 1)]


def rebuild_whole_kernel(ids_ref, base_ref, solve_ref, rows_ref, out_ref):
    rows = whole_rows(rows_ref)
    for k in range(2):
        out_ref[ids_ref[0, k]] = base_ref[k] - weigh(solve_ref, k * len(rows), rows)


def rebuild_shifted_kernel(ids_ref, base_ref, solve_ref, own_ref, *refs):
    members = own_ref.shape[0]
    rows = shifted_rows(own_ref, refs[: members - 1])
    outs = refs[members - 1 :]
    me = lax.axis_index("code")
    for k in range(2):
        rebuilt = base_ref[k] - weigh(solve_ref, k * members, rows)
        for s, out_ref in enumerate(outs):

            @pl.when(wrap(me + s, members) == ids_ref[0, k])
            def _():
                out_ref[...] = rebuilt


def parity_whole_kernel(generator_rows_ref, rows_ref, out_ref):
    parity_into(out_ref, generator_rows_ref, whole_rows(rows_ref))


def parity_shifted_kernel(generator_rows_ref, own_ref, *refs):
    parity_into(refs[-1], generator_rows_ref, shifted_rows(own_ref, refs[:-1]))


def parity_into(out_ref, generator_rows_ref, rows):
    width = generator_rows_ref.shape[1]
    for j in range(out_ref.shape[1] // width):
        out_ref[:, j * width : (j + 1) * width] = weigh(generator_rows_ref, j * len(rows), rows)


def cut_kernel(blocks_ref, *refs):
    outs, sems = refs[:-1], refs[-1]
    members = len(outs) + 1
    me = lax.axis_index("code")
    copies = [
        pltpu.make_async_copy(blocks_ref.at[wrap(me + s, members)], out, sems.at[s - 1])
        for s, out in enumerate(outs, 1)
    ]
    for copy in copies:
        copy.start()
    for copy in copies:
        copy.wait()


def restore_kernel(ids_ref, earlier_ref, *refs):
    pieces, out_ref = refs[:-1], refs[-1]
    members = len(pieces)
    me = lax.axis_index("code")
    lost = jnp.logical_or(me == ids_ref[0, 0], me == ids_ref[0, 1])

    @pl.when(lost)
    def _():
        for s, piece in enumerate(pieces):
            out_ref[wrap(me - s, members)] = piece[...]

    @pl.when(jnp.logical_not(lost))
    def _():
        out_ref[...] = earlier_ref[...]


def call(kernel, specs, outs, args, flops, **options):
    total = sum(x.size for x in args) + sum(o.size for o in jax.tree.leaves(outs))
    options.setdefault("out_specs", jax.tree.map(lambda _: IN_VMEM, outs))
    return pl.pallas_call(
        kernel,
        in_specs=specs,
        out_shape=outs,
        cost_estimate=pl.CostEstimate(flops=flops, bytes_accessed=4 * total, transcendentals=0),
        **options,
    )(*args)


def floats(*shape):
    return jax.ShapeDtypeStruct(shape, jnp.float32)


def send(pieces, members):
    return [
        lax.ppermute(piece, "code", [(d, (d + s) % members) for d in range(members)])
        for s, piece in enumerate(pieces, 1)
    ]


def cut(blocks):
    members = blocks.shape[0]
    return call(
        cut_kernel,
        [ANYWHERE],
        [floats(*blocks.shape[1:])] * (members - 1),
        (blocks,),
        0,
        out_specs=[ANYWHERE] * (members - 1),
        scratch_shapes=[pltpu.SemaphoreType.DMA((members - 1,))],
    )


def local(state_slab, previous_slab, previous_parity, generator, failed_ids):
    position = lax.axis_index("code")
    members = lax.axis_size("code")
    slab_rows, width = state_slab.shape[2:]
    spans = generator.shape[0]
    own_rows = slab_rows // members
    blocks = (members, own_rows, width)
    earlier = previous_slab.reshape(blocks)
    current = state_slab.reshape(blocks)
    direct = members <= DIRECT_MEMBERS

    if direct:
        earlier_rows = send(cut(earlier), members)
        current_rows = send(cut(current), members)
    else:
        earlier_rows = lax.all_to_all(earlier, "code", 0, 0, tiled=True)
        current_rows = lax.all_to_all(current, "code", 0, 0, tiled=True)
    base, solve_rows, generator_rows = call(
        plan_kernel,
        [IN_SMEM, IN_SMEM, IN_VMEM],
        (floats(2, own_rows, width), floats(2 * members, width), floats(spans * members, width)),
        (failed_ids, generator, previous_parity[0]),
        4 * spans * own_rows * width,
    )
    parity_shape = floats(own_rows, spans * width)
    rebuild_cost = 4 * slab_rows * width
    parity_cost = 2 * spans * slab_rows * width
    if direct:
        outgoing = call(
            rebuild_shifted_kernel,
            [IN_SMEM] + [IN_VMEM] * (members + 2),
            [floats(own_rows, width)] * members,
            (failed_ids, base, solve_rows, earlier, *earlier_rows),
            rebuild_cost,
        )
        incoming = send(outgoing[1:], members)
        new_parity = call(
            parity_shifted_kernel,
            [IN_VMEM] * (members + 1),
            parity_shape,
            (generator_rows, current, *current_rows),
            parity_cost,
        )
        restored_state = call(
            restore_kernel,
            [IN_SMEM] + [IN_VMEM] * (members + 1),
            floats(*blocks),
            (failed_ids, earlier, outgoing[0], *incoming),
            0,
        )
    else:
        outgoing = call(
            rebuild_whole_kernel,
            [IN_SMEM] + [IN_VMEM] * 3,
            floats(*blocks),
            (failed_ids, base, solve_rows, earlier_rows),
            rebuild_cost,
        )
        incoming = lax.all_to_all(outgoing, "code", 0, 0, tiled=True)
        new_parity = call(
            parity_whole_kernel,
            [IN_VMEM] * 2,
            parity_shape,
            (generator_rows, current_rows),
            parity_cost,
        )
        lost = (position == failed_ids[0, 0]) | (position == failed_ids[0, 1])
        restored_state = jnp.where(lost, incoming, earlier)
    return (new_parity[None], restored_state.reshape(state_slab.shape))


def solution(mesh):
    placed = (
        P(("grp", "rep"), "code", None, None),
        P(("grp", "rep"), "code", None, None),
        P(("grp", "rep"), "code", None),
        P(),
        P(("grp", "rep"), None),
    )
    return jax.shard_map(
        local,
        mesh=mesh,
        in_specs=placed,
        out_specs=(P(("grp", "rep"), "code", None), P(("grp", "rep"), "code", None, None)),
        check_vma=False,
    )
```

time: 38.6 us -> 40.1 us (1.039)
  Pallas kernels: 5.27 us -> 21.3 us
  blocking collectives: 15.3 us -> 0 us
  starting transfers between devices: 6.81 us -> 15.9 us
  waiting for transfers between devices: 6.83 us -> 0.02 us
  between operations: 1.96 us -> 0.74 us
  other arithmetic: 0.74 us -> 0 us
  local copies, waits for them, and re-layouts: 1.24 us -> 1.91 us
    pallas_call x3 -> x6, Pallas kernels: 5.27 us -> 21.3 us  [call(): pl.pallas_call(kernel, in_specs=specs, out_shape=outs, cost_estimate=pl.C...]
    ppermute x0 -> x9, starting transfers between devices: none -> 15.9 us  [send(): lax.ppermute(piece, 'code', [(d, (d + s) % members) for d in range(member...]
    all_to_all x1 -> x0, blocking collectives: 15.3 us -> none  [local(): lax.all_to_all(earlier.reshape(blocks), 'code', 0, 0, tiled=True)]
    all_to_all x2 -> x0, waiting for transfers between devices: 6.83 us -> none  [the longest x1 4.43 us: local(): lax.all_to_all(state_slab.reshape(blocks), 'code', 0, 0, tiled=True)]
    all_to_all x2 -> x0, starting transfers between devices: 6.81 us -> none  [the longest x1 3.41 us: local(): lax.all_to_all(state_slab.reshape(blocks), 'code', 0, 0, tiled=True)]
    unnamed x6 -> x20, local copies, waits for them, and re-layouts: 0.66 us -> 1.91 us
    select_n x1 -> x0, other arithmetic: 0.74 us -> none  [local(): jnp.where(lost, incoming.reshape(slab_rows, width), earlier)]
    slice x1 -> x0, local copies, waits for them, and re-layouts: 0.58 us -> none  [local(): lost = (position == failed_ids[0, 0]) | (position == failed_ids[0, 1])]
  transfers between devices with their start and end apart: 2 -> 9, of which waited for: 2 -> 0; matrix products, arithmetic and copies ran while one was open for 2% -> 0% of each run, Pallas kernels for 14% -> 31%
where the time goes in v3:
time: 40.1 us; the launch traced here: 39.9 us
  Pallas kernels  21.3 us (53%)
  starting transfers between devices  15.9 us (40%)
  local copies, waits for them, and re-layouts  1.91 us (5%)
  between operations  0.74 us (2%)
    pallas_call x6, Pallas kernels, call(): pl.pallas_call(kernel, in_specs=specs, out_shape=outs, cost_estimate=pl.C...  21.3 us
    ppermute x9, starting transfers between devices, send(): lax.ppermute(piece, 'code', [(d, (d + s) % members) for d in range(member...  15.9 us
    unnamed x20, local copies, waits for them, and re-layouts  1.91 us
  transfers between devices with their start and end apart: 9, of which 0 were waited for; matrix products, arithmetic and copies ran while one was open for 0% of the time, Pallas kernels for 31%

profile of v3, /device:TPU:0, one launch (start us, length us, event | category | flops | bytes accessed | tf_op | source)
XLA Modules:
  0.0 39.9 jit_solution(12277042505912838732)
XLA Ops:
  0.6 7.1 %shard_map.71 = (f32[32,512]{1,0:T(8,128)}, f32[32,512]{1,0:T(8,128)}, f32[32,512]{1,0:T(8,128)}) custom-call(f32[4,32,512]{2,1,0:T(8,128)} %bitcast.5), custom_call_target="tpu_custom_call" | custom-call | bytes 458752 | tf_op jit(solution)/shard_map/pallas_call | solution.py:141
  7.7 3.1 %collective-permute-start.3 = (f32[32,512]{1,0:T(8,128)}, f32[32,512]{1,0:T(8,128)S(1)}, u32[]{:S(2)}, u32[]{:S(2)}) collective-permute-start(f32[32,512]{1,0:T(8,128)} %get-tuple-element.21), channel_id=1, source_target_pairs={{0,4},{4,8},{8,12},{12,0},{1,5},{5,9},{9,13},{13,1},{2,6},{6,10},{... | collective-permute-start | bytes 196616 | tf_op jit(solution)/shard_map/ppermute | solution.py:156
  10.8 2.6 %collective-permute-start.4 = (f32[32,512]{1,0:T(8,128)}, f32[32,512]{1,0:T(8,128)S(1)}, u32[]{:S(2)}, u32[]{:S(2)}) collective-permute-start(f32[32,512]{1,0:T(8,128)} %get-tuple-element.22), channel_id=1, source_target_pairs={{0,8},{4,12},{8,0},{12,4},{1,9},{5,13},{9,1},{13,5},{2,10},{6,14},... | collective-permute-start | bytes 196616 | tf_op jit(solution)/shard_map/ppermute | solution.py:156
  13.4 1.3 %collective-permute-start.5 = (f32[32,512]{1,0:T(8,128)}, f32[32,512]{1,0:T(8,128)S(1)}, u32[]{:S(2)}, u32[]{:S(2)}) collective-permute-start(f32[32,512]{1,0:T(8,128)} %get-tuple-element.23), channel_id=1, source_target_pairs={{0,12},{4,0},{8,4},{12,8},{1,13},{5,1},{9,5},{13,9},{2,14},{6,2},{... | collective-permute-start | bytes 196616 | tf_op jit(solution)/shard_map/ppermute | solution.py:156
  14.7 7.1 %shard_map.69 = (f32[32,512]{1,0:T(8,128)}, f32[32,512]{1,0:T(8,128)}, f32[32,512]{1,0:T(8,128)}) custom-call(f32[4,32,512]{2,1,0:T(8,128)} %bitcast.8), custom_call_target="tpu_custom_call" | custom-call | bytes 458752 | tf_op jit(solution)/shard_map/pallas_call | solution.py:141
  21.8 0.7 %collective-permute-start = (f32[32,512]{1,0:T(8,128)}, f32[32,512]{1,0:T(8,128)S(1)}, u32[]{:S(2)}, u32[]{:S(2)}) collective-permute-start(f32[32,512]{1,0:T(8,128)} %get-tuple-element.16), channel_id=1, source_target_pairs={{0,4},{4,8},{8,12},{12,0},{1,5},{5,9},{9,13},{13,1},{2,6},{6,10},{... | collective-permute-start | bytes 196616 | tf_op jit(solution)/shard_map/ppermute | solution.py:156
  22.6 0.3 collective-permute-start.1
  22.9 0.0 copy-start.9
  22.9 1.7 %shard_map.68 = (f32[2,32,512]{2,1,0:T(8,128)}, f32[8,512]{1,0:T(8,128)}, f32[16,512]{1,0:T(8,128)}) custom-call(s32[1,2]{1,0:T(1,128)} %ids_ref.5, f32[4,4]{1,0:T(4,128)} %generator_ref.1, f32[32,2048]{1,0:T(8,128)} %bitcast.11), custom_call_target="tpu_custom_call" | custom-call | flops 262144 | bytes 442440 | tf_op jit(solution)/shard_map/pallas_call | solution.py:141
  24.6 0.0 collective-permute-done.3.refs_0_
  24.6 0.0 copy-start.3
  24.6 0.0 copy-done.9
  24.7 2.9 %collective-permute-start.2 = (f32[32,512]{1,0:T(8,128)S(1)}, f32[32,512]{1,0:T(8,128)S(1)}, u32[]{:S(2)}, u32[]{:S(2)}) collective-permute-start(f32[32,512]{1,0:T(8,128)S(1)} %copy-done.9), channel_id=1, source_target_pairs={{0,12},{4,0},{8,4},{12,8},{1,13},{5,1},{9,5},{13,9},{2,14},{6,2},{... | collective-permute-start | bytes 196616 | tf_op jit(solution)/shard_map/ppermute | solution.py:156
  27.5 0.0 collective-permute-done.4.refs_1_
  27.5 0.0 copy-start.4
  27.5 0.0 collective-permute-done.5.refs_2_
  27.5 0.0 copy-start.6
  27.5 0.0 copy-done.3
  27.6 0.6 %copy-done.4 = f32[32,512]{1,0:T(8,128)} copy-done((f32[32,512]{1,0:T(8,128)}, f32[32,512]{1,0:T(8,128)S(1)}, u32[]{:S(2)}) %copy-start.4) | copy-done | bytes 65560
  28.1 0.0 copy-done.6
  28.2 1.9 %shard_map.72 = (f32[32,512]{1,0:T(8,128)}, f32[32,512]{1,0:T(8,128)}, f32[32,512]{1,0:T(8,128)}, f32[32,512]{1,0:T(8,128)}) custom-call(s32[1,2]{1,0:T(1,128)} %ids_ref.5, f32[2,32,512]{2,1,0:T(8,128)} %get-tuple-element.19.base_ref, f32[8,512]{1,0:T(8,128)} %get-tuple-element.20.solve_ref, f32[4,32,512]{2,1,0:T(8,128)} %bitcast.6, f32[32,512]{1,0:T(8,128)} %copy-done.3, ...), custom_call_target="tpu_custom_call" | custom-call | flops 262144 | bytes 868360 | tf_op jit(solution)/shard_map/pallas_call | solution.py:141
  30.1 0.6 %collective-permute-start.6 = (f32[32,512]{1,0:T(8,128)}, f32[32,512]{1,0:T(8,128)S(1)}, u32[]{:S(2)}, u32[]{:S(2)}) collective-permute-start(f32[32,512]{1,0:T(8,128)} %get-tuple-element.25), channel_id=1, source_target_pairs={{0,4},{4,8},{8,12},{12,0},{1,5},{5,9},{9,13},{13,1},{2,6},{6,10},{... | collective-permute-start | bytes 196616 | tf_op jit(solution)/shard_map/ppermute | solution.py:156
  30.7 1.5 %collective-permute-start.7 = (f32[32,512]{1,0:T(8,128)}, f32[32,512]{1,0:T(8,128)S(1)}, u32[]{:S(2)}, u32[]{:S(2)}) collective-permute-start(f32[32,512]{1,0:T(8,128)} %get-tuple-element.26), channel_id=1, source_target_pairs={{0,8},{4,12},{8,0},{12,4},{1,9},{5,13},{9,1},{13,5},{2,10},{6,14},... | collective-permute-start | bytes 196616 | tf_op jit(solution)/shard_map/ppermute | solution.py:156
  32.1 0.0 collective-permute-done.refs_0_
  32.1 0.0 copy-start
  32.1 2.9 %collective-permute-start.8 = (f32[32,512]{1,0:T(8,128)}, f32[32,512]{1,0:T(8,128)S(1)}, u32[]{:S(2)}, u32[]{:S(2)}) collective-permute-start(f32[32,512]{1,0:T(8,128)} %get-tuple-element.27), channel_id=1, source_target_pairs={{0,12},{4,0},{8,4},{12,8},{1,13},{5,1},{9,5},{13,9},{2,14},{6,2},{... | collective-permute-start | bytes 196616 | tf_op jit(solution)/shard_map/ppermute | solution.py:156
  35.0 0.0 collective-permute-done.1.refs_1_
  35.0 0.0 copy-start.1
  35.0 0.0 collective-permute-done.2.refs_2_
  35.0 0.0 copy-start.2
  35.0 0.0 copy-done
  35.1 0.6 %copy-done.1 = f32[32,512]{1,0:T(8,128)} copy-done((f32[32,512]{1,0:T(8,128)}, f32[32,512]{1,0:T(8,128)S(1)}, u32[]{:S(2)}) %copy-start.1) | copy-done | bytes 65560
  35.6 0.0 copy-done.2
  35.7 1.8 %shard_map.70 = f32[32,2048]{1,0:T(8,128)} custom-call(f32[16,512]{1,0:T(8,128)} %get-tuple-element.15.generator_rows_ref, f32[4,32,512]{2,1,0:T(8,128)} %bitcast.9, f32[32,512]{1,0:T(8,128)} %copy-done, f32[32,512]{1,0:T(8,128)} %copy-done.1, f32[32,512]{1,0:T(8,128)} %copy-done.2), custom_call_target="tpu_custom_call" | custom-call | flops 524288 | bytes 753664 | tf_op jit(solution)/shard_map/pallas_call | solution.py:141
  37.5 0.0 collective-permute-done.6.refs_1_
  37.5 0.0 copy-start.5
  37.5 0.0 collective-permute-done.7.refs_2_
  37.5 0.0 copy-start.7
  37.5 0.0 collective-permute-done.8.refs_3_
  37.5 0.0 copy-start.8
  37.5 0.6 %copy-done.5 = f32[32,512]{1,0:T(8,128)} copy-done((f32[32,512]{1,0:T(8,128)}, f32[32,512]{1,0:T(8,128)S(1)}, u32[]{:S(2)}) %copy-start.5) | copy-done | bytes 65560
  38.1 0.0 copy-done.7
  38.1 0.0 copy-done.8
  38.1 1.8 %shard_map.73 = f32[4,32,512]{2,1,0:T(8,128)} custom-call(s32[1,2]{1,0:T(1,128)} %ids_ref.5, f32[4,32,512]{2,1,0:T(8,128)} %bitcast.7, f32[32,512]{1,0:T(8,128)} %get-tuple-element.24.refs_0_, f32[32,512]{1,0:T(8,128)} %copy-done.5, f32[32,512]{1,0:T(8,128)} %copy-done.7, f32[32,512]{1,0:T(8,128)} %copy-done.8), custom_call_target="tpu_custom_call" | custom-call | bytes 786440 | tf_op jit(solution)/shard_map/pallas_call | solution.py:141
Async XLA Ops:
  7.7 16.9 %collective-permute-start.3 = (f32[32,512]{1,0:T(8,128)}, f32[32,512]{1,0:T(8,128)S(1)}, u32[]{:S(2)}, u32[]{:S(2)}) collective-permute-start(f32[32,512]{1,0:T(8,128)} %get-tuple-element.21), channel_id=1, source_target_pairs={{0,4},{4,8},{8,12},{12,0},{1,5},{5,9},{9,13},{13,1},{2,6},{6,10},{... | collective-permute-start | bytes 196616 | tf_op jit(solution)/shard_map/ppermute | solution.py:156
  10.8 16.7 %collective-permute-start.4 = (f32[32,512]{1,0:T(8,128)}, f32[32,512]{1,0:T(8,128)S(1)}, u32[]{:S(2)}, u32[]{:S(2)}) collective-permute-start(f32[32,512]{1,0:T(8,128)} %get-tuple-element.22), channel_id=1, source_target_pairs={{0,8},{4,12},{8,0},{12,4},{1,9},{5,13},{9,1},{13,5},{2,10},{6,14},... | collective-permute-start | bytes 196616 | tf_op jit(solution)/shard_map/ppermute | solution.py:156
  13.4 14.1 %collective-permute-start.5 = (f32[32,512]{1,0:T(8,128)}, f32[32,512]{1,0:T(8,128)S(1)}, u32[]{:S(2)}, u32[]{:S(2)}) collective-permute-start(f32[32,512]{1,0:T(8,128)} %get-tuple-element.23), channel_id=1, source_target_pairs={{0,12},{4,0},{8,4},{12,8},{1,13},{5,1},{9,5},{13,9},{2,14},{6,2},{... | collective-permute-start | bytes 196616 | tf_op jit(solution)/shard_map/ppermute | solution.py:156
  21.8 10.3 %collective-permute-start = (f32[32,512]{1,0:T(8,128)}, f32[32,512]{1,0:T(8,128)S(1)}, u32[]{:S(2)}, u32[]{:S(2)}) collective-permute-start(f32[32,512]{1,0:T(8,128)} %get-tuple-element.16), channel_id=1, source_target_pairs={{0,4},{4,8},{8,12},{12,0},{1,5},{5,9},{9,13},{13,1},{2,6},{6,10},{... | collective-permute-start | bytes 196616 | tf_op jit(solution)/shard_map/ppermute | solution.py:156
  22.6 12.5 %collective-permute-start.1 = (f32[32,512]{1,0:T(8,128)}, f32[32,512]{1,0:T(8,128)S(1)}, u32[]{:S(2)}, u32[]{:S(2)}) collective-permute-start(f32[32,512]{1,0:T(8,128)} %get-tuple-element.17), channel_id=1, source_target_pairs={{0,8},{4,12},{8,0},{12,4},{1,9},{5,13},{9,1},{13,5},{2,10},{6,14},... | collective-permute-start | bytes 196616 | tf_op jit(solution)/shard_map/ppermute | solution.py:156
  22.9 1.7 %copy-start.9 = (f32[32,512]{1,0:T(8,128)S(1)}, f32[32,512]{1,0:T(8,128)}, u32[]{:S(2)}) copy-start(f32[32,512]{1,0:T(8,128)} %get-tuple-element.18) | copy-start | bytes 196612
  24.6 2.9 %copy-start.3 = (f32[32,512]{1,0:T(8,128)}, f32[32,512]{1,0:T(8,128)S(1)}, u32[]{:S(2)}) copy-start(f32[32,512]{1,0:T(8,128)S(1)} %collective-permute-done.3.refs_0_) | copy-start | bytes 196612
  24.7 10.4 %collective-permute-start.2 = (f32[32,512]{1,0:T(8,128)S(1)}, f32[32,512]{1,0:T(8,128)S(1)}, u32[]{:S(2)}, u32[]{:S(2)}) collective-permute-start(f32[32,512]{1,0:T(8,128)S(1)} %copy-done.9), channel_id=1, source_target_pairs={{0,12},{4,0},{8,4},{12,8},{1,13},{5,1},{9,5},{13,9},{2,14},{6,2},{... | collective-permute-start | bytes 196616 | tf_op jit(solution)/shard_map/ppermute | solution.py:156
  27.5 0.6 %copy-start.4 = (f32[32,512]{1,0:T(8,128)}, f32[32,512]{1,0:T(8,128)S(1)}, u32[]{:S(2)}) copy-start(f32[32,512]{1,0:T(8,128)S(1)} %collective-permute-done.4.refs_1_) | copy-start | bytes 196612
  27.5 0.6 %copy-start.6 = (f32[32,512]{1,0:T(8,128)}, f32[32,512]{1,0:T(8,128)S(1)}, u32[]{:S(2)}) copy-start(f32[32,512]{1,0:T(8,128)S(1)} %collective-permute-done.5.refs_2_) | copy-start | bytes 196612
  30.1 7.4 %collective-permute-start.6 = (f32[32,512]{1,0:T(8,128)}, f32[32,512]{1,0:T(8,128)S(1)}, u32[]{:S(2)}, u32[]{:S(2)}) collective-permute-start(f32[32,512]{1,0:T(8,128)} %get-tuple-element.25), channel_id=1, source_target_pairs={{0,4},{4,8},{8,12},{12,0},{1,5},{5,9},{9,13},{13,1},{2,6},{6,10},{... | collective-permute-start | bytes 196616 | tf_op jit(solution)/shard_map/ppermute | solution.py:156
  30.7 6.8 %collective-permute-start.7 = (f32[32,512]{1,0:T(8,128)}, f32[32,512]{1,0:T(8,128)S(1)}, u32[]{:S(2)}, u32[]{:S(2)}) collective-permute-start(f32[32,512]{1,0:T(8,128)} %get-tuple-element.26), channel_id=1, source_target_pairs={{0,8},{4,12},{8,0},{12,4},{1,9},{5,13},{9,1},{13,5},{2,10},{6,14},... | collective-permute-start | bytes 196616 | tf_op jit(solution)/shard_map/ppermute | solution.py:156
  32.1 2.9 %copy-start = (f32[32,512]{1,0:T(8,128)}, f32[32,512]{1,0:T(8,128)S(1)}, u32[]{:S(2)}) copy-start(f32[32,512]{1,0:T(8,128)S(1)} %collective-permute-done.refs_0_) | copy-start | bytes 196612
  32.1 5.3 %collective-permute-start.8 = (f32[32,512]{1,0:T(8,128)}, f32[32,512]{1,0:T(8,128)S(1)}, u32[]{:S(2)}, u32[]{:S(2)}) collective-permute-start(f32[32,512]{1,0:T(8,128)} %get-tuple-element.27), channel_id=1, source_target_pairs={{0,12},{4,0},{8,4},{12,8},{1,13},{5,1},{9,5},{13,9},{2,14},{6,2},{... | collective-permute-start | bytes 196616 | tf_op jit(solution)/shard_map/ppermute | solution.py:156
  35.0 0.6 %copy-start.1 = (f32[32,512]{1,0:T(8,128)}, f32[32,512]{1,0:T(8,128)S(1)}, u32[]{:S(2)}) copy-start(f32[32,512]{1,0:T(8,128)S(1)} %collective-permute-done.1.refs_1_) | copy-start | bytes 196612
  35.0 0.6 %copy-start.2 = (f32[32,512]{1,0:T(8,128)}, f32[32,512]{1,0:T(8,128)S(1)}, u32[]{:S(2)}) copy-start(f32[32,512]{1,0:T(8,128)S(1)} %collective-permute-done.2.refs_2_) | copy-start | bytes 196612
  37.5 0.6 %copy-start.5 = (f32[32,512]{1,0:T(8,128)}, f32[32,512]{1,0:T(8,128)S(1)}, u32[]{:S(2)}) copy-start(f32[32,512]{1,0:T(8,128)S(1)} %collective-permute-done.6.refs_1_) | copy-start | bytes 196612
  37.5 0.6 %copy-start.7 = (f32[32,512]{1,0:T(8,128)}, f32[32,512]{1,0:T(8,128)S(1)}, u32[]{:S(2)}) copy-start(f32[32,512]{1,0:T(8,128)S(1)} %collective-permute-done.7.refs_2_) | copy-start | bytes 196612
  37.5 0.7 %copy-start.8 = (f32[32,512]{1,0:T(8,128)}, f32[32,512]{1,0:T(8,128)S(1)}, u32[]{:S(2)}) copy-start(f32[32,512]{1,0:T(8,128)S(1)} %collective-permute-done.8.refs_3_) | copy-start | bytes 196612

commit v4 on v3

--- a/solution.py
+++ b/solution.py
@@ -10,10 +10,11 @@
 ANYWHERE = pl.BlockSpec(memory_space=pl.ANY)
 
 DIRECT_MEMBERS = 8
-
-
-def wrap(index, members):
-    return lax.rem(index + 2 * members, members)
+KERNEL_VMEM = 8 * 2**20
+
+
+def rounds_of(members):
+    return range(members - 1, 0, -1)
 
 
 def plan_kernel(ids_ref, generator_ref, parity_ref, base_ref, solve_ref, generator_rows_ref):
@@ -64,11 +65,10 @@
     return [(c, rows_ref[c]) for c in range(rows_ref.shape[0])]
 
 
-def shifted_rows(own_ref, refs):
-    members = len(refs) + 1
-    me = lax.axis_index("code")
-    rows = [(me, own_ref[me])]
-    return rows + [(wrap(me - s, members), ref[...]) for s, ref in enumerate(refs, 1)]
+def paired_rows(own_ref, refs):
+    me = lax.axis_index("code")
+    rounds = rounds_of(own_ref.shape[0])
+    return [(me, own_ref[me])] + [(me ^ r, ref[...]) for r, ref in zip(rounds, refs)]
 
 
 def rebuild_whole_kernel(ids_ref, base_ref, solve_ref, rows_ref, out_ref):
@@ -77,62 +77,56 @@
         out_ref[ids_ref[0, k]] = base_ref[k] - weigh(solve_ref, k * len(rows), rows)
 
 
-def rebuild_shifted_kernel(ids_ref, base_ref, solve_ref, own_ref, *refs):
+def rebuild_paired_kernel(ids_ref, base_ref, solve_ref, own_ref, *refs):
     members = own_ref.shape[0]
-    rows = shifted_rows(own_ref, refs[: members - 1])
+    rows = paired_rows(own_ref, refs[: members - 1])
     outs = refs[members - 1 :]
     me = lax.axis_index("code")
     for k in range(2):
         rebuilt = base_ref[k] - weigh(solve_ref, k * members, rows)
-        for s, out_ref in enumerate(outs):
-
-            @pl.when(wrap(me + s, members) == ids_ref[0, k])
+        for r, out_ref in zip((0, *rounds_of(members)), outs):
+
+            @pl.when((me ^ r) == ids_ref[0, k])
             def _():
                 out_ref[...] = rebuilt
 
 
-def parity_whole_kernel(generator_rows_ref, rows_ref, out_ref):
-    parity_into(out_ref, generator_rows_ref, whole_rows(rows_ref))
-
-
-def parity_shifted_kernel(generator_rows_ref, own_ref, *refs):
-    parity_into(refs[-1], generator_rows_ref, shifted_rows(own_ref, refs[:-1]))
-
-
-def parity_into(out_ref, generator_rows_ref, rows):
+def parity_kernel(generator_rows_ref, rows_ref, out_ref):
+    rows = whole_rows(rows_ref)
     width = generator_rows_ref.shape[1]
     for j in range(out_ref.shape[1] // width):
         out_ref[:, j * width : (j + 1) * width] = weigh(generator_rows_ref, j * len(rows), rows)
 
 
-def cut_kernel(blocks_ref, *refs):
-    outs, sems = refs[:-1], refs[-1]
-    members = len(outs) + 1
-    me = lax.axis_index("code")
-    copies = [
-        pltpu.make_async_copy(blocks_ref.at[wrap(me + s, members)], out, sems.at[s - 1])
-        for s, out in enumerate(outs, 1)
-    ]
+def run_copies(pairs, sems):
+    copies = [pltpu.make_async_copy(*pair, sems.at[i]) for i, pair in enumerate(pairs)]
     for copy in copies:
         copy.start()
     for copy in copies:
         copy.wait()
 
 
+def cut_kernel(blocks_ref, *refs):
+    outs, sems = refs[:-1], refs[-1]
+    me = lax.axis_index("code")
+    rounds = rounds_of(blocks_ref.shape[0])
+    run_copies([(blocks_ref.at[me ^ r], out) for r, out in zip(rounds, outs)], sems)
+
+
 def restore_kernel(ids_ref, earlier_ref, *refs):
-    pieces, out_ref = refs[:-1], refs[-1]
+    *pieces, out_ref, sems = refs
     members = len(pieces)
     me = lax.axis_index("code")
     lost = jnp.logical_or(me == ids_ref[0, 0], me == ids_ref[0, 1])
 
     @pl.when(lost)
     def _():
-        for s, piece in enumerate(pieces):
-            out_ref[wrap(me - s, members)] = piece[...]
+        places = [out_ref.at[me ^ r] for r in (0, *rounds_of(members))]
+        run_copies(zip(pieces, places), sems)
 
     @pl.when(jnp.logical_not(lost))
     def _():
-        out_ref[...] = earlier_ref[...]
+        run_copies([(earlier_ref, out_ref)], sems)
 
 
 def call(kernel, specs, outs, args, flops, **options):
@@ -142,6 +136,7 @@
         kernel,
         in_specs=specs,
         out_shape=outs,
+        compiler_params=pltpu.CompilerParams(vmem_limit_bytes=KERNEL_VMEM),
         cost_estimate=pl.CostEstimate(flops=flops, bytes_accessed=4 * total, transcendentals=0),
         **options,
     )(*args)
@@ -151,23 +146,22 @@
     return jax.ShapeDtypeStruct(shape, jnp.float32)
 
 
-def send(pieces, members):
+def trade(pieces, members):
     return [
-        lax.ppermute(piece, "code", [(d, (d + s) % members) for d in range(members)])
-        for s, piece in enumerate(pieces, 1)
+        lax.ppermute(piece, "code", [(d, d ^ r) for d in range(members)])
+        for r, piece in zip(rounds_of(members), pieces)
     ]
 
 
 def cut(blocks):
-    members = blocks.shape[0]
+    others = blocks.shape[0] - 1
     return call(
         cut_kernel,
         [ANYWHERE],
-        [floats(*blocks.shape[1:])] * (members - 1),
+        [floats(*blocks.shape[1:])] * others,
         (blocks,),
         0,
-        out_specs=[ANYWHERE] * (members - 1),
-        scratch_shapes=[pltpu.SemaphoreType.DMA((members - 1,))],
+        scratch_shapes=[pltpu.SemaphoreType.DMA((others,))],
     )
 
 
@@ -180,14 +174,13 @@
     blocks = (members, own_rows, width)
     earlier = previous_slab.reshape(blocks)
     current = state_slab.reshape(blocks)
-    direct = members <= DIRECT_MEMBERS
+    direct = members <= DIRECT_MEMBERS and members & (members - 1) == 0
 
     if direct:
-        earlier_rows = send(cut(earlier), members)
-        current_rows = send(cut(current), members)
+        earlier_rows = trade(cut(earlier), members)
     else:
         earlier_rows = lax.all_to_all(earlier, "code", 0, 0, tiled=True)
-        current_rows = lax.all_to_all(current, "code", 0, 0, tiled=True)
+    current_rows = lax.all_to_all(current, "code", 0, 0, tiled=True)
     base, solve_rows, generator_rows = call(
         plan_kernel,
         [IN_SMEM, IN_SMEM, IN_VMEM],
@@ -195,31 +188,23 @@
         (failed_ids, generator, previous_parity[0]),
         4 * spans * own_rows * width,
     )
-    parity_shape = floats(own_rows, spans * width)
     rebuild_cost = 4 * slab_rows * width
-    parity_cost = 2 * spans * slab_rows * width
     if direct:
         outgoing = call(
-            rebuild_shifted_kernel,
+            rebuild_paired_kernel,
             [IN_SMEM] + [IN_VMEM] * (members + 2),
             [floats(own_rows, width)] * members,
             (failed_ids, base, solve_rows, earlier, *earlier_rows),
             rebuild_cost,
         )
-        incoming = send(outgoing[1:], members)
-        new_parity = call(
-            parity_shifted_kernel,
-            [IN_VMEM] * (members + 1),
-            parity_shape,
-            (generator_rows, current, *current_rows),
-            parity_cost,
-        )
         restored_state = call(
             restore_kernel,
             [IN_SMEM] + [IN_VMEM] * (members + 1),
             floats(*blocks),
-            (failed_ids, earlier, outgoing[0], *incoming),
+            (failed_ids, earlier, outgoing[0], *trade(outgoing[1:], members)),
             0,
+            out_specs=ANYWHERE,
+            scratch_shapes=[pltpu.SemaphoreType.DMA((members,))],
         )
     else:
         outgoing = call(
@@ -230,15 +215,15 @@
             rebuild_cost,
         )
         incoming = lax.all_to_all(outgoing, "code", 0, 0, tiled=True)
-        new_parity = call(
-            parity_whole_kernel,
-            [IN_VMEM] * 2,
-            parity_shape,
-            (generator_rows, current_rows),
-            parity_cost,
-        )
         lost = (position == failed_ids[0, 0]) | (position == failed_ids[0, 1])
         restored_state = jnp.where(lost, incoming, earlier)
+    new_parity = call(
+        parity_kernel,
+        [IN_VMEM] * 2,
+        floats(own_rows, spans * width),
+        (generator_rows, current_rows),
+        2 * spans * slab_rows * width,
+    )
     return (new_parity[None], restored_state.reshape(state_slab.shape))
 
 

time: 40.1 us -> 32.5 us (0.81)
  Pallas kernels: 21.3 us -> 3.63 us
  waiting for transfers between devices: 0.02 us -> 12.4 us
  local copies, waits for them, and re-layouts: 1.91 us -> 0.03 us
  starting transfers between devices: 15.9 us -> 15.4 us
    pallas_call x6 -> x5, Pallas kernels: 21.3 us -> 3.63 us  [call(): pl.pallas_call(kernel, in_specs=specs, out_shape=outs, compiler_params=pl...]
    ppermute x9 -> x6, waiting for transfers between devices: 0.02 us -> 12.4 us  [trade(): lax.ppermute(piece, 'code', [(d, d ^ r) for d in range(members)])]
    ppermute x9 -> x6, starting transfers between devices: 15.9 us -> 8.99 us  [trade(): lax.ppermute(piece, 'code', [(d, d ^ r) for d in range(members)])]
    all_to_all x0 -> x1, starting transfers between devices: none -> 6.46 us  [local(): current_rows = lax.all_to_all(current, 'code', 0, 0, tiled=True)]
    unnamed x20 -> x8, local copies, waits for them, and re-layouts: 1.91 us -> 0.03 us
  transfers between devices with their start and end apart: 9 -> 7, of which waited for: 0 -> 4; matrix products, arithmetic and copies ran while one was open for 0% -> 0% of each run, Pallas kernels for 31% -> 9%
where the time goes in v4:
time: 32.5 us; the launch traced here: 32.2 us
  starting transfers between devices  15.4 us (47%)
  waiting for transfers between devices  12.4 us (38%)
  Pallas kernels  3.63 us (11%)
  between operations  0.69 us (2%)
    ppermute x6, waiting for transfers between devices, trade(): lax.ppermute(piece, 'code', [(d, d ^ r) for d in range(members)])  12.4 us
    ppermute x6, starting transfers between devices, trade(): lax.ppermute(piece, 'code', [(d, d ^ r) for d in range(members)])  8.99 us
    all_to_all x1, starting transfers between devices, local(): current_rows = lax.all_to_all(current, 'code', 0, 0, tiled=True)  6.46 us
    pallas_call x5, Pallas kernels, call(): pl.pallas_call(kernel, in_specs=specs, out_shape=outs, compiler_params=pl...  3.63 us
  transfers between devices with their start and end apart: 7, of which 4 were waited for; matrix products, arithmetic and copies ran while one was open for 0% of the time, Pallas kernels for 9%

profile of v4, /device:TPU:0, one launch (start us, length us, event | category | flops | bytes accessed | tf_op | source)
XLA Modules:
  0.0 32.2 jit_solution(7769982010596784281)
XLA Ops:
  0.6 0.0 copy-start
  0.6 6.5 %all-to-all-start = ((f32[4,32,512]{2,1,0:T(8,128)}), f32[4,32,512]{2,1,0:T(8,128)S(1)}, u32[]{:S(2)}, u32[]{:S(2)}) async-start(f32[4,32,512]{2,1,0:T(8,128)} %bitcast.9), calls=%async_computation | async-start | bytes 524288 | tf_op jit(solution)/shard_map/all_to_all | solution.py:183
  7.1 0.0 copy-start.1
  7.1 0.0 copy-done
  7.1 0.3 shard_map.70
  7.4 3.9 %collective-permute-start = (f32[32,512]{1,0:T(8,128)S(1)}, f32[32,512]{1,0:T(8,128)S(1)}, u32[]{:S(2)}, u32[]{:S(2)}) collective-permute-start(f32[32,512]{1,0:T(8,128)S(1)} %get-tuple-element.15), channel_id=1, source_target_pairs={{0,12},{4,8},{8,4},{12,0},{1,13},{5,9},{9,5},{13,1},{2,14},{6,10},... | collective-permute-start | bytes 196616 | tf_op jit(solution)/shard_map/ppermute | solution.py:151
  11.3 0.0 copy-start.3
  11.3 0.0 collective-permute-start.1
  11.3 0.0 copy-start.2
  11.3 0.6 %collective-permute-start.2 = (f32[32,512]{1,0:T(8,128)S(1)}, f32[32,512]{1,0:T(8,128)S(1)}, u32[]{:S(2)}, u32[]{:S(2)}) collective-permute-start(f32[32,512]{1,0:T(8,128)S(1)} %get-tuple-element.17), channel_id=1, source_target_pairs={{0,4},{4,0},{8,12},{12,8},{1,5},{5,1},{9,13},{13,9},{2,6},{6,2},{1... | collective-permute-start | bytes 196616 | tf_op jit(solution)/shard_map/ppermute | solution.py:151
  11.9 0.0 copy-done.1
  11.9 0.0 copy-done.3
  12.0 0.0 copy-done.2
  12.0 0.6 %shard_map.68 = (f32[2,32,512]{2,1,0:T(8,128)S(1)}, f32[8,512]{1,0:T(8,128)S(1)}, f32[16,512]{1,0:T(8,128)S(1)}) custom-call(s32[1,2]{1,0:T(1,128)S(1)} %copy-done.2, f32[4,4]{1,0:T(4,128)S(1)} %copy-done.3, f32[32,2048]{1,0:T(8,128)S(1)} %bitcast.8), custom_call_target="tpu_custom_call" | custom-call | flops 262144 | bytes 442440 | tf_op jit(solution)/shard_map/pallas_call | solution.py:135
  12.6 5.7 %collective-permute-done.refs_0_ = f32[32,512]{1,0:T(8,128)S(1)} collective-permute-done((f32[32,512]{1,0:T(8,128)S(1)}, f32[32,512]{1,0:T(8,128)S(1)}, u32[]{:S(2)}, u32[]{:S(2)}) %collective-permute-start) | collective-permute-done | bytes 65568 | tf_op jit(solution)/shard_map/ppermute | solution.py:151
  18.3 3.3 %collective-permute-done.1.refs_1_ = f32[32,512]{1,0:T(8,128)S(1)} collective-permute-done((f32[32,512]{1,0:T(8,128)S(1)}, f32[32,512]{1,0:T(8,128)S(1)}, u32[]{:S(2)}, u32[]{:S(2)}) %collective-permute-start.1) | collective-permute-done | bytes 65568 | tf_op jit(solution)/shard_map/ppermute | solution.py:151
  21.6 0.0 collective-permute-done.2.refs_2_
  21.6 0.6 %shard_map.71 = (f32[32,512]{1,0:T(8,128)S(1)}, f32[32,512]{1,0:T(8,128)S(1)}, f32[32,512]{1,0:T(8,128)S(1)}, f32[32,512]{1,0:T(8,128)S(1)}) custom-call(s32[1,2]{1,0:T(1,128)S(1)} %copy-done.2, f32[2,32,512]{2,1,0:T(8,128)S(1)} %get-tuple-element.13.base_ref, f32[8,512]{1,0:T(8,128)S(1)} %get-tuple-element.14.solve_ref, f32[4,32,512]{2,1,0:T(8,128)S(1)} %bitcast.6, ...), custom_call_target="tpu_custom_call" | custom-call | flops 262144 | bytes 868360 | tf_op jit(solution)/shard_map/pallas_call | solution.py:135
  22.3 1.5 %collective-permute-start.3 = (f32[32,512]{1,0:T(8,128)S(1)}, f32[32,512]{1,0:T(8,128)S(1)}, u32[]{:S(2)}, u32[]{:S(2)}) collective-permute-start(f32[32,512]{1,0:T(8,128)S(1)} %get-tuple-element.19), channel_id=1, source_target_pairs={{0,12},{4,8},{8,4},{12,0},{1,13},{5,9},{9,5},{13,1},{2,14},{6,10},... | collective-permute-start | bytes 196616 | tf_op jit(solution)/shard_map/ppermute | solution.py:151
  23.8 0.0 collective-permute-start.4
  23.8 3.0 %collective-permute-start.5 = (f32[32,512]{1,0:T(8,128)S(1)}, f32[32,512]{1,0:T(8,128)S(1)}, u32[]{:S(2)}, u32[]{:S(2)}) collective-permute-start(f32[32,512]{1,0:T(8,128)S(1)} %get-tuple-element.21), channel_id=1, source_target_pairs={{0,4},{4,0},{8,12},{12,8},{1,5},{5,1},{9,13},{13,9},{2,6},{6,2},{1... | collective-permute-start | bytes 196616 | tf_op jit(solution)/shard_map/ppermute | solution.py:151
  26.7 1.9 %collective-permute-done.3.refs_1_ = f32[32,512]{1,0:T(8,128)S(1)} collective-permute-done((f32[32,512]{1,0:T(8,128)S(1)}, f32[32,512]{1,0:T(8,128)S(1)}, u32[]{:S(2)}, u32[]{:S(2)}) %collective-permute-start.3) | collective-permute-done | bytes 65568 | tf_op jit(solution)/shard_map/ppermute | solution.py:151
  28.7 1.5 %collective-permute-done.4.refs_2_ = f32[32,512]{1,0:T(8,128)S(1)} collective-permute-done((f32[32,512]{1,0:T(8,128)S(1)}, f32[32,512]{1,0:T(8,128)S(1)}, u32[]{:S(2)}, u32[]{:S(2)}) %collective-permute-start.4) | collective-permute-done | bytes 65568 | tf_op jit(solution)/shard_map/ppermute | solution.py:151
  30.1 0.0 collective-permute-done.5.refs_3_
  30.1 1.3 %shard_map.72 = f32[4,32,512]{2,1,0:T(8,128)} custom-call(s32[1,2]{1,0:T(1,128)S(1)} %copy-done.2, f32[4,32,512]{2,1,0:T(8,128)S(1)} %bitcast.7, f32[32,512]{1,0:T(8,128)S(1)} %get-tuple-element.18.refs_0_, f32[32,512]{1,0:T(8,128)S(1)} %collective-permute-done.3.refs_1_, f32[32,512]{1,0:T(8,128)S(1)} %collective-permute-done.4.refs_2_, ...), custom_call_target="tpu_custom_call" | custom-call | bytes 786440 | tf_op jit(solution)/shard_map/pallas_call | solution.py:135
  31.4 0.0 all-to-all-done.rows_ref
  31.5 0.8 %shard_map.69 = f32[32,2048]{1,0:T(8,128)} custom-call(f32[16,512]{1,0:T(8,128)S(1)} %get-tuple-element.12.generator_rows_ref, f32[4,32,512]{2,1,0:T(8,128)S(1)} %all-to-all-done.rows_ref), custom_call_target="tpu_custom_call" | custom-call | flops 524288 | bytes 557056 | tf_op jit(solution)/shard_map/pallas_call | solution.py:135
Async XLA Ops:
  0.6 6.5 %copy-start = (f32[1,1,128,512]{3,2,1,0:T(8,128)S(1)}, f32[1,1,128,512]{3,2,1,0:T(8,128)}, u32[]{:S(2)}) copy-start(f32[1,1,128,512]{3,2,1,0:T(8,128)} %param.6) | copy-start | bytes 786436
  0.6 30.8 %all-to-all-start = ((f32[4,32,512]{2,1,0:T(8,128)}), f32[4,32,512]{2,1,0:T(8,128)S(1)}, u32[]{:S(2)}, u32[]{:S(2)}) async-start(f32[4,32,512]{2,1,0:T(8,128)} %bitcast.9), calls=%async_computation | async-start | bytes 524288 | tf_op jit(solution)/shard_map/all_to_all | solution.py:183
  7.1 4.8 %copy-start.1 = (f32[1,32,2048]{2,1,0:T(8,128)S(1)}, f32[1,32,2048]{2,1,0:T(8,128)}, u32[]{:S(2)}) copy-start(f32[1,32,2048]{2,1,0:T(8,128)} %param.7) | copy-start | bytes 786436
  7.4 10.9 %collective-permute-start = (f32[32,512]{1,0:T(8,128)S(1)}, f32[32,512]{1,0:T(8,128)S(1)}, u32[]{:S(2)}, u32[]{:S(2)}) collective-permute-start(f32[32,512]{1,0:T(8,128)S(1)} %get-tuple-element.15), channel_id=1, source_target_pairs={{0,12},{4,8},{8,4},{12,0},{1,13},{5,9},{9,5},{13,1},{2,14},{6,10},... | collective-permute-start | bytes 196616 | tf_op jit(solution)/shard_map/ppermute | solution.py:151
  11.3 0.7 %copy-start.3 = (f32[4,4]{1,0:T(4,128)S(1)}, f32[4,4]{1,0:T(4,128)}, u32[]{:S(2)}) copy-start(f32[4,4]{1,0:T(4,128)} %generator_ref.1) | copy-start | bytes 196
  11.3 10.4 %collective-permute-start.1 = (f32[32,512]{1,0:T(8,128)S(1)}, f32[32,512]{1,0:T(8,128)S(1)}, u32[]{:S(2)}, u32[]{:S(2)}) collective-permute-start(f32[32,512]{1,0:T(8,128)S(1)} %get-tuple-element.16), channel_id=1, source_target_pairs={{0,8},{4,12},{8,0},{12,4},{1,9},{5,13},{9,1},{13,5},{2,10},{6,14},... | collective-permute-start | bytes 196616 | tf_op jit(solution)/shard_map/ppermute | solution.py:151
  11.3 0.7 %copy-start.2 = (s32[1,2]{1,0:T(1,128)S(1)}, s32[1,2]{1,0:T(1,128)}, u32[]{:S(2)}) copy-start(s32[1,2]{1,0:T(1,128)} %ids_ref.5) | copy-start | bytes 28
  11.3 10.4 %collective-permute-start.2 = (f32[32,512]{1,0:T(8,128)S(1)}, f32[32,512]{1,0:T(8,128)S(1)}, u32[]{:S(2)}, u32[]{:S(2)}) collective-permute-start(f32[32,512]{1,0:T(8,128)S(1)} %get-tuple-element.17), channel_id=1, source_target_pairs={{0,4},{4,0},{8,12},{12,8},{1,5},{5,1},{9,13},{13,9},{2,6},{6,2},{1... | collective-permute-start | bytes 196616 | tf_op jit(solution)/shard_map/ppermute | solution.py:151
  22.3 6.4 %collective-permute-start.3 = (f32[32,512]{1,0:T(8,128)S(1)}, f32[32,512]{1,0:T(8,128)S(1)}, u32[]{:S(2)}, u32[]{:S(2)}) collective-permute-start(f32[32,512]{1,0:T(8,128)S(1)} %get-tuple-element.19), channel_id=1, source_target_pairs={{0,12},{4,8},{8,4},{12,0},{1,13},{5,9},{9,5},{13,1},{2,14},{6,10},... | collective-permute-start | bytes 196616 | tf_op jit(solution)/shard_map/ppermute | solution.py:151
  23.8 6.4 %collective-permute-start.4 = (f32[32,512]{1,0:T(8,128)S(1)}, f32[32,512]{1,0:T(8,128)S(1)}, u32[]{:S(2)}, u32[]{:S(2)}) collective-permute-start(f32[32,512]{1,0:T(8,128)S(1)} %get-tuple-element.20), channel_id=1, source_target_pairs={{0,8},{4,12},{8,0},{12,4},{1,9},{5,13},{9,1},{13,5},{2,10},{6,14},... | collective-permute-start | bytes 196616 | tf_op jit(solution)/shard_map/ppermute | solution.py:151
  23.8 6.4 %collective-permute-start.5 = (f32[32,512]{1,0:T(8,128)S(1)}, f32[32,512]{1,0:T(8,128)S(1)}, u32[]{:S(2)}, u32[]{:S(2)}) collective-permute-start(f32[32,512]{1,0:T(8,128)S(1)} %get-tuple-element.21), channel_id=1, source_target_pairs={{0,4},{4,0},{8,12},{12,8},{1,5},{5,1},{9,13},{13,9},{2,6},{6,2},{1... | collective-permute-start | bytes 196616 | tf_op jit(solution)/shard_map/ppermute | solution.py:151

commit v5 on v3

v5 whole, which is shorter than its diff:
```python
import functools

import jax
import jax.numpy as jnp
from jax import lax
from jax.experimental import pallas as pl
from jax.experimental.pallas import tpu as pltpu
from jax.sharding import PartitionSpec as P

IN_VMEM = pl.BlockSpec(memory_space=pltpu.VMEM)
IN_SMEM = pl.BlockSpec(memory_space=pltpu.SMEM)
ANYWHERE = pl.BlockSpec(memory_space=pl.ANY)

DIRECT_MEMBERS = 8
KERNEL_VMEM = 8 * 2**20


def rounds_of(members):
    return range(members - 1, 0, -1)


def order_of(members, direct):
    if not direct:
        return list(range(members))
    me = lax.axis_index("code")
    return [me ^ r for r in (0, *rounds_of(members))]


def plan_kernel(direct, ids_ref, generator_ref, parity_ref, base_ref, table_ref):
    spans, members = generator_ref.shape
    width = base_ref.shape[2]
    first, second = ids_ref[0, 0], ids_ref[0, 1]
    col_first = [generator_ref[j, first] for j in range(spans)]
    col_second = [generator_ref[j, second] for j in range(spans)]
    gram_first = sum(x * x for x in col_first)
    gram_cross = sum(x * y for x, y in zip(col_first, col_second))
    gram_second = sum(y * y for y in col_second)
    determinant = gram_first * gram_second - gram_cross * gram_cross

    def spread(value):
        return jnp.full((1, width), value, jnp.float32)

    def put(row, value):
        table_ref[row : row + 1, :] = value

    over = spread(determinant)
    weights = [
        [spread(gram_second * x - gram_cross * y) / over for x, y in zip(col_first, col_second)],
        [spread(gram_first * y - gram_cross * x) / over for x, y in zip(col_first, col_second)],
    ]
    for k in range(2):
        base_ref[k] = sum(
            weights[k][j] * parity_ref[:, j * width : (j + 1) * width] for j in range(spans)
        )
    for i, c in enumerate(order_of(members, direct)):
        column = [generator_ref[j, c] for j in range(spans)]
        alive = jnp.logical_and(first != c, second != c)
        for k in range(2):
            put(
                k * members + i,
                sum(weights[k][j] * jnp.where(alive, column[j], 0.0) for j in range(spans)),
            )
        for j in range(spans):
            put((2 + j) * members + i, spread(column[j]))
        put((2 + spans) * members + i, spread(jnp.where(first == c, 1.0, 0.0)))
    me = lax.axis_index("code")
    lost = jnp.logical_or(first == me, second == me)
    put((3 + spans) * members, spread(jnp.where(lost, 1.0, 0.0)))


def weigh(table_ref, start, rows):
    total = None
    for i, block in enumerate(rows):
        term = table_ref[start + i : start + i + 1, :] * block
        total = term if total is None else total + term
    return total


def rebuilt_for(base_ref, table_ref, rows):
    members = len(rows)
    rebuilt = [base_ref[k] - weigh(table_ref, k * members, rows) for k in range(2)]
    picks = table_ref.shape[0] - 1 - members
    return [
        jnp.where(table_ref[picks + i : picks + i + 1, :] > 0.5, *rebuilt) for i in range(members)
    ]


def rebuild_whole_kernel(base_ref, table_ref, rows_ref, out_ref):
    rows = [rows_ref[c] for c in range(rows_ref.shape[0])]
    for c, block in enumerate(rebuilt_for(base_ref, table_ref, rows)):
        out_ref[c] = block


def parity_whole_kernel(table_ref, rows_ref, out_ref):
    parity_into(out_ref, table_ref, [rows_ref[c] for c in range(rows_ref.shape[0])])


def parity_into(out_ref, table_ref, rows):
    members, width = len(rows), table_ref.shape[1]
    for j in range(out_ref.shape[1] // width):
        out_ref[:, j * width : (j + 1) * width] = weigh(table_ref, (2 + j) * members, rows)


def cut_kernel(rounds, blocks_ref, *refs):
    outs, sems = refs[-1 - len(rounds) : -1], refs[-1]
    me = lax.axis_index("code")
    copies = [
        pltpu.make_async_copy(blocks_ref.at[me ^ r], out, sems.at[i])
        for i, (r, out) in enumerate(zip(rounds, outs))
    ]
    for copy in copies:
        copy.start()
    for copy in copies:
        copy.wait()


def rebuild_paired_kernel(base_ref, table_ref, *refs):
    rows, outs = refs[: len(refs) // 2], refs[len(refs) // 2 :]
    for out_ref, block in zip(outs, rebuilt_for(base_ref, table_ref, [r[...] for r in rows])):
        out_ref[...] = block


def parity_paired_kernel(table_ref, *refs):
    rows, out_ref, done_ref = refs[:-2], refs[-2], refs[-1]
    parity_into(out_ref, table_ref, [r[...] for r in rows])
    done_ref[...] = jnp.zeros(done_ref.shape, done_ref.dtype)


def restore_kernel(table_ref, earlier_ref, held_back_by, *refs):
    pieces, out_ref = refs[:-1], refs[-1]
    members = len(pieces)
    last = table_ref.shape[0] - 1
    lost = table_ref[last : last + 1, :] > 0.5
    for c, piece in zip(order_of(members, True), pieces):
        out_ref[c] = jnp.where(lost, piece[...], earlier_ref[c])


def call(kernel, specs, outs, args, flops, **options):
    total = sum(x.size for x in args) + sum(o.size for o in jax.tree.leaves(outs))
    return pl.pallas_call(
        kernel,
        in_specs=specs,
        out_specs=jax.tree.map(lambda _: IN_VMEM, outs),
        out_shape=outs,
        compiler_params=pltpu.CompilerParams(vmem_limit_bytes=KERNEL_VMEM),
        cost_estimate=pl.CostEstimate(flops=flops, bytes_accessed=4 * total, transcendentals=0),
        **options,
    )(*args)


def floats(*shape):
    return jax.ShapeDtypeStruct(shape, jnp.float32)


def trade(pieces, rounds, members):
    return [
        lax.ppermute(piece, "code", [(d, d ^ r) for d in range(members)])
        for r, piece in zip(rounds, pieces)
    ]


def cut(blocks, rounds, *held_back_by):
    return call(
        functools.partial(cut_kernel, rounds),
        [ANYWHERE] * (1 + len(held_back_by)),
        [floats(*blocks.shape[1:])] * len(rounds),
        (blocks, *held_back_by),
        0,
        scratch_shapes=[pltpu.SemaphoreType.DMA((len(rounds),))],
    )


def local(state_slab, previous_slab, previous_parity, generator, failed_ids):
    position = lax.axis_index("code")
    members = lax.axis_size("code")
    slab_rows, width = state_slab.shape[2:]
    spans = generator.shape[0]
    own_rows = slab_rows // members
    blocks = (members, own_rows, width)
    earlier = previous_slab.reshape(blocks)
    current = state_slab.reshape(blocks)
    direct = 4 <= members <= DIRECT_MEMBERS and members & (members - 1) == 0

    base, table = call(
        functools.partial(plan_kernel, direct),
        [IN_SMEM, IN_SMEM, IN_VMEM],
        (floats(2, own_rows, width), floats((3 + spans) * members + 1, width)),
        (failed_ids, generator, previous_parity[0]),
        4 * spans * own_rows * width,
    )
    parity_shape = floats(own_rows, spans * width)
    rebuild_cost = 4 * slab_rows * width
    parity_cost = 2 * spans * slab_rows * width
    if direct:
        rounds = list(rounds_of(members))
        block = floats(own_rows, width)
        own_earlier, *cut_earlier = cut(earlier, [0] + rounds)
        earlier_rows = trade(cut_earlier, rounds, members)
        own_current, *cut_current = cut(current, [0] + rounds, earlier_rows[0])
        outgoing = call(
            rebuild_paired_kernel,
            [IN_VMEM] * (members + 2),
            [block] * members,
            (base, table, own_earlier, *earlier_rows),
            rebuild_cost,
        )
        incoming = trade(outgoing[1:], rounds, members)
        current_rows = [own_current, *trade(cut_current, rounds, members)]
        new_parity, parity_done = call(
            parity_paired_kernel,
            [IN_VMEM] * (members + 1),
            (parity_shape, floats(8, 128)),
            (table, *current_rows),
            parity_cost,
        )
        restored_state = call(
            restore_kernel,
            [IN_VMEM, IN_VMEM, ANYWHERE] + [IN_VMEM] * members,
            floats(*blocks),
            (table, earlier, parity_done, outgoing[0], *incoming),
            0,
        )
    else:
        earlier_rows = lax.all_to_all(earlier, "code", 0, 0, tiled=True)
        current_rows = lax.all_to_all(current, "code", 0, 0, tiled=True)
        outgoing = call(
            rebuild_whole_kernel,
            [IN_VMEM] * 3,
            floats(*blocks),
            (base, table, earlier_rows),
            rebuild_cost,
        )
        incoming = lax.all_to_all(outgoing, "code", 0, 0, tiled=True)
        lost = (position == failed_ids[0, 0]) | (position == failed_ids[0, 1])
        restored_state = jnp.where(lost, incoming, earlier)
        new_parity = call(
            parity_whole_kernel,
            [IN_VMEM] * 2,
            parity_shape,
            (table, current_rows),
            parity_cost,
        )
    return (new_parity[None], restored_state.reshape(state_slab.shape))


def solution(mesh):
    placed = (
        P(("grp", "rep"), "code", None, None),
        P(("grp", "rep"), "code", None, None),
        P(("grp", "rep"), "code", None),
        P(),
        P(("grp", "rep"), None),
    )
    return jax.shard_map(
        local,
        mesh=mesh,
        in_specs=placed,
        out_specs=(P(("grp", "rep"), "code", None), P(("grp", "rep"), "code", None, None)),
        check_vma=False,
    )
```

time: 40.1 us -> 25.8 us (0.64)
  Pallas kernels: 21.3 us -> 2.96 us
  waiting for transfers between devices: 0.02 us -> 5.29 us
  local copies, waits for them, and re-layouts: 1.91 us -> 0.97 us
    pallas_call x6, Pallas kernels: 21.3 us -> 2.96 us  [call(): pl.pallas_call(kernel, in_specs=specs, out_specs=jax.tree.map(lambda _: I...]
    ppermute x9, waiting for transfers between devices: 0.02 us -> 5.29 us  [trade(): lax.ppermute(piece, 'code', [(d, d ^ r) for d in range(members)])]
    unnamed x20 -> x12, local copies, waits for them, and re-layouts: 1.91 us -> 0.97 us
  transfers between devices with their start and end apart: 9 -> 9, of which waited for: 0 -> 4; matrix products, arithmetic and copies ran while one was open for 0% -> 0% of each run, Pallas kernels for 31% -> 7%
where the time goes in v5:
time: 25.8 us; the launch traced here: 25.6 us
  starting transfers between devices  15.7 us (61%)
  waiting for transfers between devices  5.29 us (21%)
  Pallas kernels  2.96 us (11%)
  local copies, waits for them, and re-layouts  0.97 us (4%)
  between operations  0.7 us (3%)
    ppermute x9, starting transfers between devices, trade(): lax.ppermute(piece, 'code', [(d, d ^ r) for d in range(members)])  15.7 us
    ppermute x9, waiting for transfers between devices, trade(): lax.ppermute(piece, 'code', [(d, d ^ r) for d in range(members)])  5.29 us
    pallas_call x6, Pallas kernels, call(): pl.pallas_call(kernel, in_specs=specs, out_specs=jax.tree.map(lambda _: I...  2.96 us
    unnamed x12, local copies, waits for them, and re-layouts  0.97 us
  transfers between devices with their start and end apart: 9, of which 4 were waited for; matrix products, arithmetic and copies ran while one was open for 0% of the time, Pallas kernels for 7%

profile of v5, /device:TPU:0, one launch (start us, length us, event | category | flops | bytes accessed | tf_op | source)
XLA Modules:
  0.0 25.6 jit_solution(17562146938985773952)
XLA Ops:
  0.6 0.0 copy-start
  0.6 0.9 %copy-done = f32[1,1,128,512]{3,2,1,0:T(8,128)S(1)} copy-done((f32[1,1,128,512]{3,2,1,0:T(8,128)S(1)}, f32[1,1,128,512]{3,2,1,0:T(8,128)}, u32[]{:S(2)}) %copy-start) | copy-done | bytes 262168
  1.6 0.0 copy-start.2
  1.6 0.0 copy-start.3
  1.6 0.4 %shard_map.69 = (f32[32,512]{1,0:T(8,128)S(1)}, f32[32,512]{1,0:T(8,128)S(1)}, f32[32,512]{1,0:T(8,128)S(1)}, f32[32,512]{1,0:T(8,128)S(1)}) custom-call(f32[4,32,512]{2,1,0:T(8,128)S(1)} %bitcast.5), custom_call_target="tpu_custom_call" | custom-call | bytes 524288 | tf_op jit(solution)/shard_map/pallas_call | solution.py:140
  2.0 5.1 %collective-permute-start = (f32[32,512]{1,0:T(8,128)S(1)}, f32[32,512]{1,0:T(8,128)S(1)}, u32[]{:S(2)}, u32[]{:S(2)}) collective-permute-start(f32[32,512]{1,0:T(8,128)S(1)} %get-tuple-element.19), channel_id=1, source_target_pairs={{0,12},{4,8},{8,4},{12,0},{1,13},{5,9},{9,5},{13,1},{2,14},{6,10},... | collective-permute-start | bytes 196616 | tf_op jit(solution)/shard_map/ppermute | solution.py:157
  7.1 0.0 collective-permute-start.4
  7.1 0.6 %collective-permute-start.5 = (f32[32,512]{1,0:T(8,128)S(1)}, f32[32,512]{1,0:T(8,128)S(1)}, u32[]{:S(2)}, u32[]{:S(2)}) collective-permute-start(f32[32,512]{1,0:T(8,128)S(1)} %get-tuple-element.29), channel_id=1, source_target_pairs={{0,4},{4,0},{8,12},{12,8},{1,5},{5,1},{9,13},{13,9},{2,6},{6,2},{1... | collective-permute-start | bytes 196616 | tf_op jit(solution)/shard_map/ppermute | solution.py:157
  7.7 1.9 %collective-permute-done.refs_0_.refs_1_ = f32[32,512]{1,0:T(8,128)S(1)} collective-permute-done((f32[32,512]{1,0:T(8,128)S(1)}, f32[32,512]{1,0:T(8,128)S(1)}, u32[]{:S(2)}, u32[]{:S(2)}) %collective-permute-start) | collective-permute-done | bytes 65568 | tf_op jit(solution)/shard_map/ppermute | solution.py:157
  9.7 0.0 copy-done.2
  9.7 0.4 %shard_map.70 = (f32[32,512]{1,0:T(8,128)S(1)}, f32[32,512]{1,0:T(8,128)S(1)}, f32[32,512]{1,0:T(8,128)S(1)}, f32[32,512]{1,0:T(8,128)S(1)}) custom-call(f32[4,32,512]{2,1,0:T(8,128)S(1)} %bitcast.7, f32[32,512]{1,0:T(8,128)S(1)} %collective-permute-done.refs_0_.refs_1_), custom_call_target="tpu_custom_call" | custom-call | bytes 589824 | tf_op jit(solution)/shard_map/pallas_call | solution.py:140
  10.0 0.0 copy-start.4
  10.0 0.0 copy-start.5
  10.0 4.3 %collective-permute-start.1 = (f32[32,512]{1,0:T(8,128)S(1)}, f32[32,512]{1,0:T(8,128)S(1)}, u32[]{:S(2)}, u32[]{:S(2)}) collective-permute-start(f32[32,512]{1,0:T(8,128)S(1)} %get-tuple-element.21), channel_id=1, source_target_pairs={{0,12},{4,8},{8,4},{12,0},{1,13},{5,9},{9,5},{13,1},{2,14},{6,10},... | collective-permute-start | bytes 196616 | tf_op jit(solution)/shard_map/ppermute | solution.py:157
  14.3 0.0 copy-done.3
  14.3 0.0 copy-done.4
  14.3 0.0 copy-done.5
  14.3 0.6 %shard_map.68 = (f32[2,32,512]{2,1,0:T(8,128)S(1)}, f32[29,512]{1,0:T(8,128)S(1)}) custom-call(s32[1,2]{1,0:T(1,128)S(1)} %copy-done.5, f32[4,4]{1,0:T(4,128)S(1)} %copy-done.4, f32[32,2048]{1,0:T(8,128)S(1)} %bitcast.8), custom_call_target="tpu_custom_call" | custom-call | flops 262144 | bytes 452680 | tf_op jit(solution)/shard_map/pallas_call | solution.py:140
  15.0 0.1 collective-permute-start.2
  15.1 1.1 %collective-permute-start.3 = (f32[32,512]{1,0:T(8,128)S(1)}, f32[32,512]{1,0:T(8,128)S(1)}, u32[]{:S(2)}, u32[]{:S(2)}) collective-permute-start(f32[32,512]{1,0:T(8,128)S(1)} %get-tuple-element.23), channel_id=1, source_target_pairs={{0,4},{4,0},{8,12},{12,8},{1,5},{5,1},{9,13},{13,9},{2,6},{6,2},{1... | collective-permute-start | bytes 196616 | tf_op jit(solution)/shard_map/ppermute | solution.py:157
  16.2 0.0 collective-permute-done.4.refs_2_
  16.2 0.0 collective-permute-done.5.refs_3_
  16.2 0.1 shard_map.72
  16.3 0.0 copy-start.1
  16.3 3.3 %collective-permute-start.6 = (f32[32,512]{1,0:T(8,128)S(1)}, f32[32,512]{1,0:T(8,128)S(1)}, u32[]{:S(2)}, u32[]{:S(2)}) collective-permute-start(f32[32,512]{1,0:T(8,128)S(1)} %get-tuple-element.31), channel_id=1, source_target_pairs={{0,12},{4,8},{8,4},{12,0},{1,13},{5,9},{9,5},{13,1},{2,14},{6,10},... | collective-permute-start | bytes 196616 | tf_op jit(solution)/shard_map/ppermute | solution.py:157
  19.6 0.0 collective-permute-start.7
  19.6 0.0 collective-permute-done.1.refs_1_
  19.6 1.2 %collective-permute-start.8 = (f32[32,512]{1,0:T(8,128)S(1)}, f32[32,512]{1,0:T(8,128)S(1)}, u32[]{:S(2)}, u32[]{:S(2)}) collective-permute-start(f32[32,512]{1,0:T(8,128)S(1)} %get-tuple-element.33), channel_id=1, source_target_pairs={{0,4},{4,0},{8,12},{12,8},{1,5},{5,1},{9,13},{13,9},{2,6},{6,2},{1... | collective-permute-start | bytes 196616 | tf_op jit(solution)/shard_map/ppermute | solution.py:157
  20.7 1.2 %collective-permute-done.2.refs_2_ = f32[32,512]{1,0:T(8,128)S(1)} collective-permute-done((f32[32,512]{1,0:T(8,128)S(1)}, f32[32,512]{1,0:T(8,128)S(1)}, u32[]{:S(2)}, u32[]{:S(2)}) %collective-permute-start.2) | collective-permute-done | bytes 65568 | tf_op jit(solution)/shard_map/ppermute | solution.py:157
  22.0 0.0 collective-permute-done.3.refs_3_
  22.0 0.8 %shard_map.71 = (f32[32,2048]{1,0:T(8,128)}, f32[8,128]{1,0:T(8,128)S(1)}) custom-call(f32[29,512]{1,0:T(8,128)S(1)} %get-tuple-element.18.table_ref, f32[32,512]{1,0:T(8,128)S(1)} %get-tuple-element.20.refs_0_, f32[32,512]{1,0:T(8,128)S(1)} %collective-permute-done.1.refs_1_, f32[32,512]{1,0:T(8,128)S(1)} %collective-permute-done.2.refs_2_, ...), custom_call_target="tpu_custom_call" | custom-call | flops 524288 | bytes 587776 | tf_op jit(solution)/shard_map/pallas_call | solution.py:140
  22.8 0.4 %collective-permute-done.6.refs_1_ = f32[32,512]{1,0:T(8,128)S(1)} collective-permute-done((f32[32,512]{1,0:T(8,128)S(1)}, f32[32,512]{1,0:T(8,128)S(1)}, u32[]{:S(2)}, u32[]{:S(2)}) %collective-permute-start.6) | collective-permute-done | bytes 65568 | tf_op jit(solution)/shard_map/ppermute | solution.py:157
  23.2 1.7 %collective-permute-done.7.refs_2_ = f32[32,512]{1,0:T(8,128)S(1)} collective-permute-done((f32[32,512]{1,0:T(8,128)S(1)}, f32[32,512]{1,0:T(8,128)S(1)}, u32[]{:S(2)}, u32[]{:S(2)}) %collective-permute-start.7) | collective-permute-done | bytes 65568 | tf_op jit(solution)/shard_map/ppermute | solution.py:157
  24.9 0.0 collective-permute-done.8.refs_3_
  24.9 0.0 copy-done.1
  24.9 0.7 %shard_map.73 = f32[4,32,512]{2,1,0:T(8,128)} custom-call(f32[29,512]{1,0:T(8,128)S(1)} %get-tuple-element.18.table_ref, f32[4,32,512]{2,1,0:T(8,128)S(1)} %bitcast.6, f32[8,128]{1,0:T(8,128)S(1)} %get-tuple-element.25.held_back_by, f32[32,512]{1,0:T(8,128)S(1)} %get-tuple-element.30.refs_0_, f32[32,512]{1,0:T(8,128)S(1)} %collective-permute-done.6.refs_1_, ...), custom_call_target="tpu_custom_call" | custom-call | bytes 849920 | tf_op jit(solution)/shard_map/pallas_call | solution.py:140
Async XLA Ops:
  0.6 1.0 %copy-start = (f32[1,1,128,512]{3,2,1,0:T(8,128)S(1)}, f32[1,1,128,512]{3,2,1,0:T(8,128)}, u32[]{:S(2)}) copy-start(f32[1,1,128,512]{3,2,1,0:T(8,128)} %param.6) | copy-start | bytes 786436
  1.6 8.1 %copy-start.2 = (f32[1,1,128,512]{3,2,1,0:T(8,128)S(1)}, f32[1,1,128,512]{3,2,1,0:T(8,128)}, u32[]{:S(2)}) copy-start(f32[1,1,128,512]{3,2,1,0:T(8,128)} %param.5) | copy-start | bytes 786436
  1.6 12.7 %copy-start.3 = (f32[1,32,2048]{2,1,0:T(8,128)S(1)}, f32[1,32,2048]{2,1,0:T(8,128)}, u32[]{:S(2)}) copy-start(f32[1,32,2048]{2,1,0:T(8,128)} %param.7) | copy-start | bytes 786436
  2.0 7.7 %collective-permute-start = (f32[32,512]{1,0:T(8,128)S(1)}, f32[32,512]{1,0:T(8,128)S(1)}, u32[]{:S(2)}, u32[]{:S(2)}) collective-permute-start(f32[32,512]{1,0:T(8,128)S(1)} %get-tuple-element.19), channel_id=1, source_target_pairs={{0,12},{4,8},{8,4},{12,0},{1,13},{5,9},{9,5},{13,1},{2,14},{6,10},... | collective-permute-start | bytes 196616 | tf_op jit(solution)/shard_map/ppermute | solution.py:157
  7.1 9.1 %collective-permute-start.4 = (f32[32,512]{1,0:T(8,128)S(1)}, f32[32,512]{1,0:T(8,128)S(1)}, u32[]{:S(2)}, u32[]{:S(2)}) collective-permute-start(f32[32,512]{1,0:T(8,128)S(1)} %get-tuple-element.28), channel_id=1, source_target_pairs={{0,8},{4,12},{8,0},{12,4},{1,9},{5,13},{9,1},{13,5},{2,10},{6,14},... | collective-permute-start | bytes 196616 | tf_op jit(solution)/shard_map/ppermute | solution.py:157
  7.1 9.1 %collective-permute-start.5 = (f32[32,512]{1,0:T(8,128)S(1)}, f32[32,512]{1,0:T(8,128)S(1)}, u32[]{:S(2)}, u32[]{:S(2)}) collective-permute-start(f32[32,512]{1,0:T(8,128)S(1)} %get-tuple-element.29), channel_id=1, source_target_pairs={{0,4},{4,0},{8,12},{12,8},{1,5},{5,1},{9,13},{13,9},{2,6},{6,2},{1... | collective-permute-start | bytes 196616 | tf_op jit(solution)/shard_map/ppermute | solution.py:157
  10.0 4.3 %copy-start.4 = (f32[4,4]{1,0:T(4,128)S(1)}, f32[4,4]{1,0:T(4,128)}, u32[]{:S(2)}) copy-start(f32[4,4]{1,0:T(4,128)} %generator_ref.1) | copy-start | bytes 196
  10.0 4.3 %copy-start.5 = (s32[1,2]{1,0:T(1,128)S(1)}, s32[1,2]{1,0:T(1,128)}, u32[]{:S(2)}) copy-start(s32[1,2]{1,0:T(1,128)} %ids_ref.1) | copy-start | bytes 28
  10.0 9.5 %collective-permute-start.1 = (f32[32,512]{1,0:T(8,128)S(1)}, f32[32,512]{1,0:T(8,128)S(1)}, u32[]{:S(2)}, u32[]{:S(2)}) collective-permute-start(f32[32,512]{1,0:T(8,128)S(1)} %get-tuple-element.21), channel_id=1, source_target_pairs={{0,12},{4,8},{8,4},{12,0},{1,13},{5,9},{9,5},{13,1},{2,14},{6,10},... | collective-permute-start | bytes 196616 | tf_op jit(solution)/shard_map/ppermute | solution.py:157
  15.0 7.0 %collective-permute-start.2 = (f32[32,512]{1,0:T(8,128)S(1)}, f32[32,512]{1,0:T(8,128)S(1)}, u32[]{:S(2)}, u32[]{:S(2)}) collective-permute-start(f32[32,512]{1,0:T(8,128)S(1)} %get-tuple-element.22), channel_id=1, source_target_pairs={{0,8},{4,12},{8,0},{12,4},{1,9},{5,13},{9,1},{13,5},{2,10},{6,14},... | collective-permute-start | bytes 196616 | tf_op jit(solution)/shard_map/ppermute | solution.py:157
  15.1 6.9 %collective-permute-start.3 = (f32[32,512]{1,0:T(8,128)S(1)}, f32[32,512]{1,0:T(8,128)S(1)}, u32[]{:S(2)}, u32[]{:S(2)}) collective-permute-start(f32[32,512]{1,0:T(8,128)S(1)} %get-tuple-element.23), channel_id=1, source_target_pairs={{0,4},{4,0},{8,12},{12,8},{1,5},{5,1},{9,13},{13,9},{2,6},{6,2},{1... | collective-permute-start | bytes 196616 | tf_op jit(solution)/shard_map/ppermute | solution.py:157
  16.3 8.6 %copy-start.1 = (f32[1,1,128,512]{3,2,1,0:T(8,128)S(1)}, f32[1,1,128,512]{3,2,1,0:T(8,128)}, u32[]{:S(2)}) copy-start(f32[1,1,128,512]{3,2,1,0:T(8,128)} %param.6) | copy-start | bytes 786436
  16.3 6.9 %collective-permute-start.6 = (f32[32,512]{1,0:T(8,128)S(1)}, f32[32,512]{1,0:T(8,128)S(1)}, u32[]{:S(2)}, u32[]{:S(2)}) collective-permute-start(f32[32,512]{1,0:T(8,128)S(1)} %get-tuple-element.31), channel_id=1, source_target_pairs={{0,12},{4,8},{8,4},{12,0},{1,13},{5,9},{9,5},{13,1},{2,14},{6,10},... | collective-permute-start | bytes 196616 | tf_op jit(solution)/shard_map/ppermute | solution.py:157
  19.6 5.3 %collective-permute-start.7 = (f32[32,512]{1,0:T(8,128)S(1)}, f32[32,512]{1,0:T(8,128)S(1)}, u32[]{:S(2)}, u32[]{:S(2)}) collective-permute-start(f32[32,512]{1,0:T(8,128)S(1)} %get-tuple-element.32), channel_id=1, source_target_pairs={{0,8},{4,12},{8,0},{12,4},{1,9},{5,13},{9,1},{13,5},{2,10},{6,14},... | collective-permute-start | bytes 196616 | tf_op jit(solution)/shard_map/ppermute | solution.py:157
  19.6 5.3 %collective-permute-start.8 = (f32[32,512]{1,0:T(8,128)S(1)}, f32[32,512]{1,0:T(8,128)S(1)}, u32[]{:S(2)}, u32[]{:S(2)}) collective-permute-start(f32[32,512]{1,0:T(8,128)S(1)} %get-tuple-element.33), channel_id=1, source_target_pairs={{0,4},{4,0},{8,12},{12,8},{1,5},{5,1},{9,13},{13,9},{2,6},{6,2},{1... | collective-permute-start | bytes 196616 | tf_op jit(solution)/shard_map/ppermute | solution.py:157

commit v6 on v5

--- a/solution.py
+++ b/solution.py
@@ -164,7 +164,7 @@
         functools.partial(cut_kernel, rounds),
         [ANYWHERE] * (1 + len(held_back_by)),
         [floats(*blocks.shape[1:])] * len(rounds),
-        (blocks, *held_back_by),
+        (pltpu.with_memory_space_constraint(blocks, pltpu.HBM), *held_back_by),
         0,
         scratch_shapes=[pltpu.SemaphoreType.DMA((len(rounds),))],
     )
@@ -196,7 +196,7 @@
         block = floats(own_rows, width)
         own_earlier, *cut_earlier = cut(earlier, [0] + rounds)
         earlier_rows = trade(cut_earlier, rounds, members)
-        own_current, *cut_current = cut(current, [0] + rounds, earlier_rows[0])
+        own_current, *cut_current = cut(current, [0] + rounds, own_earlier)
         outgoing = call(
             rebuild_paired_kernel,
             [IN_VMEM] * (members + 2),

time: 25.8 us -> 24.6 us (0.953)
  starting transfers between devices: 15.7 us -> 14.1 us
  Pallas kernels: 2.96 us -> 4.22 us
  waiting for transfers between devices: 5.29 us -> 4.69 us
  local copies, waits for them, and re-layouts: 0.97 us -> 0.66 us
    ppermute x9, starting transfers between devices: 15.7 us -> 14.1 us  [trade(): lax.ppermute(piece, 'code', [(d, d ^ r) for d in range(members)])]
    pallas_call x6, Pallas kernels: 2.96 us -> 4.22 us  [call(): pl.pallas_call(kernel, in_specs=specs, out_specs=jax.tree.map(lambda _: I...]
    ppermute x9, waiting for transfers between devices: 5.29 us -> 4.69 us  [trade(): lax.ppermute(piece, 'code', [(d, d ^ r) for d in range(members)])]
    unnamed x12 -> x8, local copies, waits for them, and re-layouts: 0.97 us -> 0.66 us
  transfers between devices with their start and end apart: 9 -> 9, of which waited for: 4 -> 4; matrix products, arithmetic and copies ran while one was open for 0% -> 0% of each run, Pallas kernels for 7% -> 10%
where the time goes in v6:
time: 24.6 us; the launch traced here: 24.4 us
  starting transfers between devices  14.1 us (57%)
  waiting for transfers between devices  4.69 us (19%)
  Pallas kernels  4.22 us (17%)
  between operations  0.71 us (3%)
  local copies, waits for them, and re-layouts  0.66 us (3%)
    ppermute x9, starting transfers between devices, trade(): lax.ppermute(piece, 'code', [(d, d ^ r) for d in range(members)])  14.1 us
    ppermute x9, waiting for transfers between devices, trade(): lax.ppermute(piece, 'code', [(d, d ^ r) for d in range(members)])  4.69 us
    pallas_call x6, Pallas kernels, call(): pl.pallas_call(kernel, in_specs=specs, out_specs=jax.tree.map(lambda _: I...  4.22 us
    unnamed x8, local copies, waits for them, and re-layouts  0.66 us
  transfers between devices with their start and end apart: 9, of which 4 were waited for; matrix products, arithmetic and copies ran while one was open for 0% of the time, Pallas kernels for 10%

profile of v6, /device:TPU:0, one launch (start us, length us, event | category | flops | bytes accessed | tf_op | source)
XLA Modules:
  0.0 24.4 jit_solution(4876275229080184127)
XLA Ops:
  0.6 0.0 copy-start.1
  0.6 1.0 %shard_map.69 = (f32[32,512]{1,0:T(8,128)S(1)}, f32[32,512]{1,0:T(8,128)S(1)}, f32[32,512]{1,0:T(8,128)S(1)}, f32[32,512]{1,0:T(8,128)S(1)}) custom-call(f32[4,32,512]{2,1,0:T(8,128)} %bitcast.5), custom_call_target="tpu_custom_call" | custom-call | bytes 524288 | tf_op jit(solution)/shard_map/pallas_call | solution.py:140
  1.7 5.1 %collective-permute-start.3 = (f32[32,512]{1,0:T(8,128)S(1)}, f32[32,512]{1,0:T(8,128)S(1)}, u32[]{:S(2)}, u32[]{:S(2)}) collective-permute-start(f32[32,512]{1,0:T(8,128)S(1)} %get-tuple-element.27), channel_id=1, source_target_pairs={{0,12},{4,8},{8,4},{12,0},{1,13},{5,9},{9,5},{13,1},{2,14},{6,10},... | collective-permute-start | bytes 196616 | tf_op jit(solution)/shard_map/ppermute | solution.py:157
  6.8 0.0 collective-permute-start.4
  6.8 0.6 %collective-permute-start.5 = (f32[32,512]{1,0:T(8,128)S(1)}, f32[32,512]{1,0:T(8,128)S(1)}, u32[]{:S(2)}, u32[]{:S(2)}) collective-permute-start(f32[32,512]{1,0:T(8,128)S(1)} %get-tuple-element.29), channel_id=1, source_target_pairs={{0,4},{4,0},{8,12},{12,8},{1,5},{5,1},{9,13},{13,9},{2,6},{6,2},{1... | collective-permute-start | bytes 196616 | tf_op jit(solution)/shard_map/ppermute | solution.py:157
  7.4 1.0 %shard_map.70 = (f32[32,512]{1,0:T(8,128)S(1)}, f32[32,512]{1,0:T(8,128)S(1)}, f32[32,512]{1,0:T(8,128)S(1)}, f32[32,512]{1,0:T(8,128)S(1)}) custom-call(f32[4,32,512]{2,1,0:T(8,128)} %bitcast.8, f32[32,512]{1,0:T(8,128)S(1)} %get-tuple-element.19.refs_0_), custom_call_target="tpu_custom_call" | custom-call | bytes 589824 | tf_op jit(solution)/shard_map/pallas_call | solution.py:140
  8.4 0.0 copy-start.2
  8.4 3.8 %collective-permute-start = (f32[32,512]{1,0:T(8,128)S(1)}, f32[32,512]{1,0:T(8,128)S(1)}, u32[]{:S(2)}, u32[]{:S(2)}) collective-permute-start(f32[32,512]{1,0:T(8,128)S(1)} %get-tuple-element.21), channel_id=1, source_target_pairs={{0,12},{4,8},{8,4},{12,0},{1,13},{5,9},{9,5},{13,1},{2,14},{6,10},... | collective-permute-start | bytes 196616 | tf_op jit(solution)/shard_map/ppermute | solution.py:157
  12.2 0.0 copy-start.3
  12.2 0.0 collective-permute-start.1
  12.2 0.0 copy-done.1
  12.2 0.0 copy-done.2
  12.2 0.6 %copy-done.3 = s32[1,2]{1,0:T(1,128)S(1)} copy-done((s32[1,2]{1,0:T(1,128)S(1)}, s32[1,2]{1,0:T(1,128)}, u32[]{:S(2)}) %copy-start.3) | copy-done | bytes 32
  12.9 0.6 %shard_map.68 = (f32[2,32,512]{2,1,0:T(8,128)S(1)}, f32[29,512]{1,0:T(8,128)S(1)}) custom-call(s32[1,2]{1,0:T(1,128)S(1)} %copy-done.3, f32[4,4]{1,0:T(4,128)S(1)} %copy-done.2, f32[32,2048]{1,0:T(8,128)S(1)} %bitcast.7), custom_call_target="tpu_custom_call" | custom-call | flops 262144 | bytes 452680 | tf_op jit(solution)/shard_map/pallas_call | solution.py:140
  13.5 0.0 collective-permute-done.3.refs_1_
  13.5 0.1 collective-permute-start.2
  13.6 0.3 %collective-permute-done.4.refs_2_ = f32[32,512]{1,0:T(8,128)S(1)} collective-permute-done((f32[32,512]{1,0:T(8,128)S(1)}, f32[32,512]{1,0:T(8,128)S(1)}, u32[]{:S(2)}, u32[]{:S(2)}) %collective-permute-start.4) | collective-permute-done | bytes 65568 | tf_op jit(solution)/shard_map/ppermute | solution.py:157
  13.9 0.0 collective-permute-done.5.refs_3_
  13.9 0.1 shard_map.72
  13.9 0.0 copy-start
  14.0 3.5 %collective-permute-start.6 = (f32[32,512]{1,0:T(8,128)S(1)}, f32[32,512]{1,0:T(8,128)S(1)}, u32[]{:S(2)}, u32[]{:S(2)}) collective-permute-start(f32[32,512]{1,0:T(8,128)S(1)} %get-tuple-element.31), channel_id=1, source_target_pairs={{0,12},{4,8},{8,4},{12,0},{1,13},{5,9},{9,5},{13,1},{2,14},{6,10},... | collective-permute-start | bytes 196616 | tf_op jit(solution)/shard_map/ppermute | solution.py:157
  17.5 0.0 collective-permute-start.7
  17.5 0.0 collective-permute-done.refs_1_
  17.5 0.9 %collective-permute-start.8 = (f32[32,512]{1,0:T(8,128)S(1)}, f32[32,512]{1,0:T(8,128)S(1)}, u32[]{:S(2)}, u32[]{:S(2)}) collective-permute-start(f32[32,512]{1,0:T(8,128)S(1)} %get-tuple-element.33), channel_id=1, source_target_pairs={{0,4},{4,0},{8,12},{12,8},{1,5},{5,1},{9,13},{13,9},{2,6},{6,2},{1... | collective-permute-start | bytes 196616 | tf_op jit(solution)/shard_map/ppermute | solution.py:157
  18.4 2.2 %collective-permute-done.1.refs_2_ = f32[32,512]{1,0:T(8,128)S(1)} collective-permute-done((f32[32,512]{1,0:T(8,128)S(1)}, f32[32,512]{1,0:T(8,128)S(1)}, u32[]{:S(2)}, u32[]{:S(2)}) %collective-permute-start.1) | collective-permute-done | bytes 65568 | tf_op jit(solution)/shard_map/ppermute | solution.py:157
  20.6 0.1 collective-permute-done.2.refs_3_
  20.7 0.8 %shard_map.71 = (f32[32,2048]{1,0:T(8,128)}, f32[8,128]{1,0:T(8,128)S(1)}) custom-call(f32[29,512]{1,0:T(8,128)S(1)} %get-tuple-element.18.table_ref, f32[32,512]{1,0:T(8,128)S(1)} %get-tuple-element.20.refs_0_, f32[32,512]{1,0:T(8,128)S(1)} %collective-permute-done.refs_1_, f32[32,512]{1,0:T(8,128)S(1)} %collective-permute-done.1.refs_2_, ...), custom_call_target="tpu_custom_call" | custom-call | flops 524288 | bytes 587776 | tf_op jit(solution)/shard_map/pallas_call | solution.py:140
  21.5 0.0 collective-permute-done.6.refs_1_
  21.5 2.2 %collective-permute-done.7.refs_2_ = f32[32,512]{1,0:T(8,128)S(1)} collective-permute-done((f32[32,512]{1,0:T(8,128)S(1)}, f32[32,512]{1,0:T(8,128)S(1)}, u32[]{:S(2)}, u32[]{:S(2)}) %collective-permute-start.7) | collective-permute-done | bytes 65568 | tf_op jit(solution)/shard_map/ppermute | solution.py:157
  23.6 0.0 collective-permute-done.8.refs_3_
  23.6 0.0 copy-done
  23.6 0.7 %shard_map.73 = f32[4,32,512]{2,1,0:T(8,128)} custom-call(f32[29,512]{1,0:T(8,128)S(1)} %get-tuple-element.18.table_ref, f32[4,32,512]{2,1,0:T(8,128)S(1)} %bitcast.6, f32[8,128]{1,0:T(8,128)S(1)} %get-tuple-element.25.held_back_by, f32[32,512]{1,0:T(8,128)S(1)} %get-tuple-element.30.refs_0_, f32[32,512]{1,0:T(8,128)S(1)} %collective-permute-done.6.refs_1_, ...), custom_call_target="tpu_custom_call" | custom-call | bytes 849920 | tf_op jit(solution)/shard_map/pallas_call | solution.py:140
Async XLA Ops:
  0.6 11.6 %copy-start.1 = (f32[1,32,2048]{2,1,0:T(8,128)S(1)}, f32[1,32,2048]{2,1,0:T(8,128)}, u32[]{:S(2)}) copy-start(f32[1,32,2048]{2,1,0:T(8,128)} %param.7) | copy-start | bytes 786436
  1.7 11.9 %collective-permute-start.3 = (f32[32,512]{1,0:T(8,128)S(1)}, f32[32,512]{1,0:T(8,128)S(1)}, u32[]{:S(2)}, u32[]{:S(2)}) collective-permute-start(f32[32,512]{1,0:T(8,128)S(1)} %get-tuple-element.27), channel_id=1, source_target_pairs={{0,12},{4,8},{8,4},{12,0},{1,13},{5,9},{9,5},{13,1},{2,14},{6,10},... | collective-permute-start | bytes 196616 | tf_op jit(solution)/shard_map/ppermute | solution.py:157
  6.8 7.1 %collective-permute-start.4 = (f32[32,512]{1,0:T(8,128)S(1)}, f32[32,512]{1,0:T(8,128)S(1)}, u32[]{:S(2)}, u32[]{:S(2)}) collective-permute-start(f32[32,512]{1,0:T(8,128)S(1)} %get-tuple-element.28), channel_id=1, source_target_pairs={{0,8},{4,12},{8,0},{12,4},{1,9},{5,13},{9,1},{13,5},{2,10},{6,14},... | collective-permute-start | bytes 196616 | tf_op jit(solution)/shard_map/ppermute | solution.py:157
  6.8 7.1 %collective-permute-start.5 = (f32[32,512]{1,0:T(8,128)S(1)}, f32[32,512]{1,0:T(8,128)S(1)}, u32[]{:S(2)}, u32[]{:S(2)}) collective-permute-start(f32[32,512]{1,0:T(8,128)S(1)} %get-tuple-element.29), channel_id=1, source_target_pairs={{0,4},{4,0},{8,12},{12,8},{1,5},{5,1},{9,13},{13,9},{2,6},{6,2},{1... | collective-permute-start | bytes 196616 | tf_op jit(solution)/shard_map/ppermute | solution.py:157
  8.4 3.8 %copy-start.2 = (f32[4,4]{1,0:T(4,128)S(1)}, f32[4,4]{1,0:T(4,128)}, u32[]{:S(2)}) copy-start(f32[4,4]{1,0:T(4,128)} %generator_ref.1) | copy-start | bytes 196
  8.4 9.1 %collective-permute-start = (f32[32,512]{1,0:T(8,128)S(1)}, f32[32,512]{1,0:T(8,128)S(1)}, u32[]{:S(2)}, u32[]{:S(2)}) collective-permute-start(f32[32,512]{1,0:T(8,128)S(1)} %get-tuple-element.21), channel_id=1, source_target_pairs={{0,12},{4,8},{8,4},{12,0},{1,13},{5,9},{9,5},{13,1},{2,14},{6,10},... | collective-permute-start | bytes 196616 | tf_op jit(solution)/shard_map/ppermute | solution.py:157
  12.2 0.7 %copy-start.3 = (s32[1,2]{1,0:T(1,128)S(1)}, s32[1,2]{1,0:T(1,128)}, u32[]{:S(2)}) copy-start(s32[1,2]{1,0:T(1,128)} %ids_ref.1) | copy-start | bytes 28
  12.2 8.3 %collective-permute-start.1 = (f32[32,512]{1,0:T(8,128)S(1)}, f32[32,512]{1,0:T(8,128)S(1)}, u32[]{:S(2)}, u32[]{:S(2)}) collective-permute-start(f32[32,512]{1,0:T(8,128)S(1)} %get-tuple-element.22), channel_id=1, source_target_pairs={{0,8},{4,12},{8,0},{12,4},{1,9},{5,13},{9,1},{13,5},{2,10},{6,14},... | collective-permute-start | bytes 196616 | tf_op jit(solution)/shard_map/ppermute | solution.py:157
  13.5 7.1 %collective-permute-start.2 = (f32[32,512]{1,0:T(8,128)S(1)}, f32[32,512]{1,0:T(8,128)S(1)}, u32[]{:S(2)}, u32[]{:S(2)}) collective-permute-start(f32[32,512]{1,0:T(8,128)S(1)} %get-tuple-element.23), channel_id=1, source_target_pairs={{0,4},{4,0},{8,12},{12,8},{1,5},{5,1},{9,13},{13,9},{2,6},{6,2},{1... | collective-permute-start | bytes 196616 | tf_op jit(solution)/shard_map/ppermute | solution.py:157
  13.9 9.7 %copy-start = (f32[1,1,128,512]{3,2,1,0:T(8,128)S(1)}, f32[1,1,128,512]{3,2,1,0:T(8,128)}, u32[]{:S(2)}) copy-start(f32[1,1,128,512]{3,2,1,0:T(8,128)} %param.6) | copy-start | bytes 786436
  14.0 7.5 %collective-permute-start.6 = (f32[32,512]{1,0:T(8,128)S(1)}, f32[32,512]{1,0:T(8,128)S(1)}, u32[]{:S(2)}, u32[]{:S(2)}) collective-permute-start(f32[32,512]{1,0:T(8,128)S(1)} %get-tuple-element.31), channel_id=1, source_target_pairs={{0,12},{4,8},{8,4},{12,0},{1,13},{5,9},{9,5},{13,1},{2,14},{6,10},... | collective-permute-start | bytes 196616 | tf_op jit(solution)/shard_map/ppermute | solution.py:157
  17.5 6.1 %collective-permute-start.7 = (f32[32,512]{1,0:T(8,128)S(1)}, f32[32,512]{1,0:T(8,128)S(1)}, u32[]{:S(2)}, u32[]{:S(2)}) collective-permute-start(f32[32,512]{1,0:T(8,128)S(1)} %get-tuple-element.32), channel_id=1, source_target_pairs={{0,8},{4,12},{8,0},{12,4},{1,9},{5,13},{9,1},{13,5},{2,10},{6,14},... | collective-permute-start | bytes 196616 | tf_op jit(solution)/shard_map/ppermute | solution.py:157
  17.5 6.1 %collective-permute-start.8 = (f32[32,512]{1,0:T(8,128)S(1)}, f32[32,512]{1,0:T(8,128)S(1)}, u32[]{:S(2)}, u32[]{:S(2)}) collective-permute-start(f32[32,512]{1,0:T(8,128)S(1)} %get-tuple-element.33), channel_id=1, source_target_pairs={{0,4},{4,0},{8,12},{12,8},{1,5},{5,1},{9,13},{13,9},{2,6},{6,2},{1... | collective-permute-start | bytes 196616 | tf_op jit(solution)/shard_map/ppermute | solution.py:157

commit v7 on v6

--- a/solution.py
+++ b/solution.py
@@ -126,21 +126,30 @@
     done_ref[...] = jnp.zeros(done_ref.shape, done_ref.dtype)
 
 
-def restore_kernel(table_ref, earlier_ref, held_back_by, *refs):
-    pieces, out_ref = refs[:-1], refs[-1]
-    members = len(pieces)
+def restore_kernel(rounds, table_ref, *refs):
+    count = len(rounds)
+    arrived, own = refs[:count], refs[count : 2 * count]
+    out_ref, stage_ref, sems = refs[-3:]
+    me = lax.axis_index("code")
     last = table_ref.shape[0] - 1
     lost = table_ref[last : last + 1, :] > 0.5
-    for c, piece in zip(order_of(members, True), pieces):
-        out_ref[c] = jnp.where(lost, piece[...], earlier_ref[c])
+    copies = []
+    for i, r in enumerate(rounds):
+        stage_ref[i] = jnp.where(lost, arrived[i][...], own[i][...])
+        copies.append(
+            pltpu.make_async_copy(stage_ref.at[i], out_ref.at[me ^ r], sems.at[i])
+        )
+        copies[-1].start()
+    for copy in copies:
+        copy.wait()
 
 
 def call(kernel, specs, outs, args, flops, **options):
     total = sum(x.size for x in args) + sum(o.size for o in jax.tree.leaves(outs))
+    options.setdefault("out_specs", jax.tree.map(lambda _: IN_VMEM, outs))
     return pl.pallas_call(
         kernel,
         in_specs=specs,
-        out_specs=jax.tree.map(lambda _: IN_VMEM, outs),
         out_shape=outs,
         compiler_params=pltpu.CompilerParams(vmem_limit_bytes=KERNEL_VMEM),
         cost_estimate=pl.CostEstimate(flops=flops, bytes_accessed=4 * total, transcendentals=0),
@@ -164,9 +173,28 @@
         functools.partial(cut_kernel, rounds),
         [ANYWHERE] * (1 + len(held_back_by)),
         [floats(*blocks.shape[1:])] * len(rounds),
-        (pltpu.with_memory_space_constraint(blocks, pltpu.HBM), *held_back_by),
+        (blocks, *held_back_by),
         0,
         scratch_shapes=[pltpu.SemaphoreType.DMA((len(rounds),))],
+    )
+
+
+def restore(members, table, rounds, arrived, own, others=(), held_back_by=()):
+    count = len(rounds)
+    own_rows, width = own[0].shape
+    extra = [*others, *held_back_by]
+    return call(
+        functools.partial(restore_kernel, rounds),
+        [IN_VMEM] * (1 + 2 * count) + [ANYWHERE] * len(extra),
+        floats(members, own_rows, width),
+        (table, *arrived, *own, *extra),
+        0,
+        out_specs=ANYWHERE,
+        scratch_shapes=[
+            pltpu.VMEM((count, own_rows, width), jnp.float32),
+            pltpu.SemaphoreType.DMA((count,)),
+        ],
+        input_output_aliases={1 + 2 * count: 0} if others else {},
     )
 
 
@@ -194,7 +222,10 @@
     if direct:
         rounds = list(rounds_of(members))
         block = floats(own_rows, width)
-        own_earlier, *cut_earlier = cut(earlier, [0] + rounds)
+        lead, rest = rounds[:1], rounds[1:]
+        cut_lead = cut(pltpu.with_memory_space_constraint(earlier, pltpu.HBM), lead)
+        own_earlier, *cut_rest = cut(earlier, [0] + rest, *cut_lead)
+        cut_earlier = [*cut_lead, *cut_rest]
         earlier_rows = trade(cut_earlier, rounds, members)
         own_current, *cut_current = cut(current, [0] + rounds, own_earlier)
         outgoing = call(
@@ -213,12 +244,20 @@
             (table, *current_rows),
             parity_cost,
         )
-        restored_state = call(
-            restore_kernel,
-            [IN_VMEM, IN_VMEM, ANYWHERE] + [IN_VMEM] * members,
-            floats(*blocks),
-            (table, earlier, parity_done, outgoing[0], *incoming),
-            0,
+        slow = rounds.index(members // 2) + 1
+        arrived, own = [outgoing[0], *incoming], [own_earlier, *cut_earlier]
+        all_rounds = [0] + rounds
+        quick = [i for i in range(members) if i != slow]
+        first_blocks = restore(
+            members,
+            table,
+            [all_rounds[i] for i in quick],
+            [arrived[i] for i in quick],
+            [own[i] for i in quick],
+            held_back_by=[parity_done],
+        )
+        restored_state = restore(
+            members, table, [all_rounds[slow]], [arrived[slow]], [own[slow]], [first_blocks]
         )
     else:
         earlier_rows = lax.all_to_all(earlier, "code", 0, 0, tiled=True)

time: 24.6 us -> 24.7 us (level)
    pallas_call x6 -> x8, Pallas kernels: 4.22 us -> 4.37 us  [call(): pl.pallas_call(kernel, in_specs=specs, out_shape=outs, compiler_params=pl...]
    unnamed x8 -> x10, local copies, waits for them, and re-layouts: 0.66 us -> 0.66 us
  transfers between devices with their start and end apart: 9 -> 9, of which waited for: 4 -> 3; matrix products, arithmetic and copies ran while one was open for 0% -> 0% of each run, Pallas kernels for 10% -> 11%
where the time goes in v7:
time: 24.7 us; the launch traced here: 24.6 us
  starting transfers between devices  14.2 us (57%)
  waiting for transfers between devices  4.63 us (19%)
  Pallas kernels  4.37 us (18%)
  between operations  0.75 us (3%)
  local copies, waits for them, and re-layouts  0.66 us (3%)
    ppermute x9, starting transfers between devices, trade(): lax.ppermute(piece, 'code', [(d, d ^ r) for d in range(members)])  14.2 us
    ppermute x9, waiting for transfers between devices, trade(): lax.ppermute(piece, 'code', [(d, d ^ r) for d in range(members)])  4.63 us
    pallas_call x8, Pallas kernels, call(): pl.pallas_call(kernel, in_specs=specs, out_shape=outs, compiler_params=pl...  4.37 us
    unnamed x10, local copies, waits for them, and re-layouts  0.66 us
  transfers between devices with their start and end apart: 9, of which 3 were waited for; matrix products, arithmetic and copies ran while one was open for 0% of the time, Pallas kernels for 11%

profile of v7, /device:TPU:0, one launch (start us, length us, event | category | flops | bytes accessed | tf_op | source)
XLA Modules:
  0.0 24.6 jit_solution(1096078852634432078)
XLA Ops:
  0.6 0.0 copy-start
  0.6 0.0 copy-start.1
  0.6 0.9 %shard_map.69.refs_0_.refs_4_ = f32[32,512]{1,0:T(8,128)S(1)} custom-call(f32[4,32,512]{2,1,0:T(8,128)} %bitcast.5), custom_call_target="tpu_custom_call" | custom-call | bytes 327680 | tf_op jit(solution)/shard_map/pallas_call | solution.py:150
  1.6 0.0 copy-start.2
  1.6 5.1 %collective-permute-start.3 = (f32[32,512]{1,0:T(8,128)S(1)}, f32[32,512]{1,0:T(8,128)S(1)}, u32[]{:S(2)}, u32[]{:S(2)}) collective-permute-start(f32[32,512]{1,0:T(8,128)S(1)} %shard_map.69.refs_0_.refs_4_), channel_id=1, source_target_pairs={{0,12},{4,8},{8,4},{12,0},{1,13},{5,9},{9,5},{13,1},{2,14},{6,10},... | collective-permute-start | bytes 196616 | tf_op jit(solution)/shard_map/ppermute | solution.py:166
  6.7 0.0 copy-done
  6.7 0.3 %shard_map.70 = (f32[32,512]{1,0:T(8,128)S(1)}, f32[32,512]{1,0:T(8,128)S(1)}, f32[32,512]{1,0:T(8,128)S(1)}) custom-call(f32[4,32,512]{2,1,0:T(8,128)S(1)} %bitcast.6, f32[32,512]{1,0:T(8,128)S(1)} %shard_map.69.refs_0_.refs_4_), custom_call_target="tpu_custom_call" | custom-call | bytes 524288 | tf_op jit(solution)/shard_map/pallas_call | solution.py:150
  7.0 0.1 collective-permute-start.4
  7.0 0.6 %collective-permute-start.5 = (f32[32,512]{1,0:T(8,128)S(1)}, f32[32,512]{1,0:T(8,128)S(1)}, u32[]{:S(2)}, u32[]{:S(2)}) collective-permute-start(f32[32,512]{1,0:T(8,128)S(1)} %get-tuple-element.26.refs_5_), channel_id=1, source_target_pairs={{0,4},{4,0},{8,12},{12,8},{1,5},{5,1},{9,13},{13,9},{2,6},{6,2},{1... | collective-permute-start | bytes 196616 | tf_op jit(solution)/shard_map/ppermute | solution.py:166
  7.7 0.0 copy-done.1
  7.7 0.4 %shard_map.71 = (f32[32,512]{1,0:T(8,128)S(1)}, f32[32,512]{1,0:T(8,128)S(1)}, f32[32,512]{1,0:T(8,128)S(1)}, f32[32,512]{1,0:T(8,128)S(1)}) custom-call(f32[4,32,512]{2,1,0:T(8,128)S(1)} %bitcast.7, f32[32,512]{1,0:T(8,128)S(1)} %get-tuple-element.18.refs_0_.refs_3_), custom_call_target="tpu_custom_call" | custom-call | bytes 589824 | tf_op jit(solution)/shard_map/pallas_call | solution.py:150
  8.0 0.0 copy-start.3
  8.0 3.8 %collective-permute-start = (f32[32,512]{1,0:T(8,128)S(1)}, f32[32,512]{1,0:T(8,128)S(1)}, u32[]{:S(2)}, u32[]{:S(2)}) collective-permute-start(f32[32,512]{1,0:T(8,128)S(1)} %get-tuple-element.20), channel_id=1, source_target_pairs={{0,12},{4,8},{8,4},{12,0},{1,13},{5,9},{9,5},{13,1},{2,14},{6,10},... | collective-permute-start | bytes 196616 | tf_op jit(solution)/shard_map/ppermute | solution.py:166
  11.9 0.0 copy-start.4
  11.9 0.0 collective-permute-start.1
  11.9 0.0 copy-done.2
  11.9 0.0 copy-done.3
  11.9 0.6 %copy-done.4 = s32[1,2]{1,0:T(1,128)S(1)} copy-done((s32[1,2]{1,0:T(1,128)S(1)}, s32[1,2]{1,0:T(1,128)}, u32[]{:S(2)}) %copy-start.4) | copy-done | bytes 32
  12.5 0.6 %shard_map.68 = (f32[2,32,512]{2,1,0:T(8,128)S(1)}, f32[29,512]{1,0:T(8,128)S(1)}) custom-call(s32[1,2]{1,0:T(1,128)S(1)} %copy-done.4, f32[4,4]{1,0:T(4,128)S(1)} %copy-done.3, f32[32,2048]{1,0:T(8,128)S(1)} %bitcast.8), custom_call_target="tpu_custom_call" | custom-call | flops 262144 | bytes 452680 | tf_op jit(solution)/shard_map/pallas_call | solution.py:150
  13.2 0.0 collective-permute-done.3.refs_1_
  13.2 0.1 collective-permute-start.2
  13.3 2.5 %collective-permute-done.4.refs_2_ = f32[32,512]{1,0:T(8,128)S(1)} collective-permute-done((f32[32,512]{1,0:T(8,128)S(1)}, f32[32,512]{1,0:T(8,128)S(1)}, u32[]{:S(2)}, u32[]{:S(2)}) %collective-permute-start.4) | collective-permute-done | bytes 65568 | tf_op jit(solution)/shard_map/ppermute | solution.py:166
  15.8 0.0 collective-permute-done.5.refs_3_
  15.8 0.1 shard_map.73
  15.8 1.3 %collective-permute-start.7 = (f32[32,512]{1,0:T(8,128)S(1)}, f32[32,512]{1,0:T(8,128)S(1)}, u32[]{:S(2)}, u32[]{:S(2)}) collective-permute-start(f32[32,512]{1,0:T(8,128)S(1)} %get-tuple-element.29), channel_id=1, source_target_pairs={{0,12},{4,8},{8,4},{12,0},{1,13},{5,9},{9,5},{13,1},{2,14},{6,10},... | collective-permute-start | bytes 196616 | tf_op jit(solution)/shard_map/ppermute | solution.py:166
  17.1 0.0 collective-permute-start.8
  17.1 0.0 collective-permute-done.refs_1_
  17.1 3.2 %collective-permute-start.6 = (f32[32,512]{1,0:T(8,128)S(1)}, f32[32,512]{1,0:T(8,128)S(1)}, u32[]{:S(2)}, u32[]{:S(2)}) collective-permute-start(f32[32,512]{1,0:T(8,128)S(1)} %get-tuple-element.27), channel_id=1, source_target_pairs={{0,8},{4,12},{8,0},{12,4},{1,9},{5,13},{9,1},{13,5},{2,10},{6,14},... | collective-permute-start | bytes 196616 | tf_op jit(solution)/shard_map/ppermute | solution.py:166
  20.3 0.0 collective-permute-done.1.refs_2_
  20.3 0.0 collective-permute-done.2.refs_3_
  20.3 0.8 %shard_map.72 = (f32[32,2048]{1,0:T(8,128)}, f32[8,128]{1,0:T(8,128)S(1)}) custom-call(f32[29,512]{1,0:T(8,128)S(1)} %get-tuple-element.17.table_ref, f32[32,512]{1,0:T(8,128)S(1)} %get-tuple-element.19.refs_0_, f32[32,512]{1,0:T(8,128)S(1)} %collective-permute-done.refs_1_, f32[32,512]{1,0:T(8,128)S(1)} %collective-permute-done.1.refs_2_, ...), custom_call_target="tpu_custom_call" | custom-call | flops 524288 | bytes 587776 | tf_op jit(solution)/shard_map/pallas_call | solution.py:150
  21.1 1.0 %collective-permute-done.7.refs_1_ = f32[32,512]{1,0:T(8,128)S(1)} collective-permute-done((f32[32,512]{1,0:T(8,128)S(1)}, f32[32,512]{1,0:T(8,128)S(1)}, u32[]{:S(2)}, u32[]{:S(2)}) %collective-permute-start.7) | collective-permute-done | bytes 65568 | tf_op jit(solution)/shard_map/ppermute | solution.py:166
  22.1 1.1 %collective-permute-done.8.refs_2_ = f32[32,512]{1,0:T(8,128)S(1)} collective-permute-done((f32[32,512]{1,0:T(8,128)S(1)}, f32[32,512]{1,0:T(8,128)S(1)}, u32[]{:S(2)}, u32[]{:S(2)}) %collective-permute-start.8) | collective-permute-done | bytes 65568 | tf_op jit(solution)/shard_map/ppermute | solution.py:166
  23.2 0.7 %shard_map.74.refs_2_ = f32[4,32,512]{2,1,0:T(8,128)} custom-call(f32[29,512]{1,0:T(8,128)S(1)} %get-tuple-element.17.table_ref, f32[32,512]{1,0:T(8,128)S(1)} %get-tuple-element.28.refs_0_, f32[32,512]{1,0:T(8,128)S(1)} %collective-permute-done.7.refs_1_, f32[32,512]{1,0:T(8,128)S(1)} %collective-permute-done.8.refs_2_, ...), custom_call_target="tpu_custom_call" | custom-call | bytes 718848 | tf_op jit(solution)/shard_map/pallas_call | solution.py:150
  23.9 0.0 collective-permute-done.6.refs_0_
  23.9 0.7 %shard_map.75 = f32[4,32,512]{2,1,0:T(8,128)} custom-call(f32[29,512]{1,0:T(8,128)S(1)} %get-tuple-element.17.table_ref, f32[32,512]{1,0:T(8,128)S(1)} %collective-permute-done.6.refs_0_, f32[32,512]{1,0:T(8,128)S(1)} %get-tuple-element.25.refs_1_, f32[4,32,512]{2,1,0:T(8,128)} %shard_map.74.refs_2_), custom_call_target="tpu_custom_call", output_to_operand_aliasing={{}: (3, {})} | custom-call | bytes 714752 | tf_op jit(solution)/shard_map/pallas_call | solution.py:150
Async XLA Ops:
  0.6 6.1 %copy-start = (f32[1,1,128,512]{3,2,1,0:T(8,128)S(1)}, f32[1,1,128,512]{3,2,1,0:T(8,128)}, u32[]{:S(2)}) copy-start(f32[1,1,128,512]{3,2,1,0:T(8,128)} %param.6) | copy-start | bytes 786436
  0.6 7.0 %copy-start.1 = (f32[1,1,128,512]{3,2,1,0:T(8,128)S(1)}, f32[1,1,128,512]{3,2,1,0:T(8,128)}, u32[]{:S(2)}) copy-start(f32[1,1,128,512]{3,2,1,0:T(8,128)} %param.5) | copy-start | bytes 786436
  1.6 10.3 %copy-start.2 = (f32[1,32,2048]{2,1,0:T(8,128)S(1)}, f32[1,32,2048]{2,1,0:T(8,128)}, u32[]{:S(2)}) copy-start(f32[1,32,2048]{2,1,0:T(8,128)} %param.7) | copy-start | bytes 786436
  1.6 11.6 %collective-permute-start.3 = (f32[32,512]{1,0:T(8,128)S(1)}, f32[32,512]{1,0:T(8,128)S(1)}, u32[]{:S(2)}, u32[]{:S(2)}) collective-permute-start(f32[32,512]{1,0:T(8,128)S(1)} %shard_map.69.refs_0_.refs_4_), channel_id=1, source_target_pairs={{0,12},{4,8},{8,4},{12,0},{1,13},{5,9},{9,5},{13,1},{2,14},{6,10},... | collective-permute-start | bytes 196616 | tf_op jit(solution)/shard_map/ppermute | solution.py:166
  7.0 8.8 %collective-permute-start.4 = (f32[32,512]{1,0:T(8,128)S(1)}, f32[32,512]{1,0:T(8,128)S(1)}, u32[]{:S(2)}, u32[]{:S(2)}) collective-permute-start(f32[32,512]{1,0:T(8,128)S(1)} %get-tuple-element.25.refs_1_), channel_id=1, source_target_pairs={{0,8},{4,12},{8,0},{12,4},{1,9},{5,13},{9,1},{13,5},{2,10},{6,14},... | collective-permute-start | bytes 196616 | tf_op jit(solution)/shard_map/ppermute | solution.py:166
  7.0 8.7 %collective-permute-start.5 = (f32[32,512]{1,0:T(8,128)S(1)}, f32[32,512]{1,0:T(8,128)S(1)}, u32[]{:S(2)}, u32[]{:S(2)}) collective-permute-start(f32[32,512]{1,0:T(8,128)S(1)} %get-tuple-element.26.refs_5_), channel_id=1, source_target_pairs={{0,4},{4,0},{8,12},{12,8},{1,5},{5,1},{9,13},{13,9},{2,6},{6,2},{1... | collective-permute-start | bytes 196616 | tf_op jit(solution)/shard_map/ppermute | solution.py:166
  8.0 3.9 %copy-start.3 = (f32[4,4]{1,0:T(4,128)S(1)}, f32[4,4]{1,0:T(4,128)}, u32[]{:S(2)}) copy-start(f32[4,4]{1,0:T(4,128)} %generator_ref.1) | copy-start | bytes 196
  8.0 9.1 %collective-permute-start = (f32[32,512]{1,0:T(8,128)S(1)}, f32[32,512]{1,0:T(8,128)S(1)}, u32[]{:S(2)}, u32[]{:S(2)}) collective-permute-start(f32[32,512]{1,0:T(8,128)S(1)} %get-tuple-element.20), channel_id=1, source_target_pairs={{0,12},{4,8},{8,4},{12,0},{1,13},{5,9},{9,5},{13,1},{2,14},{6,10},... | collective-permute-start | bytes 196616 | tf_op jit(solution)/shard_map/ppermute | solution.py:166
  11.9 0.7 %copy-start.4 = (s32[1,2]{1,0:T(1,128)S(1)}, s32[1,2]{1,0:T(1,128)}, u32[]{:S(2)}) copy-start(s32[1,2]{1,0:T(1,128)} %ids_ref.1) | copy-start | bytes 28
  11.9 8.4 %collective-permute-start.1 = (f32[32,512]{1,0:T(8,128)S(1)}, f32[32,512]{1,0:T(8,128)S(1)}, u32[]{:S(2)}, u32[]{:S(2)}) collective-permute-start(f32[32,512]{1,0:T(8,128)S(1)} %get-tuple-element.21), channel_id=1, source_target_pairs={{0,8},{4,12},{8,0},{12,4},{1,9},{5,13},{9,1},{13,5},{2,10},{6,14},... | collective-permute-start | bytes 196616 | tf_op jit(solution)/shard_map/ppermute | solution.py:166
  13.2 7.1 %collective-permute-start.2 = (f32[32,512]{1,0:T(8,128)S(1)}, f32[32,512]{1,0:T(8,128)S(1)}, u32[]{:S(2)}, u32[]{:S(2)}) collective-permute-start(f32[32,512]{1,0:T(8,128)S(1)} %get-tuple-element.22), channel_id=1, source_target_pairs={{0,4},{4,0},{8,12},{12,8},{1,5},{5,1},{9,13},{13,9},{2,6},{6,2},{1... | collective-permute-start | bytes 196616 | tf_op jit(solution)/shard_map/ppermute | solution.py:166
  15.8 6.3 %collective-permute-start.7 = (f32[32,512]{1,0:T(8,128)S(1)}, f32[32,512]{1,0:T(8,128)S(1)}, u32[]{:S(2)}, u32[]{:S(2)}) collective-permute-start(f32[32,512]{1,0:T(8,128)S(1)} %get-tuple-element.29), channel_id=1, source_target_pairs={{0,12},{4,8},{8,4},{12,0},{1,13},{5,9},{9,5},{13,1},{2,14},{6,10},... | collective-permute-start | bytes 196616 | tf_op jit(solution)/shard_map/ppermute | solution.py:166
  17.1 6.1 %collective-permute-start.8 = (f32[32,512]{1,0:T(8,128)S(1)}, f32[32,512]{1,0:T(8,128)S(1)}, u32[]{:S(2)}, u32[]{:S(2)}) collective-permute-start(f32[32,512]{1,0:T(8,128)S(1)} %get-tuple-element.30), channel_id=1, source_target_pairs={{0,4},{4,0},{8,12},{12,8},{1,5},{5,1},{9,13},{13,9},{2,6},{6,2},{1... | collective-permute-start | bytes 196616 | tf_op jit(solution)/shard_map/ppermute | solution.py:166
  17.1 6.8 %collective-permute-start.6 = (f32[32,512]{1,0:T(8,128)S(1)}, f32[32,512]{1,0:T(8,128)S(1)}, u32[]{:S(2)}, u32[]{:S(2)}) collective-permute-start(f32[32,512]{1,0:T(8,128)S(1)} %get-tuple-element.27), channel_id=1, source_target_pairs={{0,8},{4,12},{8,0},{12,4},{1,9},{5,13},{9,1},{13,5},{2,10},{6,14},... | collective-permute-start | bytes 196616 | tf_op jit(solution)/shard_map/ppermute | solution.py:166

commit v8 on v6

--- a/solution.py
+++ b/solution.py
@@ -101,29 +101,41 @@
         out_ref[:, j * width : (j + 1) * width] = weigh(table_ref, (2 + j) * members, rows)
 
 
-def cut_kernel(rounds, blocks_ref, *refs):
-    outs, sems = refs[-1 - len(rounds) : -1], refs[-1]
+def cut_kernel(plan, *refs):
+    outs, sems = refs[-1 - len(plan) : -1], refs[-1]
     me = lax.axis_index("code")
-    copies = [
-        pltpu.make_async_copy(blocks_ref.at[me ^ r], out, sems.at[i])
-        for i, (r, out) in enumerate(zip(rounds, outs))
-    ]
+    copies = []
+    for pieces, out in zip(plan, outs):
+        for i, (operand, r) in enumerate(pieces):
+            place = out if len(pieces) == 1 else out.at[i]
+            source = refs[operand].at[me ^ r]
+            copies.append(pltpu.make_async_copy(source, place, sems.at[len(copies)]))
     for copy in copies:
         copy.start()
     for copy in copies:
         copy.wait()
 
 
-def rebuild_paired_kernel(base_ref, table_ref, *refs):
-    rows, outs = refs[: len(refs) // 2], refs[len(refs) // 2 :]
+def rebuild_paired_kernel(base_ref, table_ref, current_ref, *refs):
+    members = len(refs) // 2
+    rows, outs, current_out_ref = refs[:members], refs[members:-1], refs[-1]
     for out_ref, block in zip(outs, rebuilt_for(base_ref, table_ref, [r[...] for r in rows])):
         out_ref[...] = block
+    current_out_ref[...] = current_ref[...]
 
 
 def parity_paired_kernel(table_ref, *refs):
     rows, out_ref, done_ref = refs[:-2], refs[-2], refs[-1]
-    parity_into(out_ref, table_ref, [r[...] for r in rows])
+    parity_into(out_ref, table_ref, [last_of(row) for row in rows])
     done_ref[...] = jnp.zeros(done_ref.shape, done_ref.dtype)
+
+
+def first_of(ref):
+    return ref[0] if len(ref.shape) == 3 else ref[...]
+
+
+def last_of(ref):
+    return ref[1] if len(ref.shape) == 3 else ref[...]
 
 
 def restore_kernel(table_ref, earlier_ref, held_back_by, *refs):
@@ -132,7 +144,7 @@
     last = table_ref.shape[0] - 1
     lost = table_ref[last : last + 1, :] > 0.5
     for c, piece in zip(order_of(members, True), pieces):
-        out_ref[c] = jnp.where(lost, piece[...], earlier_ref[c])
+        out_ref[c] = jnp.where(lost, first_of(piece), earlier_ref[c])
 
 
 def call(kernel, specs, outs, args, flops, **options):
@@ -159,14 +171,16 @@
     ]
 
 
-def cut(blocks, rounds, *held_back_by):
+def cut(slabs, plan, *held_back_by):
+    count = sum(len(pieces) for pieces in plan)
+    block = slabs[0].shape[1:]
     return call(
-        functools.partial(cut_kernel, rounds),
-        [ANYWHERE] * (1 + len(held_back_by)),
-        [floats(*blocks.shape[1:])] * len(rounds),
-        (pltpu.with_memory_space_constraint(blocks, pltpu.HBM), *held_back_by),
+        functools.partial(cut_kernel, plan),
+        [ANYWHERE] * (len(slabs) + len(held_back_by)),
+        [floats(*block) if len(p) == 1 else floats(len(p), *block) for p in plan],
+        (*slabs, *held_back_by),
         0,
-        scratch_shapes=[pltpu.SemaphoreType.DMA((len(rounds),))],
+        scratch_shapes=[pltpu.SemaphoreType.DMA((count,))],
     )
 
 
@@ -194,18 +208,21 @@
     if direct:
         rounds = list(rounds_of(members))
         block = floats(own_rows, width)
-        own_earlier, *cut_earlier = cut(earlier, [0] + rounds)
+        pinned = [pltpu.with_memory_space_constraint(x, pltpu.HBM) for x in (earlier, current)]
+        cut_all = cut(pinned, [[(slab, r)] for slab in range(2) for r in [0] + rounds])
+        own_earlier, *cut_earlier = cut_all[:members]
+        own_current, *cut_current, last_current = cut_all[members:]
         earlier_rows = trade(cut_earlier, rounds, members)
-        own_current, *cut_current = cut(current, [0] + rounds, own_earlier)
-        outgoing = call(
+        current_rows = trade(cut_current, rounds[:-1], members)
+        *outgoing, last_current = call(
             rebuild_paired_kernel,
-            [IN_VMEM] * (members + 2),
-            [block] * members,
-            (base, table, own_earlier, *earlier_rows),
+            [IN_VMEM] * (members + 3),
+            [block] * (members + 1),
+            (base, table, last_current, own_earlier, *earlier_rows),
             rebuild_cost,
         )
         incoming = trade(outgoing[1:], rounds, members)
-        current_rows = [own_current, *trade(cut_current, rounds, members)]
+        current_rows = [own_current, *current_rows, *trade([last_current], rounds[-1:], members)]
         new_parity, parity_done = call(
             parity_paired_kernel,
             [IN_VMEM] * (members + 1),

time: 24.6 us -> 25.8 us (1.049)
  waiting for transfers between devices: 4.69 us -> 6.87 us
  Pallas kernels: 4.22 us -> 3.41 us
    ppermute x9, waiting for transfers between devices: 4.69 us -> 6.87 us  [trade(): lax.ppermute(piece, 'code', [(d, d ^ r) for d in range(members)])]
    pallas_call x6 -> x5, Pallas kernels: 4.22 us -> 3.41 us  [call(): pl.pallas_call(kernel, in_specs=specs, out_specs=jax.tree.map(lambda _: I...]
  transfers between devices with their start and end apart: 9 -> 9, of which waited for: 4 -> 4; matrix products, arithmetic and copies ran while one was open for 0% -> 0% of each run, Pallas kernels for 10% -> 6%
where the time goes in v8:
time: 25.8 us; the launch traced here: 25.7 us
  starting transfers between devices  14 us (54%)
  waiting for transfers between devices  6.87 us (27%)
  Pallas kernels  3.41 us (13%)
  between operations  0.69 us (3%)
  local copies, waits for them, and re-layouts  0.66 us (3%)
    ppermute x9, starting transfers between devices, trade(): lax.ppermute(piece, 'code', [(d, d ^ r) for d in range(members)])  14 us
    ppermute x9, waiting for transfers between devices, trade(): lax.ppermute(piece, 'code', [(d, d ^ r) for d in range(members)])  6.87 us
    pallas_call x5, Pallas kernels, call(): pl.pallas_call(kernel, in_specs=specs, out_specs=jax.tree.map(lambda _: I...  3.41 us
    unnamed x8, local copies, waits for them, and re-layouts  0.66 us
  transfers between devices with their start and end apart: 9, of which 4 were waited for; matrix products, arithmetic and copies ran while one was open for 0% of the time, Pallas kernels for 6%

profile of v8, /device:TPU:0, one launch (start us, length us, event | category | flops | bytes accessed | tf_op | source)
XLA Modules:
  0.0 25.7 jit_solution(13366538891495623081)
XLA Ops:
  0.6 0.0 copy-start.1
  0.6 1.2 %shard_map.69 = (f32[32,512]{1,0:T(8,128)S(1)}, f32[32,512]{1,0:T(8,128)S(1)}, f32[32,512]{1,0:T(8,128)S(1)}, f32[32,512]{1,0:T(8,128)S(1)}, f32[32,512]{1,0:T(8...) custom-call(f32[4,32,512]{2,1,0:T(8,128)} %bitcast.5, f32[4,32,512]{2,1,0:T(8,128)} %bitcast.8), custom_call_target="tpu_custom_call" | custom-call | bytes 1048576 | tf_op jit(solution)/shard_map/pallas_call | solution.py:152
  1.8 5.1 %collective-permute-start.2 = (f32[32,512]{1,0:T(8,128)S(1)}, f32[32,512]{1,0:T(8,128)S(1)}, u32[]{:S(2)}, u32[]{:S(2)}) collective-permute-start(f32[32,512]{1,0:T(8,128)S(1)} %get-tuple-element.26), channel_id=1, source_target_pairs={{0,12},{4,8},{8,4},{12,0},{1,13},{5,9},{9,5},{13,1},{2,14},{6,10},... | collective-permute-start | bytes 196616 | tf_op jit(solution)/shard_map/ppermute | solution.py:169
  6.9 0.0 collective-permute-start.3
  6.9 0.6 %collective-permute-start.4 = (f32[32,512]{1,0:T(8,128)S(1)}, f32[32,512]{1,0:T(8,128)S(1)}, u32[]{:S(2)}, u32[]{:S(2)}) collective-permute-start(f32[32,512]{1,0:T(8,128)S(1)} %get-tuple-element.28), channel_id=1, source_target_pairs={{0,4},{4,0},{8,12},{12,8},{1,5},{5,1},{9,13},{13,9},{2,6},{6,2},{1... | collective-permute-start | bytes 196616 | tf_op jit(solution)/shard_map/ppermute | solution.py:169
  7.6 0.0 copy-start.2
  7.6 3.7 %collective-permute-start = (f32[32,512]{1,0:T(8,128)S(1)}, f32[32,512]{1,0:T(8,128)S(1)}, u32[]{:S(2)}, u32[]{:S(2)}) collective-permute-start(f32[32,512]{1,0:T(8,128)S(1)} %get-tuple-element.21), channel_id=1, source_target_pairs={{0,12},{4,8},{8,4},{12,0},{1,13},{5,9},{9,5},{13,1},{2,14},{6,10},... | collective-permute-start | bytes 196616 | tf_op jit(solution)/shard_map/ppermute | solution.py:169
  11.3 0.0 copy-start.3
  11.3 0.0 collective-permute-start.1
  11.3 0.0 copy-done.1
  11.3 0.0 copy-done.2
  11.3 0.6 %copy-done.3 = s32[1,2]{1,0:T(1,128)S(1)} copy-done((s32[1,2]{1,0:T(1,128)S(1)}, s32[1,2]{1,0:T(1,128)}, u32[]{:S(2)}) %copy-start.3) | copy-done | bytes 32
  12.0 0.6 %shard_map.68 = (f32[2,32,512]{2,1,0:T(8,128)S(1)}, f32[29,512]{1,0:T(8,128)S(1)}) custom-call(s32[1,2]{1,0:T(1,128)S(1)} %copy-done.3, f32[4,4]{1,0:T(4,128)S(1)} %copy-done.2, f32[32,2048]{1,0:T(8,128)S(1)} %bitcast.7), custom_call_target="tpu_custom_call" | custom-call | flops 262144 | bytes 452680 | tf_op jit(solution)/shard_map/pallas_call | solution.py:152
  12.6 0.0 collective-permute-done.2.refs_1_
  12.6 3.1 %collective-permute-done.3.refs_2_ = f32[32,512]{1,0:T(8,128)S(1)} collective-permute-done((f32[32,512]{1,0:T(8,128)S(1)}, f32[32,512]{1,0:T(8,128)S(1)}, u32[]{:S(2)}, u32[]{:S(2)}) %collective-permute-start.3) | collective-permute-done | bytes 65568 | tf_op jit(solution)/shard_map/ppermute | solution.py:169
  15.8 0.0 collective-permute-done.4.refs_3_
  15.8 0.1 shard_map.70
  15.9 0.0 copy-start
  15.9 0.1 collective-permute-start.5
  16.0 3.0 %collective-permute-start.6 = (f32[32,512]{1,0:T(8,128)S(1)}, f32[32,512]{1,0:T(8,128)S(1)}, u32[]{:S(2)}, u32[]{:S(2)}) collective-permute-start(f32[32,512]{1,0:T(8,128)S(1)} %get-tuple-element.33), channel_id=1, source_target_pairs={{0,12},{4,8},{8,4},{12,0},{1,13},{5,9},{9,5},{13,1},{2,14},{6,10},... | collective-permute-start | bytes 196616 | tf_op jit(solution)/shard_map/ppermute | solution.py:169
  19.0 0.5 %collective-permute-start.7 = (f32[32,512]{1,0:T(8,128)S(1)}, f32[32,512]{1,0:T(8,128)S(1)}, u32[]{:S(2)}, u32[]{:S(2)}) collective-permute-start(f32[32,512]{1,0:T(8,128)S(1)} %get-tuple-element.34), channel_id=1, source_target_pairs={{0,8},{4,12},{8,0},{12,4},{1,9},{5,13},{9,1},{13,5},{2,10},{6,14},... | collective-permute-start | bytes 196616 | tf_op jit(solution)/shard_map/ppermute | solution.py:169
  19.5 0.0 collective-permute-done.refs_1_
  19.5 0.9 %collective-permute-start.8 = (f32[32,512]{1,0:T(8,128)S(1)}, f32[32,512]{1,0:T(8,128)S(1)}, u32[]{:S(2)}, u32[]{:S(2)}) collective-permute-start(f32[32,512]{1,0:T(8,128)S(1)} %get-tuple-element.35), channel_id=1, source_target_pairs={{0,4},{4,0},{8,12},{12,8},{1,5},{5,1},{9,13},{13,9},{2,6},{6,2},{1... | collective-permute-start | bytes 196616 | tf_op jit(solution)/shard_map/ppermute | solution.py:169
  20.4 0.0 collective-permute-done.1.refs_2_
  20.4 0.8 %collective-permute-done.5.refs_3_ = f32[32,512]{1,0:T(8,128)S(1)} collective-permute-done((f32[32,512]{1,0:T(8,128)S(1)}, f32[32,512]{1,0:T(8,128)S(1)}, u32[]{:S(2)}, u32[]{:S(2)}) %collective-permute-start.5) | collective-permute-done | bytes 65568 | tf_op jit(solution)/shard_map/ppermute | solution.py:169
  21.2 0.8 %shard_map.71 = (f32[32,2048]{1,0:T(8,128)}, f32[8,128]{1,0:T(8,128)S(1)}) custom-call(f32[29,512]{1,0:T(8,128)S(1)} %get-tuple-element.19.table_ref, f32[32,512]{1,0:T(8,128)S(1)} %get-tuple-element.20.refs_0_, f32[32,512]{1,0:T(8,128)S(1)} %collective-permute-done.refs_1_, f32[32,512]{1,0:T(8,128)S(1)} %collective-permute-done.1.refs_2_, ...), custom_call_target="tpu_custom_call" | custom-call | flops 524288 | bytes 587776 | tf_op jit(solution)/shard_map/pallas_call | solution.py:152
  22.0 0.2 collective-permute-done.6.refs_1_
  22.2 2.7 %collective-permute-done.7.refs_2_ = f32[32,512]{1,0:T(8,128)S(1)} collective-permute-done((f32[32,512]{1,0:T(8,128)S(1)}, f32[32,512]{1,0:T(8,128)S(1)}, u32[]{:S(2)}, u32[]{:S(2)}) %collective-permute-start.7) | collective-permute-done | bytes 65568 | tf_op jit(solution)/shard_map/ppermute | solution.py:169
  24.9 0.0 collective-permute-done.8.refs_3_
  24.9 0.0 copy-done
  24.9 0.8 %shard_map.72 = f32[4,32,512]{2,1,0:T(8,128)} custom-call(f32[29,512]{1,0:T(8,128)S(1)} %get-tuple-element.19.table_ref, f32[4,32,512]{2,1,0:T(8,128)S(1)} %bitcast.6, f32[8,128]{1,0:T(8,128)S(1)} %get-tuple-element.31.held_back_by, f32[32,512]{1,0:T(8,128)S(1)} %get-tuple-element.32.refs_0_, f32[32,512]{1,0:T(8,128)S(1)} %collective-permute-done.6.refs_1_, ...), custom_call_target="tpu_custom_call" | custom-call | bytes 849920 | tf_op jit(solution)/shard_map/pallas_call | solution.py:152
Async XLA Ops:
  0.6 10.7 %copy-start.1 = (f32[1,32,2048]{2,1,0:T(8,128)S(1)}, f32[1,32,2048]{2,1,0:T(8,128)}, u32[]{:S(2)}) copy-start(f32[1,32,2048]{2,1,0:T(8,128)} %param.7) | copy-start | bytes 786436
  1.8 10.8 %collective-permute-start.2 = (f32[32,512]{1,0:T(8,128)S(1)}, f32[32,512]{1,0:T(8,128)S(1)}, u32[]{:S(2)}, u32[]{:S(2)}) collective-permute-start(f32[32,512]{1,0:T(8,128)S(1)} %get-tuple-element.26), channel_id=1, source_target_pairs={{0,12},{4,8},{8,4},{12,0},{1,13},{5,9},{9,5},{13,1},{2,14},{6,10},... | collective-permute-start | bytes 196616 | tf_op jit(solution)/shard_map/ppermute | solution.py:169
  6.9 8.9 %collective-permute-start.3 = (f32[32,512]{1,0:T(8,128)S(1)}, f32[32,512]{1,0:T(8,128)S(1)}, u32[]{:S(2)}, u32[]{:S(2)}) collective-permute-start(f32[32,512]{1,0:T(8,128)S(1)} %get-tuple-element.27), channel_id=1, source_target_pairs={{0,8},{4,12},{8,0},{12,4},{1,9},{5,13},{9,1},{13,5},{2,10},{6,14},... | collective-permute-start | bytes 196616 | tf_op jit(solution)/shard_map/ppermute | solution.py:169
  6.9 8.9 %collective-permute-start.4 = (f32[32,512]{1,0:T(8,128)S(1)}, f32[32,512]{1,0:T(8,128)S(1)}, u32[]{:S(2)}, u32[]{:S(2)}) collective-permute-start(f32[32,512]{1,0:T(8,128)S(1)} %get-tuple-element.28), channel_id=1, source_target_pairs={{0,4},{4,0},{8,12},{12,8},{1,5},{5,1},{9,13},{13,9},{2,6},{6,2},{1... | collective-permute-start | bytes 196616 | tf_op jit(solution)/shard_map/ppermute | solution.py:169
  7.6 3.8 %copy-start.2 = (f32[4,4]{1,0:T(4,128)S(1)}, f32[4,4]{1,0:T(4,128)}, u32[]{:S(2)}) copy-start(f32[4,4]{1,0:T(4,128)} %generator_ref.1) | copy-start | bytes 196
  7.6 11.9 %collective-permute-start = (f32[32,512]{1,0:T(8,128)S(1)}, f32[32,512]{1,0:T(8,128)S(1)}, u32[]{:S(2)}, u32[]{:S(2)}) collective-permute-start(f32[32,512]{1,0:T(8,128)S(1)} %get-tuple-element.21), channel_id=1, source_target_pairs={{0,12},{4,8},{8,4},{12,0},{1,13},{5,9},{9,5},{13,1},{2,14},{6,10},... | collective-permute-start | bytes 196616 | tf_op jit(solution)/shard_map/ppermute | solution.py:169
  11.3 0.7 %copy-start.3 = (s32[1,2]{1,0:T(1,128)S(1)}, s32[1,2]{1,0:T(1,128)}, u32[]{:S(2)}) copy-start(s32[1,2]{1,0:T(1,128)} %ids_ref.1) | copy-start | bytes 28
  11.3 9.1 %collective-permute-start.1 = (f32[32,512]{1,0:T(8,128)S(1)}, f32[32,512]{1,0:T(8,128)S(1)}, u32[]{:S(2)}, u32[]{:S(2)}) collective-permute-start(f32[32,512]{1,0:T(8,128)S(1)} %get-tuple-element.22), channel_id=1, source_target_pairs={{0,8},{4,12},{8,0},{12,4},{1,9},{5,13},{9,1},{13,5},{2,10},{6,14},... | collective-permute-start | bytes 196616 | tf_op jit(solution)/shard_map/ppermute | solution.py:169
  15.9 9.0 %copy-start = (f32[1,1,128,512]{3,2,1,0:T(8,128)S(1)}, f32[1,1,128,512]{3,2,1,0:T(8,128)}, u32[]{:S(2)}) copy-start(f32[1,1,128,512]{3,2,1,0:T(8,128)} %param.6) | copy-start | bytes 786436
  15.9 5.3 %collective-permute-start.5 = (f32[32,512]{1,0:T(8,128)S(1)}, f32[32,512]{1,0:T(8,128)S(1)}, u32[]{:S(2)}, u32[]{:S(2)}) collective-permute-start(f32[32,512]{1,0:T(8,128)S(1)} %get-tuple-element.29), channel_id=1, source_target_pairs={{0,4},{4,0},{8,12},{12,8},{1,5},{5,1},{9,13},{13,9},{2,6},{6,2},{1... | collective-permute-start | bytes 196616 | tf_op jit(solution)/shard_map/ppermute | solution.py:169
  16.0 6.2 %collective-permute-start.6 = (f32[32,512]{1,0:T(8,128)S(1)}, f32[32,512]{1,0:T(8,128)S(1)}, u32[]{:S(2)}, u32[]{:S(2)}) collective-permute-start(f32[32,512]{1,0:T(8,128)S(1)} %get-tuple-element.33), channel_id=1, source_target_pairs={{0,12},{4,8},{8,4},{12,0},{1,13},{5,9},{9,5},{13,1},{2,14},{6,10},... | collective-permute-start | bytes 196616 | tf_op jit(solution)/shard_map/ppermute | solution.py:169
  19.0 5.9 %collective-permute-start.7 = (f32[32,512]{1,0:T(8,128)S(1)}, f32[32,512]{1,0:T(8,128)S(1)}, u32[]{:S(2)}, u32[]{:S(2)}) collective-permute-start(f32[32,512]{1,0:T(8,128)S(1)} %get-tuple-element.34), channel_id=1, source_target_pairs={{0,8},{4,12},{8,0},{12,4},{1,9},{5,13},{9,1},{13,5},{2,10},{6,14},... | collective-permute-start | bytes 196616 | tf_op jit(solution)/shard_map/ppermute | solution.py:169
  19.5 5.4 %collective-permute-start.8 = (f32[32,512]{1,0:T(8,128)S(1)}, f32[32,512]{1,0:T(8,128)S(1)}, u32[]{:S(2)}, u32[]{:S(2)}) collective-permute-start(f32[32,512]{1,0:T(8,128)S(1)} %get-tuple-element.35), channel_id=1, source_target_pairs={{0,4},{4,0},{8,12},{12,8},{1,5},{5,1},{9,13},{13,9},{2,6},{6,2},{1... | collective-permute-start | bytes 196616 | tf_op jit(solution)/shard_map/ppermute | solution.py:169

commit v9 on v6

--- a/solution.py
+++ b/solution.py
@@ -101,19 +101,6 @@
         out_ref[:, j * width : (j + 1) * width] = weigh(table_ref, (2 + j) * members, rows)
 
 
-def cut_kernel(rounds, blocks_ref, *refs):
-    outs, sems = refs[-1 - len(rounds) : -1], refs[-1]
-    me = lax.axis_index("code")
-    copies = [
-        pltpu.make_async_copy(blocks_ref.at[me ^ r], out, sems.at[i])
-        for i, (r, out) in enumerate(zip(rounds, outs))
-    ]
-    for copy in copies:
-        copy.start()
-    for copy in copies:
-        copy.wait()
-
-
 def rebuild_paired_kernel(base_ref, table_ref, *refs):
     rows, outs = refs[: len(refs) // 2], refs[len(refs) // 2 :]
     for out_ref, block in zip(outs, rebuilt_for(base_ref, table_ref, [r[...] for r in rows])):
@@ -159,15 +146,9 @@
     ]
 
 
-def cut(blocks, rounds, *held_back_by):
-    return call(
-        functools.partial(cut_kernel, rounds),
-        [ANYWHERE] * (1 + len(held_back_by)),
-        [floats(*blocks.shape[1:])] * len(rounds),
-        (pltpu.with_memory_space_constraint(blocks, pltpu.HBM), *held_back_by),
-        0,
-        scratch_shapes=[pltpu.SemaphoreType.DMA((len(rounds),))],
-    )
+def cut(blocks, rounds):
+    me = lax.axis_index("code")
+    return [lax.dynamic_index_in_dim(blocks, me ^ r, 0, keepdims=False) for r in rounds]
 
 
 def local(state_slab, previous_slab, previous_parity, generator, failed_ids):
@@ -196,7 +177,7 @@
         block = floats(own_rows, width)
         own_earlier, *cut_earlier = cut(earlier, [0] + rounds)
         earlier_rows = trade(cut_earlier, rounds, members)
-        own_current, *cut_current = cut(current, [0] + rounds, own_earlier)
+        own_current, *cut_current = cut(current, [0] + rounds)
         outgoing = call(
             rebuild_paired_kernel,
             [IN_VMEM] * (members + 2),

time: 24.6 us -> 24.5 us (level)
  Pallas kernels: 4.22 us -> 2.23 us
  local copies, waits for them, and re-layouts: 0.66 us -> 1.69 us
  waiting for transfers between devices: 4.69 us -> 5.64 us
    pallas_call x6 -> x4, Pallas kernels: 4.22 us -> 2.23 us  [call(): pl.pallas_call(kernel, in_specs=specs, out_specs=jax.tree.map(lambda _: I...]
    squeeze x0 -> x2, local copies, waits for them, and re-layouts: none -> 1.02 us  [cut(): lax.dynamic_index_in_dim(blocks, me ^ r, 0, keepdims=False)]
    ppermute x9, waiting for transfers between devices: 4.69 us -> 5.64 us  [trade(): lax.ppermute(piece, 'code', [(d, d ^ r) for d in range(members)])]
    unnamed x8 -> x10, local copies, waits for them, and re-layouts: 0.66 us -> 0.66 us
  transfers between devices with their start and end apart: 9 -> 9, of which waited for: 4 -> 3; matrix products, arithmetic and copies ran while one was open for 0% -> 0% of each run, Pallas kernels for 10% -> 6%
where the time goes in v9:
time: 24.5 us; the launch traced here: 24.4 us
  starting transfers between devices  14.1 us (58%)
  waiting for transfers between devices  5.64 us (23%)
  Pallas kernels  2.23 us (9%)
  local copies, waits for them, and re-layouts  1.69 us (7%)
  between operations  0.72 us (3%)
    ppermute x9, starting transfers between devices, trade(): lax.ppermute(piece, 'code', [(d, d ^ r) for d in range(members)])  14.1 us
    ppermute x9, waiting for transfers between devices, trade(): lax.ppermute(piece, 'code', [(d, d ^ r) for d in range(members)])  5.64 us
    pallas_call x4, Pallas kernels, call(): pl.pallas_call(kernel, in_specs=specs, out_specs=jax.tree.map(lambda _: I...  2.23 us
    squeeze x2, local copies, waits for them, and re-layouts, cut(): lax.dynamic_index_in_dim(blocks, me ^ r, 0, keepdims=False)  1.02 us
    unnamed x10, local copies, waits for them, and re-layouts  0.66 us
  transfers between devices with their start and end apart: 9, of which 3 were waited for; matrix products, arithmetic and copies ran while one was open for 0% of the time, Pallas kernels for 6%

profile of v9, /device:TPU:0, one launch (start us, length us, event | category | flops | bytes accessed | tf_op | source)
XLA Modules:
  0.0 24.4 jit_solution(2411597229839353742)
XLA Ops:
  0.6 0.0 copy-start.4
  0.7 1.0 %dynamic-slice_bitcast_fusion = (f32[32,512]{1,0:T(8,128)S(1)}, f32[32,512]{1,0:T(8,128)S(1)}, f32[32,512]{1,0:T(8,128)S(1)}, f32[32,512]{1,0:T(8,128)S(1)}) fusion(f32[4,32,512]{2,1,0:T(8,128)} %bitcast.21, s32[]{:T(128)S(6)} %select_n.20, s32[]{:T(128)S(6)} %select_n.19, s32[]{:T(128)S(6)} %select_n.18, s32[]{:T(128)S(6)} %select_n.17), kind=kLoop, calls=%fused_computation | loop fusion | bytes 524304 | tf_op jit(solution)/shard_map/jit(dynamic_index_in_dim)/squeeze | solution.py:151
  1.7 5.1 %collective-permute-start.3 = (f32[32,512]{1,0:T(8,128)S(1)}, f32[32,512]{1,0:T(8,128)S(1)}, u32[]{:S(2)}, u32[]{:S(2)}) collective-permute-start(f32[32,512]{1,0:T(8,128)S(1)} %get-tuple-element.20), channel_id=1, source_target_pairs={{0,12},{4,8},{8,4},{12,0},{1,13},{5,9},{9,5},{13,1},{2,14},{6,10},... | collective-permute-start | bytes 196616 | tf_op jit(solution)/shard_map/ppermute | solution.py:144
  6.8 0.0 collective-permute-start.4
  6.8 0.6 %collective-permute-start.5 = (f32[32,512]{1,0:T(8,128)S(1)}, f32[32,512]{1,0:T(8,128)S(1)}, u32[]{:S(2)}, u32[]{:S(2)}) collective-permute-start(f32[32,512]{1,0:T(8,128)S(1)} %get-tuple-element.18), channel_id=1, source_target_pairs={{0,4},{4,0},{8,12},{12,8},{1,5},{5,1},{9,13},{13,9},{2,6},{6,2},{1... | collective-permute-start | bytes 196616 | tf_op jit(solution)/shard_map/ppermute | solution.py:144
  7.4 0.0 copy-done.4
  7.4 0.0 copy-start.1
  7.4 0.0 copy-start.2
  7.5 3.8 %collective-permute-start = (f32[32,512]{1,0:T(8,128)S(1)}, f32[32,512]{1,0:T(8,128)S(1)}, u32[]{:S(2)}, u32[]{:S(2)}) collective-permute-start(f32[32,512]{1,0:T(8,128)S(1)} %get-tuple-element.24), channel_id=1, source_target_pairs={{0,12},{4,8},{8,4},{12,0},{1,13},{5,9},{9,5},{13,1},{2,14},{6,10},... | collective-permute-start | bytes 196616 | tf_op jit(solution)/shard_map/ppermute | solution.py:144
  11.3 0.0 copy-start.3
  11.3 0.0 collective-permute-start.1
  11.3 0.0 copy-done.1
  11.3 0.0 copy-done.2
  11.3 0.6 %copy-done.3 = s32[1,2]{1,0:T(1,128)S(1)} copy-done((s32[1,2]{1,0:T(1,128)S(1)}, s32[1,2]{1,0:T(1,128)}, u32[]{:S(2)}) %copy-start.3) | copy-done | bytes 32
  11.9 0.6 %shard_map.68 = (f32[2,32,512]{2,1,0:T(8,128)S(1)}, f32[29,512]{1,0:T(8,128)S(1)}) custom-call(s32[1,2]{1,0:T(1,128)S(1)} %copy-done.3, f32[4,4]{1,0:T(4,128)S(1)} %copy-done.2, f32[32,2048]{1,0:T(8,128)S(1)} %bitcast.23), custom_call_target="tpu_custom_call" | custom-call | flops 262144 | bytes 452680 | tf_op jit(solution)/shard_map/pallas_call | solution.py:127
  12.6 0.0 collective-permute-done.3.refs_1_
  12.6 0.1 collective-permute-start.2
  12.7 3.0 %collective-permute-done.4.refs_2_ = f32[32,512]{1,0:T(8,128)S(1)} collective-permute-done((f32[32,512]{1,0:T(8,128)S(1)}, f32[32,512]{1,0:T(8,128)S(1)}, u32[]{:S(2)}, u32[]{:S(2)}) %collective-permute-start.4) | collective-permute-done | bytes 65568 | tf_op jit(solution)/shard_map/ppermute | solution.py:144
  15.6 0.0 collective-permute-done.5.refs_3_
  15.6 0.1 shard_map.70
  15.7 0.0 copy-start
  15.7 2.2 %collective-permute-start.6 = (f32[32,512]{1,0:T(8,128)S(1)}, f32[32,512]{1,0:T(8,128)S(1)}, u32[]{:S(2)}, u32[]{:S(2)}) collective-permute-start(f32[32,512]{1,0:T(8,128)S(1)} %get-tuple-element.15), channel_id=1, source_target_pairs={{0,12},{4,8},{8,4},{12,0},{1,13},{5,9},{9,5},{13,1},{2,14},{6,10},... | collective-permute-start | bytes 196616 | tf_op jit(solution)/shard_map/ppermute | solution.py:144
  17.9 0.0 collective-permute-start.7
  17.9 0.0 collective-permute-done.refs_1_
  17.9 2.2 %collective-permute-start.8 = (f32[32,512]{1,0:T(8,128)S(1)}, f32[32,512]{1,0:T(8,128)S(1)}, u32[]{:S(2)}, u32[]{:S(2)}) collective-permute-start(f32[32,512]{1,0:T(8,128)S(1)} %get-tuple-element.17), channel_id=1, source_target_pairs={{0,4},{4,0},{8,12},{12,8},{1,5},{5,1},{9,13},{13,9},{2,6},{6,2},{1... | collective-permute-start | bytes 196616 | tf_op jit(solution)/shard_map/ppermute | solution.py:144
  20.2 0.0 collective-permute-done.1.refs_2_
  20.2 0.0 collective-permute-done.2.refs_3_
  20.2 0.8 %shard_map.69 = (f32[32,2048]{1,0:T(8,128)}, f32[8,128]{1,0:T(8,128)S(1)}) custom-call(f32[29,512]{1,0:T(8,128)S(1)} %get-tuple-element.10.table_ref, f32[32,512]{1,0:T(8,128)S(1)} %get-tuple-element.25.refs_0_, f32[32,512]{1,0:T(8,128)S(1)} %collective-permute-done.refs_1_, f32[32,512]{1,0:T(8,128)S(1)} %collective-permute-done.1.refs_2_, ...), custom_call_target="tpu_custom_call" | custom-call | flops 524288 | bytes 587776 | tf_op jit(solution)/shard_map/pallas_call | solution.py:127
  21.0 1.0 %collective-permute-done.6.refs_1_ = f32[32,512]{1,0:T(8,128)S(1)} collective-permute-done((f32[32,512]{1,0:T(8,128)S(1)}, f32[32,512]{1,0:T(8,128)S(1)}, u32[]{:S(2)}, u32[]{:S(2)}) %collective-permute-start.6) | collective-permute-done | bytes 65568 | tf_op jit(solution)/shard_map/ppermute | solution.py:144
  22.0 1.7 %collective-permute-done.7.refs_2_ = f32[32,512]{1,0:T(8,128)S(1)} collective-permute-done((f32[32,512]{1,0:T(8,128)S(1)}, f32[32,512]{1,0:T(8,128)S(1)}, u32[]{:S(2)}, u32[]{:S(2)}) %collective-permute-start.7) | collective-permute-done | bytes 65568 | tf_op jit(solution)/shard_map/ppermute | solution.py:144
  23.6 0.0 collective-permute-done.8.refs_3_
  23.6 0.0 copy-done
  23.6 0.8 %shard_map.71 = f32[4,32,512]{2,1,0:T(8,128)} custom-call(f32[29,512]{1,0:T(8,128)S(1)} %get-tuple-element.10.table_ref, f32[4,32,512]{2,1,0:T(8,128)S(1)} %bitcast.22, f32[8,128]{1,0:T(8,128)S(1)} %get-tuple-element.12.held_back_by, f32[32,512]{1,0:T(8,128)S(1)} %get-tuple-element.14.refs_0_, f32[32,512]{1,0:T(8,128)S(1)} %collective-permute-done.6.refs_1_, ...), custom_call_target="tpu_custom_call" | custom-call | bytes 849920 | tf_op jit(solution)/shard_map/pallas_call | solution.py:127
  (1 shorter events, 0.0 us)
Async XLA Ops:
  0.6 6.8 %copy-start.4 = (f32[1,1,128,512]{3,2,1,0:T(8,128)S(1)}, f32[1,1,128,512]{3,2,1,0:T(8,128)}, u32[]{:S(2)}) copy-start(f32[1,1,128,512]{3,2,1,0:T(8,128)} %param.5) | copy-start | bytes 786436
  1.7 10.9 %collective-permute-start.3 = (f32[32,512]{1,0:T(8,128)S(1)}, f32[32,512]{1,0:T(8,128)S(1)}, u32[]{:S(2)}, u32[]{:S(2)}) collective-permute-start(f32[32,512]{1,0:T(8,128)S(1)} %get-tuple-element.20), channel_id=1, source_target_pairs={{0,12},{4,8},{8,4},{12,0},{1,13},{5,9},{9,5},{13,1},{2,14},{6,10},... | collective-permute-start | bytes 196616 | tf_op jit(solution)/shard_map/ppermute | solution.py:144
  6.8 8.9 %collective-permute-start.4 = (f32[32,512]{1,0:T(8,128)S(1)}, f32[32,512]{1,0:T(8,128)S(1)}, u32[]{:S(2)}, u32[]{:S(2)}) collective-permute-start(f32[32,512]{1,0:T(8,128)S(1)} %get-tuple-element.19), channel_id=1, source_target_pairs={{0,8},{4,12},{8,0},{12,4},{1,9},{5,13},{9,1},{13,5},{2,10},{6,14},... | collective-permute-start | bytes 196616 | tf_op jit(solution)/shard_map/ppermute | solution.py:144
  6.8 8.9 %collective-permute-start.5 = (f32[32,512]{1,0:T(8,128)S(1)}, f32[32,512]{1,0:T(8,128)S(1)}, u32[]{:S(2)}, u32[]{:S(2)}) collective-permute-start(f32[32,512]{1,0:T(8,128)S(1)} %get-tuple-element.18), channel_id=1, source_target_pairs={{0,4},{4,0},{8,12},{12,8},{1,5},{5,1},{9,13},{13,9},{2,6},{6,2},{1... | collective-permute-start | bytes 196616 | tf_op jit(solution)/shard_map/ppermute | solution.py:144
  7.4 3.9 %copy-start.1 = (f32[1,32,2048]{2,1,0:T(8,128)S(1)}, f32[1,32,2048]{2,1,0:T(8,128)}, u32[]{:S(2)}) copy-start(f32[1,32,2048]{2,1,0:T(8,128)} %param.7) | copy-start | bytes 786436
  7.4 3.8 %copy-start.2 = (f32[4,4]{1,0:T(4,128)S(1)}, f32[4,4]{1,0:T(4,128)}, u32[]{:S(2)}) copy-start(f32[4,4]{1,0:T(4,128)} %generator_ref.1) | copy-start | bytes 196
  7.5 10.5 %collective-permute-start = (f32[32,512]{1,0:T(8,128)S(1)}, f32[32,512]{1,0:T(8,128)S(1)}, u32[]{:S(2)}, u32[]{:S(2)}) collective-permute-start(f32[32,512]{1,0:T(8,128)S(1)} %get-tuple-element.24), channel_id=1, source_target_pairs={{0,12},{4,8},{8,4},{12,0},{1,13},{5,9},{9,5},{13,1},{2,14},{6,10},... | collective-permute-start | bytes 196616 | tf_op jit(solution)/shard_map/ppermute | solution.py:144
  11.3 0.7 %copy-start.3 = (s32[1,2]{1,0:T(1,128)S(1)}, s32[1,2]{1,0:T(1,128)}, u32[]{:S(2)}) copy-start(s32[1,2]{1,0:T(1,128)} %ids_ref.1) | copy-start | bytes 28
  11.3 8.9 %collective-permute-start.1 = (f32[32,512]{1,0:T(8,128)S(1)}, f32[32,512]{1,0:T(8,128)S(1)}, u32[]{:S(2)}, u32[]{:S(2)}) collective-permute-start(f32[32,512]{1,0:T(8,128)S(1)} %get-tuple-element.23), channel_id=1, source_target_pairs={{0,8},{4,12},{8,0},{12,4},{1,9},{5,13},{9,1},{13,5},{2,10},{6,14},... | collective-permute-start | bytes 196616 | tf_op jit(solution)/shard_map/ppermute | solution.py:144
  12.6 7.6 %collective-permute-start.2 = (f32[32,512]{1,0:T(8,128)S(1)}, f32[32,512]{1,0:T(8,128)S(1)}, u32[]{:S(2)}, u32[]{:S(2)}) collective-permute-start(f32[32,512]{1,0:T(8,128)S(1)} %get-tuple-element.22), channel_id=1, source_target_pairs={{0,4},{4,0},{8,12},{12,8},{1,5},{5,1},{9,13},{13,9},{2,6},{6,2},{1... | collective-permute-start | bytes 196616 | tf_op jit(solution)/shard_map/ppermute | solution.py:144
  15.7 7.9 %copy-start = (f32[1,1,128,512]{3,2,1,0:T(8,128)S(1)}, f32[1,1,128,512]{3,2,1,0:T(8,128)}, u32[]{:S(2)}) copy-start(f32[1,1,128,512]{3,2,1,0:T(8,128)} %param.6) | copy-start | bytes 786436
  15.7 6.3 %collective-permute-start.6 = (f32[32,512]{1,0:T(8,128)S(1)}, f32[32,512]{1,0:T(8,128)S(1)}, u32[]{:S(2)}, u32[]{:S(2)}) collective-permute-start(f32[32,512]{1,0:T(8,128)S(1)} %get-tuple-element.15), channel_id=1, source_target_pairs={{0,12},{4,8},{8,4},{12,0},{1,13},{5,9},{9,5},{13,1},{2,14},{6,10},... | collective-permute-start | bytes 196616 | tf_op jit(solution)/shard_map/ppermute | solution.py:144
  17.9 5.7 %collective-permute-start.7 = (f32[32,512]{1,0:T(8,128)S(1)}, f32[32,512]{1,0:T(8,128)S(1)}, u32[]{:S(2)}, u32[]{:S(2)}) collective-permute-start(f32[32,512]{1,0:T(8,128)S(1)} %get-tuple-element.16), channel_id=1, source_target_pairs={{0,8},{4,12},{8,0},{12,4},{1,9},{5,13},{9,1},{13,5},{2,10},{6,14},... | collective-permute-start | bytes 196616 | tf_op jit(solution)/shard_map/ppermute | solution.py:144
  17.9 5.7 %collective-permute-start.8 = (f32[32,512]{1,0:T(8,128)S(1)}, f32[32,512]{1,0:T(8,128)S(1)}, u32[]{:S(2)}, u32[]{:S(2)}) collective-permute-start(f32[32,512]{1,0:T(8,128)S(1)} %get-tuple-element.17), channel_id=1, source_target_pairs={{0,4},{4,0},{8,12},{12,8},{1,5},{5,1},{9,13},{13,9},{2,6},{6,2},{1... | collective-permute-start | bytes 196616 | tf_op jit(solution)/shard_map/ppermute | solution.py:144

commit v10 on v9

--- a/solution.py
+++ b/solution.py
@@ -24,6 +24,18 @@
         return list(range(members))
     me = lax.axis_index("code")
     return [me ^ r for r in (0, *rounds_of(members))]
+
+
+def targets_of(members, direct):
+    if not direct:
+        return list(range(members))
+    me = lax.axis_index("code")
+    return [lax.rem(me + s, members) for s in range(members)]
+
+
+def sources_of(members):
+    me = lax.axis_index("code")
+    return [lax.rem(me + members - s, members) for s in range(members)]
 
 
 def plan_kernel(direct, ids_ref, generator_ref, parity_ref, base_ref, table_ref):
@@ -62,6 +74,7 @@
             )
         for j in range(spans):
             put((2 + j) * members + i, spread(column[j]))
+    for i, c in enumerate(targets_of(members, direct)):
         put((2 + spans) * members + i, spread(jnp.where(first == c, 1.0, 0.0)))
     me = lax.axis_index("code")
     lost = jnp.logical_or(first == me, second == me)
@@ -118,7 +131,7 @@
     members = len(pieces)
     last = table_ref.shape[0] - 1
     lost = table_ref[last : last + 1, :] > 0.5
-    for c, piece in zip(order_of(members, True), pieces):
+    for c, piece in zip(sources_of(members), pieces):
         out_ref[c] = jnp.where(lost, piece[...], earlier_ref[c])
 
 
@@ -137,6 +150,13 @@
 
 def floats(*shape):
     return jax.ShapeDtypeStruct(shape, jnp.float32)
+
+
+def pass_on(pieces, members):
+    return [
+        lax.ppermute(piece, "code", [(d, (d + s) % members) for d in range(members)])
+        for s, piece in enumerate(pieces, 1)
+    ]
 
 
 def trade(pieces, rounds, members):
@@ -185,7 +205,7 @@
             (base, table, own_earlier, *earlier_rows),
             rebuild_cost,
         )
-        incoming = trade(outgoing[1:], rounds, members)
+        incoming = pass_on(outgoing[1:], members)
         current_rows = [own_current, *trade(cut_current, rounds, members)]
         new_parity, parity_done = call(
             parity_paired_kernel,

time: 24.5 us -> 24 us (0.980)
  starting transfers between devices: 14.1 us -> 13.5 us
    ppermute x9 -> x6, starting transfers between devices: 14.1 us -> 9.64 us  [trade(): lax.ppermute(piece, 'code', [(d, d ^ r) for d in range(members)])]
    ppermute x0 -> x3, starting transfers between devices: none -> 3.87 us  [pass_on(): lax.ppermute(piece, 'code', [(d, (d + s) % members) for d in range(member...]
    ppermute x0 -> x3, waiting for transfers between devices: none -> 2.4 us  [pass_on(): lax.ppermute(piece, 'code', [(d, (d + s) % members) for d in range(member...]
    ppermute x9 -> x6, waiting for transfers between devices: 5.64 us -> 3.27 us  [trade(): lax.ppermute(piece, 'code', [(d, d ^ r) for d in range(members)])]
  transfers between devices with their start and end apart: 9 -> 9, of which waited for: 3 -> 4; matrix products, arithmetic and copies ran while one was open for 0% -> 0% of each run, Pallas kernels for 6% -> 6%
where the time goes in v10:
time: 24 us; the launch traced here: 23.8 us
  starting transfers between devices  13.5 us (56%)
  waiting for transfers between devices  5.67 us (24%)
  Pallas kernels  2.22 us (9%)
  local copies, waits for them, and re-layouts  1.69 us (7%)
  between operations  0.73 us (3%)
    ppermute x6, starting transfers between devices, trade(): lax.ppermute(piece, 'code', [(d, d ^ r) for d in range(members)])  9.64 us
    ppermute x3, starting transfers between devices, pass_on(): lax.ppermute(piece, 'code', [(d, (d + s) % members) for d in range(member...  3.87 us
    ppermute x6, waiting for transfers between devices, trade(): lax.ppermute(piece, 'code', [(d, d ^ r) for d in range(members)])  3.27 us
    ppermute x3, waiting for transfers between devices, pass_on(): lax.ppermute(piece, 'code', [(d, (d + s) % members) for d in range(member...  2.4 us
    pallas_call x4, Pallas kernels, call(): pl.pallas_call(kernel, in_specs=specs, out_specs=jax.tree.map(lambda _: I...  2.22 us
    squeeze x2, local copies, waits for them, and re-layouts, cut(): lax.dynamic_index_in_dim(blocks, me ^ r, 0, keepdims=False)  1.02 us
    unnamed x10, local copies, waits for them, and re-layouts  0.66 us
  transfers between devices with their start and end apart: 9, of which 4 were waited for; matrix products, arithmetic and copies ran while one was open for 0% of the time, Pallas kernels for 6%

profile of v10, /device:TPU:0, one launch (start us, length us, event | category | flops | bytes accessed | tf_op | source)
XLA Modules:
  0.0 23.8 jit_solution(4774501473834109255)
XLA Ops:
  0.6 0.0 copy-start.4
  0.7 1.0 %dynamic-slice_bitcast_fusion = (f32[32,512]{1,0:T(8,128)S(1)}, f32[32,512]{1,0:T(8,128)S(1)}, f32[32,512]{1,0:T(8,128)S(1)}, f32[32,512]{1,0:T(8,128)S(1)}) fusion(f32[4,32,512]{2,1,0:T(8,128)} %bitcast.21, s32[]{:T(128)S(6)} %select_n.20, s32[]{:T(128)S(6)} %select_n.19, s32[]{:T(128)S(6)} %select_n.18, s32[]{:T(128)S(6)} %select_n.17), kind=kLoop, calls=%fused_computation | loop fusion | bytes 524304 | tf_op jit(solution)/shard_map/jit(dynamic_index_in_dim)/squeeze | solution.py:171
  1.7 5.1 %collective-permute-start.3 = (f32[32,512]{1,0:T(8,128)S(1)}, f32[32,512]{1,0:T(8,128)S(1)}, u32[]{:S(2)}, u32[]{:S(2)}) collective-permute-start(f32[32,512]{1,0:T(8,128)S(1)} %get-tuple-element.20), channel_id=1, source_target_pairs={{0,12},{4,8},{8,4},{12,0},{1,13},{5,9},{9,5},{13,1},{2,14},{6,10},... | collective-permute-start | bytes 196616 | tf_op jit(solution)/shard_map/ppermute | solution.py:164
  6.8 0.0 collective-permute-start.4
  6.8 0.6 %collective-permute-start.5 = (f32[32,512]{1,0:T(8,128)S(1)}, f32[32,512]{1,0:T(8,128)S(1)}, u32[]{:S(2)}, u32[]{:S(2)}) collective-permute-start(f32[32,512]{1,0:T(8,128)S(1)} %get-tuple-element.18), channel_id=1, source_target_pairs={{0,4},{4,0},{8,12},{12,8},{1,5},{5,1},{9,13},{13,9},{2,6},{6,2},{1... | collective-permute-start | bytes 196616 | tf_op jit(solution)/shard_map/ppermute | solution.py:164
  7.4 0.0 copy-done.4
  7.4 0.0 copy-start.1
  7.4 0.0 copy-start.2
  7.5 3.8 %collective-permute-start = (f32[32,512]{1,0:T(8,128)S(1)}, f32[32,512]{1,0:T(8,128)S(1)}, u32[]{:S(2)}, u32[]{:S(2)}) collective-permute-start(f32[32,512]{1,0:T(8,128)S(1)} %get-tuple-element.24), channel_id=1, source_target_pairs={{0,12},{4,8},{8,4},{12,0},{1,13},{5,9},{9,5},{13,1},{2,14},{6,10},... | collective-permute-start | bytes 196616 | tf_op jit(solution)/shard_map/ppermute | solution.py:164
  11.3 0.0 copy-start.3
  11.3 0.0 collective-permute-start.1
  11.3 0.0 copy-done.1
  11.3 0.0 copy-done.2
  11.3 0.6 %copy-done.3 = s32[1,2]{1,0:T(1,128)S(1)} copy-done((s32[1,2]{1,0:T(1,128)S(1)}, s32[1,2]{1,0:T(1,128)}, u32[]{:S(2)}) %copy-start.3) | copy-done | bytes 32
  11.9 0.6 %shard_map.68 = (f32[2,32,512]{2,1,0:T(8,128)S(1)}, f32[29,512]{1,0:T(8,128)S(1)}) custom-call(s32[1,2]{1,0:T(1,128)S(1)} %copy-done.3, f32[4,4]{1,0:T(4,128)S(1)} %copy-done.2, f32[32,2048]{1,0:T(8,128)S(1)} %bitcast.23), custom_call_target="tpu_custom_call" | custom-call | flops 262144 | bytes 452680 | tf_op jit(solution)/shard_map/pallas_call | solution.py:140
  12.6 0.0 collective-permute-done.3.refs_1_
  12.6 0.1 collective-permute-start.2
  12.7 3.0 %collective-permute-done.4.refs_2_ = f32[32,512]{1,0:T(8,128)S(1)} collective-permute-done((f32[32,512]{1,0:T(8,128)S(1)}, f32[32,512]{1,0:T(8,128)S(1)}, u32[]{:S(2)}, u32[]{:S(2)}) %collective-permute-start.4) | collective-permute-done | bytes 65568 | tf_op jit(solution)/shard_map/ppermute | solution.py:164
  15.6 0.0 collective-permute-done.5.refs_3_
  15.6 0.1 shard_map.70
  15.7 0.0 copy-start
  15.7 0.1 collective-permute-start.6
  15.8 2.8 %collective-permute-start.7 = (f32[32,512]{1,0:T(8,128)S(1)}, f32[32,512]{1,0:T(8,128)S(1)}, u32[]{:S(2)}, u32[]{:S(2)}) collective-permute-start(f32[32,512]{1,0:T(8,128)S(1)} %get-tuple-element.16), channel_id=1, source_target_pairs={{0,8},{4,12},{8,0},{12,4},{1,9},{5,13},{9,1},{13,5},{2,10},{6,14},... | collective-permute-start | bytes 196616 | tf_op jit(solution)/shard_map/ppermute | solution.py:157
  18.5 0.0 collective-permute-done.refs_1_
  18.5 1.1 %collective-permute-start.8 = (f32[32,512]{1,0:T(8,128)S(1)}, f32[32,512]{1,0:T(8,128)S(1)}, u32[]{:S(2)}, u32[]{:S(2)}) collective-permute-start(f32[32,512]{1,0:T(8,128)S(1)} %get-tuple-element.17), channel_id=1, source_target_pairs={{0,12},{4,0},{8,4},{12,8},{1,13},{5,1},{9,5},{13,9},{2,14},{6,2},{... | collective-permute-start | bytes 196616 | tf_op jit(solution)/shard_map/ppermute | solution.py:157
  19.6 0.3 %collective-permute-done.1.refs_2_ = f32[32,512]{1,0:T(8,128)S(1)} collective-permute-done((f32[32,512]{1,0:T(8,128)S(1)}, f32[32,512]{1,0:T(8,128)S(1)}, u32[]{:S(2)}, u32[]{:S(2)}) %collective-permute-start.1) | collective-permute-done | bytes 65568 | tf_op jit(solution)/shard_map/ppermute | solution.py:164
  19.9 0.0 collective-permute-done.2.refs_3_
  19.9 0.8 %shard_map.69 = (f32[32,2048]{1,0:T(8,128)}, f32[8,128]{1,0:T(8,128)S(1)}) custom-call(f32[29,512]{1,0:T(8,128)S(1)} %get-tuple-element.10.table_ref, f32[32,512]{1,0:T(8,128)S(1)} %get-tuple-element.25.refs_0_, f32[32,512]{1,0:T(8,128)S(1)} %collective-permute-done.refs_1_, f32[32,512]{1,0:T(8,128)S(1)} %collective-permute-done.1.refs_2_, ...), custom_call_target="tpu_custom_call" | custom-call | flops 524288 | bytes 587776 | tf_op jit(solution)/shard_map/pallas_call | solution.py:140
  20.7 1.3 %collective-permute-done.6.refs_1_ = f32[32,512]{1,0:T(8,128)S(1)} collective-permute-done((f32[32,512]{1,0:T(8,128)S(1)}, f32[32,512]{1,0:T(8,128)S(1)}, u32[]{:S(2)}, u32[]{:S(2)}) %collective-permute-start.6) | collective-permute-done | bytes 65568 | tf_op jit(solution)/shard_map/ppermute | solution.py:157
  21.9 1.1 %collective-permute-done.7.refs_2_ = f32[32,512]{1,0:T(8,128)S(1)} collective-permute-done((f32[32,512]{1,0:T(8,128)S(1)}, f32[32,512]{1,0:T(8,128)S(1)}, u32[]{:S(2)}, u32[]{:S(2)}) %collective-permute-start.7) | collective-permute-done | bytes 65568 | tf_op jit(solution)/shard_map/ppermute | solution.py:157
  23.1 0.0 collective-permute-done.8.refs_3_
  23.1 0.0 copy-done
  23.1 0.7 %shard_map.71 = f32[4,32,512]{2,1,0:T(8,128)} custom-call(f32[29,512]{1,0:T(8,128)S(1)} %get-tuple-element.10.table_ref, f32[4,32,512]{2,1,0:T(8,128)S(1)} %bitcast.22, f32[8,128]{1,0:T(8,128)S(1)} %get-tuple-element.12.held_back_by, f32[32,512]{1,0:T(8,128)S(1)} %get-tuple-element.14.refs_0_, f32[32,512]{1,0:T(8,128)S(1)} %collective-permute-done.6.refs_1_, ...), custom_call_target="tpu_custom_call" | custom-call | bytes 849920 | tf_op jit(solution)/shard_map/pallas_call | solution.py:140
  (1 shorter events, 0.0 us)
Async XLA Ops:
  0.6 6.8 %copy-start.4 = (f32[1,1,128,512]{3,2,1,0:T(8,128)S(1)}, f32[1,1,128,512]{3,2,1,0:T(8,128)}, u32[]{:S(2)}) copy-start(f32[1,1,128,512]{3,2,1,0:T(8,128)} %param.5) | copy-start | bytes 786436
  1.7 10.9 %collective-permute-start.3 = (f32[32,512]{1,0:T(8,128)S(1)}, f32[32,512]{1,0:T(8,128)S(1)}, u32[]{:S(2)}, u32[]{:S(2)}) collective-permute-start(f32[32,512]{1,0:T(8,128)S(1)} %get-tuple-element.20), channel_id=1, source_target_pairs={{0,12},{4,8},{8,4},{12,0},{1,13},{5,9},{9,5},{13,1},{2,14},{6,10},... | collective-permute-start | bytes 196616 | tf_op jit(solution)/shard_map/ppermute | solution.py:164
  6.8 8.9 %collective-permute-start.4 = (f32[32,512]{1,0:T(8,128)S(1)}, f32[32,512]{1,0:T(8,128)S(1)}, u32[]{:S(2)}, u32[]{:S(2)}) collective-permute-start(f32[32,512]{1,0:T(8,128)S(1)} %get-tuple-element.19), channel_id=1, source_target_pairs={{0,8},{4,12},{8,0},{12,4},{1,9},{5,13},{9,1},{13,5},{2,10},{6,14},... | collective-permute-start | bytes 196616 | tf_op jit(solution)/shard_map/ppermute | solution.py:164
  6.8 8.9 %collective-permute-start.5 = (f32[32,512]{1,0:T(8,128)S(1)}, f32[32,512]{1,0:T(8,128)S(1)}, u32[]{:S(2)}, u32[]{:S(2)}) collective-permute-start(f32[32,512]{1,0:T(8,128)S(1)} %get-tuple-element.18), channel_id=1, source_target_pairs={{0,4},{4,0},{8,12},{12,8},{1,5},{5,1},{9,13},{13,9},{2,6},{6,2},{1... | collective-permute-start | bytes 196616 | tf_op jit(solution)/shard_map/ppermute | solution.py:164
  7.4 3.9 %copy-start.1 = (f32[1,32,2048]{2,1,0:T(8,128)S(1)}, f32[1,32,2048]{2,1,0:T(8,128)}, u32[]{:S(2)}) copy-start(f32[1,32,2048]{2,1,0:T(8,128)} %param.7) | copy-start | bytes 786436
  7.4 3.8 %copy-start.2 = (f32[4,4]{1,0:T(4,128)S(1)}, f32[4,4]{1,0:T(4,128)}, u32[]{:S(2)}) copy-start(f32[4,4]{1,0:T(4,128)} %generator_ref.1) | copy-start | bytes 196
  7.5 11.1 %collective-permute-start = (f32[32,512]{1,0:T(8,128)S(1)}, f32[32,512]{1,0:T(8,128)S(1)}, u32[]{:S(2)}, u32[]{:S(2)}) collective-permute-start(f32[32,512]{1,0:T(8,128)S(1)} %get-tuple-element.24), channel_id=1, source_target_pairs={{0,12},{4,8},{8,4},{12,0},{1,13},{5,9},{9,5},{13,1},{2,14},{6,10},... | collective-permute-start | bytes 196616 | tf_op jit(solution)/shard_map/ppermute | solution.py:164
  11.3 0.7 %copy-start.3 = (s32[1,2]{1,0:T(1,128)S(1)}, s32[1,2]{1,0:T(1,128)}, u32[]{:S(2)}) copy-start(s32[1,2]{1,0:T(1,128)} %ids_ref.1) | copy-start | bytes 28
  11.3 8.6 %collective-permute-start.1 = (f32[32,512]{1,0:T(8,128)S(1)}, f32[32,512]{1,0:T(8,128)S(1)}, u32[]{:S(2)}, u32[]{:S(2)}) collective-permute-start(f32[32,512]{1,0:T(8,128)S(1)} %get-tuple-element.23), channel_id=1, source_target_pairs={{0,8},{4,12},{8,0},{12,4},{1,9},{5,13},{9,1},{13,5},{2,10},{6,14},... | collective-permute-start | bytes 196616 | tf_op jit(solution)/shard_map/ppermute | solution.py:164
  12.6 7.3 %collective-permute-start.2 = (f32[32,512]{1,0:T(8,128)S(1)}, f32[32,512]{1,0:T(8,128)S(1)}, u32[]{:S(2)}, u32[]{:S(2)}) collective-permute-start(f32[32,512]{1,0:T(8,128)S(1)} %get-tuple-element.22), channel_id=1, source_target_pairs={{0,4},{4,0},{8,12},{12,8},{1,5},{5,1},{9,13},{13,9},{2,6},{6,2},{1... | collective-permute-start | bytes 196616 | tf_op jit(solution)/shard_map/ppermute | solution.py:164
  15.7 7.4 %copy-start = (f32[1,1,128,512]{3,2,1,0:T(8,128)S(1)}, f32[1,1,128,512]{3,2,1,0:T(8,128)}, u32[]{:S(2)}) copy-start(f32[1,1,128,512]{3,2,1,0:T(8,128)} %param.6) | copy-start | bytes 786436
  15.7 6.2 %collective-permute-start.6 = (f32[32,512]{1,0:T(8,128)S(1)}, f32[32,512]{1,0:T(8,128)S(1)}, u32[]{:S(2)}, u32[]{:S(2)}) collective-permute-start(f32[32,512]{1,0:T(8,128)S(1)} %get-tuple-element.15), channel_id=1, source_target_pairs={{0,4},{4,8},{8,12},{12,0},{1,5},{5,9},{9,13},{13,1},{2,6},{6,10},{... | collective-permute-start | bytes 196616 | tf_op jit(solution)/shard_map/ppermute | solution.py:157
  15.8 7.3 %collective-permute-start.7 = (f32[32,512]{1,0:T(8,128)S(1)}, f32[32,512]{1,0:T(8,128)S(1)}, u32[]{:S(2)}, u32[]{:S(2)}) collective-permute-start(f32[32,512]{1,0:T(8,128)S(1)} %get-tuple-element.16), channel_id=1, source_target_pairs={{0,8},{4,12},{8,0},{12,4},{1,9},{5,13},{9,1},{13,5},{2,10},{6,14},... | collective-permute-start | bytes 196616 | tf_op jit(solution)/shard_map/ppermute | solution.py:157
  18.5 4.5 %collective-permute-start.8 = (f32[32,512]{1,0:T(8,128)S(1)}, f32[32,512]{1,0:T(8,128)S(1)}, u32[]{:S(2)}, u32[]{:S(2)}) collective-permute-start(f32[32,512]{1,0:T(8,128)S(1)} %get-tuple-element.17), channel_id=1, source_target_pairs={{0,12},{4,0},{8,4},{12,8},{1,13},{5,1},{9,5},{13,9},{2,14},{6,2},{... | collective-permute-start | bytes 196616 | tf_op jit(solution)/shard_map/ppermute | solution.py:157

commit v11 on v10

--- a/solution.py
+++ b/solution.py
@@ -33,7 +33,9 @@
     return [lax.rem(me + s, members) for s in range(members)]
 
 
-def sources_of(members):
+def sources_of(members, direct):
+    if not direct:
+        return list(range(members))
     me = lax.axis_index("code")
     return [lax.rem(me + members - s, members) for s in range(members)]
 
@@ -72,8 +74,9 @@
                 k * members + i,
                 sum(weights[k][j] * jnp.where(alive, column[j], 0.0) for j in range(spans)),
             )
+    for i, c in enumerate(sources_of(members, direct)):
         for j in range(spans):
-            put((2 + j) * members + i, spread(column[j]))
+            put((2 + j) * members + i, spread(generator_ref[j, c]))
     for i, c in enumerate(targets_of(members, direct)):
         put((2 + spans) * members + i, spread(jnp.where(first == c, 1.0, 0.0)))
     me = lax.axis_index("code")
@@ -131,7 +134,7 @@
     members = len(pieces)
     last = table_ref.shape[0] - 1
     lost = table_ref[last : last + 1, :] > 0.5
-    for c, piece in zip(sources_of(members), pieces):
+    for c, piece in zip(sources_of(members, True), pieces):
         out_ref[c] = jnp.where(lost, piece[...], earlier_ref[c])
 
 
@@ -166,9 +169,8 @@
     ]
 
 
-def cut(blocks, rounds):
-    me = lax.axis_index("code")
-    return [lax.dynamic_index_in_dim(blocks, me ^ r, 0, keepdims=False) for r in rounds]
+def cut(blocks, order):
+    return [lax.dynamic_index_in_dim(blocks, c, 0, keepdims=False) for c in order]
 
 
 def local(state_slab, previous_slab, previous_parity, generator, failed_ids):
@@ -195,9 +197,9 @@
     if direct:
         rounds = list(rounds_of(members))
         block = floats(own_rows, width)
-        own_earlier, *cut_earlier = cut(earlier, [0] + rounds)
+        own_earlier, *cut_earlier = cut(earlier, order_of(members, True))
         earlier_rows = trade(cut_earlier, rounds, members)
-        own_current, *cut_current = cut(current, [0] + rounds)
+        own_current, *cut_current = cut(current, targets_of(members, True))
         outgoing = call(
             rebuild_paired_kernel,
             [IN_VMEM] * (members + 2),
@@ -206,7 +208,7 @@
             rebuild_cost,
         )
         incoming = pass_on(outgoing[1:], members)
-        current_rows = [own_current, *trade(cut_current, rounds, members)]
+        current_rows = [own_current, *pass_on(cut_current, members)]
         new_parity, parity_done = call(
             parity_paired_kernel,
             [IN_VMEM] * (members + 1),

time: 24 us -> 23.6 us (0.983)
  starting transfers between devices: 13.5 us -> 15 us
  waiting for transfers between devices: 5.67 us -> 4.37 us
  local copies, waits for them, and re-layouts: 1.69 us -> 1.04 us
    ppermute x3 -> x6, starting transfers between devices: 3.87 us -> 9.28 us  [pass_on(): lax.ppermute(piece, 'code', [(d, (d + s) % members) for d in range(member...]
    ppermute x6 -> x3, starting transfers between devices: 9.64 us -> 5.76 us  [trade(): lax.ppermute(piece, 'code', [(d, d ^ r) for d in range(members)])]
    ppermute x6 -> x3, waiting for transfers between devices: 3.27 us -> 1.26 us  [trade(): lax.ppermute(piece, 'code', [(d, d ^ r) for d in range(members)])]
    ppermute x3 -> x6, waiting for transfers between devices: 2.4 us -> 3.11 us  [pass_on(): lax.ppermute(piece, 'code', [(d, (d + s) % members) for d in range(member...]
    unnamed x10, local copies, waits for them, and re-layouts: 0.66 us -> 0.02 us
  transfers between devices with their start and end apart: 9 -> 9, of which waited for: 4 -> 3; matrix products, arithmetic and copies ran while one was open for 0% -> 0% of each run, Pallas kernels for 6% -> 6%
where the time goes in v11:
time: 23.6 us; the launch traced here: 23.4 us
  starting transfers between devices  15 us (64%)
  waiting for transfers between devices  4.37 us (19%)
  Pallas kernels  2.24 us (9%)
  local copies, waits for them, and re-layouts  1.04 us (4%)
  between operations  0.72 us (3%)
    ppermute x6, starting transfers between devices, pass_on(): lax.ppermute(piece, 'code', [(d, (d + s) % members) for d in range(member...  9.28 us
    ppermute x3, starting transfers between devices, trade(): lax.ppermute(piece, 'code', [(d, d ^ r) for d in range(members)])  5.76 us
    ppermute x6, waiting for transfers between devices, pass_on(): lax.ppermute(piece, 'code', [(d, (d + s) % members) for d in range(member...  3.11 us
    pallas_call x4, Pallas kernels, call(): pl.pallas_call(kernel, in_specs=specs, out_specs=jax.tree.map(lambda _: I...  2.24 us
    ppermute x3, waiting for transfers between devices, trade(): lax.ppermute(piece, 'code', [(d, d ^ r) for d in range(members)])  1.26 us
    squeeze x2, local copies, waits for them, and re-layouts, cut(): lax.dynamic_index_in_dim(blocks, c, 0, keepdims=False)  1.02 us
  transfers between devices with their start and end apart: 9, of which 3 were waited for; matrix products, arithmetic and copies ran while one was open for 0% of the time, Pallas kernels for 6%

profile of v11, /device:TPU:0, one launch (start us, length us, event | category | flops | bytes accessed | tf_op | source)
XLA Modules:
  0.0 23.4 jit_solution(10445585810772724347)
XLA Ops:
  0.6 0.0 copy-start.4
  0.7 1.0 %dynamic-slice_bitcast_fusion = (f32[32,512]{1,0:T(8,128)S(1)}, f32[32,512]{1,0:T(8,128)S(1)}, f32[32,512]{1,0:T(8,128)S(1)}, f32[32,512]{1,0:T(8,128)S(1)}) fusion(f32[4,32,512]{2,1,0:T(8,128)} %bitcast.21, s32[]{:T(128)S(6)} %select_n.32, s32[]{:T(128)S(6)} %select_n.31, s32[]{:T(128)S(6)} %select_n.30, s32[]{:T(128)S(6)} %select_n.29), kind=kLoop, calls=%fused_computation | loop fusion | bytes 524304 | tf_op jit(solution)/shard_map/jit(dynamic_index_in_dim)/squeeze | solution.py:173
  1.7 5.1 %collective-permute-start.3 = (f32[32,512]{1,0:T(8,128)S(1)}, f32[32,512]{1,0:T(8,128)S(1)}, u32[]{:S(2)}, u32[]{:S(2)}) collective-permute-start(f32[32,512]{1,0:T(8,128)S(1)} %get-tuple-element.20), channel_id=1, source_target_pairs={{0,12},{4,8},{8,4},{12,0},{1,13},{5,9},{9,5},{13,1},{2,14},{6,10},... | collective-permute-start | bytes 196616 | tf_op jit(solution)/shard_map/ppermute | solution.py:167
  6.8 0.0 collective-permute-start.4
  6.8 0.6 %collective-permute-start.5 = (f32[32,512]{1,0:T(8,128)S(1)}, f32[32,512]{1,0:T(8,128)S(1)}, u32[]{:S(2)}, u32[]{:S(2)}) collective-permute-start(f32[32,512]{1,0:T(8,128)S(1)} %get-tuple-element.18), channel_id=1, source_target_pairs={{0,4},{4,0},{8,12},{12,8},{1,5},{5,1},{9,13},{13,9},{2,6},{6,2},{1... | collective-permute-start | bytes 196616 | tf_op jit(solution)/shard_map/ppermute | solution.py:167
  7.4 0.0 copy-done.4
  7.4 0.0 copy-start.1
  7.4 0.0 copy-start.2
  7.5 1.4 %collective-permute-start = (f32[32,512]{1,0:T(8,128)S(1)}, f32[32,512]{1,0:T(8,128)S(1)}, u32[]{:S(2)}, u32[]{:S(2)}) collective-permute-start(f32[32,512]{1,0:T(8,128)S(1)} %get-tuple-element.24), channel_id=1, source_target_pairs={{0,4},{4,8},{8,12},{12,0},{1,5},{5,9},{9,13},{13,1},{2,6},{6,10},{... | collective-permute-start | bytes 196616 | tf_op jit(solution)/shard_map/ppermute | solution.py:160
  8.9 0.0 copy-start.3
  8.9 2.9 %collective-permute-start.1 = (f32[32,512]{1,0:T(8,128)S(1)}, f32[32,512]{1,0:T(8,128)S(1)}, u32[]{:S(2)}, u32[]{:S(2)}) collective-permute-start(f32[32,512]{1,0:T(8,128)S(1)} %get-tuple-element.23), channel_id=1, source_target_pairs={{0,8},{4,12},{8,0},{12,4},{1,9},{5,13},{9,1},{13,5},{2,10},{6,14},... | collective-permute-start | bytes 196616 | tf_op jit(solution)/shard_map/ppermute | solution.py:160
  11.8 0.0 copy-done.1
  11.8 0.0 copy-done.2
  11.8 0.0 copy-done.3
  11.8 0.7 %shard_map.68 = (f32[2,32,512]{2,1,0:T(8,128)S(1)}, f32[29,512]{1,0:T(8,128)S(1)}) custom-call(s32[1,2]{1,0:T(1,128)S(1)} %copy-done.3, f32[4,4]{1,0:T(4,128)S(1)} %copy-done.2, f32[32,2048]{1,0:T(8,128)S(1)} %bitcast.23), custom_call_target="tpu_custom_call" | custom-call | flops 262144 | bytes 452680 | tf_op jit(solution)/shard_map/pallas_call | solution.py:143
  12.5 0.0 collective-permute-done.3.refs_1_
  12.5 1.1 %collective-permute-start.2 = (f32[32,512]{1,0:T(8,128)S(1)}, f32[32,512]{1,0:T(8,128)S(1)}, u32[]{:S(2)}, u32[]{:S(2)}) collective-permute-start(f32[32,512]{1,0:T(8,128)S(1)} %get-tuple-element.22), channel_id=1, source_target_pairs={{0,12},{4,0},{8,4},{12,8},{1,13},{5,1},{9,5},{13,9},{2,14},{6,2},{... | collective-permute-start | bytes 196616 | tf_op jit(solution)/shard_map/ppermute | solution.py:160
  13.6 1.3 %collective-permute-done.4.refs_2_ = f32[32,512]{1,0:T(8,128)S(1)} collective-permute-done((f32[32,512]{1,0:T(8,128)S(1)}, f32[32,512]{1,0:T(8,128)S(1)}, u32[]{:S(2)}, u32[]{:S(2)}) %collective-permute-start.4) | collective-permute-done | bytes 65568 | tf_op jit(solution)/shard_map/ppermute | solution.py:167
  14.8 0.0 collective-permute-done.5.refs_3_
  14.8 0.1 shard_map.70
  14.9 0.0 copy-start
  14.9 0.1 collective-permute-start.6
  15.0 1.9 %collective-permute-start.7 = (f32[32,512]{1,0:T(8,128)S(1)}, f32[32,512]{1,0:T(8,128)S(1)}, u32[]{:S(2)}, u32[]{:S(2)}) collective-permute-start(f32[32,512]{1,0:T(8,128)S(1)} %get-tuple-element.16), channel_id=1, source_target_pairs={{0,8},{4,12},{8,0},{12,4},{1,9},{5,13},{9,1},{13,5},{2,10},{6,14},... | collective-permute-start | bytes 196616 | tf_op jit(solution)/shard_map/ppermute | solution.py:160
  16.8 0.0 collective-permute-done.refs_1_
  16.8 2.0 %collective-permute-start.8 = (f32[32,512]{1,0:T(8,128)S(1)}, f32[32,512]{1,0:T(8,128)S(1)}, u32[]{:S(2)}, u32[]{:S(2)}) collective-permute-start(f32[32,512]{1,0:T(8,128)S(1)} %get-tuple-element.17), channel_id=1, source_target_pairs={{0,12},{4,0},{8,4},{12,8},{1,13},{5,1},{9,5},{13,9},{2,14},{6,2},{... | collective-permute-start | bytes 196616 | tf_op jit(solution)/shard_map/ppermute | solution.py:160
  18.8 0.0 collective-permute-done.1.refs_2_
  18.8 0.0 collective-permute-done.2.refs_3_
  18.8 0.8 %shard_map.69 = (f32[32,2048]{1,0:T(8,128)}, f32[8,128]{1,0:T(8,128)S(1)}) custom-call(f32[29,512]{1,0:T(8,128)S(1)} %get-tuple-element.10.table_ref, f32[32,512]{1,0:T(8,128)S(1)} %get-tuple-element.25.refs_0_, f32[32,512]{1,0:T(8,128)S(1)} %collective-permute-done.refs_1_, f32[32,512]{1,0:T(8,128)S(1)} %collective-permute-done.1.refs_2_, ...), custom_call_target="tpu_custom_call" | custom-call | flops 524288 | bytes 587776 | tf_op jit(solution)/shard_map/pallas_call | solution.py:143
  19.6 1.6 %collective-permute-done.6.refs_1_ = f32[32,512]{1,0:T(8,128)S(1)} collective-permute-done((f32[32,512]{1,0:T(8,128)S(1)}, f32[32,512]{1,0:T(8,128)S(1)}, u32[]{:S(2)}, u32[]{:S(2)}) %collective-permute-start.6) | collective-permute-done | bytes 65568 | tf_op jit(solution)/shard_map/ppermute | solution.py:160
  21.1 1.5 %collective-permute-done.7.refs_2_ = f32[32,512]{1,0:T(8,128)S(1)} collective-permute-done((f32[32,512]{1,0:T(8,128)S(1)}, f32[32,512]{1,0:T(8,128)S(1)}, u32[]{:S(2)}, u32[]{:S(2)}) %collective-permute-start.7) | collective-permute-done | bytes 65568 | tf_op jit(solution)/shard_map/ppermute | solution.py:160
  22.7 0.0 collective-permute-done.8.refs_3_
  22.7 0.0 copy-done
  22.7 0.7 %shard_map.71 = f32[4,32,512]{2,1,0:T(8,128)} custom-call(f32[29,512]{1,0:T(8,128)S(1)} %get-tuple-element.10.table_ref, f32[4,32,512]{2,1,0:T(8,128)S(1)} %bitcast.22, f32[8,128]{1,0:T(8,128)S(1)} %get-tuple-element.12.held_back_by, f32[32,512]{1,0:T(8,128)S(1)} %get-tuple-element.14.refs_0_, f32[32,512]{1,0:T(8,128)S(1)} %collective-permute-done.6.refs_1_, ...), custom_call_target="tpu_custom_call" | custom-call | bytes 849920 | tf_op jit(solution)/shard_map/pallas_call | solution.py:143
  (1 shorter events, 0.0 us)
Async XLA Ops:
  0.6 6.8 %copy-start.4 = (f32[1,1,128,512]{3,2,1,0:T(8,128)S(1)}, f32[1,1,128,512]{3,2,1,0:T(8,128)}, u32[]{:S(2)}) copy-start(f32[1,1,128,512]{3,2,1,0:T(8,128)} %param.5) | copy-start | bytes 786436
  1.7 10.8 %collective-permute-start.3 = (f32[32,512]{1,0:T(8,128)S(1)}, f32[32,512]{1,0:T(8,128)S(1)}, u32[]{:S(2)}, u32[]{:S(2)}) collective-permute-start(f32[32,512]{1,0:T(8,128)S(1)} %get-tuple-element.20), channel_id=1, source_target_pairs={{0,12},{4,8},{8,4},{12,0},{1,13},{5,9},{9,5},{13,1},{2,14},{6,10},... | collective-permute-start | bytes 196616 | tf_op jit(solution)/shard_map/ppermute | solution.py:167
  6.8 8.0 %collective-permute-start.4 = (f32[32,512]{1,0:T(8,128)S(1)}, f32[32,512]{1,0:T(8,128)S(1)}, u32[]{:S(2)}, u32[]{:S(2)}) collective-permute-start(f32[32,512]{1,0:T(8,128)S(1)} %get-tuple-element.19), channel_id=1, source_target_pairs={{0,8},{4,12},{8,0},{12,4},{1,9},{5,13},{9,1},{13,5},{2,10},{6,14},... | collective-permute-start | bytes 196616 | tf_op jit(solution)/shard_map/ppermute | solution.py:167
  6.8 8.0 %collective-permute-start.5 = (f32[32,512]{1,0:T(8,128)S(1)}, f32[32,512]{1,0:T(8,128)S(1)}, u32[]{:S(2)}, u32[]{:S(2)}) collective-permute-start(f32[32,512]{1,0:T(8,128)S(1)} %get-tuple-element.18), channel_id=1, source_target_pairs={{0,4},{4,0},{8,12},{12,8},{1,5},{5,1},{9,13},{13,9},{2,6},{6,2},{1... | collective-permute-start | bytes 196616 | tf_op jit(solution)/shard_map/ppermute | solution.py:167
  7.4 4.4 %copy-start.1 = (f32[1,32,2048]{2,1,0:T(8,128)S(1)}, f32[1,32,2048]{2,1,0:T(8,128)}, u32[]{:S(2)}) copy-start(f32[1,32,2048]{2,1,0:T(8,128)} %param.7) | copy-start | bytes 786436
  7.4 4.4 %copy-start.2 = (f32[4,4]{1,0:T(4,128)S(1)}, f32[4,4]{1,0:T(4,128)}, u32[]{:S(2)}) copy-start(f32[4,4]{1,0:T(4,128)} %generator_ref.1) | copy-start | bytes 196
  7.5 9.4 %collective-permute-start = (f32[32,512]{1,0:T(8,128)S(1)}, f32[32,512]{1,0:T(8,128)S(1)}, u32[]{:S(2)}, u32[]{:S(2)}) collective-permute-start(f32[32,512]{1,0:T(8,128)S(1)} %get-tuple-element.24), channel_id=1, source_target_pairs={{0,4},{4,8},{8,12},{12,0},{1,5},{5,9},{9,13},{13,1},{2,6},{6,10},{... | collective-permute-start | bytes 196616 | tf_op jit(solution)/shard_map/ppermute | solution.py:160
  8.9 2.9 %copy-start.3 = (s32[1,2]{1,0:T(1,128)S(1)}, s32[1,2]{1,0:T(1,128)}, u32[]{:S(2)}) copy-start(s32[1,2]{1,0:T(1,128)} %ids_ref.1) | copy-start | bytes 28
  8.9 9.9 %collective-permute-start.1 = (f32[32,512]{1,0:T(8,128)S(1)}, f32[32,512]{1,0:T(8,128)S(1)}, u32[]{:S(2)}, u32[]{:S(2)}) collective-permute-start(f32[32,512]{1,0:T(8,128)S(1)} %get-tuple-element.23), channel_id=1, source_target_pairs={{0,8},{4,12},{8,0},{12,4},{1,9},{5,13},{9,1},{13,5},{2,10},{6,14},... | collective-permute-start | bytes 196616 | tf_op jit(solution)/shard_map/ppermute | solution.py:160
  12.5 6.3 %collective-permute-start.2 = (f32[32,512]{1,0:T(8,128)S(1)}, f32[32,512]{1,0:T(8,128)S(1)}, u32[]{:S(2)}, u32[]{:S(2)}) collective-permute-start(f32[32,512]{1,0:T(8,128)S(1)} %get-tuple-element.22), channel_id=1, source_target_pairs={{0,12},{4,0},{8,4},{12,8},{1,13},{5,1},{9,5},{13,9},{2,14},{6,2},{... | collective-permute-start | bytes 196616 | tf_op jit(solution)/shard_map/ppermute | solution.py:160
  14.9 7.8 %copy-start = (f32[1,1,128,512]{3,2,1,0:T(8,128)S(1)}, f32[1,1,128,512]{3,2,1,0:T(8,128)}, u32[]{:S(2)}) copy-start(f32[1,1,128,512]{3,2,1,0:T(8,128)} %param.6) | copy-start | bytes 786436
  14.9 6.2 %collective-permute-start.6 = (f32[32,512]{1,0:T(8,128)S(1)}, f32[32,512]{1,0:T(8,128)S(1)}, u32[]{:S(2)}, u32[]{:S(2)}) collective-permute-start(f32[32,512]{1,0:T(8,128)S(1)} %get-tuple-element.15), channel_id=1, source_target_pairs={{0,4},{4,8},{8,12},{12,0},{1,5},{5,9},{9,13},{13,1},{2,6},{6,10},{... | collective-permute-start | bytes 196616 | tf_op jit(solution)/shard_map/ppermute | solution.py:160
  15.0 7.7 %collective-permute-start.7 = (f32[32,512]{1,0:T(8,128)S(1)}, f32[32,512]{1,0:T(8,128)S(1)}, u32[]{:S(2)}, u32[]{:S(2)}) collective-permute-start(f32[32,512]{1,0:T(8,128)S(1)} %get-tuple-element.16), channel_id=1, source_target_pairs={{0,8},{4,12},{8,0},{12,4},{1,9},{5,13},{9,1},{13,5},{2,10},{6,14},... | collective-permute-start | bytes 196616 | tf_op jit(solution)/shard_map/ppermute | solution.py:160
  16.8 5.9 %collective-permute-start.8 = (f32[32,512]{1,0:T(8,128)S(1)}, f32[32,512]{1,0:T(8,128)S(1)}, u32[]{:S(2)}, u32[]{:S(2)}) collective-permute-start(f32[32,512]{1,0:T(8,128)S(1)} %get-tuple-element.17), channel_id=1, source_target_pairs={{0,12},{4,0},{8,4},{12,8},{1,13},{5,1},{9,5},{13,9},{2,14},{6,2},{... | collective-permute-start | bytes 196616 | tf_op jit(solution)/shard_map/ppermute | solution.py:160

commit v12 on v9

--- a/solution.py
+++ b/solution.py
@@ -15,15 +15,27 @@
 KERNEL_VMEM = 8 * 2**20
 
 
-def rounds_of(members):
-    return range(members - 1, 0, -1)
-
-
-def order_of(members, direct):
-    if not direct:
-        return list(range(members))
-    me = lax.axis_index("code")
-    return [me ^ r for r in (0, *rounds_of(members))]
+def partners_of(members):
+    return list(range(1, members))
+
+
+def shifts_of(members):
+    return list(range(members)), [0, *range(members - 2, 0, -1), members - 1]
+
+
+def met(members):
+    me = lax.axis_index("code")
+    return [me ^ r for r in [0] + partners_of(members)]
+
+
+def ahead(members, shifts):
+    me = lax.axis_index("code")
+    return [lax.rem(me + s, members) for s in shifts]
+
+
+def behind(members, shifts):
+    me = lax.axis_index("code")
+    return [lax.rem(me + members - s, members) for s in shifts]
 
 
 def plan_kernel(direct, ids_ref, generator_ref, parity_ref, base_ref, table_ref):
@@ -52,7 +64,13 @@
         base_ref[k] = sum(
             weights[k][j] * parity_ref[:, j * width : (j + 1) * width] for j in range(spans)
         )
-    for i, c in enumerate(order_of(members, direct)):
+    from_earlier = from_current = to_rebuilt = list(range(members))
+    if direct:
+        rebuilt_shifts, current_shifts = shifts_of(members)
+        from_earlier = met(members)
+        from_current = behind(members, current_shifts)
+        to_rebuilt = ahead(members, rebuilt_shifts)
+    for i, c in enumerate(from_earlier):
         column = [generator_ref[j, c] for j in range(spans)]
         alive = jnp.logical_and(first != c, second != c)
         for k in range(2):
@@ -60,8 +78,10 @@
                 k * members + i,
                 sum(weights[k][j] * jnp.where(alive, column[j], 0.0) for j in range(spans)),
             )
+    for i, c in enumerate(from_current):
         for j in range(spans):
-            put((2 + j) * members + i, spread(column[j]))
+            put((2 + j) * members + i, spread(generator_ref[j, c]))
+    for i, c in enumerate(to_rebuilt):
         put((2 + spans) * members + i, spread(jnp.where(first == c, 1.0, 0.0)))
     me = lax.axis_index("code")
     lost = jnp.logical_or(first == me, second == me)
@@ -101,24 +121,21 @@
         out_ref[:, j * width : (j + 1) * width] = weigh(table_ref, (2 + j) * members, rows)
 
 
-def rebuild_paired_kernel(base_ref, table_ref, *refs):
-    rows, outs = refs[: len(refs) // 2], refs[len(refs) // 2 :]
+def rebuild_paired_kernel(base_ref, table_ref, current_ref, *refs):
+    members = len(refs) // 2
+    rows, outs, current_out_ref = refs[:members], refs[members:-1], refs[-1]
     for out_ref, block in zip(outs, rebuilt_for(base_ref, table_ref, [r[...] for r in rows])):
         out_ref[...] = block
-
-
-def parity_paired_kernel(table_ref, *refs):
-    rows, out_ref, done_ref = refs[:-2], refs[-2], refs[-1]
-    parity_into(out_ref, table_ref, [r[...] for r in rows])
-    done_ref[...] = jnp.zeros(done_ref.shape, done_ref.dtype)
-
-
-def restore_kernel(table_ref, earlier_ref, held_back_by, *refs):
-    pieces, out_ref = refs[:-1], refs[-1]
-    members = len(pieces)
+    current_out_ref[...] = current_ref[...]
+
+
+def finish_kernel(table_ref, earlier_ref, *refs):
+    members = (len(refs) - 2) // 2
+    pieces, rows, (parity_ref, out_ref) = refs[:members], refs[members:-2], refs[-2:]
+    parity_into(parity_ref, table_ref, [r[...] for r in rows])
     last = table_ref.shape[0] - 1
     lost = table_ref[last : last + 1, :] > 0.5
-    for c, piece in zip(order_of(members, True), pieces):
+    for c, piece in zip(behind(members, shifts_of(members)[0]), pieces):
         out_ref[c] = jnp.where(lost, piece[...], earlier_ref[c])
 
 
@@ -139,16 +156,20 @@
     return jax.ShapeDtypeStruct(shape, jnp.float32)
 
 
+def permute(pieces, targets):
+    return [lax.ppermute(p, "code", list(enumerate(t))) for p, t in zip(pieces, targets)]
+
+
+def pass_on(pieces, shifts, members):
+    return permute(pieces, [[(d + s) % members for d in range(members)] for s in shifts])
+
+
 def trade(pieces, rounds, members):
-    return [
-        lax.ppermute(piece, "code", [(d, d ^ r) for d in range(members)])
-        for r, piece in zip(rounds, pieces)
-    ]
-
-
-def cut(blocks, rounds):
-    me = lax.axis_index("code")
-    return [lax.dynamic_index_in_dim(blocks, me ^ r, 0, keepdims=False) for r in rounds]
+    return permute(pieces, [[d ^ r for d in range(members)] for r in rounds])
+
+
+def cut(blocks, order):
+    return [lax.dynamic_index_in_dim(blocks, c, 0, keepdims=False) for c in order]
 
 
 def local(state_slab, previous_slab, previous_parity, generator, failed_ids):
@@ -173,33 +194,27 @@
     rebuild_cost = 4 * slab_rows * width
     parity_cost = 2 * spans * slab_rows * width
     if direct:
-        rounds = list(rounds_of(members))
+        rebuilt_shifts, current_shifts = shifts_of(members)
         block = floats(own_rows, width)
-        own_earlier, *cut_earlier = cut(earlier, [0] + rounds)
-        earlier_rows = trade(cut_earlier, rounds, members)
-        own_current, *cut_current = cut(current, [0] + rounds)
-        outgoing = call(
+        own_earlier, *cut_earlier = cut(earlier, met(members))
+        earlier_rows = trade(cut_earlier, partners_of(members), members)
+        own_current, *cut_current = cut(current, ahead(members, current_shifts))
+        *outgoing, last_current = call(
             rebuild_paired_kernel,
-            [IN_VMEM] * (members + 2),
-            [block] * members,
-            (base, table, own_earlier, *earlier_rows),
+            [IN_VMEM] * (members + 3),
+            [block] * (members + 1),
+            (base, table, cut_current[-1], own_earlier, *earlier_rows),
             rebuild_cost,
         )
-        incoming = trade(outgoing[1:], rounds, members)
-        current_rows = [own_current, *trade(cut_current, rounds, members)]
-        new_parity, parity_done = call(
-            parity_paired_kernel,
-            [IN_VMEM] * (members + 1),
-            (parity_shape, floats(8, 128)),
-            (table, *current_rows),
+        incoming = pass_on(outgoing[1:], rebuilt_shifts[1:], members)
+        cut_current[-1] = last_current
+        current_rows = [own_current, *pass_on(cut_current, current_shifts[1:], members)]
+        new_parity, restored_state = call(
+            finish_kernel,
+            [IN_VMEM] * (2 + 2 * members),
+            (parity_shape, floats(*blocks)),
+            (table, earlier, outgoing[0], *incoming, *current_rows),
             parity_cost,
-        )
-        restored_state = call(
-            restore_kernel,
-            [IN_VMEM, IN_VMEM, ANYWHERE] + [IN_VMEM] * members,
-            floats(*blocks),
-            (table, earlier, parity_done, outgoing[0], *incoming),
-            0,
         )
     else:
         earlier_rows = lax.all_to_all(earlier, "code", 0, 0, tiled=True)

time: 24.5 us -> 24.9 us (1.016)
  waiting for transfers between devices: 5.64 us -> 6.76 us
  local copies, waits for them, and re-layouts: 1.69 us -> 1.04 us
  Pallas kernels: 2.23 us -> 1.6 us
  starting transfers between devices: 14.1 us -> 14.6 us
    ppermute x9, waiting for transfers between devices: 5.64 us -> 6.76 us  [permute(): lax.ppermute(p, 'code', list(enumerate(t)))]
    unnamed x10, local copies, waits for them, and re-layouts: 0.66 us -> 0.02 us
    pallas_call x4 -> x3, Pallas kernels: 2.23 us -> 1.6 us  [call(): pl.pallas_call(kernel, in_specs=specs, out_specs=jax.tree.map(lambda _: I...]
    ppermute x9, starting transfers between devices: 14.1 us -> 14.6 us  [permute(): lax.ppermute(p, 'code', list(enumerate(t)))]
  transfers between devices with their start and end apart: 9 -> 9, of which waited for: 3 -> 4; matrix products, arithmetic and copies ran while one was open for 0% -> 0% of each run, Pallas kernels for 6% -> 3%
where the time goes in v12:
time: 24.9 us; the launch traced here: 24.7 us
  starting transfers between devices  14.6 us (59%)
  waiting for transfers between devices  6.76 us (27%)
  Pallas kernels  1.6 us (6%)
  local copies, waits for them, and re-layouts  1.04 us (4%)
  between operations  0.71 us (3%)
    ppermute x9, starting transfers between devices, permute(): lax.ppermute(p, 'code', list(enumerate(t)))  14.6 us
    ppermute x9, waiting for transfers between devices, permute(): lax.ppermute(p, 'code', list(enumerate(t)))  6.76 us
    pallas_call x3, Pallas kernels, call(): pl.pallas_call(kernel, in_specs=specs, out_specs=jax.tree.map(lambda _: I...  1.6 us
    squeeze x2, local copies, waits for them, and re-layouts, cut(): lax.dynamic_index_in_dim(blocks, c, 0, keepdims=False)  1.02 us
  transfers between devices with their start and end apart: 9, of which 4 were waited for; matrix products, arithmetic and copies ran while one was open for 0% of the time, Pallas kernels for 3%

profile of v12, /device:TPU:0, one launch (start us, length us, event | category | flops | bytes accessed | tf_op | source)
XLA Modules:
  0.0 24.7 jit_solution(17832562876218574982)
XLA Ops:
  0.6 0.0 copy-start.4
  0.7 1.0 %dynamic-slice_bitcast_fusion.3 = (f32[32,512]{1,0:T(8,128)S(1)}, f32[32,512]{1,0:T(8,128)S(1)}, f32[32,512]{1,0:T(8,128)S(1)}, f32[32,512]{1,0:T(8,128)S(1)}) fusion(f32[4,32,512]{2,1,0:T(8,128)} %bitcast.21, s32[]{:T(128)S(6)} %select_n.29, s32[]{:T(128)S(6)} %select_n.28, s32[]{:T(128)S(6)} %select_n.27, s32[]{:T(128)S(6)} %select_n.26), kind=kLoop, calls=%fused_computation.3 | loop fusion | bytes 524304 | tf_op jit(solution)/shard_map/jit(dynamic_index_in_dim)/squeeze | solution.py:172
  1.7 5.1 %collective-permute-start.2 = (f32[32,512]{1,0:T(8,128)S(1)}, f32[32,512]{1,0:T(8,128)S(1)}, u32[]{:S(2)}, u32[]{:S(2)}) collective-permute-start(f32[32,512]{1,0:T(8,128)S(1)} %get-tuple-element.24), channel_id=1, source_target_pairs={{0,12},{4,8},{8,4},{12,0},{1,13},{5,9},{9,5},{13,1},{2,14},{6,10},... | collective-permute-start | bytes 196616 | tf_op jit(solution)/shard_map/ppermute | solution.py:160
  6.8 0.0 collective-permute-start.1
  6.8 0.6 %collective-permute-start = (f32[32,512]{1,0:T(8,128)S(1)}, f32[32,512]{1,0:T(8,128)S(1)}, u32[]{:S(2)}, u32[]{:S(2)}) collective-permute-start(f32[32,512]{1,0:T(8,128)S(1)} %get-tuple-element.26), channel_id=1, source_target_pairs={{0,4},{4,0},{8,12},{12,8},{1,5},{5,1},{9,13},{13,9},{2,6},{6,2},{1... | collective-permute-start | bytes 196616 | tf_op jit(solution)/shard_map/ppermute | solution.py:160
  7.4 0.0 copy-done.4
  7.4 0.0 copy-start.1
  7.4 0.0 copy-start.2
  7.5 1.4 %collective-permute-start.7 = (f32[32,512]{1,0:T(8,128)S(1)}, f32[32,512]{1,0:T(8,128)S(1)}, u32[]{:S(2)}, u32[]{:S(2)}) collective-permute-start(f32[32,512]{1,0:T(8,128)S(1)} %get-tuple-element.20), channel_id=1, source_target_pairs={{0,4},{4,8},{8,12},{12,0},{1,5},{5,9},{9,13},{13,1},{2,6},{6,10},{... | collective-permute-start | bytes 196616 | tf_op jit(solution)/shard_map/ppermute | solution.py:160
  8.9 0.0 copy-start.3
  8.9 2.9 %collective-permute-start.6 = (f32[32,512]{1,0:T(8,128)S(1)}, f32[32,512]{1,0:T(8,128)S(1)}, u32[]{:S(2)}, u32[]{:S(2)}) collective-permute-start(f32[32,512]{1,0:T(8,128)S(1)} %get-tuple-element.21), channel_id=1, source_target_pairs={{0,8},{4,12},{8,0},{12,4},{1,9},{5,13},{9,1},{13,5},{2,10},{6,14},... | collective-permute-start | bytes 196616 | tf_op jit(solution)/shard_map/ppermute | solution.py:160
  11.8 0.0 copy-done.1
  11.8 0.0 copy-done.2
  11.8 0.0 copy-done.3
  11.8 0.7 %shard_map.68 = (f32[2,32,512]{2,1,0:T(8,128)S(1)}, f32[29,512]{1,0:T(8,128)S(1)}) custom-call(s32[1,2]{1,0:T(1,128)S(1)} %copy-done.3, f32[4,4]{1,0:T(4,128)S(1)} %copy-done.2, f32[32,2048]{1,0:T(8,128)S(1)} %bitcast.23), custom_call_target="tpu_custom_call" | custom-call | flops 262144 | bytes 452680 | tf_op jit(solution)/shard_map/pallas_call | solution.py:144
  12.5 0.0 collective-permute-done.2.refs_3_
  12.5 3.1 %collective-permute-done.1.refs_2_ = f32[32,512]{1,0:T(8,128)S(1)} collective-permute-done((f32[32,512]{1,0:T(8,128)S(1)}, f32[32,512]{1,0:T(8,128)S(1)}, u32[]{:S(2)}, u32[]{:S(2)}) %collective-permute-start.1) | collective-permute-done | bytes 65568 | tf_op jit(solution)/shard_map/ppermute | solution.py:160
  15.6 0.0 collective-permute-done.refs_1_
  15.6 0.0 copy-start
  15.6 0.1 shard_map.69
  15.7 0.1 collective-permute-start.3
  15.8 1.0 %collective-permute-start.4 = (f32[32,512]{1,0:T(8,128)S(1)}, f32[32,512]{1,0:T(8,128)S(1)}, u32[]{:S(2)}, u32[]{:S(2)}) collective-permute-start(f32[32,512]{1,0:T(8,128)S(1)} %get-tuple-element.15), channel_id=1, source_target_pairs={{0,8},{4,12},{8,0},{12,4},{1,9},{5,13},{9,1},{13,5},{2,10},{6,14},... | collective-permute-start | bytes 196616 | tf_op jit(solution)/shard_map/ppermute | solution.py:160
  16.8 2.8 %collective-permute-start.5 = (f32[32,512]{1,0:T(8,128)S(1)}, f32[32,512]{1,0:T(8,128)S(1)}, u32[]{:S(2)}, u32[]{:S(2)}) collective-permute-start(f32[32,512]{1,0:T(8,128)S(1)} %get-tuple-element.16), channel_id=1, source_target_pairs={{0,12},{4,0},{8,4},{12,8},{1,13},{5,1},{9,5},{13,9},{2,14},{6,2},{... | collective-permute-start | bytes 196616 | tf_op jit(solution)/shard_map/ppermute | solution.py:160
  19.6 0.0 collective-permute-done.7.refs_6_
  19.6 0.6 %collective-permute-start.8 = (f32[32,512]{1,0:T(8,128)S(1)}, f32[32,512]{1,0:T(8,128)S(1)}, u32[]{:S(2)}, u32[]{:S(2)}) collective-permute-start(f32[32,512]{1,0:T(8,128)S(1)} %get-tuple-element.17), channel_id=1, source_target_pairs={{0,12},{4,0},{8,4},{12,8},{1,13},{5,1},{9,5},{13,9},{2,14},{6,2},{... | collective-permute-start | bytes 196616 | tf_op jit(solution)/shard_map/ppermute | solution.py:160
  20.2 0.0 collective-permute-done.6.refs_5_
  20.2 1.7 %collective-permute-done.3.refs_1_ = f32[32,512]{1,0:T(8,128)S(1)} collective-permute-done((f32[32,512]{1,0:T(8,128)S(1)}, f32[32,512]{1,0:T(8,128)S(1)}, u32[]{:S(2)}, u32[]{:S(2)}) %collective-permute-start.3) | collective-permute-done | bytes 65568 | tf_op jit(solution)/shard_map/ppermute | solution.py:160
  21.9 0.8 %collective-permute-done.4.refs_2_ = f32[32,512]{1,0:T(8,128)S(1)} collective-permute-done((f32[32,512]{1,0:T(8,128)S(1)}, f32[32,512]{1,0:T(8,128)S(1)}, u32[]{:S(2)}, u32[]{:S(2)}) %collective-permute-start.4) | collective-permute-done | bytes 65568 | tf_op jit(solution)/shard_map/ppermute | solution.py:160
  22.7 0.0 collective-permute-done.5.refs_3_
  22.7 1.1 %collective-permute-done.8.refs_7_ = f32[32,512]{1,0:T(8,128)S(1)} collective-permute-done((f32[32,512]{1,0:T(8,128)S(1)}, f32[32,512]{1,0:T(8,128)S(1)}, u32[]{:S(2)}, u32[]{:S(2)}) %collective-permute-start.8) | collective-permute-done | bytes 65568 | tf_op jit(solution)/shard_map/ppermute | solution.py:160
  23.9 0.0 copy-done
  23.9 0.9 %shard_map.70 = (f32[32,2048]{1,0:T(8,128)}, f32[4,32,512]{2,1,0:T(8,128)}) custom-call(f32[29,512]{1,0:T(8,128)S(1)} %get-tuple-element.11.table_ref, f32[4,32,512]{2,1,0:T(8,128)S(1)} %bitcast.22, f32[32,512]{1,0:T(8,128)S(1)} %get-tuple-element.13.refs_0_, f32[32,512]{1,0:T(8,128)S(1)} %collective-permute-done.3.refs_1_, ...), custom_call_target="tpu_custom_call" | custom-call | flops 524288 | bytes 1370112 | tf_op jit(solution)/shard_map/pallas_call | solution.py:144
  (1 shorter events, 0.0 us)
Async XLA Ops:
  0.6 6.8 %copy-start.4 = (f32[1,1,128,512]{3,2,1,0:T(8,128)S(1)}, f32[1,1,128,512]{3,2,1,0:T(8,128)}, u32[]{:S(2)}) copy-start(f32[1,1,128,512]{3,2,1,0:T(8,128)} %param.5) | copy-start | bytes 786436
  1.7 10.8 %collective-permute-start.2 = (f32[32,512]{1,0:T(8,128)S(1)}, f32[32,512]{1,0:T(8,128)S(1)}, u32[]{:S(2)}, u32[]{:S(2)}) collective-permute-start(f32[32,512]{1,0:T(8,128)S(1)} %get-tuple-element.24), channel_id=1, source_target_pairs={{0,12},{4,8},{8,4},{12,0},{1,13},{5,9},{9,5},{13,1},{2,14},{6,10},... | collective-permute-start | bytes 196616 | tf_op jit(solution)/shard_map/ppermute | solution.py:160
  6.8 8.9 %collective-permute-start.1 = (f32[32,512]{1,0:T(8,128)S(1)}, f32[32,512]{1,0:T(8,128)S(1)}, u32[]{:S(2)}, u32[]{:S(2)}) collective-permute-start(f32[32,512]{1,0:T(8,128)S(1)} %get-tuple-element.25), channel_id=1, source_target_pairs={{0,8},{4,12},{8,0},{12,4},{1,9},{5,13},{9,1},{13,5},{2,10},{6,14},... | collective-permute-start | bytes 196616 | tf_op jit(solution)/shard_map/ppermute | solution.py:160
  6.8 8.9 %collective-permute-start = (f32[32,512]{1,0:T(8,128)S(1)}, f32[32,512]{1,0:T(8,128)S(1)}, u32[]{:S(2)}, u32[]{:S(2)}) collective-permute-start(f32[32,512]{1,0:T(8,128)S(1)} %get-tuple-element.26), channel_id=1, source_target_pairs={{0,4},{4,0},{8,12},{12,8},{1,5},{5,1},{9,13},{13,9},{2,6},{6,2},{1... | collective-permute-start | bytes 196616 | tf_op jit(solution)/shard_map/ppermute | solution.py:160
  7.4 4.4 %copy-start.1 = (f32[1,32,2048]{2,1,0:T(8,128)S(1)}, f32[1,32,2048]{2,1,0:T(8,128)}, u32[]{:S(2)}) copy-start(f32[1,32,2048]{2,1,0:T(8,128)} %param.7) | copy-start | bytes 786436
  7.4 4.4 %copy-start.2 = (f32[4,4]{1,0:T(4,128)S(1)}, f32[4,4]{1,0:T(4,128)}, u32[]{:S(2)}) copy-start(f32[4,4]{1,0:T(4,128)} %generator_ref.1) | copy-start | bytes 196
  7.5 12.1 %collective-permute-start.7 = (f32[32,512]{1,0:T(8,128)S(1)}, f32[32,512]{1,0:T(8,128)S(1)}, u32[]{:S(2)}, u32[]{:S(2)}) collective-permute-start(f32[32,512]{1,0:T(8,128)S(1)} %get-tuple-element.20), channel_id=1, source_target_pairs={{0,4},{4,8},{8,12},{12,0},{1,5},{5,9},{9,13},{13,1},{2,6},{6,10},{... | collective-permute-start | bytes 196616 | tf_op jit(solution)/shard_map/ppermute | solution.py:160
  8.9 2.9 %copy-start.3 = (s32[1,2]{1,0:T(1,128)S(1)}, s32[1,2]{1,0:T(1,128)}, u32[]{:S(2)}) copy-start(s32[1,2]{1,0:T(1,128)} %ids_ref.1) | copy-start | bytes 28
  8.9 11.3 %collective-permute-start.6 = (f32[32,512]{1,0:T(8,128)S(1)}, f32[32,512]{1,0:T(8,128)S(1)}, u32[]{:S(2)}, u32[]{:S(2)}) collective-permute-start(f32[32,512]{1,0:T(8,128)S(1)} %get-tuple-element.21), channel_id=1, source_target_pairs={{0,8},{4,12},{8,0},{12,4},{1,9},{5,13},{9,1},{13,5},{2,10},{6,14},... | collective-permute-start | bytes 196616 | tf_op jit(solution)/shard_map/ppermute | solution.py:160
  15.6 8.2 %copy-start = (f32[1,1,128,512]{3,2,1,0:T(8,128)S(1)}, f32[1,1,128,512]{3,2,1,0:T(8,128)}, u32[]{:S(2)}) copy-start(f32[1,1,128,512]{3,2,1,0:T(8,128)} %param.6) | copy-start | bytes 786436
  15.7 6.2 %collective-permute-start.3 = (f32[32,512]{1,0:T(8,128)S(1)}, f32[32,512]{1,0:T(8,128)S(1)}, u32[]{:S(2)}, u32[]{:S(2)}) collective-permute-start(f32[32,512]{1,0:T(8,128)S(1)} %get-tuple-element.14), channel_id=1, source_target_pairs={{0,4},{4,8},{8,12},{12,0},{1,5},{5,9},{9,13},{13,1},{2,6},{6,10},{... | collective-permute-start | bytes 196616 | tf_op jit(solution)/shard_map/ppermute | solution.py:160
  15.8 7.0 %collective-permute-start.4 = (f32[32,512]{1,0:T(8,128)S(1)}, f32[32,512]{1,0:T(8,128)S(1)}, u32[]{:S(2)}, u32[]{:S(2)}) collective-permute-start(f32[32,512]{1,0:T(8,128)S(1)} %get-tuple-element.15), channel_id=1, source_target_pairs={{0,8},{4,12},{8,0},{12,4},{1,9},{5,13},{9,1},{13,5},{2,10},{6,14},... | collective-permute-start | bytes 196616 | tf_op jit(solution)/shard_map/ppermute | solution.py:160
  16.8 5.9 %collective-permute-start.5 = (f32[32,512]{1,0:T(8,128)S(1)}, f32[32,512]{1,0:T(8,128)S(1)}, u32[]{:S(2)}, u32[]{:S(2)}) collective-permute-start(f32[32,512]{1,0:T(8,128)S(1)} %get-tuple-element.16), channel_id=1, source_target_pairs={{0,12},{4,0},{8,4},{12,8},{1,13},{5,1},{9,5},{13,9},{2,14},{6,2},{... | collective-permute-start | bytes 196616 | tf_op jit(solution)/shard_map/ppermute | solution.py:160
  19.6 4.3 %collective-permute-start.8 = (f32[32,512]{1,0:T(8,128)S(1)}, f32[32,512]{1,0:T(8,128)S(1)}, u32[]{:S(2)}, u32[]{:S(2)}) collective-permute-start(f32[32,512]{1,0:T(8,128)S(1)} %get-tuple-element.17), channel_id=1, source_target_pairs={{0,12},{4,0},{8,4},{12,8},{1,13},{5,1},{9,5},{13,9},{2,14},{6,2},{... | collective-permute-start | bytes 196616 | tf_op jit(solution)/shard_map/ppermute | solution.py:160

commit v13 on v11

--- a/solution.py
+++ b/solution.py
@@ -199,6 +199,7 @@
         block = floats(own_rows, width)
         own_earlier, *cut_earlier = cut(earlier, order_of(members, True))
         earlier_rows = trade(cut_earlier, rounds, members)
+        current, table = lax.optimization_barrier((current, table))
         own_current, *cut_current = cut(current, targets_of(members, True))
         outgoing = call(
             rebuild_paired_kernel,

time: 23.6 us -> 24.1 us (1.021)
  waiting for transfers between devices: 4.37 us -> 3.45 us
  local copies, waits for them, and re-layouts: 1.04 us -> 1.74 us
  starting transfers between devices: 15 us -> 15.7 us
    ppermute x3, waiting for transfers between devices: 1.26 us -> 0.01 us  [trade(): lax.ppermute(piece, 'code', [(d, d ^ r) for d in range(members)])]
    ppermute x6, starting transfers between devices: 9.28 us -> 9.98 us  [pass_on(): lax.ppermute(piece, 'code', [(d, (d + s) % members) for d in range(member...]
    unnamed x10, local copies, waits for them, and re-layouts: 0.02 us -> 0.69 us
    ppermute x6, waiting for transfers between devices: 3.11 us -> 3.45 us  [pass_on(): lax.ppermute(piece, 'code', [(d, (d + s) % members) for d in range(member...]
  transfers between devices with their start and end apart: 9 -> 9, of which waited for: 3 -> 4; matrix products, arithmetic and copies ran while one was open for 0% -> 0% of each run, Pallas kernels for 6% -> 6%
where the time goes in v13:
time: 24.1 us; the launch traced here: 23.9 us
  starting transfers between devices  15.7 us (65%)
  waiting for transfers between devices  3.45 us (14%)
  Pallas kernels  2.22 us (9%)
  local copies, waits for them, and re-layouts  1.74 us (7%)
  between operations  0.74 us (3%)
    ppermute x6, starting transfers between devices, pass_on(): lax.ppermute(piece, 'code', [(d, (d + s) % members) for d in range(member...  9.98 us
    ppermute x3, starting transfers between devices, trade(): lax.ppermute(piece, 'code', [(d, d ^ r) for d in range(members)])  5.76 us
    ppermute x6, waiting for transfers between devices, pass_on(): lax.ppermute(piece, 'code', [(d, (d + s) % members) for d in range(member...  3.45 us
    pallas_call x4, Pallas kernels, call(): pl.pallas_call(kernel, in_specs=specs, out_specs=jax.tree.map(lambda _: I...  2.22 us
    squeeze x2, local copies, waits for them, and re-layouts, cut(): lax.dynamic_index_in_dim(blocks, c, 0, keepdims=False)  1.04 us
    unnamed x10, local copies, waits for them, and re-layouts  0.69 us
  transfers between devices with their start and end apart: 9, of which 4 were waited for; matrix products, arithmetic and copies ran while one was open for 0% of the time, Pallas kernels for 6%

profile of v13, /device:TPU:0, one launch (start us, length us, event | category | flops | bytes accessed | tf_op | source)
XLA Modules:
  0.0 23.9 jit_solution(10365688305439028694)
XLA Ops:
  0.6 0.0 copy-start.1
  0.7 0.0 copy-start.4
  0.7 1.0 %dynamic-slice_bitcast_fusion = (f32[32,512]{1,0:T(8,128)S(1)}, f32[32,512]{1,0:T(8,128)S(1)}, f32[32,512]{1,0:T(8,128)S(1)}, f32[32,512]{1,0:T(8,128)S(1)}) fusion(f32[4,32,512]{2,1,0:T(8,128)} %bitcast.21, s32[]{:T(128)S(6)} %select_n.32, s32[]{:T(128)S(6)} %select_n.31, s32[]{:T(128)S(6)} %select_n.30, s32[]{:T(128)S(6)} %select_n.29), kind=kLoop, calls=%fused_computation | loop fusion | bytes 524304 | tf_op jit(solution)/shard_map/jit(dynamic_index_in_dim)/squeeze | solution.py:173
  1.7 5.1 %collective-permute-start.3 = (f32[32,512]{1,0:T(8,128)S(1)}, f32[32,512]{1,0:T(8,128)S(1)}, u32[]{:S(2)}, u32[]{:S(2)}) collective-permute-start(f32[32,512]{1,0:T(8,128)S(1)} %get-tuple-element.24), channel_id=1, source_target_pairs={{0,12},{4,8},{8,4},{12,0},{1,13},{5,9},{9,5},{13,1},{2,14},{6,10},... | collective-permute-start | bytes 196616 | tf_op jit(solution)/shard_map/ppermute | solution.py:167
  6.8 0.0 collective-permute-start.4
  6.8 0.6 %collective-permute-start.5 = (f32[32,512]{1,0:T(8,128)S(1)}, f32[32,512]{1,0:T(8,128)S(1)}, u32[]{:S(2)}, u32[]{:S(2)}) collective-permute-start(f32[32,512]{1,0:T(8,128)S(1)} %get-tuple-element.22), channel_id=1, source_target_pairs={{0,4},{4,0},{8,12},{12,8},{1,5},{5,1},{9,13},{13,9},{2,6},{6,2},{1... | collective-permute-start | bytes 196616 | tf_op jit(solution)/shard_map/ppermute | solution.py:167
  7.4 0.0 copy-start.2
  7.4 0.0 copy-start.3
  7.4 0.0 copy-done.1
  7.5 0.7 %copy-done.2 = f32[4,4]{1,0:T(4,128)S(1)} copy-done((f32[4,4]{1,0:T(4,128)S(1)}, f32[4,4]{1,0:T(4,128)}, u32[]{:S(2)}) %copy-start.2) | copy-done | bytes 88
  8.1 0.0 copy-done.3
  8.1 0.7 %shard_map.68 = (f32[2,32,512]{2,1,0:T(8,128)S(1)}, f32[29,512]{1,0:T(8,128)S(1)}) custom-call(s32[1,2]{1,0:T(1,128)S(1)} %copy-done.3, f32[4,4]{1,0:T(4,128)S(1)} %copy-done.2, f32[32,2048]{1,0:T(8,128)S(1)} %bitcast.23), custom_call_target="tpu_custom_call" | custom-call | flops 262144 | bytes 452680 | tf_op jit(solution)/shard_map/pallas_call | solution.py:143
  8.8 0.0 copy-done.4
  8.9 1.4 %collective-permute-start = (f32[32,512]{1,0:T(8,128)S(1)}, f32[32,512]{1,0:T(8,128)S(1)}, u32[]{:S(2)}, u32[]{:S(2)}) collective-permute-start(f32[32,512]{1,0:T(8,128)S(1)} %get-tuple-element.28), channel_id=1, source_target_pairs={{0,4},{4,8},{8,12},{12,0},{1,5},{5,9},{9,13},{13,1},{2,6},{6,10},{... | collective-permute-start | bytes 196616 | tf_op jit(solution)/shard_map/ppermute | solution.py:160
  10.3 2.9 %collective-permute-start.1 = (f32[32,512]{1,0:T(8,128)S(1)}, f32[32,512]{1,0:T(8,128)S(1)}, u32[]{:S(2)}, u32[]{:S(2)}) collective-permute-start(f32[32,512]{1,0:T(8,128)S(1)} %get-tuple-element.27), channel_id=1, source_target_pairs={{0,8},{4,12},{8,0},{12,4},{1,9},{5,13},{9,1},{13,5},{2,10},{6,14},... | collective-permute-start | bytes 196616 | tf_op jit(solution)/shard_map/ppermute | solution.py:160
  13.2 0.0 collective-permute-done.3.refs_1_
  13.2 0.9 %collective-permute-start.2 = (f32[32,512]{1,0:T(8,128)S(1)}, f32[32,512]{1,0:T(8,128)S(1)}, u32[]{:S(2)}, u32[]{:S(2)}) collective-permute-start(f32[32,512]{1,0:T(8,128)S(1)} %get-tuple-element.26), channel_id=1, source_target_pairs={{0,12},{4,0},{8,4},{12,8},{1,13},{5,1},{9,5},{13,9},{2,14},{6,2},{... | collective-permute-start | bytes 196616 | tf_op jit(solution)/shard_map/ppermute | solution.py:160
  14.1 0.0 collective-permute-done.4.refs_2_
  14.1 0.0 collective-permute-done.5.refs_3_
  14.1 0.1 shard_map.70
  14.2 0.0 copy-start
  14.2 1.2 %collective-permute-start.6 = (f32[32,512]{1,0:T(8,128)S(1)}, f32[32,512]{1,0:T(8,128)S(1)}, u32[]{:S(2)}, u32[]{:S(2)}) collective-permute-start(f32[32,512]{1,0:T(8,128)S(1)} %get-tuple-element.19), channel_id=1, source_target_pairs={{0,4},{4,8},{8,12},{12,0},{1,5},{5,9},{9,13},{13,1},{2,6},{6,10},{... | collective-permute-start | bytes 196616 | tf_op jit(solution)/shard_map/ppermute | solution.py:160
  15.4 1.0 %collective-permute-start.7 = (f32[32,512]{1,0:T(8,128)S(1)}, f32[32,512]{1,0:T(8,128)S(1)}, u32[]{:S(2)}, u32[]{:S(2)}) collective-permute-start(f32[32,512]{1,0:T(8,128)S(1)} %get-tuple-element.20), channel_id=1, source_target_pairs={{0,8},{4,12},{8,0},{12,4},{1,9},{5,13},{9,1},{13,5},{2,10},{6,14},... | collective-permute-start | bytes 196616 | tf_op jit(solution)/shard_map/ppermute | solution.py:160
  16.4 0.0 collective-permute-done.refs_1_
  16.4 2.5 %collective-permute-start.8 = (f32[32,512]{1,0:T(8,128)S(1)}, f32[32,512]{1,0:T(8,128)S(1)}, u32[]{:S(2)}, u32[]{:S(2)}) collective-permute-start(f32[32,512]{1,0:T(8,128)S(1)} %get-tuple-element.21), channel_id=1, source_target_pairs={{0,12},{4,0},{8,4},{12,8},{1,13},{5,1},{9,5},{13,9},{2,14},{6,2},{... | collective-permute-start | bytes 196616 | tf_op jit(solution)/shard_map/ppermute | solution.py:160
  18.9 0.2 collective-permute-done.1.refs_2_
  19.2 0.2 collective-permute-done.2.refs_3_
  19.4 0.8 %shard_map.69 = (f32[32,2048]{1,0:T(8,128)}, f32[8,128]{1,0:T(8,128)S(1)}) custom-call(f32[29,512]{1,0:T(8,128)S(1)} %get-tuple-element.13.table_ref, f32[32,512]{1,0:T(8,128)S(1)} %get-tuple-element.29.refs_0_, f32[32,512]{1,0:T(8,128)S(1)} %collective-permute-done.refs_1_, f32[32,512]{1,0:T(8,128)S(1)} %collective-permute-done.1.refs_2_, ...), custom_call_target="tpu_custom_call" | custom-call | flops 524288 | bytes 587776 | tf_op jit(solution)/shard_map/pallas_call | solution.py:143
  20.1 0.3 %collective-permute-done.6.refs_1_ = f32[32,512]{1,0:T(8,128)S(1)} collective-permute-done((f32[32,512]{1,0:T(8,128)S(1)}, f32[32,512]{1,0:T(8,128)S(1)}, u32[]{:S(2)}, u32[]{:S(2)}) %collective-permute-start.6) | collective-permute-done | bytes 65568 | tf_op jit(solution)/shard_map/ppermute | solution.py:160
  20.5 2.7 %collective-permute-done.7.refs_2_ = f32[32,512]{1,0:T(8,128)S(1)} collective-permute-done((f32[32,512]{1,0:T(8,128)S(1)}, f32[32,512]{1,0:T(8,128)S(1)}, u32[]{:S(2)}, u32[]{:S(2)}) %collective-permute-start.7) | collective-permute-done | bytes 65568 | tf_op jit(solution)/shard_map/ppermute | solution.py:160
  23.1 0.0 collective-permute-done.8.refs_3_
  23.1 0.0 copy-done
  23.2 0.7 %shard_map.71 = f32[4,32,512]{2,1,0:T(8,128)} custom-call(f32[29,512]{1,0:T(8,128)S(1)} %get-tuple-element.13.table_ref, f32[4,32,512]{2,1,0:T(8,128)S(1)} %bitcast.22, f32[8,128]{1,0:T(8,128)S(1)} %get-tuple-element.16.held_back_by, f32[32,512]{1,0:T(8,128)S(1)} %get-tuple-element.18.refs_0_, f32[32,512]{1,0:T(8,128)S(1)} %collective-permute-done.6.refs_1_, ...), custom_call_target="tpu_custom_call" | custom-call | bytes 849920 | tf_op jit(solution)/shard_map/pallas_call | solution.py:143
  (1 shorter events, 0.0 us)
Async XLA Ops:
  0.6 6.8 %copy-start.1 = (f32[1,32,2048]{2,1,0:T(8,128)S(1)}, f32[1,32,2048]{2,1,0:T(8,128)}, u32[]{:S(2)}) copy-start(f32[1,32,2048]{2,1,0:T(8,128)} %param.7) | copy-start | bytes 786436
  0.7 8.2 %copy-start.4 = (f32[1,1,128,512]{3,2,1,0:T(8,128)S(1)}, f32[1,1,128,512]{3,2,1,0:T(8,128)}, u32[]{:S(2)}) copy-start(f32[1,1,128,512]{3,2,1,0:T(8,128)} %param.5) | copy-start | bytes 786436
  1.7 11.5 %collective-permute-start.3 = (f32[32,512]{1,0:T(8,128)S(1)}, f32[32,512]{1,0:T(8,128)S(1)}, u32[]{:S(2)}, u32[]{:S(2)}) collective-permute-start(f32[32,512]{1,0:T(8,128)S(1)} %get-tuple-element.24), channel_id=1, source_target_pairs={{0,12},{4,8},{8,4},{12,0},{1,13},{5,9},{9,5},{13,1},{2,14},{6,10},... | collective-permute-start | bytes 196616 | tf_op jit(solution)/shard_map/ppermute | solution.py:167
  6.8 7.3 %collective-permute-start.4 = (f32[32,512]{1,0:T(8,128)S(1)}, f32[32,512]{1,0:T(8,128)S(1)}, u32[]{:S(2)}, u32[]{:S(2)}) collective-permute-start(f32[32,512]{1,0:T(8,128)S(1)} %get-tuple-element.23), channel_id=1, source_target_pairs={{0,8},{4,12},{8,0},{12,4},{1,9},{5,13},{9,1},{13,5},{2,10},{6,14},... | collective-permute-start | bytes 196616 | tf_op jit(solution)/shard_map/ppermute | solution.py:167
  6.8 7.3 %collective-permute-start.5 = (f32[32,512]{1,0:T(8,128)S(1)}, f32[32,512]{1,0:T(8,128)S(1)}, u32[]{:S(2)}, u32[]{:S(2)}) collective-permute-start(f32[32,512]{1,0:T(8,128)S(1)} %get-tuple-element.22), channel_id=1, source_target_pairs={{0,4},{4,0},{8,12},{12,8},{1,5},{5,1},{9,13},{13,9},{2,6},{6,2},{1... | collective-permute-start | bytes 196616 | tf_op jit(solution)/shard_map/ppermute | solution.py:167
  7.4 0.7 %copy-start.2 = (f32[4,4]{1,0:T(4,128)S(1)}, f32[4,4]{1,0:T(4,128)}, u32[]{:S(2)}) copy-start(f32[4,4]{1,0:T(4,128)} %generator_ref.1) | copy-start | bytes 196
  7.4 0.7 %copy-start.3 = (s32[1,2]{1,0:T(1,128)S(1)}, s32[1,2]{1,0:T(1,128)}, u32[]{:S(2)}) copy-start(s32[1,2]{1,0:T(1,128)} %ids_ref.1) | copy-start | bytes 28
  8.9 7.5 %collective-permute-start = (f32[32,512]{1,0:T(8,128)S(1)}, f32[32,512]{1,0:T(8,128)S(1)}, u32[]{:S(2)}, u32[]{:S(2)}) collective-permute-start(f32[32,512]{1,0:T(8,128)S(1)} %get-tuple-element.28), channel_id=1, source_target_pairs={{0,4},{4,8},{8,12},{12,0},{1,5},{5,9},{9,13},{13,1},{2,6},{6,10},{... | collective-permute-start | bytes 196616 | tf_op jit(solution)/shard_map/ppermute | solution.py:160
  10.3 8.9 %collective-permute-start.1 = (f32[32,512]{1,0:T(8,128)S(1)}, f32[32,512]{1,0:T(8,128)S(1)}, u32[]{:S(2)}, u32[]{:S(2)}) collective-permute-start(f32[32,512]{1,0:T(8,128)S(1)} %get-tuple-element.27), channel_id=1, source_target_pairs={{0,8},{4,12},{8,0},{12,4},{1,9},{5,13},{9,1},{13,5},{2,10},{6,14},... | collective-permute-start | bytes 196616 | tf_op jit(solution)/shard_map/ppermute | solution.py:160
  13.2 6.1 %collective-permute-start.2 = (f32[32,512]{1,0:T(8,128)S(1)}, f32[32,512]{1,0:T(8,128)S(1)}, u32[]{:S(2)}, u32[]{:S(2)}) collective-permute-start(f32[32,512]{1,0:T(8,128)S(1)} %get-tuple-element.26), channel_id=1, source_target_pairs={{0,12},{4,0},{8,4},{12,8},{1,13},{5,1},{9,5},{13,9},{2,14},{6,2},{... | collective-permute-start | bytes 196616 | tf_op jit(solution)/shard_map/ppermute | solution.py:160
  14.2 9.0 %copy-start = (f32[1,1,128,512]{3,2,1,0:T(8,128)S(1)}, f32[1,1,128,512]{3,2,1,0:T(8,128)}, u32[]{:S(2)}) copy-start(f32[1,1,128,512]{3,2,1,0:T(8,128)} %param.6) | copy-start | bytes 786436
  14.2 6.3 %collective-permute-start.6 = (f32[32,512]{1,0:T(8,128)S(1)}, f32[32,512]{1,0:T(8,128)S(1)}, u32[]{:S(2)}, u32[]{:S(2)}) collective-permute-start(f32[32,512]{1,0:T(8,128)S(1)} %get-tuple-element.19), channel_id=1, source_target_pairs={{0,4},{4,8},{8,12},{12,0},{1,5},{5,9},{9,13},{13,1},{2,6},{6,10},{... | collective-permute-start | bytes 196616 | tf_op jit(solution)/shard_map/ppermute | solution.py:160
  15.4 7.8 %collective-permute-start.7 = (f32[32,512]{1,0:T(8,128)S(1)}, f32[32,512]{1,0:T(8,128)S(1)}, u32[]{:S(2)}, u32[]{:S(2)}) collective-permute-start(f32[32,512]{1,0:T(8,128)S(1)} %get-tuple-element.20), channel_id=1, source_target_pairs={{0,8},{4,12},{8,0},{12,4},{1,9},{5,13},{9,1},{13,5},{2,10},{6,14},... | collective-permute-start | bytes 196616 | tf_op jit(solution)/shard_map/ppermute | solution.py:160
  16.4 6.8 %collective-permute-start.8 = (f32[32,512]{1,0:T(8,128)S(1)}, f32[32,512]{1,0:T(8,128)S(1)}, u32[]{:S(2)}, u32[]{:S(2)}) collective-permute-start(f32[32,512]{1,0:T(8,128)S(1)} %get-tuple-element.21), channel_id=1, source_target_pairs={{0,12},{4,0},{8,4},{12,8},{1,13},{5,1},{9,5},{13,9},{2,14},{6,2},{... | collective-permute-start | bytes 196616 | tf_op jit(solution)/shard_map/ppermute | solution.py:160

commit v14 on v9

--- a/solution.py
+++ b/solution.py
@@ -11,22 +11,18 @@
 IN_SMEM = pl.BlockSpec(memory_space=pltpu.SMEM)
 ANYWHERE = pl.BlockSpec(memory_space=pl.ANY)
 
-DIRECT_MEMBERS = 8
 KERNEL_VMEM = 8 * 2**20
 
-
-def rounds_of(members):
-    return range(members - 1, 0, -1)
-
-
-def order_of(members, direct):
-    if not direct:
-        return list(range(members))
+PAIRED_MEMBERS = 4
+PARTNERS = (0, 1, 2, 3)
+
+
+def partners():
     me = lax.axis_index("code")
-    return [me ^ r for r in (0, *rounds_of(members))]
-
-
-def plan_kernel(direct, ids_ref, generator_ref, parity_ref, base_ref, table_ref):
+    return [me ^ r for r in PARTNERS]
+
+
+def plan_kernel(paired, ids_ref, generator_ref, parity_ref, base_ref, table_ref):
     spans, members = generator_ref.shape
     width = base_ref.shape[2]
     first, second = ids_ref[0, 0], ids_ref[0, 1]
@@ -52,7 +48,7 @@
         base_ref[k] = sum(
             weights[k][j] * parity_ref[:, j * width : (j + 1) * width] for j in range(spans)
         )
-    for i, c in enumerate(order_of(members, direct)):
+    for i, c in enumerate(partners() if paired else range(members)):
         column = [generator_ref[j, c] for j in range(spans)]
         alive = jnp.logical_and(first != c, second != c)
         for k in range(2):
@@ -102,24 +98,46 @@
 
 
 def rebuild_paired_kernel(base_ref, table_ref, *refs):
-    rows, outs = refs[: len(refs) // 2], refs[len(refs) // 2 :]
-    for out_ref, block in zip(outs, rebuilt_for(base_ref, table_ref, [r[...] for r in rows])):
+    rows, current_ref, outs = refs[:4], refs[4], refs[5:]
+    rebuilt = rebuilt_for(base_ref, table_ref, [r[...] for r in rows])
+    for out_ref, block in zip(outs, rebuilt + rebuilt[2:]):
         out_ref[...] = block
-
-
-def parity_paired_kernel(table_ref, *refs):
-    rows, out_ref, done_ref = refs[:-2], refs[-2], refs[-1]
-    parity_into(out_ref, table_ref, [r[...] for r in rows])
-    done_ref[...] = jnp.zeros(done_ref.shape, done_ref.dtype)
-
-
-def restore_kernel(table_ref, earlier_ref, held_back_by, *refs):
-    pieces, out_ref = refs[:-1], refs[-1]
-    members = len(pieces)
+    outs[6][...] = current_ref[...]
+
+
+def finish_kernel(table_ref, earlier_ref, *refs):
+    (
+        rebuilt_3_outer,
+        rebuilt_2_even,
+        rebuilt_1,
+        rebuilt_3_inner,
+        rebuilt_2_odd,
+        current_2_odd,
+        rebuilt_own,
+        current_own,
+        current_1,
+        current_2_even,
+        current_3,
+        parity_ref,
+        out_ref,
+    ) = refs
+    current = [
+        current_own[...],
+        current_1[...],
+        current_2_even[...] + current_2_odd[...],
+        current_3[...],
+    ]
+    rebuilt = [
+        rebuilt_own[...],
+        rebuilt_1[...],
+        rebuilt_2_even[...] + rebuilt_2_odd[...],
+        rebuilt_3_outer[...] + rebuilt_3_inner[...],
+    ]
+    parity_into(parity_ref, table_ref, current)
     last = table_ref.shape[0] - 1
     lost = table_ref[last : last + 1, :] > 0.5
-    for c, piece in zip(order_of(members, True), pieces):
-        out_ref[c] = jnp.where(lost, piece[...], earlier_ref[c])
+    for c, block in zip(partners(), rebuilt):
+        out_ref[c] = jnp.where(lost, block, earlier_ref[c])
 
 
 def call(kernel, specs, outs, args, flops, **options):
@@ -139,16 +157,13 @@
     return jax.ShapeDtypeStruct(shape, jnp.float32)
 
 
-def trade(pieces, rounds, members):
-    return [
-        lax.ppermute(piece, "code", [(d, d ^ r) for d in range(members)])
-        for r, piece in zip(rounds, pieces)
-    ]
-
-
-def cut(blocks, rounds):
-    me = lax.axis_index("code")
-    return [lax.dynamic_index_in_dim(blocks, me ^ r, 0, keepdims=False) for r in rounds]
+def swap(piece, *pairs):
+    both_ways = [way for a, b in pairs for way in ((a, b), (b, a))]
+    return lax.ppermute(piece, "code", both_ways)
+
+
+def cut(blocks, order):
+    return [lax.dynamic_index_in_dim(blocks, c, 0, keepdims=False) for c in order]
 
 
 def local(state_slab, previous_slab, previous_parity, generator, failed_ids):
@@ -160,10 +175,10 @@
     blocks = (members, own_rows, width)
     earlier = previous_slab.reshape(blocks)
     current = state_slab.reshape(blocks)
-    direct = 4 <= members <= DIRECT_MEMBERS and members & (members - 1) == 0
+    paired = members == PAIRED_MEMBERS
 
     base, table = call(
-        functools.partial(plan_kernel, direct),
+        functools.partial(plan_kernel, paired),
         [IN_SMEM, IN_SMEM, IN_VMEM],
         (floats(2, own_rows, width), floats((3 + spans) * members + 1, width)),
         (failed_ids, generator, previous_parity[0]),
@@ -172,34 +187,54 @@
     parity_shape = floats(own_rows, spans * width)
     rebuild_cost = 4 * slab_rows * width
     parity_cost = 2 * spans * slab_rows * width
-    if direct:
-        rounds = list(rounds_of(members))
-        block = floats(own_rows, width)
-        own_earlier, *cut_earlier = cut(earlier, [0] + rounds)
-        earlier_rows = trade(cut_earlier, rounds, members)
-        own_current, *cut_current = cut(current, [0] + rounds)
-        outgoing = call(
+    if paired:
+        block, stack = floats(own_rows, width), floats(2, own_rows, width)
+        own_earlier, earlier_1, earlier_2, earlier_3 = cut(earlier, partners())
+        earlier_rows = [
+            own_earlier,
+            swap(earlier_1, (0, 1), (2, 3)),
+            swap(earlier_2, (0, 2), (1, 3)),
+            swap(earlier_3, (0, 3), (1, 2)),
+        ]
+        own_current, current_1, current_2, current_3 = cut(current, partners())
+        current_3 = swap(current_3, (0, 3), (1, 2))
+        current_2_even = swap(current_2, (0, 2))
+        current_1 = swap(current_1, (0, 1), (2, 3))
+        (
+            rebuilt_own,
+            rebuilt_1,
+            rebuilt_2_even,
+            rebuilt_3_outer,
+            rebuilt_2_odd,
+            rebuilt_3_inner,
+            current_2_odd,
+        ) = call(
             rebuild_paired_kernel,
-            [IN_VMEM] * (members + 2),
-            [block] * members,
-            (base, table, own_earlier, *earlier_rows),
+            [IN_VMEM] * 7,
+            [block] * 7,
+            (base, table, *earlier_rows, current_2),
             rebuild_cost,
         )
-        incoming = trade(outgoing[1:], rounds, members)
-        current_rows = [own_current, *trade(cut_current, rounds, members)]
-        new_parity, parity_done = call(
-            parity_paired_kernel,
-            [IN_VMEM] * (members + 1),
-            (parity_shape, floats(8, 128)),
-            (table, *current_rows),
+        new_parity, restored_state = call(
+            finish_kernel,
+            [IN_VMEM] * 13,
+            (parity_shape, floats(*blocks)),
+            (
+                table,
+                earlier,
+                swap(rebuilt_3_outer, (0, 3)),
+                swap(rebuilt_2_even, (0, 2)),
+                swap(rebuilt_1, (0, 1), (2, 3)),
+                swap(rebuilt_3_inner, (1, 2)),
+                swap(rebuilt_2_odd, (1, 3)),
+                swap(current_2_odd, (1, 3)),
+                rebuilt_own,
+                own_current,
+                current_1,
+                current_2_even,
+                current_3,
+            ),
             parity_cost,
-        )
-        restored_state = call(
-            restore_kernel,
-            [IN_VMEM, IN_VMEM, ANYWHERE] + [IN_VMEM] * members,
-            floats(*blocks),
-            (table, earlier, parity_done, outgoing[0], *incoming),
-            0,
         )
     else:
         earlier_rows = lax.all_to_all(earlier, "code", 0, 0, tiled=True)

time: 24.5 us -> 33.4 us (1.36)
  the two profiles are of different devices: /device:TPU:0 before, /device:TPU:24 now
where the time goes in v14:
time: 33.4 us; the launch traced here: 33.1 us
  starting transfers between devices  21.4 us (64%)
  waiting for transfers between devices  8.01 us (24%)
  Pallas kernels  1.57 us (5%)
  local copies, waits for them, and re-layouts  1.32 us (4%)
  between operations  0.8 us (2%)
    ppermute x12, starting transfers between devices, swap(): return lax.ppermute(piece, 'code', both_ways)  21.4 us
    ppermute x12, waiting for transfers between devices, swap(): return lax.ppermute(piece, 'code', both_ways)  8.01 us
    pallas_call x3, Pallas kernels, call(): pl.pallas_call(kernel, in_specs=specs, out_specs=jax.tree.map(lambda _: I...  1.57 us
    squeeze x2, local copies, waits for them, and re-layouts, cut(): lax.dynamic_index_in_dim(blocks, c, 0, keepdims=False)  1.02 us
  transfers between devices with their start and end apart: 12, of which 4 were waited for; matrix products, arithmetic and copies ran while one was open for 0% of the time, Pallas kernels for 2%

profile of v14, /device:TPU:24, one launch (start us, length us, event | category | flops | bytes accessed | tf_op | source)
XLA Modules:
  0.0 33.1 jit_solution(1374051855135973595)
XLA Ops:
  0.6 0.0 copy-start.4
  0.7 1.0 %dynamic-slice_bitcast_fusion.4 = (f32[32,512]{1,0:T(8,128)S(1)}, f32[32,512]{1,0:T(8,128)S(1)}, f32[32,512]{1,0:T(8,128)S(1)}, f32[32,512]{1,0:T(8,128)S(1)}) fusion(f32[4,32,512]{2,1,0:T(8,128)} %bitcast.21, s32[]{:T(128)S(6)} %select_n.20, s32[]{:T(128)S(6)} %select_n.19, s32[]{:T(128)S(6)} %select_n.18, s32[]{:T(128)S(6)} %select_n.17), kind=kLoop, calls=%fused_computation.4 | loop fusion | bytes 524304 | tf_op jit(solution)/shard_map/jit(dynamic_index_in_dim)/squeeze | solution.py:166
  1.7 0.1 collective-permute-start.2
  1.7 1.9 %collective-permute-start.1 = (f32[32,512]{1,0:T(8,128)S(1)}, f32[32,512]{1,0:T(8,128)S(1)}, u32[]{:S(2)}, u32[]{:S(2)}) collective-permute-start(f32[32,512]{1,0:T(8,128)S(1)} %get-tuple-element.29), channel_id=1, source_target_pairs={{0,8},{8,0},{4,12},{12,4},{1,9},{9,1},{5,13},{13,5},{2,10},{10,2},... | collective-permute-start | bytes 196616 | tf_op jit(solution)/shard_map/ppermute | solution.py:162
  3.6 2.5 %collective-permute-start = (f32[32,512]{1,0:T(8,128)S(1)}, f32[32,512]{1,0:T(8,128)S(1)}, u32[]{:S(2)}, u32[]{:S(2)}) collective-permute-start(f32[32,512]{1,0:T(8,128)S(1)} %get-tuple-element.30), channel_id=1, source_target_pairs={{0,4},{4,0},{8,12},{12,8},{1,5},{5,1},{9,13},{13,9},{2,6},{6,2},{1... | collective-permute-start | bytes 196616 | tf_op jit(solution)/shard_map/ppermute | solution.py:162
  6.1 0.0 copy-done.4
  6.1 0.0 copy-start.1
  6.1 0.0 copy-start.2
  6.2 0.1 collective-permute-start.11
  6.3 0.0 copy-start.3
  6.3 0.5 %collective-permute-start.9 = (f32[32,512]{1,0:T(8,128)S(1)}, f32[32,512]{1,0:T(8,128)S(1)}, u32[]{:S(2)}, u32[]{:S(2)}) collective-permute-start(f32[32,512]{1,0:T(8,128)S(1)} %get-tuple-element.25), channel_id=1, source_target_pairs={{0,4},{4,0},{8,12},{12,8},{1,5},{5,1},{9,13},{13,9},{2,6},{6,2},{1... | collective-permute-start | bytes 196616 | tf_op jit(solution)/shard_map/ppermute | solution.py:162
  6.8 0.3 copy-done.1
  7.1 0.0 copy-done.2
  7.1 0.0 copy-done.3
  7.1 0.6 %shard_map.68 = (f32[2,32,512]{2,1,0:T(8,128)S(1)}, f32[29,512]{1,0:T(8,128)S(1)}) custom-call(s32[1,2]{1,0:T(1,128)S(1)} %copy-done.3, f32[4,4]{1,0:T(4,128)S(1)} %copy-done.2, f32[32,2048]{1,0:T(8,128)S(1)} %bitcast.23), custom_call_target="tpu_custom_call" | custom-call | flops 262144 | bytes 452680 | tf_op jit(solution)/shard_map/pallas_call | solution.py:145
  7.7 0.8 %collective-permute-done.2.refs_3_ = f32[32,512]{1,0:T(8,128)S(1)} collective-permute-done((f32[32,512]{1,0:T(8,128)S(1)}, f32[32,512]{1,0:T(8,128)S(1)}, u32[]{:S(2)}, u32[]{:S(2)}) %collective-permute-start.2) | collective-permute-done | bytes 65568 | tf_op jit(solution)/shard_map/ppermute | solution.py:162
  8.5 0.7 %collective-permute-start.10 = (f32[32,512]{1,0:T(8,128)S(1)}, f32[32,512]{1,0:T(8,128)S(1)}, u32[]{:S(2)}, u32[]{:S(2)}) collective-permute-start(f32[32,512]{1,0:T(8,128)S(1)} %get-tuple-element.27.refs_4_), channel_id=1, source_target_pairs={{0,8},{8,0},{1,9},{9,1},{2,10},{10,2},{3,11},{11,3},{16,24},{24,16... | collective-permute-start | bytes 196616 | tf_op jit(solution)/shard_map/ppermute | solution.py:162
  9.2 2.3 %collective-permute-done.1.refs_2_ = f32[32,512]{1,0:T(8,128)S(1)} collective-permute-done((f32[32,512]{1,0:T(8,128)S(1)}, f32[32,512]{1,0:T(8,128)S(1)}, u32[]{:S(2)}, u32[]{:S(2)}) %collective-permute-start.1) | collective-permute-done | bytes 65568 | tf_op jit(solution)/shard_map/ppermute | solution.py:162
  11.5 0.0 collective-permute-done.refs_1_
  11.5 0.0 copy-start
  11.5 0.1 shard_map.69
  11.5 4.2 %collective-permute-start.3 = (f32[32,512]{1,0:T(8,128)S(1)}, f32[32,512]{1,0:T(8,128)S(1)}, u32[]{:S(2)}, u32[]{:S(2)}) collective-permute-start(f32[32,512]{1,0:T(8,128)S(1)} %get-tuple-element.15), channel_id=1, source_target_pairs={{0,12},{12,0},{1,13},{13,1},{2,14},{14,2},{3,15},{15,3},{16,28},{2... | collective-permute-start | bytes 196616 | tf_op jit(solution)/shard_map/ppermute | solution.py:162
  15.7 0.7 %collective-permute-start.4 = (f32[32,512]{1,0:T(8,128)S(1)}, f32[32,512]{1,0:T(8,128)S(1)}, u32[]{:S(2)}, u32[]{:S(2)}) collective-permute-start(f32[32,512]{1,0:T(8,128)S(1)} %get-tuple-element.16), channel_id=1, source_target_pairs={{0,8},{8,0},{1,9},{9,1},{2,10},{10,2},{3,11},{11,3},{16,24},{24,16... | collective-permute-start | bytes 196616 | tf_op jit(solution)/shard_map/ppermute | solution.py:162
  16.4 0.0 collective-permute-done.11.refs_10_
  16.4 3.4 %collective-permute-start.5 = (f32[32,512]{1,0:T(8,128)S(1)}, f32[32,512]{1,0:T(8,128)S(1)}, u32[]{:S(2)}, u32[]{:S(2)}) collective-permute-start(f32[32,512]{1,0:T(8,128)S(1)} %get-tuple-element.17), channel_id=1, source_target_pairs={{0,4},{4,0},{8,12},{12,8},{1,5},{5,1},{9,13},{13,9},{2,6},{6,2},{1... | collective-permute-start | bytes 196616 | tf_op jit(solution)/shard_map/ppermute | solution.py:162
  19.8 0.0 collective-permute-done.9.refs_8_
  19.8 0.7 %collective-permute-start.6 = (f32[32,512]{1,0:T(8,128)S(1)}, f32[32,512]{1,0:T(8,128)S(1)}, u32[]{:S(2)}, u32[]{:S(2)}) collective-permute-start(f32[32,512]{1,0:T(8,128)S(1)} %get-tuple-element.18), channel_id=1, source_target_pairs={{4,8},{8,4},{5,9},{9,5},{6,10},{10,6},{7,11},{11,7},{20,24},{24,20... | collective-permute-start | bytes 196616 | tf_op jit(solution)/shard_map/ppermute | solution.py:162
  20.5 0.0 collective-permute-done.10.refs_9_
  20.5 4.6 %collective-permute-start.7 = (f32[32,512]{1,0:T(8,128)S(1)}, f32[32,512]{1,0:T(8,128)S(1)}, u32[]{:S(2)}, u32[]{:S(2)}) collective-permute-start(f32[32,512]{1,0:T(8,128)S(1)} %get-tuple-element.19), channel_id=1, source_target_pairs={{4,12},{12,4},{5,13},{13,5},{6,14},{14,6},{7,15},{15,7},{20,28},{2... | collective-permute-start | bytes 196616 | tf_op jit(solution)/shard_map/ppermute | solution.py:162
  25.2 0.0 collective-permute-done.3.refs_0_
  25.2 2.1 %collective-permute-start.8 = (f32[32,512]{1,0:T(8,128)S(1)}, f32[32,512]{1,0:T(8,128)S(1)}, u32[]{:S(2)}, u32[]{:S(2)}) collective-permute-start(f32[32,512]{1,0:T(8,128)S(1)} %get-tuple-element.20), channel_id=1, source_target_pairs={{4,12},{12,4},{5,13},{13,5},{6,14},{14,6},{7,15},{15,7},{20,28},{2... | collective-permute-start | bytes 196616 | tf_op jit(solution)/shard_map/ppermute | solution.py:162
  27.3 0.0 collective-permute-done.4.refs_1_
  27.3 0.0 collective-permute-done.5.refs_2_
  27.3 0.0 collective-permute-done.6.refs_3_
  27.3 0.7 %collective-permute-done.7.refs_4_ = f32[32,512]{1,0:T(8,128)S(1)} collective-permute-done((f32[32,512]{1,0:T(8,128)S(1)}, f32[32,512]{1,0:T(8,128)S(1)}, u32[]{:S(2)}, u32[]{:S(2)}) %collective-permute-start.7) | collective-permute-done | bytes 65568 | tf_op jit(solution)/shard_map/ppermute | solution.py:162
  28.0 4.2 %collective-permute-done.8.refs_5_ = f32[32,512]{1,0:T(8,128)S(1)} collective-permute-done((f32[32,512]{1,0:T(8,128)S(1)}, f32[32,512]{1,0:T(8,128)S(1)}, u32[]{:S(2)}, u32[]{:S(2)}) %collective-permute-start.8) | collective-permute-done | bytes 65568 | tf_op jit(solution)/shard_map/ppermute | solution.py:162
  32.2 0.0 copy-done
  32.2 0.9 %shard_map.70 = (f32[32,2048]{1,0:T(8,128)}, f32[4,32,512]{2,1,0:T(8,128)}) custom-call(f32[29,512]{1,0:T(8,128)S(1)} %get-tuple-element.13.table_ref, f32[4,32,512]{2,1,0:T(8,128)S(1)} %bitcast.22, f32[32,512]{1,0:T(8,128)S(1)} %collective-permute-done.3.refs_0_, f32[32,512]{1,0:T(8,128)S(1)} %collective-permute-done.4.refs_1_, ...), custom_call_target="tpu_custom_call" | custom-call | flops 524288 | bytes 1566720 | tf_op jit(solution)/shard_map/pallas_call | solution.py:145
  (1 shorter events, 0.0 us)
Async XLA Ops:
  0.6 5.5 %copy-start.4 = (f32[1,1,128,512]{3,2,1,0:T(8,128)S(1)}, f32[1,1,128,512]{3,2,1,0:T(8,128)}, u32[]{:S(2)}) copy-start(f32[1,1,128,512]{3,2,1,0:T(8,128)} %param.5) | copy-start | bytes 786436
  1.7 6.8 %collective-permute-start.2 = (f32[32,512]{1,0:T(8,128)S(1)}, f32[32,512]{1,0:T(8,128)S(1)}, u32[]{:S(2)}, u32[]{:S(2)}) collective-permute-start(f32[32,512]{1,0:T(8,128)S(1)} %get-tuple-element.28), channel_id=1, source_target_pairs={{0,12},{12,0},{4,8},{8,4},{1,13},{13,1},{5,9},{9,5},{2,14},{14,2},... | collective-permute-start | bytes 196616 | tf_op jit(solution)/shard_map/ppermute | solution.py:162
  1.7 9.7 %collective-permute-start.1 = (f32[32,512]{1,0:T(8,128)S(1)}, f32[32,512]{1,0:T(8,128)S(1)}, u32[]{:S(2)}, u32[]{:S(2)}) collective-permute-start(f32[32,512]{1,0:T(8,128)S(1)} %get-tuple-element.29), channel_id=1, source_target_pairs={{0,8},{8,0},{4,12},{12,4},{1,9},{9,1},{5,13},{13,5},{2,10},{10,2},... | collective-permute-start | bytes 196616 | tf_op jit(solution)/shard_map/ppermute | solution.py:162
  3.6 7.8 %collective-permute-start = (f32[32,512]{1,0:T(8,128)S(1)}, f32[32,512]{1,0:T(8,128)S(1)}, u32[]{:S(2)}, u32[]{:S(2)}) collective-permute-start(f32[32,512]{1,0:T(8,128)S(1)} %get-tuple-element.30), channel_id=1, source_target_pairs={{0,4},{4,0},{8,12},{12,8},{1,5},{5,1},{9,13},{13,9},{2,6},{6,2},{1... | collective-permute-start | bytes 196616 | tf_op jit(solution)/shard_map/ppermute | solution.py:162
  6.1 1.0 %copy-start.1 = (f32[1,32,2048]{2,1,0:T(8,128)S(1)}, f32[1,32,2048]{2,1,0:T(8,128)}, u32[]{:S(2)}) copy-start(f32[1,32,2048]{2,1,0:T(8,128)} %param.7) | copy-start | bytes 786436
  6.1 0.9 %copy-start.2 = (f32[4,4]{1,0:T(4,128)S(1)}, f32[4,4]{1,0:T(4,128)}, u32[]{:S(2)}) copy-start(f32[4,4]{1,0:T(4,128)} %generator_ref.1) | copy-start | bytes 196
  6.2 10.2 %collective-permute-start.11 = (f32[32,512]{1,0:T(8,128)S(1)}, f32[32,512]{1,0:T(8,128)S(1)}, u32[]{:S(2)}, u32[]{:S(2)}) collective-permute-start(f32[32,512]{1,0:T(8,128)S(1)} %get-tuple-element.24), channel_id=1, source_target_pairs={{0,12},{12,0},{4,8},{8,4},{1,13},{13,1},{5,9},{9,5},{2,14},{14,2},... | collective-permute-start | bytes 196616 | tf_op jit(solution)/shard_map/ppermute | solution.py:162
  6.3 0.8 %copy-start.3 = (s32[1,2]{1,0:T(1,128)S(1)}, s32[1,2]{1,0:T(1,128)}, u32[]{:S(2)}) copy-start(s32[1,2]{1,0:T(1,128)} %ids_ref.1) | copy-start | bytes 28
  6.3 13.5 %collective-permute-start.9 = (f32[32,512]{1,0:T(8,128)S(1)}, f32[32,512]{1,0:T(8,128)S(1)}, u32[]{:S(2)}, u32[]{:S(2)}) collective-permute-start(f32[32,512]{1,0:T(8,128)S(1)} %get-tuple-element.25), channel_id=1, source_target_pairs={{0,4},{4,0},{8,12},{12,8},{1,5},{5,1},{9,13},{13,9},{2,6},{6,2},{1... | collective-permute-start | bytes 196616 | tf_op jit(solution)/shard_map/ppermute | solution.py:162
  8.5 12.0 %collective-permute-start.10 = (f32[32,512]{1,0:T(8,128)S(1)}, f32[32,512]{1,0:T(8,128)S(1)}, u32[]{:S(2)}, u32[]{:S(2)}) collective-permute-start(f32[32,512]{1,0:T(8,128)S(1)} %get-tuple-element.27.refs_4_), channel_id=1, source_target_pairs={{0,8},{8,0},{1,9},{9,1},{2,10},{10,2},{3,11},{11,3},{16,24},{24,16... | collective-permute-start | bytes 196616 | tf_op jit(solution)/shard_map/ppermute | solution.py:162
  11.5 20.8 %copy-start = (f32[1,1,128,512]{3,2,1,0:T(8,128)S(1)}, f32[1,1,128,512]{3,2,1,0:T(8,128)}, u32[]{:S(2)}) copy-start(f32[1,1,128,512]{3,2,1,0:T(8,128)} %param.6) | copy-start | bytes 786436
  11.5 13.6 %collective-permute-start.3 = (f32[32,512]{1,0:T(8,128)S(1)}, f32[32,512]{1,0:T(8,128)S(1)}, u32[]{:S(2)}, u32[]{:S(2)}) collective-permute-start(f32[32,512]{1,0:T(8,128)S(1)} %get-tuple-element.15), channel_id=1, source_target_pairs={{0,12},{12,0},{1,13},{13,1},{2,14},{14,2},{3,15},{15,3},{16,28},{2... | collective-permute-start | bytes 196616 | tf_op jit(solution)/shard_map/ppermute | solution.py:162
  15.7 11.6 %collective-permute-start.4 = (f32[32,512]{1,0:T(8,128)S(1)}, f32[32,512]{1,0:T(8,128)S(1)}, u32[]{:S(2)}, u32[]{:S(2)}) collective-permute-start(f32[32,512]{1,0:T(8,128)S(1)} %get-tuple-element.16), channel_id=1, source_target_pairs={{0,8},{8,0},{1,9},{9,1},{2,10},{10,2},{3,11},{11,3},{16,24},{24,16... | collective-permute-start | bytes 196616 | tf_op jit(solution)/shard_map/ppermute | solution.py:162
  16.4 10.9 %collective-permute-start.5 = (f32[32,512]{1,0:T(8,128)S(1)}, f32[32,512]{1,0:T(8,128)S(1)}, u32[]{:S(2)}, u32[]{:S(2)}) collective-permute-start(f32[32,512]{1,0:T(8,128)S(1)} %get-tuple-element.17), channel_id=1, source_target_pairs={{0,4},{4,0},{8,12},{12,8},{1,5},{5,1},{9,13},{13,9},{2,6},{6,2},{1... | collective-permute-start | bytes 196616 | tf_op jit(solution)/shard_map/ppermute | solution.py:162
  19.8 7.5 %collective-permute-start.6 = (f32[32,512]{1,0:T(8,128)S(1)}, f32[32,512]{1,0:T(8,128)S(1)}, u32[]{:S(2)}, u32[]{:S(2)}) collective-permute-start(f32[32,512]{1,0:T(8,128)S(1)} %get-tuple-element.18), channel_id=1, source_target_pairs={{4,8},{8,4},{5,9},{9,5},{6,10},{10,6},{7,11},{11,7},{20,24},{24,20... | collective-permute-start | bytes 196616 | tf_op jit(solution)/shard_map/ppermute | solution.py:162
  20.5 7.5 %collective-permute-start.7 = (f32[32,512]{1,0:T(8,128)S(1)}, f32[32,512]{1,0:T(8,128)S(1)}, u32[]{:S(2)}, u32[]{:S(2)}) collective-permute-start(f32[32,512]{1,0:T(8,128)S(1)} %get-tuple-element.19), channel_id=1, source_target_pairs={{4,12},{12,4},{5,13},{13,5},{6,14},{14,6},{7,15},{15,7},{20,28},{2... | collective-permute-start | bytes 196616 | tf_op jit(solution)/shard_map/ppermute | solution.py:162
  25.2 7.1 %collective-permute-start.8 = (f32[32,512]{1,0:T(8,128)S(1)}, f32[32,512]{1,0:T(8,128)S(1)}, u32[]{:S(2)}, u32[]{:S(2)}) collective-permute-start(f32[32,512]{1,0:T(8,128)S(1)} %get-tuple-element.20), channel_id=1, source_target_pairs={{4,12},{12,4},{5,13},{13,5},{6,14},{14,6},{7,15},{15,7},{20,28},{2... | collective-permute-start | bytes 196616 | tf_op jit(solution)/shard_map/ppermute | solution.py:162

commit v15 on v11

--- a/solution.py
+++ b/solution.py
@@ -11,12 +11,13 @@
 IN_SMEM = pl.BlockSpec(memory_space=pltpu.SMEM)
 ANYWHERE = pl.BlockSpec(memory_space=pl.ANY)
 
-DIRECT_MEMBERS = 8
+PAIRED_MEMBERS = 4
+SHIFTS = (0, 1, 2, 3)
 KERNEL_VMEM = 8 * 2**20
 
 
 def rounds_of(members):
-    return range(members - 1, 0, -1)
+    return range(1, members)
 
 
 def order_of(members, direct):
@@ -30,17 +31,45 @@
     if not direct:
         return list(range(members))
     me = lax.axis_index("code")
-    return [lax.rem(me + s, members) for s in range(members)]
+    return [lax.rem(me + s, members) for s in SHIFTS]
 
 
 def sources_of(members, direct):
     if not direct:
         return list(range(members))
     me = lax.axis_index("code")
-    return [lax.rem(me + members - s, members) for s in range(members)]
-
-
-def plan_kernel(direct, ids_ref, generator_ref, parity_ref, base_ref, table_ref):
+    return [lax.rem(me + members - s, members) for s in SHIFTS]
+
+
+NEXT = (1, 0, 3, 2)
+IN_ONE_HALF = ((3, 2, 1, 0), (2, 3, 0, 1), NEXT)
+DELIVERIES = {
+    (0, 1): IN_ONE_HALF,
+    (2, 3): IN_ONE_HALF,
+    (0, 2): ((1, 2, 3, 0), (2, 1, 0, 3), NEXT),
+    (1, 3): ((3, 0, 1, 2), (0, 3, 2, 1), NEXT),
+    (0, 3): ((3, 1, 2, 0), (1, 3, 0, 2), NEXT),
+    (1, 2): ((0, 2, 1, 3), (2, 0, 3, 1), NEXT),
+}
+WAYS = sorted(set(DELIVERIES.values()))
+
+
+def way_codes():
+    members = range(PAIRED_MEMBERS)
+    codes = [
+        WAYS.index(DELIVERIES[min(a, b), max(a, b)]) if a != b else 0
+        for a in members
+        for b in members
+    ]
+    for way in WAYS:
+        for me in members:
+            codes += [targets[me] for targets in way]
+            codes += [targets.index(me) for targets in way]
+    return codes
+
+
+def plan_kernel(direct, ids_ref, generator_ref, codes_ref, parity_ref, *outs):
+    base_ref, table_ref = outs[:2]
     spans, members = generator_ref.shape
     width = base_ref.shape[2]
     first, second = ids_ref[0, 0], ids_ref[0, 1]
@@ -77,11 +106,22 @@
     for i, c in enumerate(sources_of(members, direct)):
         for j in range(spans):
             put((2 + j) * members + i, spread(generator_ref[j, c]))
-    for i, c in enumerate(targets_of(members, direct)):
+    me = lax.axis_index("code")
+    targets = range(members)
+    if direct:
+        way = codes_ref[first * members + second]
+        outs[2][0] = way
+        rounds = members - 1
+        start = members * members + (way * members + me) * 2 * rounds
+        targets = [me] + [codes_ref[start + r] for r in range(rounds)]
+        for r in range(rounds):
+            source = codes_ref[start + rounds + r]
+            for c in range(members):
+                put((3 + spans + r) * members + c, spread(jnp.where(source == c, 1.0, 0.0)))
+    for i, c in enumerate(targets):
         put((2 + spans) * members + i, spread(jnp.where(first == c, 1.0, 0.0)))
-    me = lax.axis_index("code")
     lost = jnp.logical_or(first == me, second == me)
-    put((3 + spans) * members, spread(jnp.where(lost, 1.0, 0.0)))
+    put(table_ref.shape[0] - 1, spread(jnp.where(lost, 1.0, 0.0)))
 
 
 def weigh(table_ref, start, rows):
@@ -92,18 +132,18 @@
     return total
 
 
-def rebuilt_for(base_ref, table_ref, rows):
+def rebuilt_for(spans, base_ref, table_ref, rows):
     members = len(rows)
     rebuilt = [base_ref[k] - weigh(table_ref, k * members, rows) for k in range(2)]
-    picks = table_ref.shape[0] - 1 - members
+    picks = (2 + spans) * members
     return [
         jnp.where(table_ref[picks + i : picks + i + 1, :] > 0.5, *rebuilt) for i in range(members)
     ]
 
 
-def rebuild_whole_kernel(base_ref, table_ref, rows_ref, out_ref):
+def rebuild_whole_kernel(spans, base_ref, table_ref, rows_ref, out_ref):
     rows = [rows_ref[c] for c in range(rows_ref.shape[0])]
-    for c, block in enumerate(rebuilt_for(base_ref, table_ref, rows)):
+    for c, block in enumerate(rebuilt_for(spans, base_ref, table_ref, rows)):
         out_ref[c] = block
 
 
@@ -117,33 +157,33 @@
         out_ref[:, j * width : (j + 1) * width] = weigh(table_ref, (2 + j) * members, rows)
 
 
-def rebuild_paired_kernel(base_ref, table_ref, *refs):
+def rebuild_paired_kernel(spans, held_back_by, base_ref, table_ref, *refs):
     rows, outs = refs[: len(refs) // 2], refs[len(refs) // 2 :]
-    for out_ref, block in zip(outs, rebuilt_for(base_ref, table_ref, [r[...] for r in rows])):
+    for out_ref, block in zip(outs, rebuilt_for(spans, base_ref, table_ref, [r[...] for r in rows])):
         out_ref[...] = block
 
 
-def parity_paired_kernel(table_ref, *refs):
-    rows, out_ref, done_ref = refs[:-2], refs[-2], refs[-1]
-    parity_into(out_ref, table_ref, [r[...] for r in rows])
-    done_ref[...] = jnp.zeros(done_ref.shape, done_ref.dtype)
-
-
-def restore_kernel(table_ref, earlier_ref, held_back_by, *refs):
-    pieces, out_ref = refs[:-1], refs[-1]
-    members = len(pieces)
+def finish_kernel(table_ref, earlier_ref, *refs):
+    members = (len(refs) - 2) // 2
+    rows, pieces, (parity_ref, out_ref) = refs[:members], refs[members:-2], refs[-2:]
+    parity_into(parity_ref, table_ref, [r[...] for r in rows])
     last = table_ref.shape[0] - 1
     lost = table_ref[last : last + 1, :] > 0.5
-    for c, piece in zip(sources_of(members, True), pieces):
-        out_ref[c] = jnp.where(lost, piece[...], earlier_ref[c])
+    arrivals = last - (members - 1) * members
+    for c in range(members):
+        block = pieces[0][...]
+        for r, piece in enumerate(pieces[1:]):
+            i = arrivals + r * members + c
+            block = jnp.where(table_ref[i : i + 1, :] > 0.5, piece[...], block)
+        out_ref[c] = jnp.where(lost, block, earlier_ref[c])
 
 
 def call(kernel, specs, outs, args, flops, **options):
     total = sum(x.size for x in args) + sum(o.size for o in jax.tree.leaves(outs))
+    options.setdefault("out_specs", jax.tree.map(lambda _: IN_VMEM, outs))
     return pl.pallas_call(
         kernel,
         in_specs=specs,
-        out_specs=jax.tree.map(lambda _: IN_VMEM, outs),
         out_shape=outs,
         compiler_params=pltpu.CompilerParams(vmem_limit_bytes=KERNEL_VMEM),
         cost_estimate=pl.CostEstimate(flops=flops, bytes_accessed=4 * total, transcendentals=0),
@@ -158,7 +198,7 @@
 def pass_on(pieces, members):
     return [
         lax.ppermute(piece, "code", [(d, (d + s) % members) for d in range(members)])
-        for s, piece in enumerate(pieces, 1)
+        for s, piece in zip(SHIFTS[1:], pieces)
     ]
 
 
@@ -167,6 +207,10 @@
         lax.ppermute(piece, "code", [(d, d ^ r) for d in range(members)])
         for r, piece in zip(rounds, pieces)
     ]
+
+
+def deliver(way, *pieces):
+    return tuple(lax.ppermute(p, "code", list(enumerate(t))) for p, t in zip(pieces, way))
 
 
 def cut(blocks, order):
@@ -182,14 +226,22 @@
     blocks = (members, own_rows, width)
     earlier = previous_slab.reshape(blocks)
     current = state_slab.reshape(blocks)
-    direct = 4 <= members <= DIRECT_MEMBERS and members & (members - 1) == 0
-
-    base, table = call(
+    direct = members == PAIRED_MEMBERS
+
+    codes = jnp.array(way_codes() if direct else [0], jnp.int32)
+    arrivals = members * (members - 1) if direct else 0
+    plan_outs = [
+        floats(2, own_rows, width),
+        floats((3 + spans) * members + arrivals + 1, width),
+        jax.ShapeDtypeStruct((1,), jnp.int32),
+    ]
+    base, table, way = call(
         functools.partial(plan_kernel, direct),
-        [IN_SMEM, IN_SMEM, IN_VMEM],
-        (floats(2, own_rows, width), floats((3 + spans) * members + 1, width)),
-        (failed_ids, generator, previous_parity[0]),
+        [IN_SMEM, IN_SMEM, IN_SMEM, IN_VMEM],
+        plan_outs,
+        (failed_ids, generator, codes, previous_parity[0]),
         4 * spans * own_rows * width,
+        out_specs=[IN_VMEM, IN_VMEM, IN_SMEM],
     )
     parity_shape = floats(own_rows, spans * width)
     rebuild_cost = 4 * slab_rows * width
@@ -199,35 +251,30 @@
         block = floats(own_rows, width)
         own_earlier, *cut_earlier = cut(earlier, order_of(members, True))
         earlier_rows = trade(cut_earlier, rounds, members)
+        current, earlier_rows[-1] = lax.optimization_barrier((current, earlier_rows[-1]))
         own_current, *cut_current = cut(current, targets_of(members, True))
+        current_rows = [own_current, *pass_on(cut_current, members)]
         outgoing = call(
-            rebuild_paired_kernel,
-            [IN_VMEM] * (members + 2),
+            functools.partial(rebuild_paired_kernel, spans),
+            [ANYWHERE] + [IN_VMEM] * (members + 2),
             [block] * members,
-            (base, table, own_earlier, *earlier_rows),
+            (current_rows[1], base, table, own_earlier, *earlier_rows),
             rebuild_cost,
         )
-        incoming = pass_on(outgoing[1:], members)
-        current_rows = [own_current, *pass_on(cut_current, members)]
-        new_parity, parity_done = call(
-            parity_paired_kernel,
-            [IN_VMEM] * (members + 1),
-            (parity_shape, floats(8, 128)),
-            (table, *current_rows),
+        deliveries = [functools.partial(deliver, w) for w in WAYS]
+        incoming = lax.switch(way[0], deliveries, *outgoing[1:])
+        new_parity, restored_state = call(
+            finish_kernel,
+            [IN_VMEM] * (2 + 2 * members),
+            (parity_shape, floats(*blocks)),
+            (table, earlier, *current_rows, outgoing[0], *incoming),
             parity_cost,
-        )
-        restored_state = call(
-            restore_kernel,
-            [IN_VMEM, IN_VMEM, ANYWHERE] + [IN_VMEM] * members,
-            floats(*blocks),
-            (table, earlier, parity_done, outgoing[0], *incoming),
-            0,
         )
     else:
         earlier_rows = lax.all_to_all(earlier, "code", 0, 0, tiled=True)
         current_rows = lax.all_to_all(current, "code", 0, 0, tiled=True)
         outgoing = call(
-            rebuild_whole_kernel,
+            functools.partial(rebuild_whole_kernel, spans),
             [IN_VMEM] * 3,
             floats(*blocks),
             (base, table, earlier_rows),

time: 23.6 us -> 27.6 us (1.17); the launches traced: 23.4 us -> 27.9 us
  waiting for transfers between devices: 4.37 us -> 7.01 us
  Pallas kernels: 2.24 us -> 3.04 us
  between operations: 0.72 us -> 1.37 us
  starting transfers between devices: 15 us -> 15.4 us
    ppermute x0 -> x3, waiting for transfers between devices: none -> 5.06 us  [deliver(): lax.ppermute(p, 'code', list(enumerate(t)))]
    ppermute x0 -> x3, starting transfers between devices: none -> 3.93 us  [deliver(): lax.ppermute(p, 'code', list(enumerate(t)))]
    ppermute x6 -> x3, starting transfers between devices: 9.28 us -> 5.73 us  [pass_on(): lax.ppermute(piece, 'code', [(d, (d + s) % members) for d in range(member...]
    ppermute x6 -> x3, waiting for transfers between devices: 3.11 us -> 0.01 us  [pass_on(): lax.ppermute(piece, 'code', [(d, (d + s) % members) for d in range(member...]
    pallas_call x4 -> x3, Pallas kernels: 2.24 us -> 3.04 us  [call(): pl.pallas_call(kernel, in_specs=specs, out_shape=outs, compiler_params=pl...]
    ppermute x3, waiting for transfers between devices: 1.26 us -> 1.94 us  [trade(): lax.ppermute(piece, 'code', [(d, d ^ r) for d in range(members)])]
  transfers between devices with their start and end apart: 9 -> 9, of which waited for: 3 -> 4; matrix products, arithmetic and copies ran while one was open for 0% -> 0% of each run, Pallas kernels for 6% -> 5%
where the time goes in v15:
time: 27.6 us; the launch traced here: 27.9 us
  starting transfers between devices  15.4 us (56%)
  waiting for transfers between devices  7.01 us (25%)
  Pallas kernels  3.04 us (11%)
  between operations  1.37 us (5%)
  local copies, waits for them, and re-layouts  1.05 us (4%)
    ppermute x3, starting transfers between devices, trade(): lax.ppermute(piece, 'code', [(d, d ^ r) for d in range(members)])  5.76 us
    ppermute x3, starting transfers between devices, pass_on(): lax.ppermute(piece, 'code', [(d, (d + s) % members) for d in range(member...  5.73 us
    ppermute x3, waiting for transfers between devices, deliver(): lax.ppermute(p, 'code', list(enumerate(t)))  5.06 us
    ppermute x3, starting transfers between devices, deliver(): lax.ppermute(p, 'code', list(enumerate(t)))  3.93 us
    pallas_call x3, Pallas kernels, call(): pl.pallas_call(kernel, in_specs=specs, out_shape=outs, compiler_params=pl...  3.04 us
    ppermute x3, waiting for transfers between devices, trade(): lax.ppermute(piece, 'code', [(d, d ^ r) for d in range(members)])  1.94 us
    squeeze x2, local copies, waits for them, and re-layouts, cut(): lax.dynamic_index_in_dim(blocks, c, 0, keepdims=False)  1.02 us
  transfers between devices with their start and end apart: 9, of which 4 were waited for; matrix products, arithmetic and copies ran while one was open for 0% of the time, Pallas kernels for 5%

profile of v15, /device:TPU:0, one launch (start us, length us, event | category | flops | bytes accessed | tf_op | source)
XLA Modules:
  0.0 27.9 jit_solution(6270724065933777457)
XLA Ops:
  0.6 0.0 copy-start.5
  0.7 1.0 %dynamic-slice_bitcast_fusion = (f32[32,512]{1,0:T(8,128)S(1)}, f32[32,512]{1,0:T(8,128)S(1)}, f32[32,512]{1,0:T(8,128)S(1)}, f32[32,512]{1,0:T(8,128)S(1)}) fusion(f32[4,32,512]{2,1,0:T(8,128)} %bitcast.22, s32[]{:T(128)S(6)} %select_n.32, s32[]{:T(128)S(6)} %select_n.31, s32[]{:T(128)S(6)} %select_n.30, s32[]{:T(128)S(6)} %select_n.25), kind=kLoop, calls=%fused_computation | loop fusion | bytes 524304 | tf_op jit(solution)/shard_map/jit(dynamic_index_in_dim)/squeeze | solution.py:217
  1.7 5.1 %collective-permute-start.15 = (f32[32,512]{1,0:T(8,128)S(1)}, f32[32,512]{1,0:T(8,128)S(1)}, u32[]{:S(2)}, u32[]{:S(2)}) collective-permute-start(f32[32,512]{1,0:T(8,128)S(1)} %get-tuple-element.78), channel_id=1, source_target_pairs={{0,12},{4,8},{8,4},{12,0},{1,13},{5,9},{9,5},{13,1},{2,14},{6,10},... | collective-permute-start | bytes 196616 | tf_op jit(solution)/shard_map/ppermute | solution.py:207
  6.8 0.0 collective-permute-start.20
  6.8 0.6 %collective-permute-start.19 = (f32[32,512]{1,0:T(8,128)S(1)}, f32[32,512]{1,0:T(8,128)S(1)}, u32[]{:S(2)}, u32[]{:S(2)}) collective-permute-start(f32[32,512]{1,0:T(8,128)S(1)} %get-tuple-element.76), channel_id=1, source_target_pairs={{0,4},{4,0},{8,12},{12,8},{1,5},{5,1},{9,13},{13,9},{2,6},{6,2},{1... | collective-permute-start | bytes 196616 | tf_op jit(solution)/shard_map/ppermute | solution.py:207
  7.4 1.9 %collective-permute-done.15.refs_3_ = f32[32,512]{1,0:T(8,128)S(1)} collective-permute-done((f32[32,512]{1,0:T(8,128)S(1)}, f32[32,512]{1,0:T(8,128)S(1)}, u32[]{:S(2)}, u32[]{:S(2)}) %collective-permute-start.15) | collective-permute-done | bytes 65568 | tf_op jit(solution)/shard_map/ppermute | solution.py:207
  9.4 0.0 copy-done.5
  9.4 0.0 copy-start.1
  9.4 2.7 %collective-permute-start.16 = (f32[32,512]{1,0:T(8,128)S(1)}, f32[32,512]{1,0:T(8,128)S(1)}, u32[]{:S(2)}, u32[]{:S(2)}) collective-permute-start(f32[32,512]{1,0:T(8,128)S(1)} %get-tuple-element.81), channel_id=1, source_target_pairs={{0,4},{4,8},{8,12},{12,0},{1,5},{5,9},{9,13},{13,1},{2,6},{6,10},{... | collective-permute-start | bytes 196616 | tf_op jit(solution)/shard_map/ppermute | solution.py:200
  12.1 0.0 copy-start.2
  12.1 1.6 %collective-permute-start.18 = (f32[32,512]{1,0:T(8,128)S(1)}, f32[32,512]{1,0:T(8,128)S(1)}, u32[]{:S(2)}, u32[]{:S(2)}) collective-permute-start(f32[32,512]{1,0:T(8,128)S(1)} %get-tuple-element.79), channel_id=1, source_target_pairs={{0,12},{4,0},{8,4},{12,8},{1,13},{5,1},{9,5},{13,9},{2,14},{6,2},{... | collective-permute-start | bytes 196616 | tf_op jit(solution)/shard_map/ppermute | solution.py:200
  13.7 0.0 copy-start.3
  13.7 0.0 copy-start.4
  13.7 1.4 %collective-permute-start.17 = (f32[32,512]{1,0:T(8,128)S(1)}, f32[32,512]{1,0:T(8,128)S(1)}, u32[]{:S(2)}, u32[]{:S(2)}) collective-permute-start(f32[32,512]{1,0:T(8,128)S(1)} %get-tuple-element.80), channel_id=1, source_target_pairs={{0,8},{4,12},{8,0},{12,4},{1,9},{5,13},{9,1},{13,5},{2,10},{6,14},... | collective-permute-start | bytes 196616 | tf_op jit(solution)/shard_map/ppermute | solution.py:200
  15.1 0.0 copy-done.1
  15.1 0.0 copy-done.2
  15.1 0.0 copy-done.3
  15.1 0.0 copy-done.4
  15.1 1.2 %shard_map.77 = (f32[2,32,512]{2,1,0:T(8,128)S(1)}, f32[41,512]{1,0:T(8,128)S(1)}, s32[1]{0:T(128)}) custom-call(s32[1,2]{1,0:T(1,128)S(1)} %copy-done.4, f32[4,4]{1,0:T(4,128)S(1)} %copy-done.2, s32[136]{0:T(256)S(1)} %copy-done.3, f32[32,2048]{1,0:T(8,128)S(1)} %bitcast.24), custom_call_target="tpu_custom_call" | custom-call | flops 262144 | bytes 477804 | tf_op jit(solution)/shard_map/pallas_call | solution.py:184
  17.0 0.0 collective-permute-done.20.refs_2_
  17.0 0.0 collective-permute-done.19.refs_1_
  17.0 0.0 collective-permute-done.16.held_back_by.refs_1_
  17.0 0.0 copy-start
  17.0 0.1 shard_map.78
  17.1 9.0 %conditional.1 = (f32[32,512]{1,0:T(8,128)}, f32[32,512]{1,0:T(8,128)}, f32[32,512]{1,0:T(8,128)}) conditional(s32[]{:T(128)} %bitcast.11, (f32[32,512]{1,0:T(8,128)S(1)}, f32[32,512]{1,0:T(8,128)S(1)}, f32[32,512]{1,0:T(8,128)S(1)}) %tuple.30, (f32[32,512]{1,0:T(8,128)S(1)}, f32[32,512]{1,0:T(8,128)S(1)}, ...), branch_computations={%region_0.1_spmd, %region_1.2_spmd, %region_2.3_spmd, %region_3.4_... | conditional | bytes 786576 | solution.py:265
  17.1 1.2 %collective-permute-start.3 = (f32[32,512]{1,0:T(8,128)S(1)}, f32[32,512]{1,0:T(8,128)}, u32[]{:S(2)}, u32[]{:S(2)}) collective-permute-start(f32[32,512]{1,0:T(8,128)S(1)} %get-tuple-element.33), channel_id=1, source_target_pairs={{0,4},{4,8},{8,12},{12,0},{1,5},{5,9},{9,13},{13,1},{2,6},{6,10},{... | collective-permute-start | bytes 196616 | tf_op jit(solution)/shard_map/cond/branch_1_fun/ppermute | solution.py:213
  18.3 2.7 %collective-permute-start.4 = (f32[32,512]{1,0:T(8,128)S(1)}, f32[32,512]{1,0:T(8,128)}, u32[]{:S(2)}, u32[]{:S(2)}) collective-permute-start(f32[32,512]{1,0:T(8,128)S(1)} %get-tuple-element.34), channel_id=1, source_target_pairs={{0,8},{4,4},{8,0},{12,12},{1,9},{5,5},{9,1},{13,13},{2,10},{6,6},{... | collective-permute-start | bytes 196616 | tf_op jit(solution)/shard_map/cond/branch_1_fun/ppermute | solution.py:213
  21.0 0.1 collective-permute-start.5
  21.1 2.5 %collective-permute-done.3 = f32[32,512]{1,0:T(8,128)} collective-permute-done((f32[32,512]{1,0:T(8,128)S(1)}, f32[32,512]{1,0:T(8,128)}, u32[]{:S(2)}, u32[]{:S(2)}) %collective-permute-start.3) | collective-permute-done | bytes 65568 | tf_op jit(solution)/shard_map/cond/branch_1_fun/ppermute | solution.py:213
  23.6 1.9 %collective-permute-done.4 = f32[32,512]{1,0:T(8,128)} collective-permute-done((f32[32,512]{1,0:T(8,128)S(1)}, f32[32,512]{1,0:T(8,128)}, u32[]{:S(2)}, u32[]{:S(2)}) %collective-permute-start.4) | collective-permute-done | bytes 65568 | tf_op jit(solution)/shard_map/cond/branch_1_fun/ppermute | solution.py:213
  25.6 0.6 %collective-permute-done.5 = f32[32,512]{1,0:T(8,128)} collective-permute-done((f32[32,512]{1,0:T(8,128)S(1)}, f32[32,512]{1,0:T(8,128)}, u32[]{:S(2)}, u32[]{:S(2)}) %collective-permute-start.5) | collective-permute-done | bytes 65568 | tf_op jit(solution)/shard_map/cond/branch_1_fun/ppermute | solution.py:213
  26.1 0.0 collective-permute-done.18.refs_3_
  26.1 0.0 collective-permute-done.17.refs_2_
  26.1 0.0 copy-done
  26.1 1.8 %shard_map.79 = (f32[32,2048]{1,0:T(8,128)}, f32[4,32,512]{2,1,0:T(8,128)}) custom-call(f32[41,512]{1,0:T(8,128)S(1)} %get-tuple-element.61.table_ref, f32[4,32,512]{2,1,0:T(8,128)S(1)} %bitcast.23, f32[32,512]{1,0:T(8,128)S(1)} %get-tuple-element.82.refs_0_, f32[32,512]{1,0:T(8,128)S(1)} %collective-permute-done.16.held_back_by.refs_1_, ...), custom_call_target="tpu_custom_call" | custom-call | flops 524288 | bytes 1394688 | tf_op jit(solution)/shard_map/pallas_call | solution.py:184
  (1 shorter events, 0.0 us)
Async XLA Ops:
  0.6 8.7 %copy-start.5 = (f32[1,1,128,512]{3,2,1,0:T(8,128)S(1)}, f32[1,1,128,512]{3,2,1,0:T(8,128)}, u32[]{:S(2)}) copy-start(f32[1,1,128,512]{3,2,1,0:T(8,128)} %param.11) | copy-start | bytes 786436
  1.7 7.7 %collective-permute-start.15 = (f32[32,512]{1,0:T(8,128)S(1)}, f32[32,512]{1,0:T(8,128)S(1)}, u32[]{:S(2)}, u32[]{:S(2)}) collective-permute-start(f32[32,512]{1,0:T(8,128)S(1)} %get-tuple-element.78), channel_id=1, source_target_pairs={{0,12},{4,8},{8,4},{12,0},{1,13},{5,9},{9,5},{13,1},{2,14},{6,10},... | collective-permute-start | bytes 196616 | tf_op jit(solution)/shard_map/ppermute | solution.py:207
  6.8 10.2 %collective-permute-start.20 = (f32[32,512]{1,0:T(8,128)S(1)}, f32[32,512]{1,0:T(8,128)S(1)}, u32[]{:S(2)}, u32[]{:S(2)}) collective-permute-start(f32[32,512]{1,0:T(8,128)S(1)} %get-tuple-element.75), channel_id=1, source_target_pairs={{0,8},{4,12},{8,0},{12,4},{1,9},{5,13},{9,1},{13,5},{2,10},{6,14},... | collective-permute-start | bytes 196616 | tf_op jit(solution)/shard_map/ppermute | solution.py:207
  6.8 10.2 %collective-permute-start.19 = (f32[32,512]{1,0:T(8,128)S(1)}, f32[32,512]{1,0:T(8,128)S(1)}, u32[]{:S(2)}, u32[]{:S(2)}) collective-permute-start(f32[32,512]{1,0:T(8,128)S(1)} %get-tuple-element.76), channel_id=1, source_target_pairs={{0,4},{4,0},{8,12},{12,8},{1,5},{5,1},{9,13},{13,9},{2,6},{6,2},{1... | collective-permute-start | bytes 196616 | tf_op jit(solution)/shard_map/ppermute | solution.py:207
  9.4 5.8 %copy-start.1 = (f32[1,32,2048]{2,1,0:T(8,128)S(1)}, f32[1,32,2048]{2,1,0:T(8,128)}, u32[]{:S(2)}) copy-start(f32[1,32,2048]{2,1,0:T(8,128)} %param.13) | copy-start | bytes 786436
  9.4 7.6 %collective-permute-start.16 = (f32[32,512]{1,0:T(8,128)S(1)}, f32[32,512]{1,0:T(8,128)S(1)}, u32[]{:S(2)}, u32[]{:S(2)}) collective-permute-start(f32[32,512]{1,0:T(8,128)S(1)} %get-tuple-element.81), channel_id=1, source_target_pairs={{0,4},{4,8},{8,12},{12,0},{1,5},{5,9},{9,13},{13,1},{2,6},{6,10},{... | collective-permute-start | bytes 196616 | tf_op jit(solution)/shard_map/ppermute | solution.py:200
  12.1 3.1 %copy-start.2 = (f32[4,4]{1,0:T(4,128)S(1)}, f32[4,4]{1,0:T(4,128)}, u32[]{:S(2)}) copy-start(f32[4,4]{1,0:T(4,128)} %generator_ref.1) | copy-start | bytes 196
  12.1 14.1 %collective-permute-start.18 = (f32[32,512]{1,0:T(8,128)S(1)}, f32[32,512]{1,0:T(8,128)S(1)}, u32[]{:S(2)}, u32[]{:S(2)}) collective-permute-start(f32[32,512]{1,0:T(8,128)S(1)} %get-tuple-element.79), channel_id=1, source_target_pairs={{0,12},{4,0},{8,4},{12,8},{1,13},{5,1},{9,5},{13,9},{2,14},{6,2},{... | collective-permute-start | bytes 196616 | tf_op jit(solution)/shard_map/ppermute | solution.py:200
  13.7 1.4 %copy-start.3 = (s32[136]{0:T(256)S(1)}, s32[136]{0:T(256)}, u32[]{:S(2)}) copy-start(s32[136]{0:T(256)} %constant.47.clone.codes_ref) | copy-start | bytes 1636
  13.7 1.4 %copy-start.4 = (s32[1,2]{1,0:T(1,128)S(1)}, s32[1,2]{1,0:T(1,128)}, u32[]{:S(2)}) copy-start(s32[1,2]{1,0:T(1,128)} %ids_ref.1) | copy-start | bytes 28
  13.7 12.4 %collective-permute-start.17 = (f32[32,512]{1,0:T(8,128)S(1)}, f32[32,512]{1,0:T(8,128)S(1)}, u32[]{:S(2)}, u32[]{:S(2)}) collective-permute-start(f32[32,512]{1,0:T(8,128)S(1)} %get-tuple-element.80), channel_id=1, source_target_pairs={{0,8},{4,12},{8,0},{12,4},{1,9},{5,13},{9,1},{13,5},{2,10},{6,14},... | collective-permute-start | bytes 196616 | tf_op jit(solution)/shard_map/ppermute | solution.py:200
  17.0 9.1 %copy-start = (f32[1,1,128,512]{3,2,1,0:T(8,128)S(1)}, f32[1,1,128,512]{3,2,1,0:T(8,128)}, u32[]{:S(2)}) copy-start(f32[1,1,128,512]{3,2,1,0:T(8,128)} %param.12) | copy-start | bytes 786436
  17.1 6.5 %collective-permute-start.3 = (f32[32,512]{1,0:T(8,128)S(1)}, f32[32,512]{1,0:T(8,128)}, u32[]{:S(2)}, u32[]{:S(2)}) collective-permute-start(f32[32,512]{1,0:T(8,128)S(1)} %get-tuple-element.33), channel_id=1, source_target_pairs={{0,4},{4,8},{8,12},{12,0},{1,5},{5,9},{9,13},{13,1},{2,6},{6,10},{... | collective-permute-start | bytes 196616 | tf_op jit(solution)/shard_map/cond/branch_1_fun/ppermute | solution.py:213
  18.3 7.3 %collective-permute-start.4 = (f32[32,512]{1,0:T(8,128)S(1)}, f32[32,512]{1,0:T(8,128)}, u32[]{:S(2)}, u32[]{:S(2)}) collective-permute-start(f32[32,512]{1,0:T(8,128)S(1)} %get-tuple-element.34), channel_id=1, source_target_pairs={{0,8},{4,4},{8,0},{12,12},{1,9},{5,5},{9,1},{13,13},{2,10},{6,6},{... | collective-permute-start | bytes 196616 | tf_op jit(solution)/shard_map/cond/branch_1_fun/ppermute | solution.py:213
  21.0 5.1 %collective-permute-start.5 = (f32[32,512]{1,0:T(8,128)S(1)}, f32[32,512]{1,0:T(8,128)}, u32[]{:S(2)}, u32[]{:S(2)}) collective-permute-start(f32[32,512]{1,0:T(8,128)S(1)} %get-tuple-element.35), channel_id=1, source_target_pairs={{0,4},{4,0},{8,12},{12,8},{1,5},{5,1},{9,13},{13,9},{2,6},{6,2},{1... | collective-permute-start | bytes 196616 | tf_op jit(solution)/shard_map/cond/branch_1_fun/ppermute | solution.py:213

commit v16 on v15

--- a/solution.py
+++ b/solution.py
@@ -12,7 +12,6 @@
 ANYWHERE = pl.BlockSpec(memory_space=pl.ANY)
 
 PAIRED_MEMBERS = 4
-SHIFTS = (0, 1, 2, 3)
 KERNEL_VMEM = 8 * 2**20
 
 
@@ -25,20 +24,6 @@
         return list(range(members))
     me = lax.axis_index("code")
     return [me ^ r for r in (0, *rounds_of(members))]
-
-
-def targets_of(members, direct):
-    if not direct:
-        return list(range(members))
-    me = lax.axis_index("code")
-    return [lax.rem(me + s, members) for s in SHIFTS]
-
-
-def sources_of(members, direct):
-    if not direct:
-        return list(range(members))
-    me = lax.axis_index("code")
-    return [lax.rem(me + members - s, members) for s in SHIFTS]
 
 
 NEXT = (1, 0, 3, 2)
@@ -103,9 +88,8 @@
                 k * members + i,
                 sum(weights[k][j] * jnp.where(alive, column[j], 0.0) for j in range(spans)),
             )
-    for i, c in enumerate(sources_of(members, direct)):
         for j in range(spans):
-            put((2 + j) * members + i, spread(generator_ref[j, c]))
+            put((2 + j) * members + i, spread(column[j]))
     me = lax.axis_index("code")
     targets = range(members)
     if direct:
@@ -157,24 +141,30 @@
         out_ref[:, j * width : (j + 1) * width] = weigh(table_ref, (2 + j) * members, rows)
 
 
-def rebuild_paired_kernel(spans, held_back_by, base_ref, table_ref, *refs):
+def rebuild_paired_kernel(spans, base_ref, table_ref, current_ref, *refs):
     rows, outs = refs[: len(refs) // 2], refs[len(refs) // 2 :]
-    for out_ref, block in zip(outs, rebuilt_for(spans, base_ref, table_ref, [r[...] for r in rows])):
+    blocks = rebuilt_for(spans, base_ref, table_ref, [r[...] for r in rows])
+    for out_ref, block in zip(outs[:-1], blocks):
         out_ref[...] = block
+    outs[-1][0] = blocks[-1]
+    outs[-1][1] = current_ref[...]
 
 
 def finish_kernel(table_ref, earlier_ref, *refs):
-    members = (len(refs) - 2) // 2
-    rows, pieces, (parity_ref, out_ref) = refs[:members], refs[members:-2], refs[-2:]
-    parity_into(parity_ref, table_ref, [r[...] for r in rows])
+    *inputs, parity_ref, out_ref = refs
+    members = len(inputs) // 2 + 1
+    rows, pieces, both_ref = inputs[: members - 1], inputs[members - 1 : -1], inputs[-1]
+    rows = [rows[0][...], both_ref[1], *(r[...] for r in rows[1:])]
+    pieces = [*(p[...] for p in pieces), both_ref[0]]
+    parity_into(parity_ref, table_ref, rows)
     last = table_ref.shape[0] - 1
     lost = table_ref[last : last + 1, :] > 0.5
     arrivals = last - (members - 1) * members
     for c in range(members):
-        block = pieces[0][...]
+        block = pieces[0]
         for r, piece in enumerate(pieces[1:]):
             i = arrivals + r * members + c
-            block = jnp.where(table_ref[i : i + 1, :] > 0.5, piece[...], block)
+            block = jnp.where(table_ref[i : i + 1, :] > 0.5, piece, block)
         out_ref[c] = jnp.where(lost, block, earlier_ref[c])
 
 
@@ -193,13 +183,6 @@
 
 def floats(*shape):
     return jax.ShapeDtypeStruct(shape, jnp.float32)
-
-
-def pass_on(pieces, members):
-    return [
-        lax.ppermute(piece, "code", [(d, (d + s) % members) for d in range(members)])
-        for s, piece in zip(SHIFTS[1:], pieces)
-    ]
 
 
 def trade(pieces, rounds, members):
@@ -251,21 +234,21 @@
         block = floats(own_rows, width)
         own_earlier, *cut_earlier = cut(earlier, order_of(members, True))
         earlier_rows = trade(cut_earlier, rounds, members)
-        current, earlier_rows[-1] = lax.optimization_barrier((current, earlier_rows[-1]))
-        own_current, *cut_current = cut(current, targets_of(members, True))
-        current_rows = [own_current, *pass_on(cut_current, members)]
+        current, table = lax.optimization_barrier((current, table))
+        own_current, next_current, *cut_current = cut(current, order_of(members, True))
+        current_rows = [own_current, *trade(cut_current, rounds[1:], members)]
         outgoing = call(
             functools.partial(rebuild_paired_kernel, spans),
-            [ANYWHERE] + [IN_VMEM] * (members + 2),
-            [block] * members,
-            (current_rows[1], base, table, own_earlier, *earlier_rows),
+            [IN_VMEM] * (members + 3),
+            [block] * (members - 1) + [floats(2, own_rows, width)],
+            (base, table, next_current, own_earlier, *earlier_rows),
             rebuild_cost,
         )
         deliveries = [functools.partial(deliver, w) for w in WAYS]
         incoming = lax.switch(way[0], deliveries, *outgoing[1:])
         new_parity, restored_state = call(
             finish_kernel,
-            [IN_VMEM] * (2 + 2 * members),
+            [IN_VMEM] * (2 * members + 1),
             (parity_shape, floats(*blocks)),
             (table, earlier, *current_rows, outgoing[0], *incoming),
             parity_cost,

time: 27.6 us -> 24 us (0.87)
  the two profiles are of different devices: /device:TPU:0 before, /device:TPU:6 now
where the time goes in v16:
time: 24 us; the launch traced here: 24.4 us
  starting transfers between devices  12.6 us (52%)
  waiting for transfers between devices  6.3 us (26%)
  Pallas kernels  3.04 us (13%)
  between operations  1.41 us (6%)
  local copies, waits for them, and re-layouts  1.07 us (4%)
    ppermute x5, starting transfers between devices, trade(): lax.ppermute(piece, 'code', [(d, d ^ r) for d in range(members)])  8.12 us
    ppermute x3, waiting for transfers between devices, deliver(): lax.ppermute(p, 'code', list(enumerate(t)))  6.29 us
    ppermute x3, starting transfers between devices, deliver(): lax.ppermute(p, 'code', list(enumerate(t)))  4.45 us
    pallas_call x3, Pallas kernels, call(): pl.pallas_call(kernel, in_specs=specs, out_shape=outs, compiler_params=pl...  3.04 us
    squeeze x2, local copies, waits for them, and re-layouts, cut(): lax.dynamic_index_in_dim(blocks, c, 0, keepdims=False)  1.05 us
  transfers between devices with their start and end apart: 8, of which 2 were waited for; matrix products, arithmetic and copies ran while one was open for 0% of the time, Pallas kernels for 5%

profile of v16, /device:TPU:6, one launch (start us, length us, event | category | flops | bytes accessed | tf_op | source)
XLA Modules:
  0.0 24.4 jit_solution(11638617745519563978)
XLA Ops:
  0.6 0.0 copy-start.1
  0.7 0.0 copy-start.5
  0.7 1.0 %dynamic-slice_bitcast_fusion = (f32[32,512]{1,0:T(8,128)S(1)}, f32[32,512]{1,0:T(8,128)S(1)}, f32[32,512]{1,0:T(8,128)S(1)}, f32[32,512]{1,0:T(8,128)S(1)}) fusion(f32[4,32,512]{2,1,0:T(8,128)} %bitcast.22, s32[]{:T(128)S(6)} %select_n.19, s32[]{:T(128)S(6)} %select_n.18, s32[]{:T(128)S(6)} %select_n.20, s32[]{:T(128)S(6)} %select_n.17), kind=kLoop, calls=%fused_computation | loop fusion | bytes 524304 | tf_op jit(solution)/shard_map/jit(dynamic_index_in_dim)/squeeze | solution.py:200
  1.7 3.7 %collective-permute-start.19 = (f32[32,512]{1,0:T(8,128)S(1)}, f32[32,512]{1,0:T(8,128)S(1)}, u32[]{:S(2)}, u32[]{:S(2)}) collective-permute-start(f32[32,512]{1,0:T(8,128)S(1)} %get-tuple-element.75), channel_id=1, source_target_pairs={{0,12},{4,8},{8,4},{12,0},{1,13},{5,9},{9,5},{13,1},{2,14},{6,10},... | collective-permute-start | bytes 196616 | tf_op jit(solution)/shard_map/ppermute | solution.py:190
  5.4 0.0 copy-start.2
  5.4 0.0 collective-permute-start.18
  5.4 0.0 copy-start.3
  5.4 0.0 copy-start.4
  5.4 0.8 %collective-permute-start.17 = (f32[32,512]{1,0:T(8,128)S(1)}, f32[32,512]{1,0:T(8,128)S(1)}, u32[]{:S(2)}, u32[]{:S(2)}) collective-permute-start(f32[32,512]{1,0:T(8,128)S(1)} %get-tuple-element.77), channel_id=1, source_target_pairs={{0,4},{4,0},{8,12},{12,8},{1,5},{5,1},{9,13},{13,9},{2,6},{6,2},{1... | collective-permute-start | bytes 196616 | tf_op jit(solution)/shard_map/ppermute | solution.py:190
  6.2 0.0 copy-done.1
  6.2 0.0 copy-done.2
  6.2 0.0 copy-done.3
  6.2 0.0 copy-done.4
  6.2 1.1 %shard_map.77 = (f32[2,32,512]{2,1,0:T(8,128)S(1)}, f32[41,512]{1,0:T(8,128)S(1)}, s32[1]{0:T(128)}) custom-call(s32[1,2]{1,0:T(1,128)S(1)} %copy-done.4, f32[4,4]{1,0:T(4,128)S(1)} %copy-done.2, s32[136]{0:T(256)S(1)} %copy-done.3, f32[32,2048]{1,0:T(8,128)S(1)} %bitcast.24), custom_call_target="tpu_custom_call" | custom-call | flops 262144 | bytes 477804 | tf_op jit(solution)/shard_map/pallas_call | solution.py:174
  7.3 0.0 copy-done.5
  7.4 3.7 %collective-permute-start.16 = (f32[32,512]{1,0:T(8,128)S(1)}, f32[32,512]{1,0:T(8,128)S(1)}, u32[]{:S(2)}, u32[]{:S(2)}) collective-permute-start(f32[32,512]{1,0:T(8,128)S(1)} %get-tuple-element.80), channel_id=1, source_target_pairs={{0,12},{4,8},{8,4},{12,0},{1,13},{5,9},{9,5},{13,1},{2,14},{6,10},... | collective-permute-start | bytes 196616 | tf_op jit(solution)/shard_map/ppermute | solution.py:190
  11.0 0.0 collective-permute-start.15
  11.7 0.0 collective-permute-done.19.refs_3_
  11.7 0.0 collective-permute-done.18.refs_2_
  11.7 0.0 collective-permute-done.17.refs_1_
  11.7 0.0 copy-start
  11.7 0.1 shard_map.78
  11.8 10.8 %conditional.1 = (f32[32,512]{1,0:T(8,128)}, f32[32,512]{1,0:T(8,128)}, f32[2,32,512]{2,1,0:T(8,128)}) conditional(s32[]{:T(128)} %bitcast.11, (f32[32,512]{1,0:T(8,128)S(1)}, f32[32,512]{1,0:T(8,128)S(1)}, f32[2,32,512]{2,1,0:T(8,128)S(1)}) %tuple.30, (f32[32,512]{1,0:T(8,128)S(1)}, f32[32,512]{1,0:T(8,128)S(1)}, ...), branch_computations={%region_0.1_spmd, %region_1.2_spmd, %region_2.3_spmd, %region_3.4_... | conditional | bytes 1048720 | solution.py:248
  11.8 0.8 %collective-permute-start.14 = (f32[2,32,512]{2,1,0:T(8,128)S(1)}, f32[2,32,512]{2,1,0:T(8,128)}, u32[]{:S(2)}, u32[]{:S(2)}) collective-permute-start(f32[2,32,512]{2,1,0:T(8,128)S(1)} %get-tuple-element.44), channel_id=1, source_target_pairs={{0,4},{4,0},{8,12},{12,8},{1,5},{5,1},{9,13},{13,9},{2,6},{6,2},{1... | collective-permute-start | bytes 393224 | tf_op jit(solution)/shard_map/cond/branch_4_fun/ppermute | solution.py:196
  12.7 3.6 %collective-permute-start.12 = (f32[32,512]{1,0:T(8,128)S(1)}, f32[32,512]{1,0:T(8,128)}, u32[]{:S(2)}, u32[]{:S(2)}) collective-permute-start(f32[32,512]{1,0:T(8,128)S(1)} %get-tuple-element.42), channel_id=1, source_target_pairs={{0,12},{4,8},{8,4},{12,0},{1,13},{5,9},{9,5},{13,1},{2,14},{6,10},... | collective-permute-start | bytes 196616 | tf_op jit(solution)/shard_map/cond/branch_4_fun/ppermute | solution.py:196
  16.3 0.0 collective-permute-start.13
  16.3 4.9 %collective-permute-done.12 = f32[32,512]{1,0:T(8,128)} collective-permute-done((f32[32,512]{1,0:T(8,128)S(1)}, f32[32,512]{1,0:T(8,128)}, u32[]{:S(2)}, u32[]{:S(2)}) %collective-permute-start.12) | collective-permute-done | bytes 65568 | tf_op jit(solution)/shard_map/cond/branch_4_fun/ppermute | solution.py:196
  21.2 1.4 %collective-permute-done.13 = f32[32,512]{1,0:T(8,128)} collective-permute-done((f32[32,512]{1,0:T(8,128)S(1)}, f32[32,512]{1,0:T(8,128)}, u32[]{:S(2)}, u32[]{:S(2)}) %collective-permute-start.13) | collective-permute-done | bytes 65568 | tf_op jit(solution)/shard_map/cond/branch_4_fun/ppermute | solution.py:196
  22.6 0.0 collective-permute-done.14
  22.6 0.0 collective-permute-done.16.refs_2_
  22.6 0.0 collective-permute-done.15.refs_1_
  22.6 0.0 copy-done
  22.6 1.8 %shard_map.79 = (f32[32,2048]{1,0:T(8,128)}, f32[4,32,512]{2,1,0:T(8,128)}) custom-call(f32[41,512]{1,0:T(8,128)S(1)} %get-tuple-element.62.table_ref, f32[4,32,512]{2,1,0:T(8,128)S(1)} %bitcast.23, f32[32,512]{1,0:T(8,128)S(1)} %get-tuple-element.82.refs_0_, f32[32,512]{1,0:T(8,128)S(1)} %collective-permute-done.15.refs_1_, ...), custom_call_target="tpu_custom_call" | custom-call | flops 524288 | bytes 1394688 | tf_op jit(solution)/shard_map/pallas_call | solution.py:174
  (1 shorter events, 0.0 us)
Async XLA Ops:
  0.6 5.5 %copy-start.1 = (f32[1,32,2048]{2,1,0:T(8,128)S(1)}, f32[1,32,2048]{2,1,0:T(8,128)}, u32[]{:S(2)}) copy-start(f32[1,32,2048]{2,1,0:T(8,128)} %param.13) | copy-start | bytes 786436
  0.7 6.7 %copy-start.5 = (f32[1,1,128,512]{3,2,1,0:T(8,128)S(1)}, f32[1,1,128,512]{3,2,1,0:T(8,128)}, u32[]{:S(2)}) copy-start(f32[1,1,128,512]{3,2,1,0:T(8,128)} %param.11) | copy-start | bytes 786436
  1.7 10.0 %collective-permute-start.19 = (f32[32,512]{1,0:T(8,128)S(1)}, f32[32,512]{1,0:T(8,128)S(1)}, u32[]{:S(2)}, u32[]{:S(2)}) collective-permute-start(f32[32,512]{1,0:T(8,128)S(1)} %get-tuple-element.75), channel_id=1, source_target_pairs={{0,12},{4,8},{8,4},{12,0},{1,13},{5,9},{9,5},{13,1},{2,14},{6,10},... | collective-permute-start | bytes 196616 | tf_op jit(solution)/shard_map/ppermute | solution.py:190
  5.4 0.8 %copy-start.2 = (f32[4,4]{1,0:T(4,128)S(1)}, f32[4,4]{1,0:T(4,128)}, u32[]{:S(2)}) copy-start(f32[4,4]{1,0:T(4,128)} %generator_ref.1) | copy-start | bytes 196
  5.4 6.3 %collective-permute-start.18 = (f32[32,512]{1,0:T(8,128)S(1)}, f32[32,512]{1,0:T(8,128)S(1)}, u32[]{:S(2)}, u32[]{:S(2)}) collective-permute-start(f32[32,512]{1,0:T(8,128)S(1)} %get-tuple-element.76), channel_id=1, source_target_pairs={{0,8},{4,12},{8,0},{12,4},{1,9},{5,13},{9,1},{13,5},{2,10},{6,14},... | collective-permute-start | bytes 196616 | tf_op jit(solution)/shard_map/ppermute | solution.py:190
  5.4 0.8 %copy-start.3 = (s32[136]{0:T(256)S(1)}, s32[136]{0:T(256)}, u32[]{:S(2)}) copy-start(s32[136]{0:T(256)} %constant.39.clone.codes_ref) | copy-start | bytes 1636
  5.4 0.8 %copy-start.4 = (s32[1,2]{1,0:T(1,128)S(1)}, s32[1,2]{1,0:T(1,128)}, u32[]{:S(2)}) copy-start(s32[1,2]{1,0:T(1,128)} %ids_ref.1) | copy-start | bytes 28
  5.4 6.3 %collective-permute-start.17 = (f32[32,512]{1,0:T(8,128)S(1)}, f32[32,512]{1,0:T(8,128)S(1)}, u32[]{:S(2)}, u32[]{:S(2)}) collective-permute-start(f32[32,512]{1,0:T(8,128)S(1)} %get-tuple-element.77), channel_id=1, source_target_pairs={{0,4},{4,0},{8,12},{12,8},{1,5},{5,1},{9,13},{13,9},{2,6},{6,2},{1... | collective-permute-start | bytes 196616 | tf_op jit(solution)/shard_map/ppermute | solution.py:190
  7.4 15.2 %collective-permute-start.16 = (f32[32,512]{1,0:T(8,128)S(1)}, f32[32,512]{1,0:T(8,128)S(1)}, u32[]{:S(2)}, u32[]{:S(2)}) collective-permute-start(f32[32,512]{1,0:T(8,128)S(1)} %get-tuple-element.80), channel_id=1, source_target_pairs={{0,12},{4,8},{8,4},{12,0},{1,13},{5,9},{9,5},{13,1},{2,14},{6,10},... | collective-permute-start | bytes 196616 | tf_op jit(solution)/shard_map/ppermute | solution.py:190
  11.0 11.6 %collective-permute-start.15 = (f32[32,512]{1,0:T(8,128)S(1)}, f32[32,512]{1,0:T(8,128)S(1)}, u32[]{:S(2)}, u32[]{:S(2)}) collective-permute-start(f32[32,512]{1,0:T(8,128)S(1)} %get-tuple-element.81), channel_id=1, source_target_pairs={{0,8},{4,12},{8,0},{12,4},{1,9},{5,13},{9,1},{13,5},{2,10},{6,14},... | collective-permute-start | bytes 196616 | tf_op jit(solution)/shard_map/ppermute | solution.py:190
  11.7 10.9 %copy-start = (f32[1,1,128,512]{3,2,1,0:T(8,128)S(1)}, f32[1,1,128,512]{3,2,1,0:T(8,128)}, u32[]{:S(2)}) copy-start(f32[1,1,128,512]{3,2,1,0:T(8,128)} %param.12) | copy-start | bytes 786436
  11.8 10.7 %collective-permute-start.14 = (f32[2,32,512]{2,1,0:T(8,128)S(1)}, f32[2,32,512]{2,1,0:T(8,128)}, u32[]{:S(2)}, u32[]{:S(2)}) collective-permute-start(f32[2,32,512]{2,1,0:T(8,128)S(1)} %get-tuple-element.44), channel_id=1, source_target_pairs={{0,4},{4,0},{8,12},{12,8},{1,5},{5,1},{9,13},{13,9},{2,6},{6,2},{1... | collective-permute-start | bytes 393224 | tf_op jit(solution)/shard_map/cond/branch_4_fun/ppermute | solution.py:196
  12.7 8.5 %collective-permute-start.12 = (f32[32,512]{1,0:T(8,128)S(1)}, f32[32,512]{1,0:T(8,128)}, u32[]{:S(2)}, u32[]{:S(2)}) collective-permute-start(f32[32,512]{1,0:T(8,128)S(1)} %get-tuple-element.42), channel_id=1, source_target_pairs={{0,12},{4,8},{8,4},{12,0},{1,13},{5,9},{9,5},{13,1},{2,14},{6,10},... | collective-permute-start | bytes 196616 | tf_op jit(solution)/shard_map/cond/branch_4_fun/ppermute | solution.py:196
  16.3 6.3 %collective-permute-start.13 = (f32[32,512]{1,0:T(8,128)S(1)}, f32[32,512]{1,0:T(8,128)}, u32[]{:S(2)}, u32[]{:S(2)}) collective-permute-start(f32[32,512]{1,0:T(8,128)S(1)} %get-tuple-element.43), channel_id=1, source_target_pairs={{0,8},{4,12},{8,0},{12,4},{1,9},{5,13},{9,1},{13,5},{2,10},{6,14},... | collective-permute-start | bytes 196616 | tf_op jit(solution)/shard_map/cond/branch_4_fun/ppermute | solution.py:196

commit v17 on v9

--- a/solution.py
+++ b/solution.py
@@ -11,22 +11,36 @@
 IN_SMEM = pl.BlockSpec(memory_space=pltpu.SMEM)
 ANYWHERE = pl.BlockSpec(memory_space=pl.ANY)
 
-DIRECT_MEMBERS = 8
+PAIRED_MEMBERS = 4
 KERNEL_VMEM = 8 * 2**20
 
 
-def rounds_of(members):
-    return range(members - 1, 0, -1)
-
-
-def order_of(members, direct):
-    if not direct:
-        return list(range(members))
+PARTNERS = ((3, 2, 1), (1, 3, 2))
+CURRENT_SHIFTS = ((1, 2, 3), (1, 3, 2))
+REBUILT_SHIFTS = ((1, 2, 3), (1, 3, 2))
+
+
+def chosen(choices):
+    odd = lax.rem(lax.axis_index("rep"), 2)
+    return [jnp.where(odd == 1, b, a) if a != b else a for a, b in zip(*choices)]
+
+
+def partners():
     me = lax.axis_index("code")
-    return [me ^ r for r in (0, *rounds_of(members))]
-
-
-def plan_kernel(direct, ids_ref, generator_ref, parity_ref, base_ref, table_ref):
+    return [me] + [me ^ r for r in chosen(PARTNERS)]
+
+
+def ahead(shifts):
+    me, members = lax.axis_index("code"), lax.axis_size("code")
+    return [me] + [lax.rem(me + s, members) for s in chosen(shifts)]
+
+
+def behind(shifts):
+    me, members = lax.axis_index("code"), lax.axis_size("code")
+    return [me] + [lax.rem(me + members - s, members) for s in chosen(shifts)]
+
+
+def plan_kernel(paired, ids_ref, generator_ref, parity_ref, base_ref, table_ref):
     spans, members = generator_ref.shape
     width = base_ref.shape[2]
     first, second = ids_ref[0, 0], ids_ref[0, 1]
@@ -52,7 +66,11 @@
         base_ref[k] = sum(
             weights[k][j] * parity_ref[:, j * width : (j + 1) * width] for j in range(spans)
         )
-    for i, c in enumerate(order_of(members, direct)):
+    from_earlier = from_current = to_rebuilt = range(members)
+    if paired:
+        from_earlier, from_current = partners(), behind(CURRENT_SHIFTS)
+        to_rebuilt = ahead(REBUILT_SHIFTS)
+    for i, c in enumerate(from_earlier):
         column = [generator_ref[j, c] for j in range(spans)]
         alive = jnp.logical_and(first != c, second != c)
         for k in range(2):
@@ -60,8 +78,10 @@
                 k * members + i,
                 sum(weights[k][j] * jnp.where(alive, column[j], 0.0) for j in range(spans)),
             )
+    for i, c in enumerate(from_current):
         for j in range(spans):
-            put((2 + j) * members + i, spread(column[j]))
+            put((2 + j) * members + i, spread(generator_ref[j, c]))
+    for i, c in enumerate(to_rebuilt):
         put((2 + spans) * members + i, spread(jnp.where(first == c, 1.0, 0.0)))
     me = lax.axis_index("code")
     lost = jnp.logical_or(first == me, second == me)
@@ -118,7 +138,7 @@
     members = len(pieces)
     last = table_ref.shape[0] - 1
     lost = table_ref[last : last + 1, :] > 0.5
-    for c, piece in zip(order_of(members, True), pieces):
+    for c, piece in zip(behind(REBUILT_SHIFTS), pieces):
         out_ref[c] = jnp.where(lost, piece[...], earlier_ref[c])
 
 
@@ -139,16 +159,32 @@
     return jax.ShapeDtypeStruct(shape, jnp.float32)
 
 
-def trade(pieces, rounds, members):
+def permute(pieces, moves, target):
+    members, reps = lax.axis_size("code"), lax.axis_size("rep")
     return [
-        lax.ppermute(piece, "code", [(d, d ^ r) for d in range(members)])
-        for r, piece in zip(rounds, pieces)
+        lax.ppermute(
+            piece,
+            ("code", "rep"),
+            [
+                (d * reps + rep, target(d, moves[rep % 2][i]) * reps + rep)
+                for d in range(members)
+                for rep in range(reps)
+            ],
+        )
+        for i, piece in enumerate(pieces)
     ]
 
 
-def cut(blocks, rounds):
-    me = lax.axis_index("code")
-    return [lax.dynamic_index_in_dim(blocks, me ^ r, 0, keepdims=False) for r in rounds]
+def trade(pieces):
+    return permute(pieces, PARTNERS, lambda d, r: d ^ r)
+
+
+def pass_on(pieces, shifts):
+    return permute(pieces, shifts, lambda d, s: (d + s) % PAIRED_MEMBERS)
+
+
+def cut(blocks, order):
+    return [lax.dynamic_index_in_dim(blocks, c, 0, keepdims=False) for c in order]
 
 
 def local(state_slab, previous_slab, previous_parity, generator, failed_ids):
@@ -160,10 +196,10 @@
     blocks = (members, own_rows, width)
     earlier = previous_slab.reshape(blocks)
     current = state_slab.reshape(blocks)
-    direct = 4 <= members <= DIRECT_MEMBERS and members & (members - 1) == 0
+    paired = members == PAIRED_MEMBERS
 
     base, table = call(
-        functools.partial(plan_kernel, direct),
+        functools.partial(plan_kernel, paired),
         [IN_SMEM, IN_SMEM, IN_VMEM],
         (floats(2, own_rows, width), floats((3 + spans) * members + 1, width)),
         (failed_ids, generator, previous_parity[0]),
@@ -172,12 +208,11 @@
     parity_shape = floats(own_rows, spans * width)
     rebuild_cost = 4 * slab_rows * width
     parity_cost = 2 * spans * slab_rows * width
-    if direct:
-        rounds = list(rounds_of(members))
+    if paired:
         block = floats(own_rows, width)
-        own_earlier, *cut_earlier = cut(earlier, [0] + rounds)
-        earlier_rows = trade(cut_earlier, rounds, members)
-        own_current, *cut_current = cut(current, [0] + rounds)
+        own_earlier, *cut_earlier = cut(earlier, partners())
+        earlier_rows = trade(cut_earlier)
+        own_current, *cut_current = cut(current, ahead(CURRENT_SHIFTS))
         outgoing = call(
             rebuild_paired_kernel,
             [IN_VMEM] * (members + 2),
@@ -185,8 +220,8 @@
             (base, table, own_earlier, *earlier_rows),
             rebuild_cost,
         )
-        incoming = trade(outgoing[1:], rounds, members)
-        current_rows = [own_current, *trade(cut_current, rounds, members)]
+        incoming = pass_on(outgoing[1:], REBUILT_SHIFTS)
+        current_rows = [own_current, *pass_on(cut_current, CURRENT_SHIFTS)]
         new_parity, parity_done = call(
             parity_paired_kernel,
             [IN_VMEM] * (members + 1),

time: 24.5 us -> 26 us (1.061)
  the two profiles are of different devices: /device:TPU:0 before, /device:TPU:1 now
where the time goes in v17:
time: 26 us; the launch traced here: 25.8 us
  starting transfers between devices  11.6 us (45%)
  waiting for transfers between devices  10.2 us (39%)
  Pallas kernels  2.24 us (9%)
  local copies, waits for them, and re-layouts  1.04 us (4%)
  between operations  0.74 us (3%)
    ppermute x9, starting transfers between devices, permute(): lax.ppermute(piece, ('code', 'rep'), [(d * reps + rep, target(d, moves[re...  11.6 us
    ppermute x9, waiting for transfers between devices, permute(): lax.ppermute(piece, ('code', 'rep'), [(d * reps + rep, target(d, moves[re...  10.2 us
    pallas_call x4, Pallas kernels, call(): pl.pallas_call(kernel, in_specs=specs, out_specs=jax.tree.map(lambda _: I...  2.24 us
    squeeze x2, local copies, waits for them, and re-layouts, cut(): lax.dynamic_index_in_dim(blocks, c, 0, keepdims=False)  1.02 us
  transfers between devices with their start and end apart: 9, of which 3 were waited for; matrix products, arithmetic and copies ran while one was open for 0% of the time, Pallas kernels for 6%

profile of v17, /device:TPU:1, one launch (start us, length us, event | category | flops | bytes accessed | tf_op | source)
XLA Modules:
  0.0 25.8 jit_solution(7959144204189423081)
XLA Ops:
  0.7 0.0 copy-start.4
  0.7 1.0 %dynamic-slice_bitcast_fusion = (f32[32,512]{1,0:T(8,128)S(1)}, f32[32,512]{1,0:T(8,128)S(1)}, f32[32,512]{1,0:T(8,128)S(1)}, f32[32,512]{1,0:T(8,128)S(1)}) fusion(f32[4,32,512]{2,1,0:T(8,128)} %bitcast.21, s32[]{:T(128)S(6)} %select_n.47, s32[]{:T(128)S(6)} %select_n.45, s32[]{:T(128)S(6)} %select_n.44, s32[]{:T(128)S(6)} %select_n.37), kind=kLoop, calls=%fused_computation | loop fusion | bytes 524304 | tf_op jit(solution)/shard_map/jit(dynamic_index_in_dim)/squeeze | solution.py:187
  1.7 2.2 %collective-permute-start.3 = (f32[32,512]{1,0:T(8,128)S(1)}, f32[32,512]{1,0:T(8,128)S(1)}, u32[]{:S(2)}, u32[]{:S(2)}) collective-permute-start(f32[32,512]{1,0:T(8,128)S(1)} %get-tuple-element.20), channel_id=1, source_target_pairs={{0,12},{1,5},{2,14},{3,7},{4,8},{5,1},{6,10},{7,3},{8,4},{9,13},{1... | collective-permute-start | bytes 196616 | tf_op jit(solution)/shard_map/ppermute | solution.py:165
  3.9 2.2 %collective-permute-start.4 = (f32[32,512]{1,0:T(8,128)S(1)}, f32[32,512]{1,0:T(8,128)S(1)}, u32[]{:S(2)}, u32[]{:S(2)}) collective-permute-start(f32[32,512]{1,0:T(8,128)S(1)} %get-tuple-element.19), channel_id=1, source_target_pairs={{0,8},{1,13},{2,10},{3,15},{4,12},{5,9},{6,14},{7,11},{8,0},{9,5},... | collective-permute-start | bytes 196616 | tf_op jit(solution)/shard_map/ppermute | solution.py:165
  6.1 0.1 collective-permute-start.5
  6.2 0.0 copy-done.4
  6.2 0.0 copy-start.1
  6.2 0.0 copy-start.2
  6.2 1.3 %collective-permute-start = (f32[32,512]{1,0:T(8,128)S(1)}, f32[32,512]{1,0:T(8,128)S(1)}, u32[]{:S(2)}, u32[]{:S(2)}) collective-permute-start(f32[32,512]{1,0:T(8,128)S(1)} %get-tuple-element.24), channel_id=1, source_target_pairs={{0,4},{1,5},{2,6},{3,7},{4,8},{5,9},{6,10},{7,11},{8,12},{9,13},{1... | collective-permute-start | bytes 196616 | tf_op jit(solution)/shard_map/ppermute | solution.py:165
  7.5 0.0 copy-start.3
  7.5 2.0 %collective-permute-start.1 = (f32[32,512]{1,0:T(8,128)S(1)}, f32[32,512]{1,0:T(8,128)S(1)}, u32[]{:S(2)}, u32[]{:S(2)}) collective-permute-start(f32[32,512]{1,0:T(8,128)S(1)} %get-tuple-element.23), channel_id=1, source_target_pairs={{0,8},{1,13},{2,10},{3,15},{4,12},{5,1},{6,14},{7,3},{8,0},{9,5},{... | collective-permute-start | bytes 196616 | tf_op jit(solution)/shard_map/ppermute | solution.py:165
  9.5 0.0 copy-done.1
  9.5 0.0 copy-done.2
  9.5 0.0 copy-done.3
  9.5 0.7 %shard_map.68 = (f32[2,32,512]{2,1,0:T(8,128)S(1)}, f32[29,512]{1,0:T(8,128)S(1)}) custom-call(s32[1,2]{1,0:T(1,128)S(1)} %copy-done.3, f32[4,4]{1,0:T(4,128)S(1)} %copy-done.2, f32[32,2048]{1,0:T(8,128)S(1)} %bitcast.23), custom_call_target="tpu_custom_call" | custom-call | flops 262144 | bytes 452680 | tf_op jit(solution)/shard_map/pallas_call | solution.py:147
  10.2 0.0 collective-permute-done.3.refs_1_
  10.2 0.5 %collective-permute-start.2 = (f32[32,512]{1,0:T(8,128)S(1)}, f32[32,512]{1,0:T(8,128)S(1)}, u32[]{:S(2)}, u32[]{:S(2)}) collective-permute-start(f32[32,512]{1,0:T(8,128)S(1)} %get-tuple-element.22), channel_id=1, source_target_pairs={{0,12},{1,9},{2,14},{3,11},{4,0},{5,13},{6,2},{7,15},{8,4},{9,1},{... | collective-permute-start | bytes 196616 | tf_op jit(solution)/shard_map/ppermute | solution.py:165
  10.7 0.0 collective-permute-done.4.refs_2_
  10.7 5.1 %collective-permute-done.5.refs_3_ = f32[32,512]{1,0:T(8,128)S(1)} collective-permute-done((f32[32,512]{1,0:T(8,128)S(1)}, f32[32,512]{1,0:T(8,128)S(1)}, u32[]{:S(2)}, u32[]{:S(2)}) %collective-permute-start.5) | collective-permute-done | bytes 65568 | tf_op jit(solution)/shard_map/ppermute | solution.py:165
  15.8 0.1 shard_map.70
  15.9 0.0 copy-start
  15.9 0.1 collective-permute-start.6
  16.0 3.3 %collective-permute-start.7 = (f32[32,512]{1,0:T(8,128)S(1)}, f32[32,512]{1,0:T(8,128)S(1)}, u32[]{:S(2)}, u32[]{:S(2)}) collective-permute-start(f32[32,512]{1,0:T(8,128)S(1)} %get-tuple-element.16), channel_id=1, source_target_pairs={{0,8},{1,13},{2,10},{3,15},{4,12},{5,1},{6,14},{7,3},{8,0},{9,5},{... | collective-permute-start | bytes 196616 | tf_op jit(solution)/shard_map/ppermute | solution.py:165
  19.2 0.0 collective-permute-done.refs_1_
  19.2 0.0 collective-permute-start.8
  19.2 0.0 collective-permute-done.1.refs_2_
  19.2 0.0 collective-permute-done.2.refs_3_
  19.3 0.8 %shard_map.69 = (f32[32,2048]{1,0:T(8,128)}, f32[8,128]{1,0:T(8,128)S(1)}) custom-call(f32[29,512]{1,0:T(8,128)S(1)} %get-tuple-element.10.table_ref, f32[32,512]{1,0:T(8,128)S(1)} %get-tuple-element.25.refs_0_, f32[32,512]{1,0:T(8,128)S(1)} %collective-permute-done.refs_1_, f32[32,512]{1,0:T(8,128)S(1)} %collective-permute-done.1.refs_2_, ...), custom_call_target="tpu_custom_call" | custom-call | flops 524288 | bytes 587776 | tf_op jit(solution)/shard_map/pallas_call | solution.py:147
  20.0 0.9 %collective-permute-done.6.refs_1_ = f32[32,512]{1,0:T(8,128)S(1)} collective-permute-done((f32[32,512]{1,0:T(8,128)S(1)}, f32[32,512]{1,0:T(8,128)S(1)}, u32[]{:S(2)}, u32[]{:S(2)}) %collective-permute-start.6) | collective-permute-done | bytes 65568 | tf_op jit(solution)/shard_map/ppermute | solution.py:165
  21.0 0.0 collective-permute-done.7.refs_2_
  21.0 4.1 %collective-permute-done.8.refs_3_ = f32[32,512]{1,0:T(8,128)S(1)} collective-permute-done((f32[32,512]{1,0:T(8,128)S(1)}, f32[32,512]{1,0:T(8,128)S(1)}, u32[]{:S(2)}, u32[]{:S(2)}) %collective-permute-start.8) | collective-permute-done | bytes 65568 | tf_op jit(solution)/shard_map/ppermute | solution.py:165
  25.1 0.0 copy-done
  25.1 0.7 %shard_map.71 = f32[4,32,512]{2,1,0:T(8,128)} custom-call(f32[29,512]{1,0:T(8,128)S(1)} %get-tuple-element.10.table_ref, f32[4,32,512]{2,1,0:T(8,128)S(1)} %bitcast.22, f32[8,128]{1,0:T(8,128)S(1)} %get-tuple-element.12.held_back_by, f32[32,512]{1,0:T(8,128)S(1)} %get-tuple-element.14.refs_0_, f32[32,512]{1,0:T(8,128)S(1)} %collective-permute-done.6.refs_1_, ...), custom_call_target="tpu_custom_call" | custom-call | bytes 849920 | tf_op jit(solution)/shard_map/pallas_call | solution.py:147
  (1 shorter events, 0.0 us)
Async XLA Ops:
  0.7 5.5 %copy-start.4 = (f32[1,1,128,512]{3,2,1,0:T(8,128)S(1)}, f32[1,1,128,512]{3,2,1,0:T(8,128)}, u32[]{:S(2)}) copy-start(f32[1,1,128,512]{3,2,1,0:T(8,128)} %param.5) | copy-start | bytes 786436
  1.7 8.5 %collective-permute-start.3 = (f32[32,512]{1,0:T(8,128)S(1)}, f32[32,512]{1,0:T(8,128)S(1)}, u32[]{:S(2)}, u32[]{:S(2)}) collective-permute-start(f32[32,512]{1,0:T(8,128)S(1)} %get-tuple-element.20), channel_id=1, source_target_pairs={{0,12},{1,5},{2,14},{3,7},{4,8},{5,1},{6,10},{7,3},{8,4},{9,13},{1... | collective-permute-start | bytes 196616 | tf_op jit(solution)/shard_map/ppermute | solution.py:165
  3.9 6.9 %collective-permute-start.4 = (f32[32,512]{1,0:T(8,128)S(1)}, f32[32,512]{1,0:T(8,128)S(1)}, u32[]{:S(2)}, u32[]{:S(2)}) collective-permute-start(f32[32,512]{1,0:T(8,128)S(1)} %get-tuple-element.19), channel_id=1, source_target_pairs={{0,8},{1,13},{2,10},{3,15},{4,12},{5,9},{6,14},{7,11},{8,0},{9,5},... | collective-permute-start | bytes 196616 | tf_op jit(solution)/shard_map/ppermute | solution.py:165
  6.1 9.8 %collective-permute-start.5 = (f32[32,512]{1,0:T(8,128)S(1)}, f32[32,512]{1,0:T(8,128)S(1)}, u32[]{:S(2)}, u32[]{:S(2)}) collective-permute-start(f32[32,512]{1,0:T(8,128)S(1)} %get-tuple-element.18), channel_id=1, source_target_pairs={{0,4},{1,9},{2,6},{3,11},{4,0},{5,13},{6,2},{7,15},{8,12},{9,1},{1... | collective-permute-start | bytes 196616 | tf_op jit(solution)/shard_map/ppermute | solution.py:165
  6.2 3.4 %copy-start.1 = (f32[1,32,2048]{2,1,0:T(8,128)S(1)}, f32[1,32,2048]{2,1,0:T(8,128)}, u32[]{:S(2)}) copy-start(f32[1,32,2048]{2,1,0:T(8,128)} %param.7) | copy-start | bytes 786436
  6.2 3.3 %copy-start.2 = (f32[4,4]{1,0:T(4,128)S(1)}, f32[4,4]{1,0:T(4,128)}, u32[]{:S(2)}) copy-start(f32[4,4]{1,0:T(4,128)} %generator_ref.1) | copy-start | bytes 196
  6.2 13.0 %collective-permute-start = (f32[32,512]{1,0:T(8,128)S(1)}, f32[32,512]{1,0:T(8,128)S(1)}, u32[]{:S(2)}, u32[]{:S(2)}) collective-permute-start(f32[32,512]{1,0:T(8,128)S(1)} %get-tuple-element.24), channel_id=1, source_target_pairs={{0,4},{1,5},{2,6},{3,7},{4,8},{5,9},{6,10},{7,11},{8,12},{9,13},{1... | collective-permute-start | bytes 196616 | tf_op jit(solution)/shard_map/ppermute | solution.py:165
  7.5 2.0 %copy-start.3 = (s32[1,2]{1,0:T(1,128)S(1)}, s32[1,2]{1,0:T(1,128)}, u32[]{:S(2)}) copy-start(s32[1,2]{1,0:T(1,128)} %ids_ref.1) | copy-start | bytes 28
  7.5 11.7 %collective-permute-start.1 = (f32[32,512]{1,0:T(8,128)S(1)}, f32[32,512]{1,0:T(8,128)S(1)}, u32[]{:S(2)}, u32[]{:S(2)}) collective-permute-start(f32[32,512]{1,0:T(8,128)S(1)} %get-tuple-element.23), channel_id=1, source_target_pairs={{0,8},{1,13},{2,10},{3,15},{4,12},{5,1},{6,14},{7,3},{8,0},{9,5},{... | collective-permute-start | bytes 196616 | tf_op jit(solution)/shard_map/ppermute | solution.py:165
  10.2 9.0 %collective-permute-start.2 = (f32[32,512]{1,0:T(8,128)S(1)}, f32[32,512]{1,0:T(8,128)S(1)}, u32[]{:S(2)}, u32[]{:S(2)}) collective-permute-start(f32[32,512]{1,0:T(8,128)S(1)} %get-tuple-element.22), channel_id=1, source_target_pairs={{0,12},{1,9},{2,14},{3,11},{4,0},{5,13},{6,2},{7,15},{8,4},{9,1},{... | collective-permute-start | bytes 196616 | tf_op jit(solution)/shard_map/ppermute | solution.py:165
  15.9 9.2 %copy-start = (f32[1,1,128,512]{3,2,1,0:T(8,128)S(1)}, f32[1,1,128,512]{3,2,1,0:T(8,128)}, u32[]{:S(2)}) copy-start(f32[1,1,128,512]{3,2,1,0:T(8,128)} %param.6) | copy-start | bytes 786436
  15.9 5.0 %collective-permute-start.6 = (f32[32,512]{1,0:T(8,128)S(1)}, f32[32,512]{1,0:T(8,128)S(1)}, u32[]{:S(2)}, u32[]{:S(2)}) collective-permute-start(f32[32,512]{1,0:T(8,128)S(1)} %get-tuple-element.15), channel_id=1, source_target_pairs={{0,4},{1,5},{2,6},{3,7},{4,8},{5,9},{6,10},{7,11},{8,12},{9,13},{1... | collective-permute-start | bytes 196616 | tf_op jit(solution)/shard_map/ppermute | solution.py:165
  16.0 5.0 %collective-permute-start.7 = (f32[32,512]{1,0:T(8,128)S(1)}, f32[32,512]{1,0:T(8,128)S(1)}, u32[]{:S(2)}, u32[]{:S(2)}) collective-permute-start(f32[32,512]{1,0:T(8,128)S(1)} %get-tuple-element.16), channel_id=1, source_target_pairs={{0,8},{1,13},{2,10},{3,15},{4,12},{5,1},{6,14},{7,3},{8,0},{9,5},{... | collective-permute-start | bytes 196616 | tf_op jit(solution)/shard_map/ppermute | solution.py:165
  19.2 5.9 %collective-permute-start.8 = (f32[32,512]{1,0:T(8,128)S(1)}, f32[32,512]{1,0:T(8,128)S(1)}, u32[]{:S(2)}, u32[]{:S(2)}) collective-permute-start(f32[32,512]{1,0:T(8,128)S(1)} %get-tuple-element.17), channel_id=1, source_target_pairs={{0,12},{1,9},{2,14},{3,11},{4,0},{5,13},{6,2},{7,15},{8,4},{9,1},{... | collective-permute-start | bytes 196616 | tf_op jit(solution)/shard_map/ppermute | solution.py:165

commit v18 on v11

--- a/solution.py
+++ b/solution.py
@@ -16,7 +16,8 @@
 
 
 def rounds_of(members):
-    return range(members - 1, 0, -1)
+    half = members // 2
+    return [half] + [r for r in range(members - 1, 0, -1) if r != half]
 
 
 def order_of(members, direct):

time: 23.6 us -> 23.4 us (level)
  waiting for transfers between devices: 4.37 us -> 2.79 us
  starting transfers between devices: 15 us -> 16.4 us
    ppermute x6, starting transfers between devices: 9.28 us -> 10.8 us  [pass_on(): lax.ppermute(piece, 'code', [(d, (d + s) % members) for d in range(member...]
    ppermute x3, waiting for transfers between devices: 1.26 us -> 0.01 us  [trade(): lax.ppermute(piece, 'code', [(d, d ^ r) for d in range(members)])]
    ppermute x6, waiting for transfers between devices: 3.11 us -> 2.78 us  [pass_on(): lax.ppermute(piece, 'code', [(d, (d + s) % members) for d in range(member...]
  transfers between devices with their start and end apart: 9 -> 9, of which waited for: 3 -> 2; matrix products, arithmetic and copies ran while one was open for 0% -> 0% of each run, Pallas kernels for 6% -> 6%
where the time goes in v18:
time: 23.4 us; the launch traced here: 23.2 us
  starting transfers between devices  16.4 us (70%)
  waiting for transfers between devices  2.79 us (12%)
  Pallas kernels  2.24 us (10%)
  local copies, waits for them, and re-layouts  1.04 us (4%)
  between operations  0.72 us (3%)
    ppermute x6, starting transfers between devices, pass_on(): lax.ppermute(piece, 'code', [(d, (d + s) % members) for d in range(member...  10.8 us
    ppermute x3, starting transfers between devices, trade(): lax.ppermute(piece, 'code', [(d, d ^ r) for d in range(members)])  5.68 us
    ppermute x6, waiting for transfers between devices, pass_on(): lax.ppermute(piece, 'code', [(d, (d + s) % members) for d in range(member...  2.78 us
    pallas_call x4, Pallas kernels, call(): pl.pallas_call(kernel, in_specs=specs, out_specs=jax.tree.map(lambda _: I...  2.24 us
    squeeze x2, local copies, waits for them, and re-layouts, cut(): lax.dynamic_index_in_dim(blocks, c, 0, keepdims=False)  1.02 us
  transfers between devices with their start and end apart: 9, of which 2 were waited for; matrix products, arithmetic and copies ran while one was open for 0% of the time, Pallas kernels for 6%

profile of v18, /device:TPU:0, one launch (start us, length us, event | category | flops | bytes accessed | tf_op | source)
XLA Modules:
  0.0 23.2 jit_solution(15451590448053306340)
XLA Ops:
  0.6 0.0 copy-start.4
  0.7 1.0 %dynamic-slice_bitcast_fusion = (f32[32,512]{1,0:T(8,128)S(1)}, f32[32,512]{1,0:T(8,128)S(1)}, f32[32,512]{1,0:T(8,128)S(1)}, f32[32,512]{1,0:T(8,128)S(1)}) fusion(f32[4,32,512]{2,1,0:T(8,128)} %bitcast.21, s32[]{:T(128)S(6)} %select_n.32, s32[]{:T(128)S(6)} %select_n.31, s32[]{:T(128)S(6)} %select_n.30, s32[]{:T(128)S(6)} %select_n.29), kind=kLoop, calls=%fused_computation | loop fusion | bytes 524304 | tf_op jit(solution)/shard_map/jit(dynamic_index_in_dim)/squeeze | solution.py:174
  1.7 4.1 %collective-permute-start.3 = (f32[32,512]{1,0:T(8,128)S(1)}, f32[32,512]{1,0:T(8,128)S(1)}, u32[]{:S(2)}, u32[]{:S(2)}) collective-permute-start(f32[32,512]{1,0:T(8,128)S(1)} %get-tuple-element.20), channel_id=1, source_target_pairs={{0,8},{4,12},{8,0},{12,4},{1,9},{5,13},{9,1},{13,5},{2,10},{6,14},... | collective-permute-start | bytes 196616 | tf_op jit(solution)/shard_map/ppermute | solution.py:168
  5.8 1.3 %collective-permute-start.4 = (f32[32,512]{1,0:T(8,128)S(1)}, f32[32,512]{1,0:T(8,128)S(1)}, u32[]{:S(2)}, u32[]{:S(2)}) collective-permute-start(f32[32,512]{1,0:T(8,128)S(1)} %get-tuple-element.19), channel_id=1, source_target_pairs={{0,12},{4,8},{8,4},{12,0},{1,13},{5,9},{9,5},{13,1},{2,14},{6,10},... | collective-permute-start | bytes 196616 | tf_op jit(solution)/shard_map/ppermute | solution.py:168
  7.1 0.2 collective-permute-start.5
  7.3 0.0 copy-done.4
  7.3 0.0 copy-start.1
  7.4 0.0 copy-start.2
  7.4 1.8 %collective-permute-start = (f32[32,512]{1,0:T(8,128)S(1)}, f32[32,512]{1,0:T(8,128)S(1)}, u32[]{:S(2)}, u32[]{:S(2)}) collective-permute-start(f32[32,512]{1,0:T(8,128)S(1)} %get-tuple-element.24), channel_id=1, source_target_pairs={{0,4},{4,8},{8,12},{12,0},{1,5},{5,9},{9,13},{13,1},{2,6},{6,10},{... | collective-permute-start | bytes 196616 | tf_op jit(solution)/shard_map/ppermute | solution.py:161
  9.2 0.0 copy-start.3
  9.2 1.7 %collective-permute-start.1 = (f32[32,512]{1,0:T(8,128)S(1)}, f32[32,512]{1,0:T(8,128)S(1)}, u32[]{:S(2)}, u32[]{:S(2)}) collective-permute-start(f32[32,512]{1,0:T(8,128)S(1)} %get-tuple-element.23), channel_id=1, source_target_pairs={{0,8},{4,12},{8,0},{12,4},{1,9},{5,13},{9,1},{13,5},{2,10},{6,14},... | collective-permute-start | bytes 196616 | tf_op jit(solution)/shard_map/ppermute | solution.py:161
  10.9 0.0 copy-done.1
  10.9 0.0 copy-done.2
  10.9 0.0 copy-done.3
  10.9 0.7 %shard_map.68 = (f32[2,32,512]{2,1,0:T(8,128)S(1)}, f32[29,512]{1,0:T(8,128)S(1)}) custom-call(s32[1,2]{1,0:T(1,128)S(1)} %copy-done.3, f32[4,4]{1,0:T(4,128)S(1)} %copy-done.2, f32[32,2048]{1,0:T(8,128)S(1)} %bitcast.23), custom_call_target="tpu_custom_call" | custom-call | flops 262144 | bytes 452680 | tf_op jit(solution)/shard_map/pallas_call | solution.py:144
  11.6 0.0 collective-permute-done.3.refs_1_
  11.6 3.0 %collective-permute-start.2 = (f32[32,512]{1,0:T(8,128)S(1)}, f32[32,512]{1,0:T(8,128)S(1)}, u32[]{:S(2)}, u32[]{:S(2)}) collective-permute-start(f32[32,512]{1,0:T(8,128)S(1)} %get-tuple-element.22), channel_id=1, source_target_pairs={{0,12},{4,0},{8,4},{12,8},{1,13},{5,1},{9,5},{13,9},{2,14},{6,2},{... | collective-permute-start | bytes 196616 | tf_op jit(solution)/shard_map/ppermute | solution.py:161
  14.7 0.0 collective-permute-done.4.refs_2_
  14.7 0.0 collective-permute-done.5.refs_3_
  14.7 0.1 shard_map.70
  14.7 0.0 copy-start
  14.7 0.1 collective-permute-start.6
  14.8 1.7 %collective-permute-start.7 = (f32[32,512]{1,0:T(8,128)S(1)}, f32[32,512]{1,0:T(8,128)S(1)}, u32[]{:S(2)}, u32[]{:S(2)}) collective-permute-start(f32[32,512]{1,0:T(8,128)S(1)} %get-tuple-element.16), channel_id=1, source_target_pairs={{0,8},{4,12},{8,0},{12,4},{1,9},{5,13},{9,1},{13,5},{2,10},{6,14},... | collective-permute-start | bytes 196616 | tf_op jit(solution)/shard_map/ppermute | solution.py:161
  16.5 0.0 collective-permute-done.refs_1_
  16.5 2.5 %collective-permute-start.8 = (f32[32,512]{1,0:T(8,128)S(1)}, f32[32,512]{1,0:T(8,128)S(1)}, u32[]{:S(2)}, u32[]{:S(2)}) collective-permute-start(f32[32,512]{1,0:T(8,128)S(1)} %get-tuple-element.17), channel_id=1, source_target_pairs={{0,12},{4,0},{8,4},{12,8},{1,13},{5,1},{9,5},{13,9},{2,14},{6,2},{... | collective-permute-start | bytes 196616 | tf_op jit(solution)/shard_map/ppermute | solution.py:161
  18.9 0.0 collective-permute-done.1.refs_2_
  18.9 0.0 collective-permute-done.2.refs_3_
  18.9 0.8 %shard_map.69 = (f32[32,2048]{1,0:T(8,128)}, f32[8,128]{1,0:T(8,128)S(1)}) custom-call(f32[29,512]{1,0:T(8,128)S(1)} %get-tuple-element.10.table_ref, f32[32,512]{1,0:T(8,128)S(1)} %get-tuple-element.25.refs_0_, f32[32,512]{1,0:T(8,128)S(1)} %collective-permute-done.refs_1_, f32[32,512]{1,0:T(8,128)S(1)} %collective-permute-done.1.refs_2_, ...), custom_call_target="tpu_custom_call" | custom-call | flops 524288 | bytes 587776 | tf_op jit(solution)/shard_map/pallas_call | solution.py:144
  19.7 1.4 %collective-permute-done.6.refs_1_ = f32[32,512]{1,0:T(8,128)S(1)} collective-permute-done((f32[32,512]{1,0:T(8,128)S(1)}, f32[32,512]{1,0:T(8,128)S(1)}, u32[]{:S(2)}, u32[]{:S(2)}) %collective-permute-start.6) | collective-permute-done | bytes 65568 | tf_op jit(solution)/shard_map/ppermute | solution.py:161
  21.1 1.4 %collective-permute-done.7.refs_2_ = f32[32,512]{1,0:T(8,128)S(1)} collective-permute-done((f32[32,512]{1,0:T(8,128)S(1)}, f32[32,512]{1,0:T(8,128)S(1)}, u32[]{:S(2)}, u32[]{:S(2)}) %collective-permute-start.7) | collective-permute-done | bytes 65568 | tf_op jit(solution)/shard_map/ppermute | solution.py:161
  22.5 0.0 collective-permute-done.8.refs_3_
  22.5 0.0 copy-done
  22.5 0.7 %shard_map.71 = f32[4,32,512]{2,1,0:T(8,128)} custom-call(f32[29,512]{1,0:T(8,128)S(1)} %get-tuple-element.10.table_ref, f32[4,32,512]{2,1,0:T(8,128)S(1)} %bitcast.22, f32[8,128]{1,0:T(8,128)S(1)} %get-tuple-element.12.held_back_by, f32[32,512]{1,0:T(8,128)S(1)} %get-tuple-element.14.refs_0_, f32[32,512]{1,0:T(8,128)S(1)} %collective-permute-done.6.refs_1_, ...), custom_call_target="tpu_custom_call" | custom-call | bytes 849920 | tf_op jit(solution)/shard_map/pallas_call | solution.py:144
  (1 shorter events, 0.0 us)
Async XLA Ops:
  0.6 6.7 %copy-start.4 = (f32[1,1,128,512]{3,2,1,0:T(8,128)S(1)}, f32[1,1,128,512]{3,2,1,0:T(8,128)}, u32[]{:S(2)}) copy-start(f32[1,1,128,512]{3,2,1,0:T(8,128)} %param.5) | copy-start | bytes 786436
  1.7 9.9 %collective-permute-start.3 = (f32[32,512]{1,0:T(8,128)S(1)}, f32[32,512]{1,0:T(8,128)S(1)}, u32[]{:S(2)}, u32[]{:S(2)}) collective-permute-start(f32[32,512]{1,0:T(8,128)S(1)} %get-tuple-element.20), channel_id=1, source_target_pairs={{0,8},{4,12},{8,0},{12,4},{1,9},{5,13},{9,1},{13,5},{2,10},{6,14},... | collective-permute-start | bytes 196616 | tf_op jit(solution)/shard_map/ppermute | solution.py:168
  5.8 8.9 %collective-permute-start.4 = (f32[32,512]{1,0:T(8,128)S(1)}, f32[32,512]{1,0:T(8,128)S(1)}, u32[]{:S(2)}, u32[]{:S(2)}) collective-permute-start(f32[32,512]{1,0:T(8,128)S(1)} %get-tuple-element.19), channel_id=1, source_target_pairs={{0,12},{4,8},{8,4},{12,0},{1,13},{5,9},{9,5},{13,1},{2,14},{6,10},... | collective-permute-start | bytes 196616 | tf_op jit(solution)/shard_map/ppermute | solution.py:168
  7.1 7.5 %collective-permute-start.5 = (f32[32,512]{1,0:T(8,128)S(1)}, f32[32,512]{1,0:T(8,128)S(1)}, u32[]{:S(2)}, u32[]{:S(2)}) collective-permute-start(f32[32,512]{1,0:T(8,128)S(1)} %get-tuple-element.18), channel_id=1, source_target_pairs={{0,4},{4,0},{8,12},{12,8},{1,5},{5,1},{9,13},{13,9},{2,6},{6,2},{1... | collective-permute-start | bytes 196616 | tf_op jit(solution)/shard_map/ppermute | solution.py:168
  7.3 3.6 %copy-start.1 = (f32[1,32,2048]{2,1,0:T(8,128)S(1)}, f32[1,32,2048]{2,1,0:T(8,128)}, u32[]{:S(2)}) copy-start(f32[1,32,2048]{2,1,0:T(8,128)} %param.7) | copy-start | bytes 786436
  7.4 3.6 %copy-start.2 = (f32[4,4]{1,0:T(4,128)S(1)}, f32[4,4]{1,0:T(4,128)}, u32[]{:S(2)}) copy-start(f32[4,4]{1,0:T(4,128)} %generator_ref.1) | copy-start | bytes 196
  7.4 9.1 %collective-permute-start = (f32[32,512]{1,0:T(8,128)S(1)}, f32[32,512]{1,0:T(8,128)S(1)}, u32[]{:S(2)}, u32[]{:S(2)}) collective-permute-start(f32[32,512]{1,0:T(8,128)S(1)} %get-tuple-element.24), channel_id=1, source_target_pairs={{0,4},{4,8},{8,12},{12,0},{1,5},{5,9},{9,13},{13,1},{2,6},{6,10},{... | collective-permute-start | bytes 196616 | tf_op jit(solution)/shard_map/ppermute | solution.py:161
  9.2 1.7 %copy-start.3 = (s32[1,2]{1,0:T(1,128)S(1)}, s32[1,2]{1,0:T(1,128)}, u32[]{:S(2)}) copy-start(s32[1,2]{1,0:T(1,128)} %ids_ref.1) | copy-start | bytes 28
  9.2 9.7 %collective-permute-start.1 = (f32[32,512]{1,0:T(8,128)S(1)}, f32[32,512]{1,0:T(8,128)S(1)}, u32[]{:S(2)}, u32[]{:S(2)}) collective-permute-start(f32[32,512]{1,0:T(8,128)S(1)} %get-tuple-element.23), channel_id=1, source_target_pairs={{0,8},{4,12},{8,0},{12,4},{1,9},{5,13},{9,1},{13,5},{2,10},{6,14},... | collective-permute-start | bytes 196616 | tf_op jit(solution)/shard_map/ppermute | solution.py:161
  11.6 7.3 %collective-permute-start.2 = (f32[32,512]{1,0:T(8,128)S(1)}, f32[32,512]{1,0:T(8,128)S(1)}, u32[]{:S(2)}, u32[]{:S(2)}) collective-permute-start(f32[32,512]{1,0:T(8,128)S(1)} %get-tuple-element.22), channel_id=1, source_target_pairs={{0,12},{4,0},{8,4},{12,8},{1,13},{5,1},{9,5},{13,9},{2,14},{6,2},{... | collective-permute-start | bytes 196616 | tf_op jit(solution)/shard_map/ppermute | solution.py:161
  14.7 7.8 %copy-start = (f32[1,1,128,512]{3,2,1,0:T(8,128)S(1)}, f32[1,1,128,512]{3,2,1,0:T(8,128)}, u32[]{:S(2)}) copy-start(f32[1,1,128,512]{3,2,1,0:T(8,128)} %param.6) | copy-start | bytes 786436
  14.7 6.4 %collective-permute-start.6 = (f32[32,512]{1,0:T(8,128)S(1)}, f32[32,512]{1,0:T(8,128)S(1)}, u32[]{:S(2)}, u32[]{:S(2)}) collective-permute-start(f32[32,512]{1,0:T(8,128)S(1)} %get-tuple-element.15), channel_id=1, source_target_pairs={{0,4},{4,8},{8,12},{12,0},{1,5},{5,9},{9,13},{13,1},{2,6},{6,10},{... | collective-permute-start | bytes 196616 | tf_op jit(solution)/shard_map/ppermute | solution.py:161
  14.8 7.7 %collective-permute-start.7 = (f32[32,512]{1,0:T(8,128)S(1)}, f32[32,512]{1,0:T(8,128)S(1)}, u32[]{:S(2)}, u32[]{:S(2)}) collective-permute-start(f32[32,512]{1,0:T(8,128)S(1)} %get-tuple-element.16), channel_id=1, source_target_pairs={{0,8},{4,12},{8,0},{12,4},{1,9},{5,13},{9,1},{13,5},{2,10},{6,14},... | collective-permute-start | bytes 196616 | tf_op jit(solution)/shard_map/ppermute | solution.py:161
  16.5 6.0 %collective-permute-start.8 = (f32[32,512]{1,0:T(8,128)S(1)}, f32[32,512]{1,0:T(8,128)S(1)}, u32[]{:S(2)}, u32[]{:S(2)}) collective-permute-start(f32[32,512]{1,0:T(8,128)S(1)} %get-tuple-element.17), channel_id=1, source_target_pairs={{0,12},{4,0},{8,4},{12,8},{1,13},{5,1},{9,5},{13,9},{2,14},{6,2},{... | collective-permute-start | bytes 196616 | tf_op jit(solution)/shard_map/ppermute | solution.py:161

commit v19 on v18

--- a/solution.py
+++ b/solution.py
@@ -17,7 +17,7 @@
 
 def rounds_of(members):
     half = members // 2
-    return [half] + [r for r in range(members - 1, 0, -1) if r != half]
+    return [half] + [r for r in range(1, members) if r != half]
 
 
 def order_of(members, direct):
@@ -27,18 +27,23 @@
     return [me ^ r for r in (0, *rounds_of(members))]
 
 
-def targets_of(members, direct):
+def shifts_of(members, rebuilt):
+    others = list(range(1, members))
+    return [0] + (others if rebuilt else others[::-1])
+
+
+def targets_of(members, direct, rebuilt):
     if not direct:
         return list(range(members))
     me = lax.axis_index("code")
-    return [lax.rem(me + s, members) for s in range(members)]
-
-
-def sources_of(members, direct):
+    return [lax.rem(me + s, members) for s in shifts_of(members, rebuilt)]
+
+
+def sources_of(members, direct, rebuilt):
     if not direct:
         return list(range(members))
     me = lax.axis_index("code")
-    return [lax.rem(me + members - s, members) for s in range(members)]
+    return [lax.rem(me + members - s, members) for s in shifts_of(members, rebuilt)]
 
 
 def plan_kernel(direct, ids_ref, generator_ref, parity_ref, base_ref, table_ref):
@@ -75,10 +80,10 @@
                 k * members + i,
                 sum(weights[k][j] * jnp.where(alive, column[j], 0.0) for j in range(spans)),
             )
-    for i, c in enumerate(sources_of(members, direct)):
+    for i, c in enumerate(sources_of(members, direct, False)):
         for j in range(spans):
             put((2 + j) * members + i, spread(generator_ref[j, c]))
-    for i, c in enumerate(targets_of(members, direct)):
+    for i, c in enumerate(targets_of(members, direct, True)):
         put((2 + spans) * members + i, spread(jnp.where(first == c, 1.0, 0.0)))
     me = lax.axis_index("code")
     lost = jnp.logical_or(first == me, second == me)
@@ -135,7 +140,7 @@
     members = len(pieces)
     last = table_ref.shape[0] - 1
     lost = table_ref[last : last + 1, :] > 0.5
-    for c, piece in zip(sources_of(members, True), pieces):
+    for c, piece in zip(sources_of(members, True, True), pieces):
         out_ref[c] = jnp.where(lost, piece[...], earlier_ref[c])
 
 
@@ -156,10 +161,10 @@
     return jax.ShapeDtypeStruct(shape, jnp.float32)
 
 
-def pass_on(pieces, members):
+def pass_on(pieces, members, rebuilt):
     return [
         lax.ppermute(piece, "code", [(d, (d + s) % members) for d in range(members)])
-        for s, piece in enumerate(pieces, 1)
+        for s, piece in zip(shifts_of(members, rebuilt)[1:], pieces)
     ]
 
 
@@ -198,9 +203,13 @@
     if direct:
         rounds = list(rounds_of(members))
         block = floats(own_rows, width)
-        own_earlier, *cut_earlier = cut(earlier, order_of(members, True))
+        own, lead, *rest = order_of(members, True)
+        (lead_block,) = cut(earlier, [lead])
+        later, lead_block = lax.optimization_barrier((earlier, lead_block))
+        own_earlier, *cut_earlier = cut(later, [own] + rest)
+        cut_earlier = [lead_block, *cut_earlier]
         earlier_rows = trade(cut_earlier, rounds, members)
-        own_current, *cut_current = cut(current, targets_of(members, True))
+        own_current, *cut_current = cut(current, targets_of(members, True, False))
         outgoing = call(
             rebuild_paired_kernel,
             [IN_VMEM] * (members + 2),
@@ -208,8 +217,8 @@
             (base, table, own_earlier, *earlier_rows),
             rebuild_cost,
         )
-        incoming = pass_on(outgoing[1:], members)
-        current_rows = [own_current, *pass_on(cut_current, members)]
+        incoming = pass_on(outgoing[1:], members, True)
+        current_rows = [own_current, *pass_on(cut_current, members, False)]
         new_parity, parity_done = call(
             parity_paired_kernel,
             [IN_VMEM] * (members + 1),

time: 23.4 us -> 24 us (1.026)
  starting transfers between devices: 16.4 us -> 15.4 us
  waiting for transfers between devices: 2.79 us -> 3.63 us
  local copies, waits for them, and re-layouts: 1.04 us -> 1.81 us
    ppermute x6, starting transfers between devices: 10.8 us -> 9.69 us  [pass_on(): lax.ppermute(piece, 'code', [(d, (d + s) % members) for d in range(member...]
    ppermute x6, waiting for transfers between devices: 2.78 us -> 3.62 us  [pass_on(): lax.ppermute(piece, 'code', [(d, (d + s) % members) for d in range(member...]
    squeeze x2 -> x3, local copies, waits for them, and re-layouts: 1.02 us -> 1.78 us  [cut(): lax.dynamic_index_in_dim(blocks, c, 0, keepdims=False)]
  transfers between devices with their start and end apart: 9 -> 9, of which waited for: 2 -> 2; matrix products, arithmetic and copies ran while one was open for 0% -> 4% of each run, Pallas kernels for 6% -> 6%
where the time goes in v19:
time: 24 us; the launch traced here: 23.8 us
  starting transfers between devices  15.4 us (64%)
  waiting for transfers between devices  3.63 us (15%)
  Pallas kernels  2.23 us (9%)
  local copies, waits for them, and re-layouts  1.81 us (8%)
  between operations  0.7 us (3%)
    ppermute x6, starting transfers between devices, pass_on(): lax.ppermute(piece, 'code', [(d, (d + s) % members) for d in range(member...  9.69 us
    ppermute x3, starting transfers between devices, trade(): lax.ppermute(piece, 'code', [(d, d ^ r) for d in range(members)])  5.76 us
    ppermute x6, waiting for transfers between devices, pass_on(): lax.ppermute(piece, 'code', [(d, (d + s) % members) for d in range(member...  3.62 us
    pallas_call x4, Pallas kernels, call(): pl.pallas_call(kernel, in_specs=specs, out_specs=jax.tree.map(lambda _: I...  2.23 us
    squeeze x3, local copies, waits for them, and re-layouts, cut(): lax.dynamic_index_in_dim(blocks, c, 0, keepdims=False)  1.78 us
  transfers between devices with their start and end apart: 9, of which 2 were waited for; matrix products, arithmetic and copies ran while one was open for 4% of the time, Pallas kernels for 6%

profile of v19, /device:TPU:0, one launch (start us, length us, event | category | flops | bytes accessed | tf_op | source)
XLA Modules:
  0.0 23.8 jit_solution(16456074417015157119)
XLA Ops:
  0.6 0.8 %dynamic-slice_bitcast_fusion.3 = f32[32,512]{1,0:T(8,128)S(1)} fusion(f32[4,32,512]{2,1,0:T(8,128)} %bitcast.21, s32[]{:T(128)S(6)} %select_n.29), kind=kLoop, calls=%fused_computation.3 | loop fusion | bytes 131076 | tf_op jit(solution)/shard_map/jit(dynamic_index_in_dim)/squeeze | solution.py:179
  1.5 0.0 copy-start.4
  1.5 4.0 %collective-permute-start.3 = (f32[32,512]{1,0:T(8,128)S(1)}, f32[32,512]{1,0:T(8,128)S(1)}, u32[]{:S(2)}, u32[]{:S(2)}) collective-permute-start(f32[32,512]{1,0:T(8,128)S(1)} %dynamic-slice_bitcast_fusion.3), channel_id=1, source_target_pairs={{0,8},{4,12},{8,0},{12,4},{1,9},{5,13},{9,1},{13,5},{2,10},{6,14},... | collective-permute-start | bytes 196616 | tf_op jit(solution)/shard_map/ppermute | solution.py:173
  5.5 0.9 %dynamic-slice_bitcast_fusion = (f32[32,512]{1,0:T(8,128)S(1)}, f32[32,512]{1,0:T(8,128)S(1)}, f32[32,512]{1,0:T(8,128)S(1)}) fusion(f32[4,32,512]{2,1,0:T(8,128)} %bitcast.22, s32[]{:T(128)S(6)} %select_n.32, s32[]{:T(128)S(6)} %select_n.31, s32[]{:T(128)S(6)} %select_n.30), kind=kLoop, calls=%fused_computation | loop fusion | bytes 393228 | tf_op jit(solution)/shard_map/jit(dynamic_index_in_dim)/squeeze | solution.py:179
  6.4 1.4 %collective-permute-start.5 = (f32[32,512]{1,0:T(8,128)S(1)}, f32[32,512]{1,0:T(8,128)S(1)}, u32[]{:S(2)}, u32[]{:S(2)}) collective-permute-start(f32[32,512]{1,0:T(8,128)S(1)} %get-tuple-element.22), channel_id=1, source_target_pairs={{0,12},{4,8},{8,4},{12,0},{1,13},{5,9},{9,5},{13,1},{2,14},{6,10},... | collective-permute-start | bytes 196616 | tf_op jit(solution)/shard_map/ppermute | solution.py:173
  7.9 0.3 %collective-permute-start.4 = (f32[32,512]{1,0:T(8,128)S(1)}, f32[32,512]{1,0:T(8,128)S(1)}, u32[]{:S(2)}, u32[]{:S(2)}) collective-permute-start(f32[32,512]{1,0:T(8,128)S(1)} %get-tuple-element.23), channel_id=1, source_target_pairs={{0,4},{4,0},{8,12},{12,8},{1,5},{5,1},{9,13},{13,9},{2,6},{6,2},{1... | collective-permute-start | bytes 196616 | tf_op jit(solution)/shard_map/ppermute | solution.py:173
  8.2 0.0 copy-done.4
  8.2 0.0 copy-start.1
  8.2 0.0 copy-start.2
  8.2 1.8 %collective-permute-start.2 = (f32[32,512]{1,0:T(8,128)S(1)}, f32[32,512]{1,0:T(8,128)S(1)}, u32[]{:S(2)}, u32[]{:S(2)}) collective-permute-start(f32[32,512]{1,0:T(8,128)S(1)} %get-tuple-element.25), channel_id=1, source_target_pairs={{0,4},{4,8},{8,12},{12,0},{1,5},{5,9},{9,13},{13,1},{2,6},{6,10},{... | collective-permute-start | bytes 196616 | tf_op jit(solution)/shard_map/ppermute | solution.py:166
  10.0 0.0 copy-start.3
  10.0 1.7 %collective-permute-start.1 = (f32[32,512]{1,0:T(8,128)S(1)}, f32[32,512]{1,0:T(8,128)S(1)}, u32[]{:S(2)}, u32[]{:S(2)}) collective-permute-start(f32[32,512]{1,0:T(8,128)S(1)} %get-tuple-element.26), channel_id=1, source_target_pairs={{0,8},{4,12},{8,0},{12,4},{1,9},{5,13},{9,1},{13,5},{2,10},{6,14},... | collective-permute-start | bytes 196616 | tf_op jit(solution)/shard_map/ppermute | solution.py:166
  11.7 0.0 copy-done.1
  11.7 0.0 copy-done.2
  11.7 0.0 copy-done.3
  11.7 0.7 %shard_map.68 = (f32[2,32,512]{2,1,0:T(8,128)S(1)}, f32[29,512]{1,0:T(8,128)S(1)}) custom-call(s32[1,2]{1,0:T(1,128)S(1)} %copy-done.3, f32[4,4]{1,0:T(4,128)S(1)} %copy-done.2, f32[32,2048]{1,0:T(8,128)S(1)} %bitcast.24), custom_call_target="tpu_custom_call" | custom-call | flops 262144 | bytes 452680 | tf_op jit(solution)/shard_map/pallas_call | solution.py:149
  12.3 0.0 collective-permute-done.3.refs_1_
  12.4 2.3 %collective-permute-start = (f32[32,512]{1,0:T(8,128)S(1)}, f32[32,512]{1,0:T(8,128)S(1)}, u32[]{:S(2)}, u32[]{:S(2)}) collective-permute-start(f32[32,512]{1,0:T(8,128)S(1)} %get-tuple-element.27), channel_id=1, source_target_pairs={{0,12},{4,0},{8,4},{12,8},{1,13},{5,1},{9,5},{13,9},{2,14},{6,2},{... | collective-permute-start | bytes 196616 | tf_op jit(solution)/shard_map/ppermute | solution.py:166
  14.7 0.0 collective-permute-done.5.refs_3_
  14.7 0.0 collective-permute-done.4.refs_2_
  14.7 0.1 shard_map.70
  14.7 0.0 copy-start
  14.7 0.1 collective-permute-start.6
  14.8 1.6 %collective-permute-start.7 = (f32[32,512]{1,0:T(8,128)S(1)}, f32[32,512]{1,0:T(8,128)S(1)}, u32[]{:S(2)}, u32[]{:S(2)}) collective-permute-start(f32[32,512]{1,0:T(8,128)S(1)} %get-tuple-element.20), channel_id=1, source_target_pairs={{0,8},{4,12},{8,0},{12,4},{1,9},{5,13},{9,1},{13,5},{2,10},{6,14},... | collective-permute-start | bytes 196616 | tf_op jit(solution)/shard_map/ppermute | solution.py:166
  16.4 0.0 collective-permute-done.2.refs_3_
  16.4 2.3 %collective-permute-start.8 = (f32[32,512]{1,0:T(8,128)S(1)}, f32[32,512]{1,0:T(8,128)S(1)}, u32[]{:S(2)}, u32[]{:S(2)}) collective-permute-start(f32[32,512]{1,0:T(8,128)S(1)} %get-tuple-element.21), channel_id=1, source_target_pairs={{0,12},{4,0},{8,4},{12,8},{1,13},{5,1},{9,5},{13,9},{2,14},{6,2},{... | collective-permute-start | bytes 196616 | tf_op jit(solution)/shard_map/ppermute | solution.py:166
  18.7 0.0 collective-permute-done.1.refs_2_
  18.7 0.0 collective-permute-done.refs_1_
  18.7 0.8 %shard_map.69 = (f32[32,2048]{1,0:T(8,128)}, f32[8,128]{1,0:T(8,128)S(1)}) custom-call(f32[29,512]{1,0:T(8,128)S(1)} %get-tuple-element.12.table_ref, f32[32,512]{1,0:T(8,128)S(1)} %get-tuple-element.28.refs_0_, f32[32,512]{1,0:T(8,128)S(1)} %collective-permute-done.refs_1_, f32[32,512]{1,0:T(8,128)S(1)} %collective-permute-done.1.refs_2_, ...), custom_call_target="tpu_custom_call" | custom-call | flops 524288 | bytes 587776 | tf_op jit(solution)/shard_map/pallas_call | solution.py:149
  19.5 1.5 %collective-permute-done.6.refs_1_ = f32[32,512]{1,0:T(8,128)S(1)} collective-permute-done((f32[32,512]{1,0:T(8,128)S(1)}, f32[32,512]{1,0:T(8,128)S(1)}, u32[]{:S(2)}, u32[]{:S(2)}) %collective-permute-start.6) | collective-permute-done | bytes 65568 | tf_op jit(solution)/shard_map/ppermute | solution.py:166
  21.0 2.1 %collective-permute-done.7.refs_2_ = f32[32,512]{1,0:T(8,128)S(1)} collective-permute-done((f32[32,512]{1,0:T(8,128)S(1)}, f32[32,512]{1,0:T(8,128)S(1)}, u32[]{:S(2)}, u32[]{:S(2)}) %collective-permute-start.7) | collective-permute-done | bytes 65568 | tf_op jit(solution)/shard_map/ppermute | solution.py:166
  23.1 0.0 collective-permute-done.8.refs_3_
  23.1 0.0 copy-done
  23.1 0.7 %shard_map.71 = f32[4,32,512]{2,1,0:T(8,128)} custom-call(f32[29,512]{1,0:T(8,128)S(1)} %get-tuple-element.12.table_ref, f32[4,32,512]{2,1,0:T(8,128)S(1)} %bitcast.23, f32[8,128]{1,0:T(8,128)S(1)} %get-tuple-element.14.held_back_by, f32[32,512]{1,0:T(8,128)S(1)} %get-tuple-element.18.refs_0_, f32[32,512]{1,0:T(8,128)S(1)} %collective-permute-done.6.refs_1_, ...), custom_call_target="tpu_custom_call" | custom-call | bytes 849920 | tf_op jit(solution)/shard_map/pallas_call | solution.py:149
  (1 shorter events, 0.0 us)
Async XLA Ops:
  1.5 6.7 %copy-start.4 = (f32[1,1,128,512]{3,2,1,0:T(8,128)S(1)}, f32[1,1,128,512]{3,2,1,0:T(8,128)}, u32[]{:S(2)}) copy-start(f32[1,1,128,512]{3,2,1,0:T(8,128)} %param.5) | copy-start | bytes 786436
  1.5 10.9 %collective-permute-start.3 = (f32[32,512]{1,0:T(8,128)S(1)}, f32[32,512]{1,0:T(8,128)S(1)}, u32[]{:S(2)}, u32[]{:S(2)}) collective-permute-start(f32[32,512]{1,0:T(8,128)S(1)} %dynamic-slice_bitcast_fusion.3), channel_id=1, source_target_pairs={{0,8},{4,12},{8,0},{12,4},{1,9},{5,13},{9,1},{13,5},{2,10},{6,14},... | collective-permute-start | bytes 196616 | tf_op jit(solution)/shard_map/ppermute | solution.py:173
  6.4 8.2 %collective-permute-start.5 = (f32[32,512]{1,0:T(8,128)S(1)}, f32[32,512]{1,0:T(8,128)S(1)}, u32[]{:S(2)}, u32[]{:S(2)}) collective-permute-start(f32[32,512]{1,0:T(8,128)S(1)} %get-tuple-element.22), channel_id=1, source_target_pairs={{0,12},{4,8},{8,4},{12,0},{1,13},{5,9},{9,5},{13,1},{2,14},{6,10},... | collective-permute-start | bytes 196616 | tf_op jit(solution)/shard_map/ppermute | solution.py:173
  7.9 6.8 %collective-permute-start.4 = (f32[32,512]{1,0:T(8,128)S(1)}, f32[32,512]{1,0:T(8,128)S(1)}, u32[]{:S(2)}, u32[]{:S(2)}) collective-permute-start(f32[32,512]{1,0:T(8,128)S(1)} %get-tuple-element.23), channel_id=1, source_target_pairs={{0,4},{4,0},{8,12},{12,8},{1,5},{5,1},{9,13},{13,9},{2,6},{6,2},{1... | collective-permute-start | bytes 196616 | tf_op jit(solution)/shard_map/ppermute | solution.py:173
  8.2 3.5 %copy-start.1 = (f32[1,32,2048]{2,1,0:T(8,128)S(1)}, f32[1,32,2048]{2,1,0:T(8,128)}, u32[]{:S(2)}) copy-start(f32[1,32,2048]{2,1,0:T(8,128)} %param.7) | copy-start | bytes 786436
  8.2 3.5 %copy-start.2 = (f32[4,4]{1,0:T(4,128)S(1)}, f32[4,4]{1,0:T(4,128)}, u32[]{:S(2)}) copy-start(f32[4,4]{1,0:T(4,128)} %generator_ref.1) | copy-start | bytes 196
  8.2 8.2 %collective-permute-start.2 = (f32[32,512]{1,0:T(8,128)S(1)}, f32[32,512]{1,0:T(8,128)S(1)}, u32[]{:S(2)}, u32[]{:S(2)}) collective-permute-start(f32[32,512]{1,0:T(8,128)S(1)} %get-tuple-element.25), channel_id=1, source_target_pairs={{0,4},{4,8},{8,12},{12,0},{1,5},{5,9},{9,13},{13,1},{2,6},{6,10},{... | collective-permute-start | bytes 196616 | tf_op jit(solution)/shard_map/ppermute | solution.py:166
  10.0 1.7 %copy-start.3 = (s32[1,2]{1,0:T(1,128)S(1)}, s32[1,2]{1,0:T(1,128)}, u32[]{:S(2)}) copy-start(s32[1,2]{1,0:T(1,128)} %ids_ref.1) | copy-start | bytes 28
  10.0 8.7 %collective-permute-start.1 = (f32[32,512]{1,0:T(8,128)S(1)}, f32[32,512]{1,0:T(8,128)S(1)}, u32[]{:S(2)}, u32[]{:S(2)}) collective-permute-start(f32[32,512]{1,0:T(8,128)S(1)} %get-tuple-element.26), channel_id=1, source_target_pairs={{0,8},{4,12},{8,0},{12,4},{1,9},{5,13},{9,1},{13,5},{2,10},{6,14},... | collective-permute-start | bytes 196616 | tf_op jit(solution)/shard_map/ppermute | solution.py:166
  12.4 6.3 %collective-permute-start = (f32[32,512]{1,0:T(8,128)S(1)}, f32[32,512]{1,0:T(8,128)S(1)}, u32[]{:S(2)}, u32[]{:S(2)}) collective-permute-start(f32[32,512]{1,0:T(8,128)S(1)} %get-tuple-element.27), channel_id=1, source_target_pairs={{0,12},{4,0},{8,4},{12,8},{1,13},{5,1},{9,5},{13,9},{2,14},{6,2},{... | collective-permute-start | bytes 196616 | tf_op jit(solution)/shard_map/ppermute | solution.py:166
  14.7 8.4 %copy-start = (f32[1,1,128,512]{3,2,1,0:T(8,128)S(1)}, f32[1,1,128,512]{3,2,1,0:T(8,128)}, u32[]{:S(2)}) copy-start(f32[1,1,128,512]{3,2,1,0:T(8,128)} %param.6) | copy-start | bytes 786436
  14.7 6.2 %collective-permute-start.6 = (f32[32,512]{1,0:T(8,128)S(1)}, f32[32,512]{1,0:T(8,128)S(1)}, u32[]{:S(2)}, u32[]{:S(2)}) collective-permute-start(f32[32,512]{1,0:T(8,128)S(1)} %get-tuple-element.19), channel_id=1, source_target_pairs={{0,4},{4,8},{8,12},{12,0},{1,5},{5,9},{9,13},{13,1},{2,6},{6,10},{... | collective-permute-start | bytes 196616 | tf_op jit(solution)/shard_map/ppermute | solution.py:166
  14.8 8.3 %collective-permute-start.7 = (f32[32,512]{1,0:T(8,128)S(1)}, f32[32,512]{1,0:T(8,128)S(1)}, u32[]{:S(2)}, u32[]{:S(2)}) collective-permute-start(f32[32,512]{1,0:T(8,128)S(1)} %get-tuple-element.20), channel_id=1, source_target_pairs={{0,8},{4,12},{8,0},{12,4},{1,9},{5,13},{9,1},{13,5},{2,10},{6,14},... | collective-permute-start | bytes 196616 | tf_op jit(solution)/shard_map/ppermute | solution.py:166
  16.4 6.7 %collective-permute-start.8 = (f32[32,512]{1,0:T(8,128)S(1)}, f32[32,512]{1,0:T(8,128)S(1)}, u32[]{:S(2)}, u32[]{:S(2)}) collective-permute-start(f32[32,512]{1,0:T(8,128)S(1)} %get-tuple-element.21), channel_id=1, source_target_pairs={{0,12},{4,0},{8,4},{12,8},{1,13},{5,1},{9,5},{13,9},{2,14},{6,2},{... | collective-permute-start | bytes 196616 | tf_op jit(solution)/shard_map/ppermute | solution.py:166

commit v20 on v17

--- a/solution.py
+++ b/solution.py
@@ -14,30 +14,27 @@
 PAIRED_MEMBERS = 4
 KERNEL_VMEM = 8 * 2**20
 
-
-PARTNERS = ((3, 2, 1), (1, 3, 2))
-CURRENT_SHIFTS = ((1, 2, 3), (1, 3, 2))
-REBUILT_SHIFTS = ((1, 2, 3), (1, 3, 2))
-
-
-def chosen(choices):
-    odd = lax.rem(lax.axis_index("rep"), 2)
-    return [jnp.where(odd == 1, b, a) if a != b else a for a, b in zip(*choices)]
-
-
-def partners():
+EARLIER_ROUNDS = (("xor", 2), ("xor", 1), ("xor", 3))
+CURRENT_ROUNDS = (("xor", 1), ("xor", 3), ("xor", 2))
+REBUILT_ROUNDS = (("on", 3), ("on", 2), ("on", 1))
+
+
+def target(d, way, n, members):
+    return d ^ n if way == "xor" else (d + n) % members
+
+
+def source(d, way, n, members):
+    return d ^ n if way == "xor" else (d + members - n) % members
+
+
+def targets_of(rounds, members):
     me = lax.axis_index("code")
-    return [me] + [me ^ r for r in chosen(PARTNERS)]
-
-
-def ahead(shifts):
-    me, members = lax.axis_index("code"), lax.axis_size("code")
-    return [me] + [lax.rem(me + s, members) for s in chosen(shifts)]
-
-
-def behind(shifts):
-    me, members = lax.axis_index("code"), lax.axis_size("code")
-    return [me] + [lax.rem(me + members - s, members) for s in chosen(shifts)]
+    return [me] + [target(me, *way, members) for way in rounds]
+
+
+def sources_of(rounds, members):
+    me = lax.axis_index("code")
+    return [me] + [source(me, *way, members) for way in rounds]
 
 
 def plan_kernel(paired, ids_ref, generator_ref, parity_ref, base_ref, table_ref):
@@ -68,8 +65,9 @@
         )
     from_earlier = from_current = to_rebuilt = range(members)
     if paired:
-        from_earlier, from_current = partners(), behind(CURRENT_SHIFTS)
-        to_rebuilt = ahead(REBUILT_SHIFTS)
+        from_earlier = sources_of(EARLIER_ROUNDS, members)
+        from_current = sources_of(CURRENT_ROUNDS, members)
+        to_rebuilt = targets_of(REBUILT_ROUNDS, members)
     for i, c in enumerate(from_earlier):
         column = [generator_ref[j, c] for j in range(spans)]
         alive = jnp.logical_and(first != c, second != c)
@@ -138,7 +136,7 @@
     members = len(pieces)
     last = table_ref.shape[0] - 1
     lost = table_ref[last : last + 1, :] > 0.5
-    for c, piece in zip(behind(REBUILT_SHIFTS), pieces):
+    for c, piece in zip(sources_of(REBUILT_ROUNDS, members), pieces):
         out_ref[c] = jnp.where(lost, piece[...], earlier_ref[c])
 
 
@@ -159,28 +157,13 @@
     return jax.ShapeDtypeStruct(shape, jnp.float32)
 
 
-def permute(pieces, moves, target):
-    members, reps = lax.axis_size("code"), lax.axis_size("rep")
+def pass_on(pieces, rounds, members):
     return [
         lax.ppermute(
-            piece,
-            ("code", "rep"),
-            [
-                (d * reps + rep, target(d, moves[rep % 2][i]) * reps + rep)
-                for d in range(members)
-                for rep in range(reps)
-            ],
-        )
-        for i, piece in enumerate(pieces)
+            piece, "code", [(d, target(d, *way, members)) for d in range(members)]
+        )
+        for way, piece in zip(rounds, pieces)
     ]
-
-
-def trade(pieces):
-    return permute(pieces, PARTNERS, lambda d, r: d ^ r)
-
-
-def pass_on(pieces, shifts):
-    return permute(pieces, shifts, lambda d, s: (d + s) % PAIRED_MEMBERS)
 
 
 def cut(blocks, order):
@@ -210,9 +193,9 @@
     parity_cost = 2 * spans * slab_rows * width
     if paired:
         block = floats(own_rows, width)
-        own_earlier, *cut_earlier = cut(earlier, partners())
-        earlier_rows = trade(cut_earlier)
-        own_current, *cut_current = cut(current, ahead(CURRENT_SHIFTS))
+        own_earlier, *cut_earlier = cut(earlier, targets_of(EARLIER_ROUNDS, members))
+        earlier_rows = pass_on(cut_earlier, EARLIER_ROUNDS, members)
+        own_current, *cut_current = cut(current, targets_of(CURRENT_ROUNDS, members))
         outgoing = call(
             rebuild_paired_kernel,
             [IN_VMEM] * (members + 2),
@@ -220,8 +203,8 @@
             (base, table, own_earlier, *earlier_rows),
             rebuild_cost,
         )
-        incoming = pass_on(outgoing[1:], REBUILT_SHIFTS)
-        current_rows = [own_current, *pass_on(cut_current, CURRENT_SHIFTS)]
+        incoming = pass_on(outgoing[1:], REBUILT_ROUNDS, members)
+        current_rows = [own_current, *pass_on(cut_current, CURRENT_ROUNDS, members)]
         new_parity, parity_done = call(
             parity_paired_kernel,
             [IN_VMEM] * (members + 1),

time: 26 us -> 25 us (0.962)
  the two profiles are of different devices: /device:TPU:1 before, /device:TPU:0 now
where the time goes in v20:
time: 25 us; the launch traced here: 24.9 us
  starting transfers between devices  15.2 us (61%)
  waiting for transfers between devices  5.71 us (23%)
  Pallas kernels  2.25 us (9%)
  local copies, waits for them, and re-layouts  1.05 us (4%)
  between operations  0.72 us (3%)
    ppermute x9, starting transfers between devices, pass_on(): lax.ppermute(piece, 'code', [(d, target(d, *way, members)) for d in range...  15.2 us
    ppermute x9, waiting for transfers between devices, pass_on(): lax.ppermute(piece, 'code', [(d, target(d, *way, members)) for d in range...  5.71 us
    pallas_call x4, Pallas kernels, call(): pl.pallas_call(kernel, in_specs=specs, out_specs=jax.tree.map(lambda _: I...  2.25 us
    squeeze x2, local copies, waits for them, and re-layouts, cut(): lax.dynamic_index_in_dim(blocks, c, 0, keepdims=False)  1.03 us
  transfers between devices with their start and end apart: 9, of which 3 were waited for; matrix products, arithmetic and copies ran while one was open for 0% of the time, Pallas kernels for 6%

profile of v20, /device:TPU:0, one launch (start us, length us, event | category | flops | bytes accessed | tf_op | source)
XLA Modules:
  0.0 24.9 jit_solution(2339851840435214718)
XLA Ops:
  0.6 0.0 copy-start.4
  0.7 1.0 %dynamic-slice_bitcast_fusion = (f32[32,512]{1,0:T(8,128)S(1)}, f32[32,512]{1,0:T(8,128)S(1)}, f32[32,512]{1,0:T(8,128)S(1)}, f32[32,512]{1,0:T(8,128)S(1)}) fusion(f32[4,32,512]{2,1,0:T(8,128)} %bitcast.21, s32[]{:T(128)S(6)} %select_n.19, s32[]{:T(128)S(6)} %select_n.18, s32[]{:T(128)S(6)} %select_n.20, s32[]{:T(128)S(6)} %select_n.17), kind=kLoop, calls=%fused_computation | loop fusion | bytes 524304 | tf_op jit(solution)/shard_map/jit(dynamic_index_in_dim)/squeeze | solution.py:170
  1.7 4.1 %collective-permute-start.3 = (f32[32,512]{1,0:T(8,128)S(1)}, f32[32,512]{1,0:T(8,128)S(1)}, u32[]{:S(2)}, u32[]{:S(2)}) collective-permute-start(f32[32,512]{1,0:T(8,128)S(1)} %get-tuple-element.20), channel_id=1, source_target_pairs={{0,8},{4,12},{8,0},{12,4},{1,9},{5,13},{9,1},{13,5},{2,10},{6,14},... | collective-permute-start | bytes 196616 | tf_op jit(solution)/shard_map/ppermute | solution.py:162
  5.8 1.6 %collective-permute-start.4 = (f32[32,512]{1,0:T(8,128)S(1)}, f32[32,512]{1,0:T(8,128)S(1)}, u32[]{:S(2)}, u32[]{:S(2)}) collective-permute-start(f32[32,512]{1,0:T(8,128)S(1)} %get-tuple-element.19), channel_id=1, source_target_pairs={{0,4},{4,0},{8,12},{12,8},{1,5},{5,1},{9,13},{13,9},{2,6},{6,2},{1... | collective-permute-start | bytes 196616 | tf_op jit(solution)/shard_map/ppermute | solution.py:162
  7.3 0.0 collective-permute-start.5
  7.3 0.0 copy-done.4
  7.3 0.0 copy-start.1
  7.4 0.0 copy-start.2
  7.4 1.0 %collective-permute-start = (f32[32,512]{1,0:T(8,128)S(1)}, f32[32,512]{1,0:T(8,128)S(1)}, u32[]{:S(2)}, u32[]{:S(2)}) collective-permute-start(f32[32,512]{1,0:T(8,128)S(1)} %get-tuple-element.24), channel_id=1, source_target_pairs={{0,4},{4,0},{8,12},{12,8},{1,5},{5,1},{9,13},{13,9},{2,6},{6,2},{1... | collective-permute-start | bytes 196616 | tf_op jit(solution)/shard_map/ppermute | solution.py:162
  8.3 0.0 copy-start.3
  8.3 3.0 %collective-permute-start.1 = (f32[32,512]{1,0:T(8,128)S(1)}, f32[32,512]{1,0:T(8,128)S(1)}, u32[]{:S(2)}, u32[]{:S(2)}) collective-permute-start(f32[32,512]{1,0:T(8,128)S(1)} %get-tuple-element.23), channel_id=1, source_target_pairs={{0,12},{4,8},{8,4},{12,0},{1,13},{5,9},{9,5},{13,1},{2,14},{6,10},... | collective-permute-start | bytes 196616 | tf_op jit(solution)/shard_map/ppermute | solution.py:162
  11.4 0.0 copy-done.1
  11.4 0.0 copy-done.2
  11.4 0.0 copy-done.3
  11.4 0.7 %shard_map.68 = (f32[2,32,512]{2,1,0:T(8,128)S(1)}, f32[29,512]{1,0:T(8,128)S(1)}) custom-call(s32[1,2]{1,0:T(1,128)S(1)} %copy-done.3, f32[4,4]{1,0:T(4,128)S(1)} %copy-done.2, f32[32,2048]{1,0:T(8,128)S(1)} %bitcast.23), custom_call_target="tpu_custom_call" | custom-call | flops 262144 | bytes 452680 | tf_op jit(solution)/shard_map/pallas_call | solution.py:145
  12.0 0.0 collective-permute-done.3.refs_1_
  12.0 1.2 %collective-permute-start.2 = (f32[32,512]{1,0:T(8,128)S(1)}, f32[32,512]{1,0:T(8,128)S(1)}, u32[]{:S(2)}, u32[]{:S(2)}) collective-permute-start(f32[32,512]{1,0:T(8,128)S(1)} %get-tuple-element.22), channel_id=1, source_target_pairs={{0,8},{4,12},{8,0},{12,4},{1,9},{5,13},{9,1},{13,5},{2,10},{6,14},... | collective-permute-start | bytes 196616 | tf_op jit(solution)/shard_map/ppermute | solution.py:162
  13.2 0.0 collective-permute-done.4.refs_2_
  13.2 0.7 %collective-permute-done.5.refs_3_ = f32[32,512]{1,0:T(8,128)S(1)} collective-permute-done((f32[32,512]{1,0:T(8,128)S(1)}, f32[32,512]{1,0:T(8,128)S(1)}, u32[]{:S(2)}, u32[]{:S(2)}) %collective-permute-start.5) | collective-permute-done | bytes 65568 | tf_op jit(solution)/shard_map/ppermute | solution.py:162
  13.9 0.1 shard_map.70
  14.0 0.0 copy-start
  14.0 1.8 %collective-permute-start.6 = (f32[32,512]{1,0:T(8,128)S(1)}, f32[32,512]{1,0:T(8,128)S(1)}, u32[]{:S(2)}, u32[]{:S(2)}) collective-permute-start(f32[32,512]{1,0:T(8,128)S(1)} %get-tuple-element.15), channel_id=1, source_target_pairs={{0,12},{4,0},{8,4},{12,8},{1,13},{5,1},{9,5},{13,9},{2,14},{6,2},{... | collective-permute-start | bytes 196616 | tf_op jit(solution)/shard_map/ppermute | solution.py:162
  15.8 0.5 %collective-permute-start.7 = (f32[32,512]{1,0:T(8,128)S(1)}, f32[32,512]{1,0:T(8,128)S(1)}, u32[]{:S(2)}, u32[]{:S(2)}) collective-permute-start(f32[32,512]{1,0:T(8,128)S(1)} %get-tuple-element.16), channel_id=1, source_target_pairs={{0,8},{4,12},{8,0},{12,4},{1,9},{5,13},{9,1},{13,5},{2,10},{6,14},... | collective-permute-start | bytes 196616 | tf_op jit(solution)/shard_map/ppermute | solution.py:162
  16.4 0.0 collective-permute-done.refs_1_
  16.4 1.9 %collective-permute-start.8 = (f32[32,512]{1,0:T(8,128)S(1)}, f32[32,512]{1,0:T(8,128)S(1)}, u32[]{:S(2)}, u32[]{:S(2)}) collective-permute-start(f32[32,512]{1,0:T(8,128)S(1)} %get-tuple-element.17), channel_id=1, source_target_pairs={{0,4},{4,8},{8,12},{12,0},{1,5},{5,9},{9,13},{13,1},{2,6},{6,10},{... | collective-permute-start | bytes 196616 | tf_op jit(solution)/shard_map/ppermute | solution.py:162
  18.3 0.0 collective-permute-done.1.refs_2_
  18.3 2.7 %collective-permute-done.2.refs_3_ = f32[32,512]{1,0:T(8,128)S(1)} collective-permute-done((f32[32,512]{1,0:T(8,128)S(1)}, f32[32,512]{1,0:T(8,128)S(1)}, u32[]{:S(2)}, u32[]{:S(2)}) %collective-permute-start.2) | collective-permute-done | bytes 65568 | tf_op jit(solution)/shard_map/ppermute | solution.py:162
  21.0 0.8 %shard_map.69 = (f32[32,2048]{1,0:T(8,128)}, f32[8,128]{1,0:T(8,128)S(1)}) custom-call(f32[29,512]{1,0:T(8,128)S(1)} %get-tuple-element.10.table_ref, f32[32,512]{1,0:T(8,128)S(1)} %get-tuple-element.25.refs_0_, f32[32,512]{1,0:T(8,128)S(1)} %collective-permute-done.refs_1_, f32[32,512]{1,0:T(8,128)S(1)} %collective-permute-done.1.refs_2_, ...), custom_call_target="tpu_custom_call" | custom-call | flops 524288 | bytes 587776 | tf_op jit(solution)/shard_map/pallas_call | solution.py:145
  21.8 0.0 collective-permute-done.6.refs_1_
  21.8 2.3 %collective-permute-done.7.refs_2_ = f32[32,512]{1,0:T(8,128)S(1)} collective-permute-done((f32[32,512]{1,0:T(8,128)S(1)}, f32[32,512]{1,0:T(8,128)S(1)}, u32[]{:S(2)}, u32[]{:S(2)}) %collective-permute-start.7) | collective-permute-done | bytes 65568 | tf_op jit(solution)/shard_map/ppermute | solution.py:162
  24.1 0.0 collective-permute-done.8.refs_3_
  24.1 0.0 copy-done
  24.1 0.8 %shard_map.71 = f32[4,32,512]{2,1,0:T(8,128)} custom-call(f32[29,512]{1,0:T(8,128)S(1)} %get-tuple-element.10.table_ref, f32[4,32,512]{2,1,0:T(8,128)S(1)} %bitcast.22, f32[8,128]{1,0:T(8,128)S(1)} %get-tuple-element.12.held_back_by, f32[32,512]{1,0:T(8,128)S(1)} %get-tuple-element.14.refs_0_, f32[32,512]{1,0:T(8,128)S(1)} %collective-permute-done.6.refs_1_, ...), custom_call_target="tpu_custom_call" | custom-call | bytes 849920 | tf_op jit(solution)/shard_map/pallas_call | solution.py:145
  (1 shorter events, 0.0 us)
Async XLA Ops:
  0.6 6.7 %copy-start.4 = (f32[1,1,128,512]{3,2,1,0:T(8,128)S(1)}, f32[1,1,128,512]{3,2,1,0:T(8,128)}, u32[]{:S(2)}) copy-start(f32[1,1,128,512]{3,2,1,0:T(8,128)} %param.5) | copy-start | bytes 786436
  1.7 10.4 %collective-permute-start.3 = (f32[32,512]{1,0:T(8,128)S(1)}, f32[32,512]{1,0:T(8,128)S(1)}, u32[]{:S(2)}, u32[]{:S(2)}) collective-permute-start(f32[32,512]{1,0:T(8,128)S(1)} %get-tuple-element.20), channel_id=1, source_target_pairs={{0,8},{4,12},{8,0},{12,4},{1,9},{5,13},{9,1},{13,5},{2,10},{6,14},... | collective-permute-start | bytes 196616 | tf_op jit(solution)/shard_map/ppermute | solution.py:162
  5.8 7.5 %collective-permute-start.4 = (f32[32,512]{1,0:T(8,128)S(1)}, f32[32,512]{1,0:T(8,128)S(1)}, u32[]{:S(2)}, u32[]{:S(2)}) collective-permute-start(f32[32,512]{1,0:T(8,128)S(1)} %get-tuple-element.19), channel_id=1, source_target_pairs={{0,4},{4,0},{8,12},{12,8},{1,5},{5,1},{9,13},{13,9},{2,6},{6,2},{1... | collective-permute-start | bytes 196616 | tf_op jit(solution)/shard_map/ppermute | solution.py:162
  7.3 6.6 %collective-permute-start.5 = (f32[32,512]{1,0:T(8,128)S(1)}, f32[32,512]{1,0:T(8,128)S(1)}, u32[]{:S(2)}, u32[]{:S(2)}) collective-permute-start(f32[32,512]{1,0:T(8,128)S(1)} %get-tuple-element.18), channel_id=1, source_target_pairs={{0,12},{4,8},{8,4},{12,0},{1,13},{5,9},{9,5},{13,1},{2,14},{6,10},... | collective-permute-start | bytes 196616 | tf_op jit(solution)/shard_map/ppermute | solution.py:162
  7.3 4.0 %copy-start.1 = (f32[1,32,2048]{2,1,0:T(8,128)S(1)}, f32[1,32,2048]{2,1,0:T(8,128)}, u32[]{:S(2)}) copy-start(f32[1,32,2048]{2,1,0:T(8,128)} %param.7) | copy-start | bytes 786436
  7.4 4.0 %copy-start.2 = (f32[4,4]{1,0:T(4,128)S(1)}, f32[4,4]{1,0:T(4,128)}, u32[]{:S(2)}) copy-start(f32[4,4]{1,0:T(4,128)} %generator_ref.1) | copy-start | bytes 196
  7.4 9.0 %collective-permute-start = (f32[32,512]{1,0:T(8,128)S(1)}, f32[32,512]{1,0:T(8,128)S(1)}, u32[]{:S(2)}, u32[]{:S(2)}) collective-permute-start(f32[32,512]{1,0:T(8,128)S(1)} %get-tuple-element.24), channel_id=1, source_target_pairs={{0,4},{4,0},{8,12},{12,8},{1,5},{5,1},{9,13},{13,9},{2,6},{6,2},{1... | collective-permute-start | bytes 196616 | tf_op jit(solution)/shard_map/ppermute | solution.py:162
  8.3 3.0 %copy-start.3 = (s32[1,2]{1,0:T(1,128)S(1)}, s32[1,2]{1,0:T(1,128)}, u32[]{:S(2)}) copy-start(s32[1,2]{1,0:T(1,128)} %ids_ref.1) | copy-start | bytes 28
  8.3 10.0 %collective-permute-start.1 = (f32[32,512]{1,0:T(8,128)S(1)}, f32[32,512]{1,0:T(8,128)S(1)}, u32[]{:S(2)}, u32[]{:S(2)}) collective-permute-start(f32[32,512]{1,0:T(8,128)S(1)} %get-tuple-element.23), channel_id=1, source_target_pairs={{0,12},{4,8},{8,4},{12,0},{1,13},{5,9},{9,5},{13,1},{2,14},{6,10},... | collective-permute-start | bytes 196616 | tf_op jit(solution)/shard_map/ppermute | solution.py:162
  12.0 9.0 %collective-permute-start.2 = (f32[32,512]{1,0:T(8,128)S(1)}, f32[32,512]{1,0:T(8,128)S(1)}, u32[]{:S(2)}, u32[]{:S(2)}) collective-permute-start(f32[32,512]{1,0:T(8,128)S(1)} %get-tuple-element.22), channel_id=1, source_target_pairs={{0,8},{4,12},{8,0},{12,4},{1,9},{5,13},{9,1},{13,5},{2,10},{6,14},... | collective-permute-start | bytes 196616 | tf_op jit(solution)/shard_map/ppermute | solution.py:162
  14.0 10.2 %copy-start = (f32[1,1,128,512]{3,2,1,0:T(8,128)S(1)}, f32[1,1,128,512]{3,2,1,0:T(8,128)}, u32[]{:S(2)}) copy-start(f32[1,1,128,512]{3,2,1,0:T(8,128)} %param.6) | copy-start | bytes 786436
  14.0 7.8 %collective-permute-start.6 = (f32[32,512]{1,0:T(8,128)S(1)}, f32[32,512]{1,0:T(8,128)S(1)}, u32[]{:S(2)}, u32[]{:S(2)}) collective-permute-start(f32[32,512]{1,0:T(8,128)S(1)} %get-tuple-element.15), channel_id=1, source_target_pairs={{0,12},{4,0},{8,4},{12,8},{1,13},{5,1},{9,5},{13,9},{2,14},{6,2},{... | collective-permute-start | bytes 196616 | tf_op jit(solution)/shard_map/ppermute | solution.py:162
  15.8 8.3 %collective-permute-start.7 = (f32[32,512]{1,0:T(8,128)S(1)}, f32[32,512]{1,0:T(8,128)S(1)}, u32[]{:S(2)}, u32[]{:S(2)}) collective-permute-start(f32[32,512]{1,0:T(8,128)S(1)} %get-tuple-element.16), channel_id=1, source_target_pairs={{0,8},{4,12},{8,0},{12,4},{1,9},{5,13},{9,1},{13,5},{2,10},{6,14},... | collective-permute-start | bytes 196616 | tf_op jit(solution)/shard_map/ppermute | solution.py:162
  16.4 7.7 %collective-permute-start.8 = (f32[32,512]{1,0:T(8,128)S(1)}, f32[32,512]{1,0:T(8,128)S(1)}, u32[]{:S(2)}, u32[]{:S(2)}) collective-permute-start(f32[32,512]{1,0:T(8,128)S(1)} %get-tuple-element.17), channel_id=1, source_target_pairs={{0,4},{4,8},{8,12},{12,0},{1,5},{5,9},{9,13},{13,1},{2,6},{6,10},{... | collective-permute-start | bytes 196616 | tf_op jit(solution)/shard_map/ppermute | solution.py:162

commit v21 on v20

--- a/solution.py
+++ b/solution.py
@@ -14,9 +14,9 @@
 PAIRED_MEMBERS = 4
 KERNEL_VMEM = 8 * 2**20
 
-EARLIER_ROUNDS = (("xor", 2), ("xor", 1), ("xor", 3))
-CURRENT_ROUNDS = (("xor", 1), ("xor", 3), ("xor", 2))
-REBUILT_ROUNDS = (("on", 3), ("on", 2), ("on", 1))
+EARLIER_ROUNDS = (("xor", 2), ("xor", 3), ("xor", 1))
+CURRENT_ROUNDS = (("on", 1), ("on", 2), ("on", 3))
+REBUILT_ROUNDS = (("on", 2), ("on", 1), ("on", 3))
 
 
 def target(d, way, n, members):

time: 25 us -> 23.6 us (0.944)
  waiting for transfers between devices: 5.71 us -> 2.04 us
  starting transfers between devices: 15.2 us -> 17.4 us
    ppermute x9, waiting for transfers between devices: 5.71 us -> 2.04 us  [pass_on(): lax.ppermute(piece, 'code', [(d, target(d, *way, members)) for d in range...]
    ppermute x9, starting transfers between devices: 15.2 us -> 17.4 us  [pass_on(): lax.ppermute(piece, 'code', [(d, target(d, *way, members)) for d in range...]
  transfers between devices with their start and end apart: 9 -> 9, of which waited for: 3 -> 2; matrix products, arithmetic and copies ran while one was open for 0% -> 0% of each run, Pallas kernels for 6% -> 6%
where the time goes in v21:
time: 23.6 us; the launch traced here: 23.4 us
  starting transfers between devices  17.4 us (74%)
  Pallas kernels  2.24 us (9%)
  waiting for transfers between devices  2.04 us (9%)
  local copies, waits for them, and re-layouts  1.04 us (4%)
  between operations  0.71 us (3%)
    ppermute x9, starting transfers between devices, pass_on(): lax.ppermute(piece, 'code', [(d, target(d, *way, members)) for d in range...  17.4 us
    pallas_call x4, Pallas kernels, call(): pl.pallas_call(kernel, in_specs=specs, out_specs=jax.tree.map(lambda _: I...  2.24 us
    ppermute x9, waiting for transfers between devices, pass_on(): lax.ppermute(piece, 'code', [(d, target(d, *way, members)) for d in range...  2.04 us
    squeeze x2, local copies, waits for them, and re-layouts, cut(): lax.dynamic_index_in_dim(blocks, c, 0, keepdims=False)  1.02 us
  transfers between devices with their start and end apart: 9, of which 2 were waited for; matrix products, arithmetic and copies ran while one was open for 0% of the time, Pallas kernels for 6%

profile of v21, /device:TPU:0, one launch (start us, length us, event | category | flops | bytes accessed | tf_op | source)
XLA Modules:
  0.0 23.4 jit_solution(11924686745915203546)
XLA Ops:
  0.6 0.0 copy-start.4
  0.7 1.0 %dynamic-slice_bitcast_fusion = (f32[32,512]{1,0:T(8,128)S(1)}, f32[32,512]{1,0:T(8,128)S(1)}, f32[32,512]{1,0:T(8,128)S(1)}, f32[32,512]{1,0:T(8,128)S(1)}) fusion(f32[4,32,512]{2,1,0:T(8,128)} %bitcast.21, s32[]{:T(128)S(6)} %select_n.47, s32[]{:T(128)S(6)} %select_n.46, s32[]{:T(128)S(6)} %select_n.45, s32[]{:T(128)S(6)} %select_n.38), kind=kLoop, calls=%fused_computation | loop fusion | bytes 524304 | tf_op jit(solution)/shard_map/jit(dynamic_index_in_dim)/squeeze | solution.py:170
  1.7 4.1 %collective-permute-start.3 = (f32[32,512]{1,0:T(8,128)S(1)}, f32[32,512]{1,0:T(8,128)S(1)}, u32[]{:S(2)}, u32[]{:S(2)}) collective-permute-start(f32[32,512]{1,0:T(8,128)S(1)} %get-tuple-element.20), channel_id=1, source_target_pairs={{0,8},{4,12},{8,0},{12,4},{1,9},{5,13},{9,1},{13,5},{2,10},{6,14},... | collective-permute-start | bytes 196616 | tf_op jit(solution)/shard_map/ppermute | solution.py:162
  5.8 1.3 %collective-permute-start.4 = (f32[32,512]{1,0:T(8,128)S(1)}, f32[32,512]{1,0:T(8,128)S(1)}, u32[]{:S(2)}, u32[]{:S(2)}) collective-permute-start(f32[32,512]{1,0:T(8,128)S(1)} %get-tuple-element.19), channel_id=1, source_target_pairs={{0,12},{4,8},{8,4},{12,0},{1,13},{5,9},{9,5},{13,1},{2,14},{6,10},... | collective-permute-start | bytes 196616 | tf_op jit(solution)/shard_map/ppermute | solution.py:162
  7.1 0.2 collective-permute-start.5
  7.3 0.0 copy-done.4
  7.3 0.0 copy-start.1
  7.4 0.0 copy-start.2
  7.4 1.8 %collective-permute-start = (f32[32,512]{1,0:T(8,128)S(1)}, f32[32,512]{1,0:T(8,128)S(1)}, u32[]{:S(2)}, u32[]{:S(2)}) collective-permute-start(f32[32,512]{1,0:T(8,128)S(1)} %get-tuple-element.24), channel_id=1, source_target_pairs={{0,4},{4,8},{8,12},{12,0},{1,5},{5,9},{9,13},{13,1},{2,6},{6,10},{... | collective-permute-start | bytes 196616 | tf_op jit(solution)/shard_map/ppermute | solution.py:162
  9.2 0.0 copy-start.3
  9.2 1.7 %collective-permute-start.1 = (f32[32,512]{1,0:T(8,128)S(1)}, f32[32,512]{1,0:T(8,128)S(1)}, u32[]{:S(2)}, u32[]{:S(2)}) collective-permute-start(f32[32,512]{1,0:T(8,128)S(1)} %get-tuple-element.23), channel_id=1, source_target_pairs={{0,8},{4,12},{8,0},{12,4},{1,9},{5,13},{9,1},{13,5},{2,10},{6,14},... | collective-permute-start | bytes 196616 | tf_op jit(solution)/shard_map/ppermute | solution.py:162
  10.9 0.0 copy-done.1
  10.9 0.0 copy-done.2
  10.9 0.0 copy-done.3
  10.9 0.7 %shard_map.68 = (f32[2,32,512]{2,1,0:T(8,128)S(1)}, f32[29,512]{1,0:T(8,128)S(1)}) custom-call(s32[1,2]{1,0:T(1,128)S(1)} %copy-done.3, f32[4,4]{1,0:T(4,128)S(1)} %copy-done.2, f32[32,2048]{1,0:T(8,128)S(1)} %bitcast.23), custom_call_target="tpu_custom_call" | custom-call | flops 262144 | bytes 452680 | tf_op jit(solution)/shard_map/pallas_call | solution.py:145
  11.6 0.0 collective-permute-done.3.refs_1_
  11.6 3.0 %collective-permute-start.2 = (f32[32,512]{1,0:T(8,128)S(1)}, f32[32,512]{1,0:T(8,128)S(1)}, u32[]{:S(2)}, u32[]{:S(2)}) collective-permute-start(f32[32,512]{1,0:T(8,128)S(1)} %get-tuple-element.22), channel_id=1, source_target_pairs={{0,12},{4,0},{8,4},{12,8},{1,13},{5,1},{9,5},{13,9},{2,14},{6,2},{... | collective-permute-start | bytes 196616 | tf_op jit(solution)/shard_map/ppermute | solution.py:162
  14.7 0.0 collective-permute-done.4.refs_2_
  14.7 0.0 collective-permute-done.5.refs_3_
  14.7 0.1 shard_map.70
  14.7 0.0 copy-start
  14.7 1.3 %collective-permute-start.6 = (f32[32,512]{1,0:T(8,128)S(1)}, f32[32,512]{1,0:T(8,128)S(1)}, u32[]{:S(2)}, u32[]{:S(2)}) collective-permute-start(f32[32,512]{1,0:T(8,128)S(1)} %get-tuple-element.15), channel_id=1, source_target_pairs={{0,8},{4,12},{8,0},{12,4},{1,9},{5,13},{9,1},{13,5},{2,10},{6,14},... | collective-permute-start | bytes 196616 | tf_op jit(solution)/shard_map/ppermute | solution.py:162
  16.0 0.5 %collective-permute-start.7 = (f32[32,512]{1,0:T(8,128)S(1)}, f32[32,512]{1,0:T(8,128)S(1)}, u32[]{:S(2)}, u32[]{:S(2)}) collective-permute-start(f32[32,512]{1,0:T(8,128)S(1)} %get-tuple-element.16), channel_id=1, source_target_pairs={{0,4},{4,8},{8,12},{12,0},{1,5},{5,9},{9,13},{13,1},{2,6},{6,10},{... | collective-permute-start | bytes 196616 | tf_op jit(solution)/shard_map/ppermute | solution.py:162
  16.5 0.0 collective-permute-done.refs_1_
  16.5 3.4 %collective-permute-start.8 = (f32[32,512]{1,0:T(8,128)S(1)}, f32[32,512]{1,0:T(8,128)S(1)}, u32[]{:S(2)}, u32[]{:S(2)}) collective-permute-start(f32[32,512]{1,0:T(8,128)S(1)} %get-tuple-element.17), channel_id=1, source_target_pairs={{0,12},{4,0},{8,4},{12,8},{1,13},{5,1},{9,5},{13,9},{2,14},{6,2},{... | collective-permute-start | bytes 196616 | tf_op jit(solution)/shard_map/ppermute | solution.py:162
  19.8 0.0 collective-permute-done.1.refs_2_
  19.8 0.0 collective-permute-done.2.refs_3_
  19.8 0.8 %shard_map.69 = (f32[32,2048]{1,0:T(8,128)}, f32[8,128]{1,0:T(8,128)S(1)}) custom-call(f32[29,512]{1,0:T(8,128)S(1)} %get-tuple-element.10.table_ref, f32[32,512]{1,0:T(8,128)S(1)} %get-tuple-element.25.refs_0_, f32[32,512]{1,0:T(8,128)S(1)} %collective-permute-done.refs_1_, f32[32,512]{1,0:T(8,128)S(1)} %collective-permute-done.1.refs_2_, ...), custom_call_target="tpu_custom_call" | custom-call | flops 524288 | bytes 587776 | tf_op jit(solution)/shard_map/pallas_call | solution.py:145
  20.6 1.7 %collective-permute-done.6.refs_1_ = f32[32,512]{1,0:T(8,128)S(1)} collective-permute-done((f32[32,512]{1,0:T(8,128)S(1)}, f32[32,512]{1,0:T(8,128)S(1)}, u32[]{:S(2)}, u32[]{:S(2)}) %collective-permute-start.6) | collective-permute-done | bytes 65568 | tf_op jit(solution)/shard_map/ppermute | solution.py:162
  22.3 0.0 collective-permute-done.7.refs_2_
  22.3 0.3 %collective-permute-done.8.refs_3_ = f32[32,512]{1,0:T(8,128)S(1)} collective-permute-done((f32[32,512]{1,0:T(8,128)S(1)}, f32[32,512]{1,0:T(8,128)S(1)}, u32[]{:S(2)}, u32[]{:S(2)}) %collective-permute-start.8) | collective-permute-done | bytes 65568 | tf_op jit(solution)/shard_map/ppermute | solution.py:162
  22.7 0.0 copy-done
  22.7 0.7 %shard_map.71 = f32[4,32,512]{2,1,0:T(8,128)} custom-call(f32[29,512]{1,0:T(8,128)S(1)} %get-tuple-element.10.table_ref, f32[4,32,512]{2,1,0:T(8,128)S(1)} %bitcast.22, f32[8,128]{1,0:T(8,128)S(1)} %get-tuple-element.12.held_back_by, f32[32,512]{1,0:T(8,128)S(1)} %get-tuple-element.14.refs_0_, f32[32,512]{1,0:T(8,128)S(1)} %collective-permute-done.6.refs_1_, ...), custom_call_target="tpu_custom_call" | custom-call | bytes 849920 | tf_op jit(solution)/shard_map/pallas_call | solution.py:145
  (1 shorter events, 0.0 us)
Async XLA Ops:
  0.6 6.7 %copy-start.4 = (f32[1,1,128,512]{3,2,1,0:T(8,128)S(1)}, f32[1,1,128,512]{3,2,1,0:T(8,128)}, u32[]{:S(2)}) copy-start(f32[1,1,128,512]{3,2,1,0:T(8,128)} %param.5) | copy-start | bytes 786436
  1.7 9.9 %collective-permute-start.3 = (f32[32,512]{1,0:T(8,128)S(1)}, f32[32,512]{1,0:T(8,128)S(1)}, u32[]{:S(2)}, u32[]{:S(2)}) collective-permute-start(f32[32,512]{1,0:T(8,128)S(1)} %get-tuple-element.20), channel_id=1, source_target_pairs={{0,8},{4,12},{8,0},{12,4},{1,9},{5,13},{9,1},{13,5},{2,10},{6,14},... | collective-permute-start | bytes 196616 | tf_op jit(solution)/shard_map/ppermute | solution.py:162
  5.8 8.9 %collective-permute-start.4 = (f32[32,512]{1,0:T(8,128)S(1)}, f32[32,512]{1,0:T(8,128)S(1)}, u32[]{:S(2)}, u32[]{:S(2)}) collective-permute-start(f32[32,512]{1,0:T(8,128)S(1)} %get-tuple-element.19), channel_id=1, source_target_pairs={{0,12},{4,8},{8,4},{12,0},{1,13},{5,9},{9,5},{13,1},{2,14},{6,10},... | collective-permute-start | bytes 196616 | tf_op jit(solution)/shard_map/ppermute | solution.py:162
  7.1 7.5 %collective-permute-start.5 = (f32[32,512]{1,0:T(8,128)S(1)}, f32[32,512]{1,0:T(8,128)S(1)}, u32[]{:S(2)}, u32[]{:S(2)}) collective-permute-start(f32[32,512]{1,0:T(8,128)S(1)} %get-tuple-element.18), channel_id=1, source_target_pairs={{0,4},{4,0},{8,12},{12,8},{1,5},{5,1},{9,13},{13,9},{2,6},{6,2},{1... | collective-permute-start | bytes 196616 | tf_op jit(solution)/shard_map/ppermute | solution.py:162
  7.3 3.6 %copy-start.1 = (f32[1,32,2048]{2,1,0:T(8,128)S(1)}, f32[1,32,2048]{2,1,0:T(8,128)}, u32[]{:S(2)}) copy-start(f32[1,32,2048]{2,1,0:T(8,128)} %param.7) | copy-start | bytes 786436
  7.4 3.6 %copy-start.2 = (f32[4,4]{1,0:T(4,128)S(1)}, f32[4,4]{1,0:T(4,128)}, u32[]{:S(2)}) copy-start(f32[4,4]{1,0:T(4,128)} %generator_ref.1) | copy-start | bytes 196
  7.4 9.1 %collective-permute-start = (f32[32,512]{1,0:T(8,128)S(1)}, f32[32,512]{1,0:T(8,128)S(1)}, u32[]{:S(2)}, u32[]{:S(2)}) collective-permute-start(f32[32,512]{1,0:T(8,128)S(1)} %get-tuple-element.24), channel_id=1, source_target_pairs={{0,4},{4,8},{8,12},{12,0},{1,5},{5,9},{9,13},{13,1},{2,6},{6,10},{... | collective-permute-start | bytes 196616 | tf_op jit(solution)/shard_map/ppermute | solution.py:162
  9.2 1.7 %copy-start.3 = (s32[1,2]{1,0:T(1,128)S(1)}, s32[1,2]{1,0:T(1,128)}, u32[]{:S(2)}) copy-start(s32[1,2]{1,0:T(1,128)} %ids_ref.1) | copy-start | bytes 28
  9.2 10.6 %collective-permute-start.1 = (f32[32,512]{1,0:T(8,128)S(1)}, f32[32,512]{1,0:T(8,128)S(1)}, u32[]{:S(2)}, u32[]{:S(2)}) collective-permute-start(f32[32,512]{1,0:T(8,128)S(1)} %get-tuple-element.23), channel_id=1, source_target_pairs={{0,8},{4,12},{8,0},{12,4},{1,9},{5,13},{9,1},{13,5},{2,10},{6,14},... | collective-permute-start | bytes 196616 | tf_op jit(solution)/shard_map/ppermute | solution.py:162
  11.6 8.2 %collective-permute-start.2 = (f32[32,512]{1,0:T(8,128)S(1)}, f32[32,512]{1,0:T(8,128)S(1)}, u32[]{:S(2)}, u32[]{:S(2)}) collective-permute-start(f32[32,512]{1,0:T(8,128)S(1)} %get-tuple-element.22), channel_id=1, source_target_pairs={{0,12},{4,0},{8,4},{12,8},{1,13},{5,1},{9,5},{13,9},{2,14},{6,2},{... | collective-permute-start | bytes 196616 | tf_op jit(solution)/shard_map/ppermute | solution.py:162
  14.7 7.9 %copy-start = (f32[1,1,128,512]{3,2,1,0:T(8,128)S(1)}, f32[1,1,128,512]{3,2,1,0:T(8,128)}, u32[]{:S(2)}) copy-start(f32[1,1,128,512]{3,2,1,0:T(8,128)} %param.6) | copy-start | bytes 786436
  14.7 7.6 %collective-permute-start.6 = (f32[32,512]{1,0:T(8,128)S(1)}, f32[32,512]{1,0:T(8,128)S(1)}, u32[]{:S(2)}, u32[]{:S(2)}) collective-permute-start(f32[32,512]{1,0:T(8,128)S(1)} %get-tuple-element.15), channel_id=1, source_target_pairs={{0,8},{4,12},{8,0},{12,4},{1,9},{5,13},{9,1},{13,5},{2,10},{6,14},... | collective-permute-start | bytes 196616 | tf_op jit(solution)/shard_map/ppermute | solution.py:162
  16.0 6.3 %collective-permute-start.7 = (f32[32,512]{1,0:T(8,128)S(1)}, f32[32,512]{1,0:T(8,128)S(1)}, u32[]{:S(2)}, u32[]{:S(2)}) collective-permute-start(f32[32,512]{1,0:T(8,128)S(1)} %get-tuple-element.16), channel_id=1, source_target_pairs={{0,4},{4,8},{8,12},{12,0},{1,5},{5,9},{9,13},{13,1},{2,6},{6,10},{... | collective-permute-start | bytes 196616 | tf_op jit(solution)/shard_map/ppermute | solution.py:162
  16.5 6.2 %collective-permute-start.8 = (f32[32,512]{1,0:T(8,128)S(1)}, f32[32,512]{1,0:T(8,128)S(1)}, u32[]{:S(2)}, u32[]{:S(2)}) collective-permute-start(f32[32,512]{1,0:T(8,128)S(1)} %get-tuple-element.17), channel_id=1, source_target_pairs={{0,12},{4,0},{8,4},{12,8},{1,13},{5,1},{9,5},{13,9},{2,14},{6,2},{... | collective-permute-start | bytes 196616 | tf_op jit(solution)/shard_map/ppermute | solution.py:162

commit v22 on v21

--- a/solution.py
+++ b/solution.py
@@ -14,9 +14,8 @@
 PAIRED_MEMBERS = 4
 KERNEL_VMEM = 8 * 2**20
 
-EARLIER_ROUNDS = (("xor", 2), ("xor", 3), ("xor", 1))
-CURRENT_ROUNDS = (("on", 1), ("on", 2), ("on", 3))
-REBUILT_ROUNDS = (("on", 2), ("on", 1), ("on", 3))
+EARLIER_ROUNDS = (("xor", 1), ("xor", 3), ("xor", 2))
+REBUILT_ROUNDS = (("on", 1), ("on", 2), ("on", 3))
 
 
 def target(d, way, n, members):
@@ -66,7 +65,6 @@
     from_earlier = from_current = to_rebuilt = range(members)
     if paired:
         from_earlier = sources_of(EARLIER_ROUNDS, members)
-        from_current = sources_of(CURRENT_ROUNDS, members)
         to_rebuilt = targets_of(REBUILT_ROUNDS, members)
     for i, c in enumerate(from_earlier):
         column = [generator_ref[j, c] for j in range(spans)]
@@ -125,9 +123,8 @@
         out_ref[...] = block
 
 
-def parity_paired_kernel(table_ref, *refs):
-    rows, out_ref, done_ref = refs[:-2], refs[-2], refs[-1]
-    parity_into(out_ref, table_ref, [r[...] for r in rows])
+def parity_paired_kernel(table_ref, rows_ref, out_ref, done_ref):
+    parity_whole_kernel(table_ref, rows_ref, out_ref)
     done_ref[...] = jnp.zeros(done_ref.shape, done_ref.dtype)
 
 
@@ -195,7 +192,8 @@
         block = floats(own_rows, width)
         own_earlier, *cut_earlier = cut(earlier, targets_of(EARLIER_ROUNDS, members))
         earlier_rows = pass_on(cut_earlier, EARLIER_ROUNDS, members)
-        own_current, *cut_current = cut(current, targets_of(CURRENT_ROUNDS, members))
+        current, own_earlier = lax.optimization_barrier((current, own_earlier))
+        current_rows = lax.all_to_all(current, "code", 0, 0, tiled=True)
         outgoing = call(
             rebuild_paired_kernel,
             [IN_VMEM] * (members + 2),
@@ -204,12 +202,11 @@
             rebuild_cost,
         )
         incoming = pass_on(outgoing[1:], REBUILT_ROUNDS, members)
-        current_rows = [own_current, *pass_on(cut_current, CURRENT_ROUNDS, members)]
         new_parity, parity_done = call(
             parity_paired_kernel,
-            [IN_VMEM] * (members + 1),
+            [IN_VMEM] * 2,
             (parity_shape, floats(8, 128)),
-            (table, *current_rows),
+            (table, current_rows),
             parity_cost,
         )
         restored_state = call(

time: 23.6 us -> 31.1 us (1.32)
  waiting for transfers between devices: 2.04 us -> 11.5 us
  starting transfers between devices: 17.4 us -> 14.7 us
  local copies, waits for them, and re-layouts: 1.04 us -> 1.62 us
    ppermute x9 -> x6, waiting for transfers between devices: 2.04 us -> 11.5 us  [pass_on(): lax.ppermute(piece, 'code', [(d, target(d, *way, members)) for d in range...]
    ppermute x9 -> x6, starting transfers between devices: 17.4 us -> 8.26 us  [pass_on(): lax.ppermute(piece, 'code', [(d, target(d, *way, members)) for d in range...]
    all_to_all x0 -> x1, starting transfers between devices: none -> 6.46 us  [local(): current_rows = lax.all_to_all(current, 'code', 0, 0, tiled=True)]
    unnamed x10 -> x8, local copies, waits for them, and re-layouts: 0.02 us -> 0.66 us
    squeeze x2 -> x1, local copies, waits for them, and re-layouts: 1.02 us -> 0.96 us  [cut(): lax.dynamic_index_in_dim(blocks, c, 0, keepdims=False)]
  transfers between devices with their start and end apart: 9 -> 7, of which waited for: 2 -> 5; matrix products, arithmetic and copies ran while one was open for 0% -> 0% of each run, Pallas kernels for 6% -> 5%
where the time goes in v22:
time: 31.1 us; the launch traced here: 30.8 us
  starting transfers between devices  14.7 us (47%)
  waiting for transfers between devices  11.5 us (37%)
  Pallas kernels  2.22 us (7%)
  local copies, waits for them, and re-layouts  1.62 us (5%)
  between operations  0.7 us (2%)
    ppermute x6, waiting for transfers between devices, pass_on(): lax.ppermute(piece, 'code', [(d, target(d, *way, members)) for d in range...  11.5 us
    ppermute x6, starting transfers between devices, pass_on(): lax.ppermute(piece, 'code', [(d, target(d, *way, members)) for d in range...  8.26 us
    all_to_all x1, starting transfers between devices, local(): current_rows = lax.all_to_all(current, 'code', 0, 0, tiled=True)  6.46 us
    pallas_call x4, Pallas kernels, call(): pl.pallas_call(kernel, in_specs=specs, out_specs=jax.tree.map(lambda _: I...  2.22 us
    squeeze x1, local copies, waits for them, and re-layouts, cut(): lax.dynamic_index_in_dim(blocks, c, 0, keepdims=False)  0.96 us
    unnamed x8, local copies, waits for them, and re-layouts  0.66 us
  transfers between devices with their start and end apart: 7, of which 5 were waited for; matrix products, arithmetic and copies ran while one was open for 0% of the time, Pallas kernels for 5%

profile of v22, /device:TPU:0, one launch (start us, length us, event | category | flops | bytes accessed | tf_op | source)
XLA Modules:
  0.0 30.8 jit_solution(9104753871635641054)
XLA Ops:
  0.6 1.0 %dynamic-slice_bitcast_fusion = (f32[32,512]{1,0:T(8,128)S(1)}, f32[32,512]{1,0:T(8,128)S(1)}, f32[32,512]{1,0:T(8,128)S(1)}, f32[32,512]{1,0:T(8,128)S(1)}) fusion(f32[4,32,512]{2,1,0:T(8,128)} %bitcast.13, s32[]{:T(128)S(6)} %select_n.16, s32[]{:T(128)S(6)} %select_n.15, s32[]{:T(128)S(6)} %select_n.14, s32[]{:T(128)S(6)} %select_n.13), kind=kLoop, calls=%fused_computation | loop fusion | bytes 524304 | tf_op jit(solution)/shard_map/jit(dynamic_index_in_dim)/squeeze | solution.py:167
  1.6 0.0 copy-start.1
  1.6 6.5 %all-to-all-start = ((f32[4,32,512]{2,1,0:T(8,128)}), f32[4,32,512]{2,1,0:T(8,128)S(1)}, u32[]{:S(2)}, u32[]{:S(2)}) async-start(f32[4,32,512]{2,1,0:T(8,128)} %bitcast.1), calls=%async_computation | async-start | bytes 524288 | tf_op jit(solution)/shard_map/all_to_all | solution.py:196
  8.1 2.0 %collective-permute-start = (f32[32,512]{1,0:T(8,128)S(1)}, f32[32,512]{1,0:T(8,128)S(1)}, u32[]{:S(2)}, u32[]{:S(2)}) collective-permute-start(f32[32,512]{1,0:T(8,128)S(1)} %get-tuple-element.24), channel_id=1, source_target_pairs={{0,4},{4,0},{8,12},{12,8},{1,5},{5,1},{9,13},{13,9},{2,6},{6,2},{1... | collective-permute-start | bytes 196616 | tf_op jit(solution)/shard_map/ppermute | solution.py:159
  10.1 0.0 copy-start.2
  10.1 2.4 %collective-permute-start.1 = (f32[32,512]{1,0:T(8,128)S(1)}, f32[32,512]{1,0:T(8,128)S(1)}, u32[]{:S(2)}, u32[]{:S(2)}) collective-permute-start(f32[32,512]{1,0:T(8,128)S(1)} %get-tuple-element.23), channel_id=1, source_target_pairs={{0,12},{4,8},{8,4},{12,0},{1,13},{5,9},{9,5},{13,1},{2,14},{6,10},... | collective-permute-start | bytes 196616 | tf_op jit(solution)/shard_map/ppermute | solution.py:159
  12.5 0.0 copy-start.3
  12.5 0.0 collective-permute-start.2
  12.5 0.0 copy-done.1
  12.5 0.0 copy-done.2
  12.5 0.6 %copy-done.3 = s32[1,2]{1,0:T(1,128)S(1)} copy-done((s32[1,2]{1,0:T(1,128)S(1)}, s32[1,2]{1,0:T(1,128)}, u32[]{:S(2)}) %copy-start.3) | copy-done | bytes 32
  13.1 0.6 %shard_map.68 = (f32[2,32,512]{2,1,0:T(8,128)S(1)}, f32[29,512]{1,0:T(8,128)S(1)}) custom-call(s32[1,2]{1,0:T(1,128)S(1)} %copy-done.3, f32[4,4]{1,0:T(4,128)S(1)} %copy-done.2, f32[32,2048]{1,0:T(8,128)S(1)} %bitcast.15), custom_call_target="tpu_custom_call" | custom-call | flops 262144 | bytes 452680 | tf_op jit(solution)/shard_map/pallas_call | solution.py:142
  13.8 1.6 %collective-permute-done.refs_1_ = f32[32,512]{1,0:T(8,128)S(1)} collective-permute-done((f32[32,512]{1,0:T(8,128)S(1)}, f32[32,512]{1,0:T(8,128)S(1)}, u32[]{:S(2)}, u32[]{:S(2)}) %collective-permute-start) | collective-permute-done | bytes 65568 | tf_op jit(solution)/shard_map/ppermute | solution.py:159
  15.4 4.7 %collective-permute-done.1.refs_2_ = f32[32,512]{1,0:T(8,128)S(1)} collective-permute-done((f32[32,512]{1,0:T(8,128)S(1)}, f32[32,512]{1,0:T(8,128)S(1)}, u32[]{:S(2)}, u32[]{:S(2)}) %collective-permute-start.1) | collective-permute-done | bytes 65568 | tf_op jit(solution)/shard_map/ppermute | solution.py:159
  20.1 2.6 %collective-permute-done.2.refs_3_ = f32[32,512]{1,0:T(8,128)S(1)} collective-permute-done((f32[32,512]{1,0:T(8,128)S(1)}, f32[32,512]{1,0:T(8,128)S(1)}, u32[]{:S(2)}, u32[]{:S(2)}) %collective-permute-start.2) | collective-permute-done | bytes 65568 | tf_op jit(solution)/shard_map/ppermute | solution.py:159
  22.6 0.1 shard_map.70
  22.7 0.0 copy-start
  22.7 0.1 collective-permute-start.3
  22.8 2.0 %collective-permute-start.4 = (f32[32,512]{1,0:T(8,128)S(1)}, f32[32,512]{1,0:T(8,128)S(1)}, u32[]{:S(2)}, u32[]{:S(2)}) collective-permute-start(f32[32,512]{1,0:T(8,128)S(1)} %get-tuple-element.20), channel_id=1, source_target_pairs={{0,8},{4,12},{8,0},{12,4},{1,9},{5,13},{9,1},{13,5},{2,10},{6,14},... | collective-permute-start | bytes 196616 | tf_op jit(solution)/shard_map/ppermute | solution.py:159
  24.7 1.8 %collective-permute-start.5 = (f32[32,512]{1,0:T(8,128)S(1)}, f32[32,512]{1,0:T(8,128)S(1)}, u32[]{:S(2)}, u32[]{:S(2)}) collective-permute-start(f32[32,512]{1,0:T(8,128)S(1)} %get-tuple-element.21), channel_id=1, source_target_pairs={{0,12},{4,0},{8,4},{12,8},{1,13},{5,1},{9,5},{13,9},{2,14},{6,2},{... | collective-permute-start | bytes 196616 | tf_op jit(solution)/shard_map/ppermute | solution.py:159
  26.6 0.0 all-to-all-done.rows_ref
  26.6 0.8 %shard_map.69 = (f32[32,2048]{1,0:T(8,128)}, f32[8,128]{1,0:T(8,128)S(1)}) custom-call(f32[29,512]{1,0:T(8,128)S(1)} %get-tuple-element.12.table_ref, f32[4,32,512]{2,1,0:T(8,128)S(1)} %all-to-all-done.rows_ref), custom_call_target="tpu_custom_call" | custom-call | flops 524288 | bytes 587776 | tf_op jit(solution)/shard_map/pallas_call | solution.py:142
  27.4 1.6 %collective-permute-done.3.refs_1_ = f32[32,512]{1,0:T(8,128)S(1)} collective-permute-done((f32[32,512]{1,0:T(8,128)S(1)}, f32[32,512]{1,0:T(8,128)S(1)}, u32[]{:S(2)}, u32[]{:S(2)}) %collective-permute-start.3) | collective-permute-done | bytes 65568 | tf_op jit(solution)/shard_map/ppermute | solution.py:159
  28.9 1.1 %collective-permute-done.4.refs_2_ = f32[32,512]{1,0:T(8,128)S(1)} collective-permute-done((f32[32,512]{1,0:T(8,128)S(1)}, f32[32,512]{1,0:T(8,128)S(1)}, u32[]{:S(2)}, u32[]{:S(2)}) %collective-permute-start.4) | collective-permute-done | bytes 65568 | tf_op jit(solution)/shard_map/ppermute | solution.py:159
  30.1 0.0 collective-permute-done.5.refs_3_
  30.1 0.0 copy-done
  30.1 0.7 %shard_map.71 = f32[4,32,512]{2,1,0:T(8,128)} custom-call(f32[29,512]{1,0:T(8,128)S(1)} %get-tuple-element.12.table_ref, f32[4,32,512]{2,1,0:T(8,128)S(1)} %bitcast.14, f32[8,128]{1,0:T(8,128)S(1)} %get-tuple-element.15.held_back_by, f32[32,512]{1,0:T(8,128)S(1)} %get-tuple-element.18.refs_0_, f32[32,512]{1,0:T(8,128)S(1)} %collective-permute-done.3.refs_1_, ...), custom_call_target="tpu_custom_call" | custom-call | bytes 849920 | tf_op jit(solution)/shard_map/pallas_call | solution.py:142
Async XLA Ops:
  1.6 10.9 %copy-start.1 = (f32[1,32,2048]{2,1,0:T(8,128)S(1)}, f32[1,32,2048]{2,1,0:T(8,128)}, u32[]{:S(2)}) copy-start(f32[1,32,2048]{2,1,0:T(8,128)} %param.7) | copy-start | bytes 786436
  1.6 25.0 %all-to-all-start = ((f32[4,32,512]{2,1,0:T(8,128)}), f32[4,32,512]{2,1,0:T(8,128)S(1)}, u32[]{:S(2)}, u32[]{:S(2)}) async-start(f32[4,32,512]{2,1,0:T(8,128)} %bitcast.1), calls=%async_computation | async-start | bytes 524288 | tf_op jit(solution)/shard_map/all_to_all | solution.py:196
  8.1 7.3 %collective-permute-start = (f32[32,512]{1,0:T(8,128)S(1)}, f32[32,512]{1,0:T(8,128)S(1)}, u32[]{:S(2)}, u32[]{:S(2)}) collective-permute-start(f32[32,512]{1,0:T(8,128)S(1)} %get-tuple-element.24), channel_id=1, source_target_pairs={{0,4},{4,0},{8,12},{12,8},{1,5},{5,1},{9,13},{13,9},{2,6},{6,2},{1... | collective-permute-start | bytes 196616 | tf_op jit(solution)/shard_map/ppermute | solution.py:159
  10.1 2.4 %copy-start.2 = (f32[4,4]{1,0:T(4,128)S(1)}, f32[4,4]{1,0:T(4,128)}, u32[]{:S(2)}) copy-start(f32[4,4]{1,0:T(4,128)} %generator_ref.1) | copy-start | bytes 196
  10.1 9.9 %collective-permute-start.1 = (f32[32,512]{1,0:T(8,128)S(1)}, f32[32,512]{1,0:T(8,128)S(1)}, u32[]{:S(2)}, u32[]{:S(2)}) collective-permute-start(f32[32,512]{1,0:T(8,128)S(1)} %get-tuple-element.23), channel_id=1, source_target_pairs={{0,12},{4,8},{8,4},{12,0},{1,13},{5,9},{9,5},{13,1},{2,14},{6,10},... | collective-permute-start | bytes 196616 | tf_op jit(solution)/shard_map/ppermute | solution.py:159
  12.5 0.7 %copy-start.3 = (s32[1,2]{1,0:T(1,128)S(1)}, s32[1,2]{1,0:T(1,128)}, u32[]{:S(2)}) copy-start(s32[1,2]{1,0:T(1,128)} %ids_ref.1) | copy-start | bytes 28
  12.5 10.1 %collective-permute-start.2 = (f32[32,512]{1,0:T(8,128)S(1)}, f32[32,512]{1,0:T(8,128)S(1)}, u32[]{:S(2)}, u32[]{:S(2)}) collective-permute-start(f32[32,512]{1,0:T(8,128)S(1)} %get-tuple-element.22), channel_id=1, source_target_pairs={{0,8},{4,12},{8,0},{12,4},{1,9},{5,13},{9,1},{13,5},{2,10},{6,14},... | collective-permute-start | bytes 196616 | tf_op jit(solution)/shard_map/ppermute | solution.py:159
  22.7 7.4 %copy-start = (f32[1,1,128,512]{3,2,1,0:T(8,128)S(1)}, f32[1,1,128,512]{3,2,1,0:T(8,128)}, u32[]{:S(2)}) copy-start(f32[1,1,128,512]{3,2,1,0:T(8,128)} %param.6) | copy-start | bytes 786436
  22.7 6.2 %collective-permute-start.3 = (f32[32,512]{1,0:T(8,128)S(1)}, f32[32,512]{1,0:T(8,128)S(1)}, u32[]{:S(2)}, u32[]{:S(2)}) collective-permute-start(f32[32,512]{1,0:T(8,128)S(1)} %get-tuple-element.19), channel_id=1, source_target_pairs={{0,4},{4,8},{8,12},{12,0},{1,5},{5,9},{9,13},{13,1},{2,6},{6,10},{... | collective-permute-start | bytes 196616 | tf_op jit(solution)/shard_map/ppermute | solution.py:159
  22.8 7.3 %collective-permute-start.4 = (f32[32,512]{1,0:T(8,128)S(1)}, f32[32,512]{1,0:T(8,128)S(1)}, u32[]{:S(2)}, u32[]{:S(2)}) collective-permute-start(f32[32,512]{1,0:T(8,128)S(1)} %get-tuple-element.20), channel_id=1, source_target_pairs={{0,8},{4,12},{8,0},{12,4},{1,9},{5,13},{9,1},{13,5},{2,10},{6,14},... | collective-permute-start | bytes 196616 | tf_op jit(solution)/shard_map/ppermute | solution.py:159
  24.7 5.3 %collective-permute-start.5 = (f32[32,512]{1,0:T(8,128)S(1)}, f32[32,512]{1,0:T(8,128)S(1)}, u32[]{:S(2)}, u32[]{:S(2)}) collective-permute-start(f32[32,512]{1,0:T(8,128)S(1)} %get-tuple-element.21), channel_id=1, source_target_pairs={{0,12},{4,0},{8,4},{12,8},{1,13},{5,1},{9,5},{13,9},{2,14},{6,2},{... | collective-permute-start | bytes 196616 | tf_op jit(solution)/shard_map/ppermute | solution.py:159

commit v23 on v21

--- a/solution.py
+++ b/solution.py
@@ -15,8 +15,8 @@
 KERNEL_VMEM = 8 * 2**20
 
 EARLIER_ROUNDS = (("xor", 2), ("xor", 3), ("xor", 1))
-CURRENT_ROUNDS = (("on", 1), ("on", 2), ("on", 3))
-REBUILT_ROUNDS = (("on", 2), ("on", 1), ("on", 3))
+CURRENT_ROUNDS = (("on", 1), ("on", 3), ("on", 2))
+REBUILT_ROUNDS = (("on", 1), ("on", 2), ("on", 3))
 
 
 def target(d, way, n, members):

time: 23.6 us -> 23.6 us (level)
  starting transfers between devices: 17.4 us -> 16.1 us
  waiting for transfers between devices: 2.04 us -> 3.29 us
    ppermute x9, waiting for transfers between devices: 2.04 us -> 3.29 us  [pass_on(): lax.ppermute(piece, 'code', [(d, target(d, *way, members)) for d in range...]
    ppermute x9, starting transfers between devices: 17.4 us -> 16.1 us  [pass_on(): lax.ppermute(piece, 'code', [(d, target(d, *way, members)) for d in range...]
  transfers between devices with their start and end apart: 9 -> 9, of which waited for: 2 -> 3; matrix products, arithmetic and copies ran while one was open for 0% -> 0% of each run, Pallas kernels for 6% -> 6%
where the time goes in v23:
time: 23.6 us; the launch traced here: 23.4 us
  starting transfers between devices  16.1 us (68%)
  waiting for transfers between devices  3.29 us (14%)
  Pallas kernels  2.24 us (9%)
  local copies, waits for them, and re-layouts  1.04 us (4%)
  between operations  0.71 us (3%)
    ppermute x9, starting transfers between devices, pass_on(): lax.ppermute(piece, 'code', [(d, target(d, *way, members)) for d in range...  16.1 us
    ppermute x9, waiting for transfers between devices, pass_on(): lax.ppermute(piece, 'code', [(d, target(d, *way, members)) for d in range...  3.29 us
    pallas_call x4, Pallas kernels, call(): pl.pallas_call(kernel, in_specs=specs, out_specs=jax.tree.map(lambda _: I...  2.24 us
    squeeze x2, local copies, waits for them, and re-layouts, cut(): lax.dynamic_index_in_dim(blocks, c, 0, keepdims=False)  1.02 us
  transfers between devices with their start and end apart: 9, of which 3 were waited for; matrix products, arithmetic and copies ran while one was open for 0% of the time, Pallas kernels for 6%

profile of v23, /device:TPU:0, one launch (start us, length us, event | category | flops | bytes accessed | tf_op | source)
XLA Modules:
  0.0 23.4 jit_solution(11268398684904755303)
XLA Ops:
  0.6 0.0 copy-start.4
  0.7 1.0 %dynamic-slice_bitcast_fusion = (f32[32,512]{1,0:T(8,128)S(1)}, f32[32,512]{1,0:T(8,128)S(1)}, f32[32,512]{1,0:T(8,128)S(1)}, f32[32,512]{1,0:T(8,128)S(1)}) fusion(f32[4,32,512]{2,1,0:T(8,128)} %bitcast.21, s32[]{:T(128)S(6)} %select_n.47, s32[]{:T(128)S(6)} %select_n.46, s32[]{:T(128)S(6)} %select_n.45, s32[]{:T(128)S(6)} %select_n.38), kind=kLoop, calls=%fused_computation | loop fusion | bytes 524304 | tf_op jit(solution)/shard_map/jit(dynamic_index_in_dim)/squeeze | solution.py:170
  1.7 4.1 %collective-permute-start.3 = (f32[32,512]{1,0:T(8,128)S(1)}, f32[32,512]{1,0:T(8,128)S(1)}, u32[]{:S(2)}, u32[]{:S(2)}) collective-permute-start(f32[32,512]{1,0:T(8,128)S(1)} %get-tuple-element.20), channel_id=1, source_target_pairs={{0,8},{4,12},{8,0},{12,4},{1,9},{5,13},{9,1},{13,5},{2,10},{6,14},... | collective-permute-start | bytes 196616 | tf_op jit(solution)/shard_map/ppermute | solution.py:162
  5.8 1.3 %collective-permute-start.4 = (f32[32,512]{1,0:T(8,128)S(1)}, f32[32,512]{1,0:T(8,128)S(1)}, u32[]{:S(2)}, u32[]{:S(2)}) collective-permute-start(f32[32,512]{1,0:T(8,128)S(1)} %get-tuple-element.19), channel_id=1, source_target_pairs={{0,12},{4,8},{8,4},{12,0},{1,13},{5,9},{9,5},{13,1},{2,14},{6,10},... | collective-permute-start | bytes 196616 | tf_op jit(solution)/shard_map/ppermute | solution.py:162
  7.1 0.2 collective-permute-start.5
  7.3 0.0 copy-done.4
  7.3 0.0 copy-start.1
  7.4 0.0 copy-start.2
  7.4 1.8 %collective-permute-start = (f32[32,512]{1,0:T(8,128)S(1)}, f32[32,512]{1,0:T(8,128)S(1)}, u32[]{:S(2)}, u32[]{:S(2)}) collective-permute-start(f32[32,512]{1,0:T(8,128)S(1)} %get-tuple-element.24), channel_id=1, source_target_pairs={{0,4},{4,8},{8,12},{12,0},{1,5},{5,9},{9,13},{13,1},{2,6},{6,10},{... | collective-permute-start | bytes 196616 | tf_op jit(solution)/shard_map/ppermute | solution.py:162
  9.2 0.0 copy-start.3
  9.2 2.0 %collective-permute-start.1 = (f32[32,512]{1,0:T(8,128)S(1)}, f32[32,512]{1,0:T(8,128)S(1)}, u32[]{:S(2)}, u32[]{:S(2)}) collective-permute-start(f32[32,512]{1,0:T(8,128)S(1)} %get-tuple-element.23), channel_id=1, source_target_pairs={{0,12},{4,0},{8,4},{12,8},{1,13},{5,1},{9,5},{13,9},{2,14},{6,2},{... | collective-permute-start | bytes 196616 | tf_op jit(solution)/shard_map/ppermute | solution.py:162
  11.3 0.0 copy-done.1
  11.3 0.0 copy-done.2
  11.3 0.0 copy-done.3
  11.3 0.7 %shard_map.68 = (f32[2,32,512]{2,1,0:T(8,128)S(1)}, f32[29,512]{1,0:T(8,128)S(1)}) custom-call(s32[1,2]{1,0:T(1,128)S(1)} %copy-done.3, f32[4,4]{1,0:T(4,128)S(1)} %copy-done.2, f32[32,2048]{1,0:T(8,128)S(1)} %bitcast.23), custom_call_target="tpu_custom_call" | custom-call | flops 262144 | bytes 452680 | tf_op jit(solution)/shard_map/pallas_call | solution.py:145
  11.9 0.0 collective-permute-done.3.refs_1_
  11.9 1.1 %collective-permute-start.2 = (f32[32,512]{1,0:T(8,128)S(1)}, f32[32,512]{1,0:T(8,128)S(1)}, u32[]{:S(2)}, u32[]{:S(2)}) collective-permute-start(f32[32,512]{1,0:T(8,128)S(1)} %get-tuple-element.22), channel_id=1, source_target_pairs={{0,8},{4,12},{8,0},{12,4},{1,9},{5,13},{9,1},{13,5},{2,10},{6,14},... | collective-permute-start | bytes 196616 | tf_op jit(solution)/shard_map/ppermute | solution.py:162
  13.0 0.0 collective-permute-done.4.refs_2_
  13.0 0.3 %collective-permute-done.5.refs_3_ = f32[32,512]{1,0:T(8,128)S(1)} collective-permute-done((f32[32,512]{1,0:T(8,128)S(1)}, f32[32,512]{1,0:T(8,128)S(1)}, u32[]{:S(2)}, u32[]{:S(2)}) %collective-permute-start.5) | collective-permute-done | bytes 65568 | tf_op jit(solution)/shard_map/ppermute | solution.py:162
  13.4 0.1 shard_map.70
  13.4 0.0 copy-start
  13.4 1.9 %collective-permute-start.6 = (f32[32,512]{1,0:T(8,128)S(1)}, f32[32,512]{1,0:T(8,128)S(1)}, u32[]{:S(2)}, u32[]{:S(2)}) collective-permute-start(f32[32,512]{1,0:T(8,128)S(1)} %get-tuple-element.15), channel_id=1, source_target_pairs={{0,4},{4,8},{8,12},{12,0},{1,5},{5,9},{9,13},{13,1},{2,6},{6,10},{... | collective-permute-start | bytes 196616 | tf_op jit(solution)/shard_map/ppermute | solution.py:162
  15.4 1.6 %collective-permute-start.7 = (f32[32,512]{1,0:T(8,128)S(1)}, f32[32,512]{1,0:T(8,128)S(1)}, u32[]{:S(2)}, u32[]{:S(2)}) collective-permute-start(f32[32,512]{1,0:T(8,128)S(1)} %get-tuple-element.16), channel_id=1, source_target_pairs={{0,8},{4,12},{8,0},{12,4},{1,9},{5,13},{9,1},{13,5},{2,10},{6,14},... | collective-permute-start | bytes 196616 | tf_op jit(solution)/shard_map/ppermute | solution.py:162
  17.0 0.0 collective-permute-done.refs_1_
  17.0 2.0 %collective-permute-start.8 = (f32[32,512]{1,0:T(8,128)S(1)}, f32[32,512]{1,0:T(8,128)S(1)}, u32[]{:S(2)}, u32[]{:S(2)}) collective-permute-start(f32[32,512]{1,0:T(8,128)S(1)} %get-tuple-element.17), channel_id=1, source_target_pairs={{0,12},{4,0},{8,4},{12,8},{1,13},{5,1},{9,5},{13,9},{2,14},{6,2},{... | collective-permute-start | bytes 196616 | tf_op jit(solution)/shard_map/ppermute | solution.py:162
  19.0 0.0 collective-permute-done.1.refs_2_
  19.0 1.6 %collective-permute-done.2.refs_3_ = f32[32,512]{1,0:T(8,128)S(1)} collective-permute-done((f32[32,512]{1,0:T(8,128)S(1)}, f32[32,512]{1,0:T(8,128)S(1)}, u32[]{:S(2)}, u32[]{:S(2)}) %collective-permute-start.2) | collective-permute-done | bytes 65568 | tf_op jit(solution)/shard_map/ppermute | solution.py:162
  20.6 0.8 %shard_map.69 = (f32[32,2048]{1,0:T(8,128)}, f32[8,128]{1,0:T(8,128)S(1)}) custom-call(f32[29,512]{1,0:T(8,128)S(1)} %get-tuple-element.10.table_ref, f32[32,512]{1,0:T(8,128)S(1)} %get-tuple-element.25.refs_0_, f32[32,512]{1,0:T(8,128)S(1)} %collective-permute-done.refs_1_, f32[32,512]{1,0:T(8,128)S(1)} %collective-permute-done.1.refs_2_, ...), custom_call_target="tpu_custom_call" | custom-call | flops 524288 | bytes 587776 | tf_op jit(solution)/shard_map/pallas_call | solution.py:145
  21.4 0.0 collective-permute-done.6.refs_1_
  21.4 1.3 %collective-permute-done.7.refs_2_ = f32[32,512]{1,0:T(8,128)S(1)} collective-permute-done((f32[32,512]{1,0:T(8,128)S(1)}, f32[32,512]{1,0:T(8,128)S(1)}, u32[]{:S(2)}, u32[]{:S(2)}) %collective-permute-start.7) | collective-permute-done | bytes 65568 | tf_op jit(solution)/shard_map/ppermute | solution.py:162
  22.7 0.0 collective-permute-done.8.refs_3_
  22.7 0.0 copy-done
  22.7 0.7 %shard_map.71 = f32[4,32,512]{2,1,0:T(8,128)} custom-call(f32[29,512]{1,0:T(8,128)S(1)} %get-tuple-element.10.table_ref, f32[4,32,512]{2,1,0:T(8,128)S(1)} %bitcast.22, f32[8,128]{1,0:T(8,128)S(1)} %get-tuple-element.12.held_back_by, f32[32,512]{1,0:T(8,128)S(1)} %get-tuple-element.14.refs_0_, f32[32,512]{1,0:T(8,128)S(1)} %collective-permute-done.6.refs_1_, ...), custom_call_target="tpu_custom_call" | custom-call | bytes 849920 | tf_op jit(solution)/shard_map/pallas_call | solution.py:145
  (1 shorter events, 0.0 us)
Async XLA Ops:
  0.6 6.7 %copy-start.4 = (f32[1,1,128,512]{3,2,1,0:T(8,128)S(1)}, f32[1,1,128,512]{3,2,1,0:T(8,128)}, u32[]{:S(2)}) copy-start(f32[1,1,128,512]{3,2,1,0:T(8,128)} %param.5) | copy-start | bytes 786436
  1.7 10.3 %collective-permute-start.3 = (f32[32,512]{1,0:T(8,128)S(1)}, f32[32,512]{1,0:T(8,128)S(1)}, u32[]{:S(2)}, u32[]{:S(2)}) collective-permute-start(f32[32,512]{1,0:T(8,128)S(1)} %get-tuple-element.20), channel_id=1, source_target_pairs={{0,8},{4,12},{8,0},{12,4},{1,9},{5,13},{9,1},{13,5},{2,10},{6,14},... | collective-permute-start | bytes 196616 | tf_op jit(solution)/shard_map/ppermute | solution.py:162
  5.8 7.3 %collective-permute-start.4 = (f32[32,512]{1,0:T(8,128)S(1)}, f32[32,512]{1,0:T(8,128)S(1)}, u32[]{:S(2)}, u32[]{:S(2)}) collective-permute-start(f32[32,512]{1,0:T(8,128)S(1)} %get-tuple-element.19), channel_id=1, source_target_pairs={{0,12},{4,8},{8,4},{12,0},{1,13},{5,9},{9,5},{13,1},{2,14},{6,10},... | collective-permute-start | bytes 196616 | tf_op jit(solution)/shard_map/ppermute | solution.py:162
  7.1 6.3 %collective-permute-start.5 = (f32[32,512]{1,0:T(8,128)S(1)}, f32[32,512]{1,0:T(8,128)S(1)}, u32[]{:S(2)}, u32[]{:S(2)}) collective-permute-start(f32[32,512]{1,0:T(8,128)S(1)} %get-tuple-element.18), channel_id=1, source_target_pairs={{0,4},{4,0},{8,12},{12,8},{1,5},{5,1},{9,13},{13,9},{2,6},{6,2},{1... | collective-permute-start | bytes 196616 | tf_op jit(solution)/shard_map/ppermute | solution.py:162
  7.3 3.9 %copy-start.1 = (f32[1,32,2048]{2,1,0:T(8,128)S(1)}, f32[1,32,2048]{2,1,0:T(8,128)}, u32[]{:S(2)}) copy-start(f32[1,32,2048]{2,1,0:T(8,128)} %param.7) | copy-start | bytes 786436
  7.4 3.9 %copy-start.2 = (f32[4,4]{1,0:T(4,128)S(1)}, f32[4,4]{1,0:T(4,128)}, u32[]{:S(2)}) copy-start(f32[4,4]{1,0:T(4,128)} %generator_ref.1) | copy-start | bytes 196
  7.4 9.6 %collective-permute-start = (f32[32,512]{1,0:T(8,128)S(1)}, f32[32,512]{1,0:T(8,128)S(1)}, u32[]{:S(2)}, u32[]{:S(2)}) collective-permute-start(f32[32,512]{1,0:T(8,128)S(1)} %get-tuple-element.24), channel_id=1, source_target_pairs={{0,4},{4,8},{8,12},{12,0},{1,5},{5,9},{9,13},{13,1},{2,6},{6,10},{... | collective-permute-start | bytes 196616 | tf_op jit(solution)/shard_map/ppermute | solution.py:162
  9.2 2.0 %copy-start.3 = (s32[1,2]{1,0:T(1,128)S(1)}, s32[1,2]{1,0:T(1,128)}, u32[]{:S(2)}) copy-start(s32[1,2]{1,0:T(1,128)} %ids_ref.1) | copy-start | bytes 28
  9.2 9.7 %collective-permute-start.1 = (f32[32,512]{1,0:T(8,128)S(1)}, f32[32,512]{1,0:T(8,128)S(1)}, u32[]{:S(2)}, u32[]{:S(2)}) collective-permute-start(f32[32,512]{1,0:T(8,128)S(1)} %get-tuple-element.23), channel_id=1, source_target_pairs={{0,12},{4,0},{8,4},{12,8},{1,13},{5,1},{9,5},{13,9},{2,14},{6,2},{... | collective-permute-start | bytes 196616 | tf_op jit(solution)/shard_map/ppermute | solution.py:162
  11.9 8.6 %collective-permute-start.2 = (f32[32,512]{1,0:T(8,128)S(1)}, f32[32,512]{1,0:T(8,128)S(1)}, u32[]{:S(2)}, u32[]{:S(2)}) collective-permute-start(f32[32,512]{1,0:T(8,128)S(1)} %get-tuple-element.22), channel_id=1, source_target_pairs={{0,8},{4,12},{8,0},{12,4},{1,9},{5,13},{9,1},{13,5},{2,10},{6,14},... | collective-permute-start | bytes 196616 | tf_op jit(solution)/shard_map/ppermute | solution.py:162
  13.4 9.2 %copy-start = (f32[1,1,128,512]{3,2,1,0:T(8,128)S(1)}, f32[1,1,128,512]{3,2,1,0:T(8,128)}, u32[]{:S(2)}) copy-start(f32[1,1,128,512]{3,2,1,0:T(8,128)} %param.6) | copy-start | bytes 786436
  13.4 7.9 %collective-permute-start.6 = (f32[32,512]{1,0:T(8,128)S(1)}, f32[32,512]{1,0:T(8,128)S(1)}, u32[]{:S(2)}, u32[]{:S(2)}) collective-permute-start(f32[32,512]{1,0:T(8,128)S(1)} %get-tuple-element.15), channel_id=1, source_target_pairs={{0,4},{4,8},{8,12},{12,0},{1,5},{5,9},{9,13},{13,1},{2,6},{6,10},{... | collective-permute-start | bytes 196616 | tf_op jit(solution)/shard_map/ppermute | solution.py:162
  15.4 7.3 %collective-permute-start.7 = (f32[32,512]{1,0:T(8,128)S(1)}, f32[32,512]{1,0:T(8,128)S(1)}, u32[]{:S(2)}, u32[]{:S(2)}) collective-permute-start(f32[32,512]{1,0:T(8,128)S(1)} %get-tuple-element.16), channel_id=1, source_target_pairs={{0,8},{4,12},{8,0},{12,4},{1,9},{5,13},{9,1},{13,5},{2,10},{6,14},... | collective-permute-start | bytes 196616 | tf_op jit(solution)/shard_map/ppermute | solution.py:162
  17.0 5.7 %collective-permute-start.8 = (f32[32,512]{1,0:T(8,128)S(1)}, f32[32,512]{1,0:T(8,128)S(1)}, u32[]{:S(2)}, u32[]{:S(2)}) collective-permute-start(f32[32,512]{1,0:T(8,128)S(1)} %get-tuple-element.17), channel_id=1, source_target_pairs={{0,12},{4,0},{8,4},{12,8},{1,13},{5,1},{9,5},{13,9},{2,14},{6,2},{... | collective-permute-start | bytes 196616 | tf_op jit(solution)/shard_map/ppermute | solution.py:162

commit v24 on v23

--- a/solution.py
+++ b/solution.py
@@ -15,7 +15,7 @@
 KERNEL_VMEM = 8 * 2**20
 
 EARLIER_ROUNDS = (("xor", 2), ("xor", 3), ("xor", 1))
-CURRENT_ROUNDS = (("on", 1), ("on", 3), ("on", 2))
+CURRENT_ROUNDS = (("xor", 3), ("xor", 2), ("xor", 1))
 REBUILT_ROUNDS = (("on", 1), ("on", 2), ("on", 3))
 
 

time: 23.6 us -> 23.8 us (level)
  starting transfers between devices: 16.1 us -> 18.1 us
  waiting for transfers between devices: 3.29 us -> 1.32 us
  local copies, waits for them, and re-layouts: 1.04 us -> 1.35 us
    ppermute x9, waiting for transfers between devices: 3.29 us -> 1.32 us  [pass_on(): lax.ppermute(piece, 'code', [(d, target(d, *way, members)) for d in range...]
    ppermute x9, starting transfers between devices: 16.1 us -> 18.1 us  [pass_on(): lax.ppermute(piece, 'code', [(d, target(d, *way, members)) for d in range...]
    unnamed x10, local copies, waits for them, and re-layouts: 0.02 us -> 0.33 us
  transfers between devices with their start and end apart: 9 -> 9, of which waited for: 3 -> 4; matrix products, arithmetic and copies ran while one was open for 0% -> 0% of each run, Pallas kernels for 6% -> 6%
where the time goes in v24:
time: 23.8 us; the launch traced here: 23.7 us
  starting transfers between devices  18.1 us (76%)
  Pallas kernels  2.24 us (9%)
  local copies, waits for them, and re-layouts  1.35 us (6%)
  waiting for transfers between devices  1.32 us (6%)
  between operations  0.71 us (3%)
    ppermute x9, starting transfers between devices, pass_on(): lax.ppermute(piece, 'code', [(d, target(d, *way, members)) for d in range...  18.1 us
    pallas_call x4, Pallas kernels, call(): pl.pallas_call(kernel, in_specs=specs, out_specs=jax.tree.map(lambda _: I...  2.24 us
    ppermute x9, waiting for transfers between devices, pass_on(): lax.ppermute(piece, 'code', [(d, target(d, *way, members)) for d in range...  1.32 us
    squeeze x2, local copies, waits for them, and re-layouts, cut(): lax.dynamic_index_in_dim(blocks, c, 0, keepdims=False)  1.02 us
  transfers between devices with their start and end apart: 9, of which 4 were waited for; matrix products, arithmetic and copies ran while one was open for 0% of the time, Pallas kernels for 6%

profile of v24, /device:TPU:0, one launch (start us, length us, event | category | flops | bytes accessed | tf_op | source)
XLA Modules:
  0.0 23.7 jit_solution(12931926666908957065)
XLA Ops:
  0.6 0.0 copy-start.4
  0.7 1.0 %dynamic-slice_bitcast_fusion = (f32[32,512]{1,0:T(8,128)S(1)}, f32[32,512]{1,0:T(8,128)S(1)}, f32[32,512]{1,0:T(8,128)S(1)}, f32[32,512]{1,0:T(8,128)S(1)}) fusion(f32[4,32,512]{2,1,0:T(8,128)} %bitcast.21, s32[]{:T(128)S(6)} %select_n.20, s32[]{:T(128)S(6)} %select_n.18, s32[]{:T(128)S(6)} %select_n.19, s32[]{:T(128)S(6)} %select_n.17), kind=kLoop, calls=%fused_computation | loop fusion | bytes 524304 | tf_op jit(solution)/shard_map/jit(dynamic_index_in_dim)/squeeze | solution.py:170
  1.7 4.1 %collective-permute-start.3 = (f32[32,512]{1,0:T(8,128)S(1)}, f32[32,512]{1,0:T(8,128)S(1)}, u32[]{:S(2)}, u32[]{:S(2)}) collective-permute-start(f32[32,512]{1,0:T(8,128)S(1)} %get-tuple-element.20), channel_id=1, source_target_pairs={{0,8},{4,12},{8,0},{12,4},{1,9},{5,13},{9,1},{13,5},{2,10},{6,14},... | collective-permute-start | bytes 196616 | tf_op jit(solution)/shard_map/ppermute | solution.py:162
  5.8 1.3 %collective-permute-start.4 = (f32[32,512]{1,0:T(8,128)S(1)}, f32[32,512]{1,0:T(8,128)S(1)}, u32[]{:S(2)}, u32[]{:S(2)}) collective-permute-start(f32[32,512]{1,0:T(8,128)S(1)} %get-tuple-element.19), channel_id=1, source_target_pairs={{0,12},{4,8},{8,4},{12,0},{1,13},{5,9},{9,5},{13,1},{2,14},{6,10},... | collective-permute-start | bytes 196616 | tf_op jit(solution)/shard_map/ppermute | solution.py:162
  7.1 0.2 collective-permute-start.5
  7.3 0.0 copy-done.4
  7.3 0.0 copy-start.1
  7.4 0.0 copy-start.2
  7.4 3.0 %collective-permute-start = (f32[32,512]{1,0:T(8,128)S(1)}, f32[32,512]{1,0:T(8,128)S(1)}, u32[]{:S(2)}, u32[]{:S(2)}) collective-permute-start(f32[32,512]{1,0:T(8,128)S(1)} %get-tuple-element.24), channel_id=1, source_target_pairs={{0,12},{4,8},{8,4},{12,0},{1,13},{5,9},{9,5},{13,1},{2,14},{6,10},... | collective-permute-start | bytes 196616 | tf_op jit(solution)/shard_map/ppermute | solution.py:162
  10.4 0.0 copy-start.3
  10.4 0.3 %collective-permute-start.1 = (f32[32,512]{1,0:T(8,128)S(1)}, f32[32,512]{1,0:T(8,128)S(1)}, u32[]{:S(2)}, u32[]{:S(2)}) collective-permute-start(f32[32,512]{1,0:T(8,128)S(1)} %get-tuple-element.23), channel_id=1, source_target_pairs={{0,8},{4,12},{8,0},{12,4},{1,9},{5,13},{9,1},{13,5},{2,10},{6,14},... | collective-permute-start | bytes 196616 | tf_op jit(solution)/shard_map/ppermute | solution.py:162
  10.7 0.0 copy-done.1
  10.7 0.0 copy-done.2
  10.7 0.3 %copy-done.3 = s32[1,2]{1,0:T(1,128)S(1)} copy-done((s32[1,2]{1,0:T(1,128)S(1)}, s32[1,2]{1,0:T(1,128)}, u32[]{:S(2)}) %copy-start.3) | copy-done | bytes 32
  11.0 0.7 %shard_map.68 = (f32[2,32,512]{2,1,0:T(8,128)S(1)}, f32[29,512]{1,0:T(8,128)S(1)}) custom-call(s32[1,2]{1,0:T(1,128)S(1)} %copy-done.3, f32[4,4]{1,0:T(4,128)S(1)} %copy-done.2, f32[32,2048]{1,0:T(8,128)S(1)} %bitcast.23), custom_call_target="tpu_custom_call" | custom-call | flops 262144 | bytes 452680 | tf_op jit(solution)/shard_map/pallas_call | solution.py:145
  11.7 0.0 collective-permute-done.3.refs_1_
  11.7 0.9 %collective-permute-start.2 = (f32[32,512]{1,0:T(8,128)S(1)}, f32[32,512]{1,0:T(8,128)S(1)}, u32[]{:S(2)}, u32[]{:S(2)}) collective-permute-start(f32[32,512]{1,0:T(8,128)S(1)} %get-tuple-element.22), channel_id=1, source_target_pairs={{0,4},{4,0},{8,12},{12,8},{1,5},{5,1},{9,13},{13,9},{2,6},{6,2},{1... | collective-permute-start | bytes 196616 | tf_op jit(solution)/shard_map/ppermute | solution.py:162
  12.6 0.1 collective-permute-done.4.refs_2_
  12.7 0.1 collective-permute-done.5.refs_3_
  12.8 0.1 shard_map.70
  12.8 0.0 copy-start
  12.9 3.2 %collective-permute-start.6 = (f32[32,512]{1,0:T(8,128)S(1)}, f32[32,512]{1,0:T(8,128)S(1)}, u32[]{:S(2)}, u32[]{:S(2)}) collective-permute-start(f32[32,512]{1,0:T(8,128)S(1)} %get-tuple-element.15), channel_id=1, source_target_pairs={{0,4},{4,8},{8,12},{12,0},{1,5},{5,9},{9,13},{13,1},{2,6},{6,10},{... | collective-permute-start | bytes 196616 | tf_op jit(solution)/shard_map/ppermute | solution.py:162
  16.0 2.1 %collective-permute-start.7 = (f32[32,512]{1,0:T(8,128)S(1)}, f32[32,512]{1,0:T(8,128)S(1)}, u32[]{:S(2)}, u32[]{:S(2)}) collective-permute-start(f32[32,512]{1,0:T(8,128)S(1)} %get-tuple-element.16), channel_id=1, source_target_pairs={{0,8},{4,12},{8,0},{12,4},{1,9},{5,13},{9,1},{13,5},{2,10},{6,14},... | collective-permute-start | bytes 196616 | tf_op jit(solution)/shard_map/ppermute | solution.py:162
  18.2 0.0 collective-permute-done.refs_1_
  18.2 2.8 %collective-permute-start.8 = (f32[32,512]{1,0:T(8,128)S(1)}, f32[32,512]{1,0:T(8,128)S(1)}, u32[]{:S(2)}, u32[]{:S(2)}) collective-permute-start(f32[32,512]{1,0:T(8,128)S(1)} %get-tuple-element.17), channel_id=1, source_target_pairs={{0,12},{4,0},{8,4},{12,8},{1,13},{5,1},{9,5},{13,9},{2,14},{6,2},{... | collective-permute-start | bytes 196616 | tf_op jit(solution)/shard_map/ppermute | solution.py:162
  21.0 0.0 collective-permute-done.1.refs_2_
  21.0 0.0 collective-permute-done.2.refs_3_
  21.0 0.8 %shard_map.69 = (f32[32,2048]{1,0:T(8,128)}, f32[8,128]{1,0:T(8,128)S(1)}) custom-call(f32[29,512]{1,0:T(8,128)S(1)} %get-tuple-element.10.table_ref, f32[32,512]{1,0:T(8,128)S(1)} %get-tuple-element.25.refs_0_, f32[32,512]{1,0:T(8,128)S(1)} %collective-permute-done.refs_1_, f32[32,512]{1,0:T(8,128)S(1)} %collective-permute-done.1.refs_2_, ...), custom_call_target="tpu_custom_call" | custom-call | flops 524288 | bytes 587776 | tf_op jit(solution)/shard_map/pallas_call | solution.py:145
  21.8 0.0 collective-permute-done.6.refs_1_
  21.8 0.3 %collective-permute-done.7.refs_2_ = f32[32,512]{1,0:T(8,128)S(1)} collective-permute-done((f32[32,512]{1,0:T(8,128)S(1)}, f32[32,512]{1,0:T(8,128)S(1)}, u32[]{:S(2)}, u32[]{:S(2)}) %collective-permute-start.7) | collective-permute-done | bytes 65568 | tf_op jit(solution)/shard_map/ppermute | solution.py:162
  22.2 0.8 %collective-permute-done.8.refs_3_ = f32[32,512]{1,0:T(8,128)S(1)} collective-permute-done((f32[32,512]{1,0:T(8,128)S(1)}, f32[32,512]{1,0:T(8,128)S(1)}, u32[]{:S(2)}, u32[]{:S(2)}) %collective-permute-start.8) | collective-permute-done | bytes 65568 | tf_op jit(solution)/shard_map/ppermute | solution.py:162
  22.9 0.0 copy-done
  22.9 0.7 %shard_map.71 = f32[4,32,512]{2,1,0:T(8,128)} custom-call(f32[29,512]{1,0:T(8,128)S(1)} %get-tuple-element.10.table_ref, f32[4,32,512]{2,1,0:T(8,128)S(1)} %bitcast.22, f32[8,128]{1,0:T(8,128)S(1)} %get-tuple-element.12.held_back_by, f32[32,512]{1,0:T(8,128)S(1)} %get-tuple-element.14.refs_0_, f32[32,512]{1,0:T(8,128)S(1)} %collective-permute-done.6.refs_1_, ...), custom_call_target="tpu_custom_call" | custom-call | bytes 849920 | tf_op jit(solution)/shard_map/pallas_call | solution.py:145
  (1 shorter events, 0.0 us)
Async XLA Ops:
  0.6 6.7 %copy-start.4 = (f32[1,1,128,512]{3,2,1,0:T(8,128)S(1)}, f32[1,1,128,512]{3,2,1,0:T(8,128)}, u32[]{:S(2)}) copy-start(f32[1,1,128,512]{3,2,1,0:T(8,128)} %param.5) | copy-start | bytes 786436
  1.7 10.0 %collective-permute-start.3 = (f32[32,512]{1,0:T(8,128)S(1)}, f32[32,512]{1,0:T(8,128)S(1)}, u32[]{:S(2)}, u32[]{:S(2)}) collective-permute-start(f32[32,512]{1,0:T(8,128)S(1)} %get-tuple-element.20), channel_id=1, source_target_pairs={{0,8},{4,12},{8,0},{12,4},{1,9},{5,13},{9,1},{13,5},{2,10},{6,14},... | collective-permute-start | bytes 196616 | tf_op jit(solution)/shard_map/ppermute | solution.py:162
  5.8 6.9 %collective-permute-start.4 = (f32[32,512]{1,0:T(8,128)S(1)}, f32[32,512]{1,0:T(8,128)S(1)}, u32[]{:S(2)}, u32[]{:S(2)}) collective-permute-start(f32[32,512]{1,0:T(8,128)S(1)} %get-tuple-element.19), channel_id=1, source_target_pairs={{0,12},{4,8},{8,4},{12,0},{1,13},{5,9},{9,5},{13,1},{2,14},{6,10},... | collective-permute-start | bytes 196616 | tf_op jit(solution)/shard_map/ppermute | solution.py:162
  7.1 5.7 %collective-permute-start.5 = (f32[32,512]{1,0:T(8,128)S(1)}, f32[32,512]{1,0:T(8,128)S(1)}, u32[]{:S(2)}, u32[]{:S(2)}) collective-permute-start(f32[32,512]{1,0:T(8,128)S(1)} %get-tuple-element.18), channel_id=1, source_target_pairs={{0,4},{4,0},{8,12},{12,8},{1,5},{5,1},{9,13},{13,9},{2,6},{6,2},{1... | collective-permute-start | bytes 196616 | tf_op jit(solution)/shard_map/ppermute | solution.py:162
  7.3 3.4 %copy-start.1 = (f32[1,32,2048]{2,1,0:T(8,128)S(1)}, f32[1,32,2048]{2,1,0:T(8,128)}, u32[]{:S(2)}) copy-start(f32[1,32,2048]{2,1,0:T(8,128)} %param.7) | copy-start | bytes 786436
  7.4 3.3 %copy-start.2 = (f32[4,4]{1,0:T(4,128)S(1)}, f32[4,4]{1,0:T(4,128)}, u32[]{:S(2)}) copy-start(f32[4,4]{1,0:T(4,128)} %generator_ref.1) | copy-start | bytes 196
  7.4 10.8 %collective-permute-start = (f32[32,512]{1,0:T(8,128)S(1)}, f32[32,512]{1,0:T(8,128)S(1)}, u32[]{:S(2)}, u32[]{:S(2)}) collective-permute-start(f32[32,512]{1,0:T(8,128)S(1)} %get-tuple-element.24), channel_id=1, source_target_pairs={{0,12},{4,8},{8,4},{12,0},{1,13},{5,9},{9,5},{13,1},{2,14},{6,10},... | collective-permute-start | bytes 196616 | tf_op jit(solution)/shard_map/ppermute | solution.py:162
  10.4 0.7 %copy-start.3 = (s32[1,2]{1,0:T(1,128)S(1)}, s32[1,2]{1,0:T(1,128)}, u32[]{:S(2)}) copy-start(s32[1,2]{1,0:T(1,128)} %ids_ref.1) | copy-start | bytes 28
  10.4 10.7 %collective-permute-start.1 = (f32[32,512]{1,0:T(8,128)S(1)}, f32[32,512]{1,0:T(8,128)S(1)}, u32[]{:S(2)}, u32[]{:S(2)}) collective-permute-start(f32[32,512]{1,0:T(8,128)S(1)} %get-tuple-element.23), channel_id=1, source_target_pairs={{0,8},{4,12},{8,0},{12,4},{1,9},{5,13},{9,1},{13,5},{2,10},{6,14},... | collective-permute-start | bytes 196616 | tf_op jit(solution)/shard_map/ppermute | solution.py:162
  11.7 9.3 %collective-permute-start.2 = (f32[32,512]{1,0:T(8,128)S(1)}, f32[32,512]{1,0:T(8,128)S(1)}, u32[]{:S(2)}, u32[]{:S(2)}) collective-permute-start(f32[32,512]{1,0:T(8,128)S(1)} %get-tuple-element.22), channel_id=1, source_target_pairs={{0,4},{4,0},{8,12},{12,8},{1,5},{5,1},{9,13},{13,9},{2,6},{6,2},{1... | collective-permute-start | bytes 196616 | tf_op jit(solution)/shard_map/ppermute | solution.py:162
  12.8 10.1 %copy-start = (f32[1,1,128,512]{3,2,1,0:T(8,128)S(1)}, f32[1,1,128,512]{3,2,1,0:T(8,128)}, u32[]{:S(2)}) copy-start(f32[1,1,128,512]{3,2,1,0:T(8,128)} %param.6) | copy-start | bytes 786436
  12.9 9.0 %collective-permute-start.6 = (f32[32,512]{1,0:T(8,128)S(1)}, f32[32,512]{1,0:T(8,128)S(1)}, u32[]{:S(2)}, u32[]{:S(2)}) collective-permute-start(f32[32,512]{1,0:T(8,128)S(1)} %get-tuple-element.15), channel_id=1, source_target_pairs={{0,4},{4,8},{8,12},{12,0},{1,5},{5,9},{9,13},{13,1},{2,6},{6,10},{... | collective-permute-start | bytes 196616 | tf_op jit(solution)/shard_map/ppermute | solution.py:162
  16.0 6.1 %collective-permute-start.7 = (f32[32,512]{1,0:T(8,128)S(1)}, f32[32,512]{1,0:T(8,128)S(1)}, u32[]{:S(2)}, u32[]{:S(2)}) collective-permute-start(f32[32,512]{1,0:T(8,128)S(1)} %get-tuple-element.16), channel_id=1, source_target_pairs={{0,8},{4,12},{8,0},{12,4},{1,9},{5,13},{9,1},{13,5},{2,10},{6,14},... | collective-permute-start | bytes 196616 | tf_op jit(solution)/shard_map/ppermute | solution.py:162
  18.2 4.8 %collective-permute-start.8 = (f32[32,512]{1,0:T(8,128)S(1)}, f32[32,512]{1,0:T(8,128)S(1)}, u32[]{:S(2)}, u32[]{:S(2)}) collective-permute-start(f32[32,512]{1,0:T(8,128)S(1)} %get-tuple-element.17), channel_id=1, source_target_pairs={{0,12},{4,0},{8,4},{12,8},{1,13},{5,1},{9,5},{13,9},{2,14},{6,2},{... | collective-permute-start | bytes 196616 | tf_op jit(solution)/shard_map/ppermute | solution.py:162

commit v25 on v24

--- a/solution.py
+++ b/solution.py
@@ -14,8 +14,8 @@
 PAIRED_MEMBERS = 4
 KERNEL_VMEM = 8 * 2**20
 
-EARLIER_ROUNDS = (("xor", 2), ("xor", 3), ("xor", 1))
-CURRENT_ROUNDS = (("xor", 3), ("xor", 2), ("xor", 1))
+EARLIER_ROUNDS = (("xor", 1), ("xor", 3), ("xor", 2))
+CURRENT_ROUNDS = (("on", 3), ("on", 2), ("on", 1))
 REBUILT_ROUNDS = (("on", 1), ("on", 2), ("on", 3))
 
 
@@ -131,21 +131,33 @@
     done_ref[...] = jnp.zeros(done_ref.shape, done_ref.dtype)
 
 
-def restore_kernel(table_ref, earlier_ref, held_back_by, *refs):
-    pieces, out_ref = refs[:-1], refs[-1]
+def settle_kernel(earlier_ref, out_ref):
+    out_ref[...] = earlier_ref[...]
+
+
+def restore_kernel(table_ref, held_back_by, settled_ref, *refs):
+    pieces, (out_ref, sems) = refs[:-2], refs[-2:]
     members = len(pieces)
     last = table_ref.shape[0] - 1
-    lost = table_ref[last : last + 1, :] > 0.5
-    for c, piece in zip(sources_of(REBUILT_ROUNDS, members), pieces):
-        out_ref[c] = jnp.where(lost, piece[...], earlier_ref[c])
+
+    @pl.when(table_ref[last, 0] > 0.5)
+    def _():
+        copies = [
+            pltpu.make_async_copy(piece, out_ref.at[c], sems.at[i])
+            for i, (c, piece) in enumerate(zip(sources_of(REBUILT_ROUNDS, members), pieces))
+        ]
+        for copy in copies:
+            copy.start()
+        for copy in copies:
+            copy.wait()
 
 
 def call(kernel, specs, outs, args, flops, **options):
     total = sum(x.size for x in args) + sum(o.size for o in jax.tree.leaves(outs))
+    options.setdefault("out_specs", jax.tree.map(lambda _: IN_VMEM, outs))
     return pl.pallas_call(
         kernel,
         in_specs=specs,
-        out_specs=jax.tree.map(lambda _: IN_VMEM, outs),
         out_shape=outs,
         compiler_params=pltpu.CompilerParams(vmem_limit_bytes=KERNEL_VMEM),
         cost_estimate=pl.CostEstimate(flops=flops, bytes_accessed=4 * total, transcendentals=0),
@@ -212,12 +224,16 @@
             (table, *current_rows),
             parity_cost,
         )
+        settled = call(settle_kernel, [IN_VMEM], floats(*blocks), (earlier,), 0)
         restored_state = call(
             restore_kernel,
-            [IN_VMEM, IN_VMEM, ANYWHERE] + [IN_VMEM] * members,
+            [IN_VMEM, ANYWHERE, ANYWHERE] + [IN_VMEM] * members,
             floats(*blocks),
-            (table, earlier, parity_done, outgoing[0], *incoming),
+            (table, parity_done, settled, outgoing[0], *incoming),
             0,
+            out_specs=ANYWHERE,
+            input_output_aliases={2: 0},
+            scratch_shapes=[pltpu.SemaphoreType.DMA((members,))],
         )
     else:
         earlier_rows = lax.all_to_all(earlier, "code", 0, 0, tiled=True)

time: 23.8 us -> 23.4 us (0.983)
  starting transfers between devices: 18.1 us -> 16.4 us
  Pallas kernels: 2.24 us -> 3 us
  waiting for transfers between devices: 1.32 us -> 2.07 us
  local copies, waits for them, and re-layouts: 1.35 us -> 1.04 us
    ppermute x9, starting transfers between devices: 18.1 us -> 16.4 us  [pass_on(): lax.ppermute(piece, 'code', [(d, target(d, *way, members)) for d in range...]
    pallas_call x4 -> x5, Pallas kernels: 2.24 us -> 3 us  [call(): pl.pallas_call(kernel, in_specs=specs, out_shape=outs, compiler_params=pl...]
    ppermute x9, waiting for transfers between devices: 1.32 us -> 2.07 us  [pass_on(): lax.ppermute(piece, 'code', [(d, target(d, *way, members)) for d in range...]
    unnamed x10, local copies, waits for them, and re-layouts: 0.33 us -> 0.02 us
  transfers between devices with their start and end apart: 9 -> 9, of which waited for: 4 -> 2; matrix products, arithmetic and copies ran while one was open for 0% -> 0% of each run, Pallas kernels for 6% -> 10%
where the time goes in v25:
time: 23.4 us; the launch traced here: 23.3 us
  starting transfers between devices  16.4 us (70%)
  Pallas kernels  3 us (13%)
  waiting for transfers between devices  2.07 us (9%)
  local copies, waits for them, and re-layouts  1.04 us (4%)
  between operations  0.72 us (3%)
    ppermute x9, starting transfers between devices, pass_on(): lax.ppermute(piece, 'code', [(d, target(d, *way, members)) for d in range...  16.4 us
    pallas_call x5, Pallas kernels, call(): pl.pallas_call(kernel, in_specs=specs, out_shape=outs, compiler_params=pl...  3 us
    ppermute x9, waiting for transfers between devices, pass_on(): lax.ppermute(piece, 'code', [(d, target(d, *way, members)) for d in range...  2.07 us
    squeeze x2, local copies, waits for them, and re-layouts, cut(): lax.dynamic_index_in_dim(blocks, c, 0, keepdims=False)  1.02 us
  transfers between devices with their start and end apart: 9, of which 2 were waited for; matrix products, arithmetic and copies ran while one was open for 0% of the time, Pallas kernels for 10%

profile of v25, /device:TPU:0, one launch (start us, length us, event | category | flops | bytes accessed | tf_op | source)
XLA Modules:
  0.0 23.3 jit_solution(9130504050439882254)
XLA Ops:
  0.6 0.0 copy-start.4
  0.7 1.0 %dynamic-slice_bitcast_fusion = (f32[32,512]{1,0:T(8,128)S(1)}, f32[32,512]{1,0:T(8,128)S(1)}, f32[32,512]{1,0:T(8,128)S(1)}, f32[32,512]{1,0:T(8,128)S(1)}) fusion(f32[4,32,512]{2,1,0:T(8,128)} %bitcast.21, s32[]{:T(128)S(6)} %select_n.47, s32[]{:T(128)S(6)} %select_n.46, s32[]{:T(128)S(6)} %select_n.45, s32[]{:T(128)S(6)} %select_n.38), kind=kLoop, calls=%fused_computation | loop fusion | bytes 524304 | tf_op jit(solution)/shard_map/jit(dynamic_index_in_dim)/squeeze | solution.py:182
  1.7 4.1 %collective-permute-start.5 = (f32[32,512]{1,0:T(8,128)S(1)}, f32[32,512]{1,0:T(8,128)S(1)}, u32[]{:S(2)}, u32[]{:S(2)}) collective-permute-start(f32[32,512]{1,0:T(8,128)S(1)} %get-tuple-element.18), channel_id=1, source_target_pairs={{0,8},{4,12},{8,0},{12,4},{1,9},{5,13},{9,1},{13,5},{2,10},{6,14},... | collective-permute-start | bytes 196616 | tf_op jit(solution)/shard_map/ppermute | solution.py:174
  5.8 1.3 %collective-permute-start.4 = (f32[32,512]{1,0:T(8,128)S(1)}, f32[32,512]{1,0:T(8,128)S(1)}, u32[]{:S(2)}, u32[]{:S(2)}) collective-permute-start(f32[32,512]{1,0:T(8,128)S(1)} %get-tuple-element.19), channel_id=1, source_target_pairs={{0,12},{4,8},{8,4},{12,0},{1,13},{5,9},{9,5},{13,1},{2,14},{6,10},... | collective-permute-start | bytes 196616 | tf_op jit(solution)/shard_map/ppermute | solution.py:174
  7.1 0.2 collective-permute-start.3
  7.3 0.0 copy-done.4
  7.3 0.0 copy-start.1
  7.4 0.0 copy-start.2
  7.4 1.8 %collective-permute-start.2 = (f32[32,512]{1,0:T(8,128)S(1)}, f32[32,512]{1,0:T(8,128)S(1)}, u32[]{:S(2)}, u32[]{:S(2)}) collective-permute-start(f32[32,512]{1,0:T(8,128)S(1)} %get-tuple-element.22), channel_id=1, source_target_pairs={{0,4},{4,8},{8,12},{12,0},{1,5},{5,9},{9,13},{13,1},{2,6},{6,10},{... | collective-permute-start | bytes 196616 | tf_op jit(solution)/shard_map/ppermute | solution.py:174
  9.2 0.0 copy-start.3
  9.2 1.7 %collective-permute-start.1 = (f32[32,512]{1,0:T(8,128)S(1)}, f32[32,512]{1,0:T(8,128)S(1)}, u32[]{:S(2)}, u32[]{:S(2)}) collective-permute-start(f32[32,512]{1,0:T(8,128)S(1)} %get-tuple-element.23), channel_id=1, source_target_pairs={{0,8},{4,12},{8,0},{12,4},{1,9},{5,13},{9,1},{13,5},{2,10},{6,14},... | collective-permute-start | bytes 196616 | tf_op jit(solution)/shard_map/ppermute | solution.py:174
  10.9 0.0 copy-done.1
  10.9 0.0 copy-done.2
  10.9 0.0 copy-done.3
  10.9 0.7 %shard_map.68 = (f32[2,32,512]{2,1,0:T(8,128)S(1)}, f32[29,512]{1,0:T(8,128)S(1)}) custom-call(s32[1,2]{1,0:T(1,128)S(1)} %copy-done.3, f32[4,4]{1,0:T(4,128)S(1)} %copy-done.2, f32[32,2048]{1,0:T(8,128)S(1)} %bitcast.23), custom_call_target="tpu_custom_call" | custom-call | flops 262144 | bytes 452680 | tf_op jit(solution)/shard_map/pallas_call | solution.py:158
  11.6 0.0 copy-start
  11.6 0.0 collective-permute-done.5.refs_3_
  11.6 3.0 %collective-permute-start = (f32[32,512]{1,0:T(8,128)S(1)}, f32[32,512]{1,0:T(8,128)S(1)}, u32[]{:S(2)}, u32[]{:S(2)}) collective-permute-start(f32[32,512]{1,0:T(8,128)S(1)} %get-tuple-element.24), channel_id=1, source_target_pairs={{0,12},{4,0},{8,4},{12,8},{1,13},{5,1},{9,5},{13,9},{2,14},{6,2},{... | collective-permute-start | bytes 196616 | tf_op jit(solution)/shard_map/ppermute | solution.py:174
  14.7 0.0 collective-permute-done.4.refs_2_
  14.7 0.0 collective-permute-done.3.refs_1_
  14.7 0.1 shard_map.71
  14.7 0.1 collective-permute-start.6
  14.8 1.7 %collective-permute-start.7 = (f32[32,512]{1,0:T(8,128)S(1)}, f32[32,512]{1,0:T(8,128)S(1)}, u32[]{:S(2)}, u32[]{:S(2)}) collective-permute-start(f32[32,512]{1,0:T(8,128)S(1)} %get-tuple-element.16), channel_id=1, source_target_pairs={{0,8},{4,12},{8,0},{12,4},{1,9},{5,13},{9,1},{13,5},{2,10},{6,14},... | collective-permute-start | bytes 196616 | tf_op jit(solution)/shard_map/ppermute | solution.py:174
  16.5 0.0 collective-permute-done.2.refs_3_
  16.5 2.5 %collective-permute-start.8 = (f32[32,512]{1,0:T(8,128)S(1)}, f32[32,512]{1,0:T(8,128)S(1)}, u32[]{:S(2)}, u32[]{:S(2)}) collective-permute-start(f32[32,512]{1,0:T(8,128)S(1)} %get-tuple-element.17), channel_id=1, source_target_pairs={{0,12},{4,0},{8,4},{12,8},{1,13},{5,1},{9,5},{13,9},{2,14},{6,2},{... | collective-permute-start | bytes 196616 | tf_op jit(solution)/shard_map/ppermute | solution.py:174
  18.9 0.0 copy-done
  18.9 0.7 %shard_map.70.settled_ref = f32[4,32,512]{2,1,0:T(8,128)} custom-call(f32[4,32,512]{2,1,0:T(8,128)S(1)} %bitcast.22), custom_call_target="tpu_custom_call" | custom-call | bytes 524288 | tf_op jit(solution)/shard_map/pallas_call | solution.py:158
  19.6 0.0 collective-permute-done.1.refs_2_
  19.7 0.0 collective-permute-done.refs_1_
  19.7 0.8 %shard_map.69 = (f32[32,2048]{1,0:T(8,128)}, f32[8,128]{1,0:T(8,128)S(1)}) custom-call(f32[29,512]{1,0:T(8,128)S(1)} %get-tuple-element.10.table_ref, f32[32,512]{1,0:T(8,128)S(1)} %get-tuple-element.25.refs_0_, f32[32,512]{1,0:T(8,128)S(1)} %collective-permute-done.refs_1_, f32[32,512]{1,0:T(8,128)S(1)} %collective-permute-done.1.refs_2_, ...), custom_call_target="tpu_custom_call" | custom-call | flops 524288 | bytes 587776 | tf_op jit(solution)/shard_map/pallas_call | solution.py:158
  20.4 0.7 %collective-permute-done.6.refs_1_ = f32[32,512]{1,0:T(8,128)S(1)} collective-permute-done((f32[32,512]{1,0:T(8,128)S(1)}, f32[32,512]{1,0:T(8,128)S(1)}, u32[]{:S(2)}, u32[]{:S(2)}) %collective-permute-start.6) | collective-permute-done | bytes 65568 | tf_op jit(solution)/shard_map/ppermute | solution.py:174
  21.1 1.4 %collective-permute-done.7.refs_2_ = f32[32,512]{1,0:T(8,128)S(1)} collective-permute-done((f32[32,512]{1,0:T(8,128)S(1)}, f32[32,512]{1,0:T(8,128)S(1)}, u32[]{:S(2)}, u32[]{:S(2)}) %collective-permute-start.7) | collective-permute-done | bytes 65568 | tf_op jit(solution)/shard_map/ppermute | solution.py:174
  22.5 0.0 collective-permute-done.8.refs_3_
  22.5 0.8 %shard_map.72 = f32[4,32,512]{2,1,0:T(8,128)} custom-call(f32[29,512]{1,0:T(8,128)S(1)} %get-tuple-element.10.table_ref, f32[8,128]{1,0:T(8,128)S(1)} %get-tuple-element.12.held_back_by, f32[4,32,512]{2,1,0:T(8,128)} %shard_map.70.settled_ref, f32[32,512]{1,0:T(8,128)S(1)} %get-tuple-element.14.refs_0_, ...), custom_call_target="tpu_custom_call", output_to_operand_aliasing={{}: (2, {})} | custom-call | bytes 849920 | tf_op jit(solution)/shard_map/pallas_call | solution.py:158
  (1 shorter events, 0.0 us)
Async XLA Ops:
  0.6 6.7 %copy-start.4 = (f32[1,1,128,512]{3,2,1,0:T(8,128)S(1)}, f32[1,1,128,512]{3,2,1,0:T(8,128)}, u32[]{:S(2)}) copy-start(f32[1,1,128,512]{3,2,1,0:T(8,128)} %param.5) | copy-start | bytes 786436
  1.7 9.9 %collective-permute-start.5 = (f32[32,512]{1,0:T(8,128)S(1)}, f32[32,512]{1,0:T(8,128)S(1)}, u32[]{:S(2)}, u32[]{:S(2)}) collective-permute-start(f32[32,512]{1,0:T(8,128)S(1)} %get-tuple-element.18), channel_id=1, source_target_pairs={{0,8},{4,12},{8,0},{12,4},{1,9},{5,13},{9,1},{13,5},{2,10},{6,14},... | collective-permute-start | bytes 196616 | tf_op jit(solution)/shard_map/ppermute | solution.py:174
  5.8 8.9 %collective-permute-start.4 = (f32[32,512]{1,0:T(8,128)S(1)}, f32[32,512]{1,0:T(8,128)S(1)}, u32[]{:S(2)}, u32[]{:S(2)}) collective-permute-start(f32[32,512]{1,0:T(8,128)S(1)} %get-tuple-element.19), channel_id=1, source_target_pairs={{0,12},{4,8},{8,4},{12,0},{1,13},{5,9},{9,5},{13,1},{2,14},{6,10},... | collective-permute-start | bytes 196616 | tf_op jit(solution)/shard_map/ppermute | solution.py:174
  7.1 7.5 %collective-permute-start.3 = (f32[32,512]{1,0:T(8,128)S(1)}, f32[32,512]{1,0:T(8,128)S(1)}, u32[]{:S(2)}, u32[]{:S(2)}) collective-permute-start(f32[32,512]{1,0:T(8,128)S(1)} %get-tuple-element.20), channel_id=1, source_target_pairs={{0,4},{4,0},{8,12},{12,8},{1,5},{5,1},{9,13},{13,9},{2,6},{6,2},{1... | collective-permute-start | bytes 196616 | tf_op jit(solution)/shard_map/ppermute | solution.py:174
  7.3 3.6 %copy-start.1 = (f32[1,32,2048]{2,1,0:T(8,128)S(1)}, f32[1,32,2048]{2,1,0:T(8,128)}, u32[]{:S(2)}) copy-start(f32[1,32,2048]{2,1,0:T(8,128)} %param.7) | copy-start | bytes 786436
  7.4 3.6 %copy-start.2 = (f32[4,4]{1,0:T(4,128)S(1)}, f32[4,4]{1,0:T(4,128)}, u32[]{:S(2)}) copy-start(f32[4,4]{1,0:T(4,128)} %generator_ref.1) | copy-start | bytes 196
  7.4 9.1 %collective-permute-start.2 = (f32[32,512]{1,0:T(8,128)S(1)}, f32[32,512]{1,0:T(8,128)S(1)}, u32[]{:S(2)}, u32[]{:S(2)}) collective-permute-start(f32[32,512]{1,0:T(8,128)S(1)} %get-tuple-element.22), channel_id=1, source_target_pairs={{0,4},{4,8},{8,12},{12,0},{1,5},{5,9},{9,13},{13,1},{2,6},{6,10},{... | collective-permute-start | bytes 196616 | tf_op jit(solution)/shard_map/ppermute | solution.py:174
  9.2 1.7 %copy-start.3 = (s32[1,2]{1,0:T(1,128)S(1)}, s32[1,2]{1,0:T(1,128)}, u32[]{:S(2)}) copy-start(s32[1,2]{1,0:T(1,128)} %ids_ref.1) | copy-start | bytes 28
  9.2 10.4 %collective-permute-start.1 = (f32[32,512]{1,0:T(8,128)S(1)}, f32[32,512]{1,0:T(8,128)S(1)}, u32[]{:S(2)}, u32[]{:S(2)}) collective-permute-start(f32[32,512]{1,0:T(8,128)S(1)} %get-tuple-element.23), channel_id=1, source_target_pairs={{0,8},{4,12},{8,0},{12,4},{1,9},{5,13},{9,1},{13,5},{2,10},{6,14},... | collective-permute-start | bytes 196616 | tf_op jit(solution)/shard_map/ppermute | solution.py:174
  11.6 7.3 %copy-start = (f32[1,1,128,512]{3,2,1,0:T(8,128)S(1)}, f32[1,1,128,512]{3,2,1,0:T(8,128)}, u32[]{:S(2)}) copy-start(f32[1,1,128,512]{3,2,1,0:T(8,128)} %param.6) | copy-start | bytes 786436
  11.6 8.0 %collective-permute-start = (f32[32,512]{1,0:T(8,128)S(1)}, f32[32,512]{1,0:T(8,128)S(1)}, u32[]{:S(2)}, u32[]{:S(2)}) collective-permute-start(f32[32,512]{1,0:T(8,128)S(1)} %get-tuple-element.24), channel_id=1, source_target_pairs={{0,12},{4,0},{8,4},{12,8},{1,13},{5,1},{9,5},{13,9},{2,14},{6,2},{... | collective-permute-start | bytes 196616 | tf_op jit(solution)/shard_map/ppermute | solution.py:174
  14.7 6.4 %collective-permute-start.6 = (f32[32,512]{1,0:T(8,128)S(1)}, f32[32,512]{1,0:T(8,128)S(1)}, u32[]{:S(2)}, u32[]{:S(2)}) collective-permute-start(f32[32,512]{1,0:T(8,128)S(1)} %get-tuple-element.15), channel_id=1, source_target_pairs={{0,4},{4,8},{8,12},{12,0},{1,5},{5,9},{9,13},{13,1},{2,6},{6,10},{... | collective-permute-start | bytes 196616 | tf_op jit(solution)/shard_map/ppermute | solution.py:174
  14.8 7.7 %collective-permute-start.7 = (f32[32,512]{1,0:T(8,128)S(1)}, f32[32,512]{1,0:T(8,128)S(1)}, u32[]{:S(2)}, u32[]{:S(2)}) collective-permute-start(f32[32,512]{1,0:T(8,128)S(1)} %get-tuple-element.16), channel_id=1, source_target_pairs={{0,8},{4,12},{8,0},{12,4},{1,9},{5,13},{9,1},{13,5},{2,10},{6,14},... | collective-permute-start | bytes 196616 | tf_op jit(solution)/shard_map/ppermute | solution.py:174
  16.5 6.0 %collective-permute-start.8 = (f32[32,512]{1,0:T(8,128)S(1)}, f32[32,512]{1,0:T(8,128)S(1)}, u32[]{:S(2)}, u32[]{:S(2)}) collective-permute-start(f32[32,512]{1,0:T(8,128)S(1)} %get-tuple-element.17), channel_id=1, source_target_pairs={{0,12},{4,0},{8,4},{12,8},{1,13},{5,1},{9,5},{13,9},{2,14},{6,2},{... | collective-permute-start | bytes 196616 | tf_op jit(solution)/shard_map/ppermute | solution.py:174

commit v26 on v25

--- a/solution.py
+++ b/solution.py
@@ -14,7 +14,7 @@
 PAIRED_MEMBERS = 4
 KERNEL_VMEM = 8 * 2**20
 
-EARLIER_ROUNDS = (("xor", 1), ("xor", 3), ("xor", 2))
+EARLIER_ROUNDS = (("xor", 1), ("xor", 2), ("xor", 3))
 CURRENT_ROUNDS = (("on", 3), ("on", 2), ("on", 1))
 REBUILT_ROUNDS = (("on", 1), ("on", 2), ("on", 3))
 
@@ -205,7 +205,11 @@
     parity_cost = 2 * spans * slab_rows * width
     if paired:
         block = floats(own_rows, width)
-        own_earlier, *cut_earlier = cut(earlier, targets_of(EARLIER_ROUNDS, members))
+        own, *others = targets_of(EARLIER_ROUNDS, members)
+        far = cut(earlier, [others[1], others[2]])
+        later, far[0] = lax.optimization_barrier((earlier, far[0]))
+        own_earlier, next_earlier = cut(later, [own, others[0]])
+        cut_earlier = far[:0] + [next_earlier] + far[0:]
         earlier_rows = pass_on(cut_earlier, EARLIER_ROUNDS, members)
         own_current, *cut_current = cut(current, targets_of(CURRENT_ROUNDS, members))
         outgoing = call(

time: 23.4 us -> 22.7 us (0.970)
  Pallas kernels: 3 us -> 2.32 us
    pallas_call x5, Pallas kernels: 3 us -> 2.32 us  [call(): pl.pallas_call(kernel, in_specs=specs, out_shape=outs, compiler_params=pl...]
    squeeze x2 -> x3, local copies, waits for them, and re-layouts: 1.02 us -> 0.96 us  [cut(): lax.dynamic_index_in_dim(blocks, c, 0, keepdims=False)]
where the time goes in v26:
time: 22.7 us; the launch traced here: 22.5 us
  starting transfers between devices  16.4 us (72%)
  Pallas kernels  2.32 us (10%)
  waiting for transfers between devices  2.07 us (9%)
  local copies, waits for them, and re-layouts  0.99 us (4%)
  between operations  0.72 us (3%)
    ppermute x9, starting transfers between devices, pass_on(): lax.ppermute(piece, 'code', [(d, target(d, *way, members)) for d in range...  16.4 us
    pallas_call x5, Pallas kernels, call(): pl.pallas_call(kernel, in_specs=specs, out_shape=outs, compiler_params=pl...  2.32 us
    ppermute x9, waiting for transfers between devices, pass_on(): lax.ppermute(piece, 'code', [(d, target(d, *way, members)) for d in range...  2.07 us
    squeeze x3, local copies, waits for them, and re-layouts, cut(): lax.dynamic_index_in_dim(blocks, c, 0, keepdims=False)  0.96 us
  transfers between devices with their start and end apart: 9, of which 2 were waited for; matrix products, arithmetic and copies ran while one was open for 0% of the time, Pallas kernels for 10%

profile of v26, /device:TPU:0, one launch (start us, length us, event | category | flops | bytes accessed | tf_op | source)
XLA Modules:
  0.0 22.5 jit_solution(333351163589994831)
XLA Ops:
  0.6 0.0 copy-start
  0.7 0.0 copy-start.4
  0.7 0.9 %dynamic-slice_bitcast_fusion = (f32[32,512]{1,0:T(8,128)S(1)}, f32[32,512]{1,0:T(8,128)S(1)}) fusion(f32[4,32,512]{2,1,0:T(8,128)} %bitcast.21, s32[]{:T(128)S(6)} %select_n.47, s32[]{:T(128)S(6)} %select_n.45), kind=kLoop, calls=%fused_computation | loop fusion | bytes 262152 | tf_op jit(solution)/shard_map/jit(dynamic_index_in_dim)/squeeze | solution.py:182
  1.6 4.1 %collective-permute-start.4 = (f32[32,512]{1,0:T(8,128)S(1)}, f32[32,512]{1,0:T(8,128)S(1)}, u32[]{:S(2)}, u32[]{:S(2)}) collective-permute-start(f32[32,512]{1,0:T(8,128)S(1)} %get-tuple-element.17), channel_id=1, source_target_pairs={{0,8},{4,12},{8,0},{12,4},{1,9},{5,13},{9,1},{13,5},{2,10},{6,14},... | collective-permute-start | bytes 196616 | tf_op jit(solution)/shard_map/ppermute | solution.py:174
  5.7 1.3 %collective-permute-start.5 = (f32[32,512]{1,0:T(8,128)S(1)}, f32[32,512]{1,0:T(8,128)S(1)}, u32[]{:S(2)}, u32[]{:S(2)}) collective-permute-start(f32[32,512]{1,0:T(8,128)S(1)} %get-tuple-element.22), channel_id=1, source_target_pairs={{0,12},{4,8},{8,4},{12,0},{1,13},{5,9},{9,5},{13,1},{2,14},{6,10},... | collective-permute-start | bytes 196616 | tf_op jit(solution)/shard_map/ppermute | solution.py:174
  7.1 0.0 copy-done
  7.1 0.3 %collective-permute-start.3 = (f32[32,512]{1,0:T(8,128)S(1)}, f32[32,512]{1,0:T(8,128)S(1)}, u32[]{:S(2)}, u32[]{:S(2)}) collective-permute-start(f32[32,512]{1,0:T(8,128)S(1)} %get-tuple-element.24), channel_id=1, source_target_pairs={{0,4},{4,0},{8,12},{12,8},{1,5},{5,1},{9,13},{13,9},{2,6},{6,2},{1... | collective-permute-start | bytes 196616 | tf_op jit(solution)/shard_map/ppermute | solution.py:174
  7.4 0.0 copy-done.4
  7.4 0.0 copy-start.1
  7.4 0.0 copy-start.2
  7.4 1.8 %collective-permute-start.2 = (f32[32,512]{1,0:T(8,128)S(1)}, f32[32,512]{1,0:T(8,128)S(1)}, u32[]{:S(2)}, u32[]{:S(2)}) collective-permute-start(f32[32,512]{1,0:T(8,128)S(1)} %get-tuple-element.26), channel_id=1, source_target_pairs={{0,4},{4,8},{8,12},{12,0},{1,5},{5,9},{9,13},{13,1},{2,6},{6,10},{... | collective-permute-start | bytes 196616 | tf_op jit(solution)/shard_map/ppermute | solution.py:174
  9.3 0.0 copy-start.3
  9.3 1.7 %collective-permute-start.1 = (f32[32,512]{1,0:T(8,128)S(1)}, f32[32,512]{1,0:T(8,128)S(1)}, u32[]{:S(2)}, u32[]{:S(2)}) collective-permute-start(f32[32,512]{1,0:T(8,128)S(1)} %get-tuple-element.27), channel_id=1, source_target_pairs={{0,8},{4,12},{8,0},{12,4},{1,9},{5,13},{9,1},{13,5},{2,10},{6,14},... | collective-permute-start | bytes 196616 | tf_op jit(solution)/shard_map/ppermute | solution.py:174
  10.9 0.0 copy-done.1
  10.9 0.0 copy-done.2
  11.0 0.0 copy-done.3
  11.0 0.7 %shard_map.68 = (f32[2,32,512]{2,1,0:T(8,128)S(1)}, f32[29,512]{1,0:T(8,128)S(1)}) custom-call(s32[1,2]{1,0:T(1,128)S(1)} %copy-done.3, f32[4,4]{1,0:T(4,128)S(1)} %copy-done.2, f32[32,2048]{1,0:T(8,128)S(1)} %bitcast.24), custom_call_target="tpu_custom_call" | custom-call | flops 262144 | bytes 452680 | tf_op jit(solution)/shard_map/pallas_call | solution.py:158
  11.6 0.0 collective-permute-done.4.refs_2_
  11.6 3.0 %collective-permute-start = (f32[32,512]{1,0:T(8,128)S(1)}, f32[32,512]{1,0:T(8,128)S(1)}, u32[]{:S(2)}, u32[]{:S(2)}) collective-permute-start(f32[32,512]{1,0:T(8,128)S(1)} %get-tuple-element.28), channel_id=1, source_target_pairs={{0,12},{4,0},{8,4},{12,8},{1,13},{5,1},{9,5},{13,9},{2,14},{6,2},{... | collective-permute-start | bytes 196616 | tf_op jit(solution)/shard_map/ppermute | solution.py:174
  14.6 0.0 collective-permute-done.5.refs_3_
  14.6 0.0 collective-permute-done.3.refs_1_
  14.6 0.1 shard_map.71
  14.7 0.1 collective-permute-start.6
  14.7 1.7 %collective-permute-start.7 = (f32[32,512]{1,0:T(8,128)S(1)}, f32[32,512]{1,0:T(8,128)S(1)}, u32[]{:S(2)}, u32[]{:S(2)}) collective-permute-start(f32[32,512]{1,0:T(8,128)S(1)} %get-tuple-element.20), channel_id=1, source_target_pairs={{0,8},{4,12},{8,0},{12,4},{1,9},{5,13},{9,1},{13,5},{2,10},{6,14},... | collective-permute-start | bytes 196616 | tf_op jit(solution)/shard_map/ppermute | solution.py:174
  16.4 0.0 collective-permute-done.2.refs_3_
  16.4 2.5 %collective-permute-start.8 = (f32[32,512]{1,0:T(8,128)S(1)}, f32[32,512]{1,0:T(8,128)S(1)}, u32[]{:S(2)}, u32[]{:S(2)}) collective-permute-start(f32[32,512]{1,0:T(8,128)S(1)} %get-tuple-element.21), channel_id=1, source_target_pairs={{0,12},{4,0},{8,4},{12,8},{1,13},{5,1},{9,5},{13,9},{2,14},{6,2},{... | collective-permute-start | bytes 196616 | tf_op jit(solution)/shard_map/ppermute | solution.py:174
  18.9 0.7 %shard_map.70.settled_ref = f32[4,32,512]{2,1,0:T(8,128)} custom-call(f32[4,32,512]{2,1,0:T(8,128)S(1)} %bitcast.23), custom_call_target="tpu_custom_call" | custom-call | bytes 524288 | tf_op jit(solution)/shard_map/pallas_call | solution.py:158
  19.6 0.0 collective-permute-done.1.refs_2_
  19.6 0.0 collective-permute-done.refs_1_
  19.6 0.8 %shard_map.69 = (f32[32,2048]{1,0:T(8,128)}, f32[8,128]{1,0:T(8,128)S(1)}) custom-call(f32[29,512]{1,0:T(8,128)S(1)} %get-tuple-element.12.table_ref, f32[32,512]{1,0:T(8,128)S(1)} %get-tuple-element.29.refs_0_, f32[32,512]{1,0:T(8,128)S(1)} %collective-permute-done.refs_1_, f32[32,512]{1,0:T(8,128)S(1)} %collective-permute-done.1.refs_2_, ...), custom_call_target="tpu_custom_call" | custom-call | flops 524288 | bytes 587776 | tf_op jit(solution)/shard_map/pallas_call | solution.py:158
  20.4 0.7 %collective-permute-done.6.refs_1_ = f32[32,512]{1,0:T(8,128)S(1)} collective-permute-done((f32[32,512]{1,0:T(8,128)S(1)}, f32[32,512]{1,0:T(8,128)S(1)}, u32[]{:S(2)}, u32[]{:S(2)}) %collective-permute-start.6) | collective-permute-done | bytes 65568 | tf_op jit(solution)/shard_map/ppermute | solution.py:174
  21.0 1.4 %collective-permute-done.7.refs_2_ = f32[32,512]{1,0:T(8,128)S(1)} collective-permute-done((f32[32,512]{1,0:T(8,128)S(1)}, f32[32,512]{1,0:T(8,128)S(1)}, u32[]{:S(2)}, u32[]{:S(2)}) %collective-permute-start.7) | collective-permute-done | bytes 65568 | tf_op jit(solution)/shard_map/ppermute | solution.py:174
  22.4 0.0 collective-permute-done.8.refs_3_
  22.4 0.1 shard_map.72
  (2 shorter events, 0.0 us)
Async XLA Ops:
  0.6 6.4 %copy-start = (f32[1,1,128,512]{3,2,1,0:T(8,128)S(1)}, f32[1,1,128,512]{3,2,1,0:T(8,128)}, u32[]{:S(2)}) copy-start(f32[1,1,128,512]{3,2,1,0:T(8,128)} %param.6) | copy-start | bytes 786436
  0.7 6.7 %copy-start.4 = (f32[1,1,128,512]{3,2,1,0:T(8,128)S(1)}, f32[1,1,128,512]{3,2,1,0:T(8,128)}, u32[]{:S(2)}) copy-start(f32[1,1,128,512]{3,2,1,0:T(8,128)} %param.5) | copy-start | bytes 786436
  1.6 10.0 %collective-permute-start.4 = (f32[32,512]{1,0:T(8,128)S(1)}, f32[32,512]{1,0:T(8,128)S(1)}, u32[]{:S(2)}, u32[]{:S(2)}) collective-permute-start(f32[32,512]{1,0:T(8,128)S(1)} %get-tuple-element.17), channel_id=1, source_target_pairs={{0,8},{4,12},{8,0},{12,4},{1,9},{5,13},{9,1},{13,5},{2,10},{6,14},... | collective-permute-start | bytes 196616 | tf_op jit(solution)/shard_map/ppermute | solution.py:174
  5.7 8.9 %collective-permute-start.5 = (f32[32,512]{1,0:T(8,128)S(1)}, f32[32,512]{1,0:T(8,128)S(1)}, u32[]{:S(2)}, u32[]{:S(2)}) collective-permute-start(f32[32,512]{1,0:T(8,128)S(1)} %get-tuple-element.22), channel_id=1, source_target_pairs={{0,12},{4,8},{8,4},{12,0},{1,13},{5,9},{9,5},{13,1},{2,14},{6,10},... | collective-permute-start | bytes 196616 | tf_op jit(solution)/shard_map/ppermute | solution.py:174
  7.1 7.5 %collective-permute-start.3 = (f32[32,512]{1,0:T(8,128)S(1)}, f32[32,512]{1,0:T(8,128)S(1)}, u32[]{:S(2)}, u32[]{:S(2)}) collective-permute-start(f32[32,512]{1,0:T(8,128)S(1)} %get-tuple-element.24), channel_id=1, source_target_pairs={{0,4},{4,0},{8,12},{12,8},{1,5},{5,1},{9,13},{13,9},{2,6},{6,2},{1... | collective-permute-start | bytes 196616 | tf_op jit(solution)/shard_map/ppermute | solution.py:174
  7.4 3.6 %copy-start.1 = (f32[1,32,2048]{2,1,0:T(8,128)S(1)}, f32[1,32,2048]{2,1,0:T(8,128)}, u32[]{:S(2)}) copy-start(f32[1,32,2048]{2,1,0:T(8,128)} %param.7) | copy-start | bytes 786436
  7.4 3.6 %copy-start.2 = (f32[4,4]{1,0:T(4,128)S(1)}, f32[4,4]{1,0:T(4,128)}, u32[]{:S(2)}) copy-start(f32[4,4]{1,0:T(4,128)} %generator_ref.1) | copy-start | bytes 196
  7.4 9.0 %collective-permute-start.2 = (f32[32,512]{1,0:T(8,128)S(1)}, f32[32,512]{1,0:T(8,128)S(1)}, u32[]{:S(2)}, u32[]{:S(2)}) collective-permute-start(f32[32,512]{1,0:T(8,128)S(1)} %get-tuple-element.26), channel_id=1, source_target_pairs={{0,4},{4,8},{8,12},{12,0},{1,5},{5,9},{9,13},{13,1},{2,6},{6,10},{... | collective-permute-start | bytes 196616 | tf_op jit(solution)/shard_map/ppermute | solution.py:174
  9.3 1.7 %copy-start.3 = (s32[1,2]{1,0:T(1,128)S(1)}, s32[1,2]{1,0:T(1,128)}, u32[]{:S(2)}) copy-start(s32[1,2]{1,0:T(1,128)} %ids_ref.1) | copy-start | bytes 28
  9.3 10.3 %collective-permute-start.1 = (f32[32,512]{1,0:T(8,128)S(1)}, f32[32,512]{1,0:T(8,128)S(1)}, u32[]{:S(2)}, u32[]{:S(2)}) collective-permute-start(f32[32,512]{1,0:T(8,128)S(1)} %get-tuple-element.27), channel_id=1, source_target_pairs={{0,8},{4,12},{8,0},{12,4},{1,9},{5,13},{9,1},{13,5},{2,10},{6,14},... | collective-permute-start | bytes 196616 | tf_op jit(solution)/shard_map/ppermute | solution.py:174
  11.6 8.0 %collective-permute-start = (f32[32,512]{1,0:T(8,128)S(1)}, f32[32,512]{1,0:T(8,128)S(1)}, u32[]{:S(2)}, u32[]{:S(2)}) collective-permute-start(f32[32,512]{1,0:T(8,128)S(1)} %get-tuple-element.28), channel_id=1, source_target_pairs={{0,12},{4,0},{8,4},{12,8},{1,13},{5,1},{9,5},{13,9},{2,14},{6,2},{... | collective-permute-start | bytes 196616 | tf_op jit(solution)/shard_map/ppermute | solution.py:174
  14.7 6.4 %collective-permute-start.6 = (f32[32,512]{1,0:T(8,128)S(1)}, f32[32,512]{1,0:T(8,128)S(1)}, u32[]{:S(2)}, u32[]{:S(2)}) collective-permute-start(f32[32,512]{1,0:T(8,128)S(1)} %get-tuple-element.19), channel_id=1, source_target_pairs={{0,4},{4,8},{8,12},{12,0},{1,5},{5,9},{9,13},{13,1},{2,6},{6,10},{... | collective-permute-start | bytes 196616 | tf_op jit(solution)/shard_map/ppermute | solution.py:174
  14.7 7.7 %collective-permute-start.7 = (f32[32,512]{1,0:T(8,128)S(1)}, f32[32,512]{1,0:T(8,128)S(1)}, u32[]{:S(2)}, u32[]{:S(2)}) collective-permute-start(f32[32,512]{1,0:T(8,128)S(1)} %get-tuple-element.20), channel_id=1, source_target_pairs={{0,8},{4,12},{8,0},{12,4},{1,9},{5,13},{9,1},{13,5},{2,10},{6,14},... | collective-permute-start | bytes 196616 | tf_op jit(solution)/shard_map/ppermute | solution.py:174
  16.4 6.0 %collective-permute-start.8 = (f32[32,512]{1,0:T(8,128)S(1)}, f32[32,512]{1,0:T(8,128)S(1)}, u32[]{:S(2)}, u32[]{:S(2)}) collective-permute-start(f32[32,512]{1,0:T(8,128)S(1)} %get-tuple-element.21), channel_id=1, source_target_pairs={{0,12},{4,0},{8,4},{12,8},{1,13},{5,1},{9,5},{13,9},{2,14},{6,2},{... | collective-permute-start | bytes 196616 | tf_op jit(solution)/shard_map/ppermute | solution.py:174

commit v27 on v26

--- a/solution.py
+++ b/solution.py
@@ -14,7 +14,7 @@
 PAIRED_MEMBERS = 4
 KERNEL_VMEM = 8 * 2**20
 
-EARLIER_ROUNDS = (("xor", 1), ("xor", 2), ("xor", 3))
+EARLIER_ROUNDS = (("xor", 1), ("xor", 3), ("xor", 2))
 CURRENT_ROUNDS = (("on", 3), ("on", 2), ("on", 1))
 REBUILT_ROUNDS = (("on", 1), ("on", 2), ("on", 3))
 

time: 22.7 us -> 23.2 us (1.022); the launches traced: 22.5 us -> 23.4 us
  waiting for transfers between devices: 2.07 us -> 3.59 us
  starting transfers between devices: 16.4 us -> 15.1 us
  Pallas kernels: 2.32 us -> 3 us
    ppermute x9, waiting for transfers between devices: 2.07 us -> 3.59 us  [pass_on(): lax.ppermute(piece, 'code', [(d, target(d, *way, members)) for d in range...]
    ppermute x9, starting transfers between devices: 16.4 us -> 15.1 us  [pass_on(): lax.ppermute(piece, 'code', [(d, target(d, *way, members)) for d in range...]
    pallas_call x5, Pallas kernels: 2.32 us -> 3 us  [call(): pl.pallas_call(kernel, in_specs=specs, out_shape=outs, compiler_params=pl...]
  transfers between devices with their start and end apart: 9 -> 9, of which waited for: 2 -> 3; matrix products, arithmetic and copies ran while one was open for 0% -> 0% of each run, Pallas kernels for 10% -> 9%
where the time goes in v27:
time: 23.2 us; the launch traced here: 23.4 us
  starting transfers between devices  15.1 us (65%)
  waiting for transfers between devices  3.59 us (15%)
  Pallas kernels  3 us (13%)
  local copies, waits for them, and re-layouts  0.99 us (4%)
  between operations  0.72 us (3%)
    ppermute x9, starting transfers between devices, pass_on(): lax.ppermute(piece, 'code', [(d, target(d, *way, members)) for d in range...  15.1 us
    ppermute x9, waiting for transfers between devices, pass_on(): lax.ppermute(piece, 'code', [(d, target(d, *way, members)) for d in range...  3.59 us
    pallas_call x5, Pallas kernels, call(): pl.pallas_call(kernel, in_specs=specs, out_shape=outs, compiler_params=pl...  3 us
    squeeze x3, local copies, waits for them, and re-layouts, cut(): lax.dynamic_index_in_dim(blocks, c, 0, keepdims=False)  0.96 us
  transfers between devices with their start and end apart: 9, of which 3 were waited for; matrix products, arithmetic and copies ran while one was open for 0% of the time, Pallas kernels for 9%

profile of v27, /device:TPU:0, one launch (start us, length us, event | category | flops | bytes accessed | tf_op | source)
XLA Modules:
  0.0 23.4 jit_solution(12020454390639868374)
XLA Ops:
  0.6 0.0 copy-start
  0.7 0.0 copy-start.4
  0.7 0.9 %dynamic-slice_bitcast_fusion = (f32[32,512]{1,0:T(8,128)S(1)}, f32[32,512]{1,0:T(8,128)S(1)}) fusion(f32[4,32,512]{2,1,0:T(8,128)} %bitcast.21, s32[]{:T(128)S(6)} %select_n.47, s32[]{:T(128)S(6)} %select_n.45), kind=kLoop, calls=%fused_computation | loop fusion | bytes 262152 | tf_op jit(solution)/shard_map/jit(dynamic_index_in_dim)/squeeze | solution.py:182
  1.6 5.1 %collective-permute-start.4 = (f32[32,512]{1,0:T(8,128)S(1)}, f32[32,512]{1,0:T(8,128)S(1)}, u32[]{:S(2)}, u32[]{:S(2)}) collective-permute-start(f32[32,512]{1,0:T(8,128)S(1)} %get-tuple-element.17), channel_id=1, source_target_pairs={{0,12},{4,8},{8,4},{12,0},{1,13},{5,9},{9,5},{13,1},{2,14},{6,10},... | collective-permute-start | bytes 196616 | tf_op jit(solution)/shard_map/ppermute | solution.py:174
  6.7 0.0 collective-permute-start.5
  6.7 0.0 copy-done
  6.7 0.7 %collective-permute-start.3 = (f32[32,512]{1,0:T(8,128)S(1)}, f32[32,512]{1,0:T(8,128)S(1)}, u32[]{:S(2)}, u32[]{:S(2)}) collective-permute-start(f32[32,512]{1,0:T(8,128)S(1)} %get-tuple-element.24), channel_id=1, source_target_pairs={{0,4},{4,0},{8,12},{12,8},{1,5},{5,1},{9,13},{13,9},{2,6},{6,2},{1... | collective-permute-start | bytes 196616 | tf_op jit(solution)/shard_map/ppermute | solution.py:174
  7.4 0.0 copy-done.4
  7.4 0.0 copy-start.1
  7.5 0.0 copy-start.2
  7.5 1.4 %collective-permute-start.2 = (f32[32,512]{1,0:T(8,128)S(1)}, f32[32,512]{1,0:T(8,128)S(1)}, u32[]{:S(2)}, u32[]{:S(2)}) collective-permute-start(f32[32,512]{1,0:T(8,128)S(1)} %get-tuple-element.26), channel_id=1, source_target_pairs={{0,4},{4,8},{8,12},{12,0},{1,5},{5,9},{9,13},{13,1},{2,6},{6,10},{... | collective-permute-start | bytes 196616 | tf_op jit(solution)/shard_map/ppermute | solution.py:174
  8.9 0.0 copy-start.3
  8.9 2.9 %collective-permute-start.1 = (f32[32,512]{1,0:T(8,128)S(1)}, f32[32,512]{1,0:T(8,128)S(1)}, u32[]{:S(2)}, u32[]{:S(2)}) collective-permute-start(f32[32,512]{1,0:T(8,128)S(1)} %get-tuple-element.27), channel_id=1, source_target_pairs={{0,8},{4,12},{8,0},{12,4},{1,9},{5,13},{9,1},{13,5},{2,10},{6,14},... | collective-permute-start | bytes 196616 | tf_op jit(solution)/shard_map/ppermute | solution.py:174
  11.8 0.0 copy-done.1
  11.8 0.0 copy-done.2
  11.9 0.0 copy-done.3
  11.9 0.7 %shard_map.68 = (f32[2,32,512]{2,1,0:T(8,128)S(1)}, f32[29,512]{1,0:T(8,128)S(1)}) custom-call(s32[1,2]{1,0:T(1,128)S(1)} %copy-done.3, f32[4,4]{1,0:T(4,128)S(1)} %copy-done.2, f32[32,2048]{1,0:T(8,128)S(1)} %bitcast.24), custom_call_target="tpu_custom_call" | custom-call | flops 262144 | bytes 452680 | tf_op jit(solution)/shard_map/pallas_call | solution.py:158
  12.5 0.0 collective-permute-done.4.refs_2_
  12.5 1.0 %collective-permute-start = (f32[32,512]{1,0:T(8,128)S(1)}, f32[32,512]{1,0:T(8,128)S(1)}, u32[]{:S(2)}, u32[]{:S(2)}) collective-permute-start(f32[32,512]{1,0:T(8,128)S(1)} %get-tuple-element.28), channel_id=1, source_target_pairs={{0,12},{4,0},{8,4},{12,8},{1,13},{5,1},{9,5},{13,9},{2,14},{6,2},{... | collective-permute-start | bytes 196616 | tf_op jit(solution)/shard_map/ppermute | solution.py:174
  13.6 1.1 %collective-permute-done.5.refs_3_ = f32[32,512]{1,0:T(8,128)S(1)} collective-permute-done((f32[32,512]{1,0:T(8,128)S(1)}, f32[32,512]{1,0:T(8,128)S(1)}, u32[]{:S(2)}, u32[]{:S(2)}) %collective-permute-start.5) | collective-permute-done | bytes 65568 | tf_op jit(solution)/shard_map/ppermute | solution.py:174
  14.7 0.0 collective-permute-done.3.refs_1_
  14.7 0.1 shard_map.71
  14.7 0.1 collective-permute-start.6
  14.8 1.9 %collective-permute-start.7 = (f32[32,512]{1,0:T(8,128)S(1)}, f32[32,512]{1,0:T(8,128)S(1)}, u32[]{:S(2)}, u32[]{:S(2)}) collective-permute-start(f32[32,512]{1,0:T(8,128)S(1)} %get-tuple-element.20), channel_id=1, source_target_pairs={{0,8},{4,12},{8,0},{12,4},{1,9},{5,13},{9,1},{13,5},{2,10},{6,14},... | collective-permute-start | bytes 196616 | tf_op jit(solution)/shard_map/ppermute | solution.py:174
  16.7 0.0 collective-permute-done.2.refs_3_
  16.7 1.9 %collective-permute-start.8 = (f32[32,512]{1,0:T(8,128)S(1)}, f32[32,512]{1,0:T(8,128)S(1)}, u32[]{:S(2)}, u32[]{:S(2)}) collective-permute-start(f32[32,512]{1,0:T(8,128)S(1)} %get-tuple-element.21), channel_id=1, source_target_pairs={{0,12},{4,0},{8,4},{12,8},{1,13},{5,1},{9,5},{13,9},{2,14},{6,2},{... | collective-permute-start | bytes 196616 | tf_op jit(solution)/shard_map/ppermute | solution.py:174
  18.6 0.7 %shard_map.70.settled_ref = f32[4,32,512]{2,1,0:T(8,128)} custom-call(f32[4,32,512]{2,1,0:T(8,128)S(1)} %bitcast.23), custom_call_target="tpu_custom_call" | custom-call | bytes 524288 | tf_op jit(solution)/shard_map/pallas_call | solution.py:158
  19.3 0.0 collective-permute-done.1.refs_2_
  19.4 0.0 collective-permute-done.refs_1_
  19.4 0.8 %shard_map.69 = (f32[32,2048]{1,0:T(8,128)}, f32[8,128]{1,0:T(8,128)S(1)}) custom-call(f32[29,512]{1,0:T(8,128)S(1)} %get-tuple-element.12.table_ref, f32[32,512]{1,0:T(8,128)S(1)} %get-tuple-element.29.refs_0_, f32[32,512]{1,0:T(8,128)S(1)} %collective-permute-done.refs_1_, f32[32,512]{1,0:T(8,128)S(1)} %collective-permute-done.1.refs_2_, ...), custom_call_target="tpu_custom_call" | custom-call | flops 524288 | bytes 587776 | tf_op jit(solution)/shard_map/pallas_call | solution.py:158
  20.1 0.8 %collective-permute-done.6.refs_1_ = f32[32,512]{1,0:T(8,128)S(1)} collective-permute-done((f32[32,512]{1,0:T(8,128)S(1)}, f32[32,512]{1,0:T(8,128)S(1)}, u32[]{:S(2)}, u32[]{:S(2)}) %collective-permute-start.6) | collective-permute-done | bytes 65568 | tf_op jit(solution)/shard_map/ppermute | solution.py:174
  21.0 1.6 %collective-permute-done.7.refs_2_ = f32[32,512]{1,0:T(8,128)S(1)} collective-permute-done((f32[32,512]{1,0:T(8,128)S(1)}, f32[32,512]{1,0:T(8,128)S(1)}, u32[]{:S(2)}, u32[]{:S(2)}) %collective-permute-start.7) | collective-permute-done | bytes 65568 | tf_op jit(solution)/shard_map/ppermute | solution.py:174
  22.6 0.0 collective-permute-done.8.refs_3_
  22.6 0.8 %shard_map.72 = f32[4,32,512]{2,1,0:T(8,128)} custom-call(f32[29,512]{1,0:T(8,128)S(1)} %get-tuple-element.12.table_ref, f32[8,128]{1,0:T(8,128)S(1)} %get-tuple-element.14.held_back_by, f32[4,32,512]{2,1,0:T(8,128)} %shard_map.70.settled_ref, f32[32,512]{1,0:T(8,128)S(1)} %get-tuple-element.18.refs_0_, ...), custom_call_target="tpu_custom_call", output_to_operand_aliasing={{}: (2, {})} | custom-call | bytes 849920 | tf_op jit(solution)/shard_map/pallas_call | solution.py:158
  (2 shorter events, 0.0 us)
Async XLA Ops:
  0.6 6.1 %copy-start = (f32[1,1,128,512]{3,2,1,0:T(8,128)S(1)}, f32[1,1,128,512]{3,2,1,0:T(8,128)}, u32[]{:S(2)}) copy-start(f32[1,1,128,512]{3,2,1,0:T(8,128)} %param.6) | copy-start | bytes 786436
  0.7 6.8 %copy-start.4 = (f32[1,1,128,512]{3,2,1,0:T(8,128)S(1)}, f32[1,1,128,512]{3,2,1,0:T(8,128)}, u32[]{:S(2)}) copy-start(f32[1,1,128,512]{3,2,1,0:T(8,128)} %param.5) | copy-start | bytes 786436
  1.6 10.9 %collective-permute-start.4 = (f32[32,512]{1,0:T(8,128)S(1)}, f32[32,512]{1,0:T(8,128)S(1)}, u32[]{:S(2)}, u32[]{:S(2)}) collective-permute-start(f32[32,512]{1,0:T(8,128)S(1)} %get-tuple-element.17), channel_id=1, source_target_pairs={{0,12},{4,8},{8,4},{12,0},{1,13},{5,9},{9,5},{13,1},{2,14},{6,10},... | collective-permute-start | bytes 196616 | tf_op jit(solution)/shard_map/ppermute | solution.py:174
  6.7 8.0 %collective-permute-start.5 = (f32[32,512]{1,0:T(8,128)S(1)}, f32[32,512]{1,0:T(8,128)S(1)}, u32[]{:S(2)}, u32[]{:S(2)}) collective-permute-start(f32[32,512]{1,0:T(8,128)S(1)} %get-tuple-element.22), channel_id=1, source_target_pairs={{0,8},{4,12},{8,0},{12,4},{1,9},{5,13},{9,1},{13,5},{2,10},{6,14},... | collective-permute-start | bytes 196616 | tf_op jit(solution)/shard_map/ppermute | solution.py:174
  6.7 7.9 %collective-permute-start.3 = (f32[32,512]{1,0:T(8,128)S(1)}, f32[32,512]{1,0:T(8,128)S(1)}, u32[]{:S(2)}, u32[]{:S(2)}) collective-permute-start(f32[32,512]{1,0:T(8,128)S(1)} %get-tuple-element.24), channel_id=1, source_target_pairs={{0,4},{4,0},{8,12},{12,8},{1,5},{5,1},{9,13},{13,9},{2,6},{6,2},{1... | collective-permute-start | bytes 196616 | tf_op jit(solution)/shard_map/ppermute | solution.py:174
  7.4 4.4 %copy-start.1 = (f32[1,32,2048]{2,1,0:T(8,128)S(1)}, f32[1,32,2048]{2,1,0:T(8,128)}, u32[]{:S(2)}) copy-start(f32[1,32,2048]{2,1,0:T(8,128)} %param.7) | copy-start | bytes 786436
  7.5 4.4 %copy-start.2 = (f32[4,4]{1,0:T(4,128)S(1)}, f32[4,4]{1,0:T(4,128)}, u32[]{:S(2)}) copy-start(f32[4,4]{1,0:T(4,128)} %generator_ref.1) | copy-start | bytes 196
  7.5 9.3 %collective-permute-start.2 = (f32[32,512]{1,0:T(8,128)S(1)}, f32[32,512]{1,0:T(8,128)S(1)}, u32[]{:S(2)}, u32[]{:S(2)}) collective-permute-start(f32[32,512]{1,0:T(8,128)S(1)} %get-tuple-element.26), channel_id=1, source_target_pairs={{0,4},{4,8},{8,12},{12,0},{1,5},{5,9},{9,13},{13,1},{2,6},{6,10},{... | collective-permute-start | bytes 196616 | tf_op jit(solution)/shard_map/ppermute | solution.py:174
  8.9 2.9 %copy-start.3 = (s32[1,2]{1,0:T(1,128)S(1)}, s32[1,2]{1,0:T(1,128)}, u32[]{:S(2)}) copy-start(s32[1,2]{1,0:T(1,128)} %ids_ref.1) | copy-start | bytes 28
  8.9 10.4 %collective-permute-start.1 = (f32[32,512]{1,0:T(8,128)S(1)}, f32[32,512]{1,0:T(8,128)S(1)}, u32[]{:S(2)}, u32[]{:S(2)}) collective-permute-start(f32[32,512]{1,0:T(8,128)S(1)} %get-tuple-element.27), channel_id=1, source_target_pairs={{0,8},{4,12},{8,0},{12,4},{1,9},{5,13},{9,1},{13,5},{2,10},{6,14},... | collective-permute-start | bytes 196616 | tf_op jit(solution)/shard_map/ppermute | solution.py:174
  12.5 6.8 %collective-permute-start = (f32[32,512]{1,0:T(8,128)S(1)}, f32[32,512]{1,0:T(8,128)S(1)}, u32[]{:S(2)}, u32[]{:S(2)}) collective-permute-start(f32[32,512]{1,0:T(8,128)S(1)} %get-tuple-element.28), channel_id=1, source_target_pairs={{0,12},{4,0},{8,4},{12,8},{1,13},{5,1},{9,5},{13,9},{2,14},{6,2},{... | collective-permute-start | bytes 196616 | tf_op jit(solution)/shard_map/ppermute | solution.py:174
  14.7 6.2 %collective-permute-start.6 = (f32[32,512]{1,0:T(8,128)S(1)}, f32[32,512]{1,0:T(8,128)S(1)}, u32[]{:S(2)}, u32[]{:S(2)}) collective-permute-start(f32[32,512]{1,0:T(8,128)S(1)} %get-tuple-element.19), channel_id=1, source_target_pairs={{0,4},{4,8},{8,12},{12,0},{1,5},{5,9},{9,13},{13,1},{2,6},{6,10},{... | collective-permute-start | bytes 196616 | tf_op jit(solution)/shard_map/ppermute | solution.py:174
  14.8 7.8 %collective-permute-start.7 = (f32[32,512]{1,0:T(8,128)S(1)}, f32[32,512]{1,0:T(8,128)S(1)}, u32[]{:S(2)}, u32[]{:S(2)}) collective-permute-start(f32[32,512]{1,0:T(8,128)S(1)} %get-tuple-element.20), channel_id=1, source_target_pairs={{0,8},{4,12},{8,0},{12,4},{1,9},{5,13},{9,1},{13,5},{2,10},{6,14},... | collective-permute-start | bytes 196616 | tf_op jit(solution)/shard_map/ppermute | solution.py:174
  16.7 5.9 %collective-permute-start.8 = (f32[32,512]{1,0:T(8,128)S(1)}, f32[32,512]{1,0:T(8,128)S(1)}, u32[]{:S(2)}, u32[]{:S(2)}) collective-permute-start(f32[32,512]{1,0:T(8,128)S(1)} %get-tuple-element.21), channel_id=1, source_target_pairs={{0,12},{4,0},{8,4},{12,8},{1,13},{5,1},{9,5},{13,9},{2,14},{6,2},{... | collective-permute-start | bytes 196616 | tf_op jit(solution)/shard_map/ppermute | solution.py:174

commit v28 on v27

--- a/solution.py
+++ b/solution.py
@@ -16,7 +16,7 @@
 
 EARLIER_ROUNDS = (("xor", 1), ("xor", 3), ("xor", 2))
 CURRENT_ROUNDS = (("on", 3), ("on", 2), ("on", 1))
-REBUILT_ROUNDS = (("on", 1), ("on", 2), ("on", 3))
+REBUILT_ROUNDS = (("on", 2), ("on", 1), ("on", 3))
 
 
 def target(d, way, n, members):

time: 23.2 us -> 23.7 us (1.022); the launches traced: 23.4 us -> 23.5 us
  no operation moved by 1% of the time
where the time goes in v28:
time: 23.7 us; the launch traced here: 23.5 us
  starting transfers between devices  15.2 us (64%)
  waiting for transfers between devices  3.64 us (15%)
  Pallas kernels  2.99 us (13%)
  local copies, waits for them, and re-layouts  0.99 us (4%)
  between operations  0.72 us (3%)
    ppermute x9, starting transfers between devices, pass_on(): lax.ppermute(piece, 'code', [(d, target(d, *way, members)) for d in range...  15.2 us
    ppermute x9, waiting for transfers between devices, pass_on(): lax.ppermute(piece, 'code', [(d, target(d, *way, members)) for d in range...  3.64 us
    pallas_call x5, Pallas kernels, call(): pl.pallas_call(kernel, in_specs=specs, out_shape=outs, compiler_params=pl...  2.99 us
    squeeze x3, local copies, waits for them, and re-layouts, cut(): lax.dynamic_index_in_dim(blocks, c, 0, keepdims=False)  0.96 us
  transfers between devices with their start and end apart: 9, of which 3 were waited for; matrix products, arithmetic and copies ran while one was open for 0% of the time, Pallas kernels for 9%

profile of v28, /device:TPU:0, one launch (start us, length us, event | category | flops | bytes accessed | tf_op | source)
XLA Modules:
  0.0 23.5 jit_solution(1458973797725117062)
XLA Ops:
  0.6 0.0 copy-start
  0.7 0.0 copy-start.4
  0.7 0.9 %dynamic-slice_bitcast_fusion = (f32[32,512]{1,0:T(8,128)S(1)}, f32[32,512]{1,0:T(8,128)S(1)}) fusion(f32[4,32,512]{2,1,0:T(8,128)} %bitcast.21, s32[]{:T(128)S(6)} %select_n.47, s32[]{:T(128)S(6)} %select_n.45), kind=kLoop, calls=%fused_computation | loop fusion | bytes 262152 | tf_op jit(solution)/shard_map/jit(dynamic_index_in_dim)/squeeze | solution.py:182
  1.6 5.1 %collective-permute-start.4 = (f32[32,512]{1,0:T(8,128)S(1)}, f32[32,512]{1,0:T(8,128)S(1)}, u32[]{:S(2)}, u32[]{:S(2)}) collective-permute-start(f32[32,512]{1,0:T(8,128)S(1)} %get-tuple-element.17), channel_id=1, source_target_pairs={{0,12},{4,8},{8,4},{12,0},{1,13},{5,9},{9,5},{13,1},{2,14},{6,10},... | collective-permute-start | bytes 196616 | tf_op jit(solution)/shard_map/ppermute | solution.py:174
  6.7 0.0 collective-permute-start.5
  6.7 0.0 copy-done
  6.7 0.7 %collective-permute-start.3 = (f32[32,512]{1,0:T(8,128)S(1)}, f32[32,512]{1,0:T(8,128)S(1)}, u32[]{:S(2)}, u32[]{:S(2)}) collective-permute-start(f32[32,512]{1,0:T(8,128)S(1)} %get-tuple-element.24), channel_id=1, source_target_pairs={{0,4},{4,0},{8,12},{12,8},{1,5},{5,1},{9,13},{13,9},{2,6},{6,2},{1... | collective-permute-start | bytes 196616 | tf_op jit(solution)/shard_map/ppermute | solution.py:174
  7.4 0.0 copy-done.4
  7.4 0.0 copy-start.1
  7.5 0.0 copy-start.2
  7.5 1.4 %collective-permute-start.2 = (f32[32,512]{1,0:T(8,128)S(1)}, f32[32,512]{1,0:T(8,128)S(1)}, u32[]{:S(2)}, u32[]{:S(2)}) collective-permute-start(f32[32,512]{1,0:T(8,128)S(1)} %get-tuple-element.26), channel_id=1, source_target_pairs={{0,4},{4,8},{8,12},{12,0},{1,5},{5,9},{9,13},{13,1},{2,6},{6,10},{... | collective-permute-start | bytes 196616 | tf_op jit(solution)/shard_map/ppermute | solution.py:174
  8.9 0.0 copy-start.3
  8.9 2.9 %collective-permute-start.1 = (f32[32,512]{1,0:T(8,128)S(1)}, f32[32,512]{1,0:T(8,128)S(1)}, u32[]{:S(2)}, u32[]{:S(2)}) collective-permute-start(f32[32,512]{1,0:T(8,128)S(1)} %get-tuple-element.27), channel_id=1, source_target_pairs={{0,8},{4,12},{8,0},{12,4},{1,9},{5,13},{9,1},{13,5},{2,10},{6,14},... | collective-permute-start | bytes 196616 | tf_op jit(solution)/shard_map/ppermute | solution.py:174
  11.8 0.0 copy-done.1
  11.8 0.0 copy-done.2
  11.9 0.0 copy-done.3
  11.9 0.7 %shard_map.68 = (f32[2,32,512]{2,1,0:T(8,128)S(1)}, f32[29,512]{1,0:T(8,128)S(1)}) custom-call(s32[1,2]{1,0:T(1,128)S(1)} %copy-done.3, f32[4,4]{1,0:T(4,128)S(1)} %copy-done.2, f32[32,2048]{1,0:T(8,128)S(1)} %bitcast.24), custom_call_target="tpu_custom_call" | custom-call | flops 262144 | bytes 452680 | tf_op jit(solution)/shard_map/pallas_call | solution.py:158
  12.5 0.0 collective-permute-done.4.refs_2_
  12.5 1.0 %collective-permute-start = (f32[32,512]{1,0:T(8,128)S(1)}, f32[32,512]{1,0:T(8,128)S(1)}, u32[]{:S(2)}, u32[]{:S(2)}) collective-permute-start(f32[32,512]{1,0:T(8,128)S(1)} %get-tuple-element.28), channel_id=1, source_target_pairs={{0,12},{4,0},{8,4},{12,8},{1,13},{5,1},{9,5},{13,9},{2,14},{6,2},{... | collective-permute-start | bytes 196616 | tf_op jit(solution)/shard_map/ppermute | solution.py:174
  13.6 1.1 %collective-permute-done.5.refs_3_ = f32[32,512]{1,0:T(8,128)S(1)} collective-permute-done((f32[32,512]{1,0:T(8,128)S(1)}, f32[32,512]{1,0:T(8,128)S(1)}, u32[]{:S(2)}, u32[]{:S(2)}) %collective-permute-start.5) | collective-permute-done | bytes 65568 | tf_op jit(solution)/shard_map/ppermute | solution.py:174
  14.7 0.0 collective-permute-done.3.refs_1_
  14.7 0.1 shard_map.71
  14.7 0.1 collective-permute-start.6
  14.8 1.9 %collective-permute-start.7 = (f32[32,512]{1,0:T(8,128)S(1)}, f32[32,512]{1,0:T(8,128)S(1)}, u32[]{:S(2)}, u32[]{:S(2)}) collective-permute-start(f32[32,512]{1,0:T(8,128)S(1)} %get-tuple-element.20), channel_id=1, source_target_pairs={{0,4},{4,8},{8,12},{12,0},{1,5},{5,9},{9,13},{13,1},{2,6},{6,10},{... | collective-permute-start | bytes 196616 | tf_op jit(solution)/shard_map/ppermute | solution.py:174
  16.8 0.0 collective-permute-done.2.refs_3_
  16.8 1.9 %collective-permute-start.8 = (f32[32,512]{1,0:T(8,128)S(1)}, f32[32,512]{1,0:T(8,128)S(1)}, u32[]{:S(2)}, u32[]{:S(2)}) collective-permute-start(f32[32,512]{1,0:T(8,128)S(1)} %get-tuple-element.21), channel_id=1, source_target_pairs={{0,12},{4,0},{8,4},{12,8},{1,13},{5,1},{9,5},{13,9},{2,14},{6,2},{... | collective-permute-start | bytes 196616 | tf_op jit(solution)/shard_map/ppermute | solution.py:174
  18.7 0.7 %shard_map.70.settled_ref = f32[4,32,512]{2,1,0:T(8,128)} custom-call(f32[4,32,512]{2,1,0:T(8,128)S(1)} %bitcast.23), custom_call_target="tpu_custom_call" | custom-call | bytes 524288 | tf_op jit(solution)/shard_map/pallas_call | solution.py:158
  19.4 0.0 collective-permute-done.1.refs_2_
  19.4 0.0 collective-permute-done.refs_1_
  19.4 0.8 %shard_map.69 = (f32[32,2048]{1,0:T(8,128)}, f32[8,128]{1,0:T(8,128)S(1)}) custom-call(f32[29,512]{1,0:T(8,128)S(1)} %get-tuple-element.12.table_ref, f32[32,512]{1,0:T(8,128)S(1)} %get-tuple-element.29.refs_0_, f32[32,512]{1,0:T(8,128)S(1)} %collective-permute-done.refs_1_, f32[32,512]{1,0:T(8,128)S(1)} %collective-permute-done.1.refs_2_, ...), custom_call_target="tpu_custom_call" | custom-call | flops 524288 | bytes 587776 | tf_op jit(solution)/shard_map/pallas_call | solution.py:158
  20.2 2.4 %collective-permute-done.6.refs_1_ = f32[32,512]{1,0:T(8,128)S(1)} collective-permute-done((f32[32,512]{1,0:T(8,128)S(1)}, f32[32,512]{1,0:T(8,128)S(1)}, u32[]{:S(2)}, u32[]{:S(2)}) %collective-permute-start.6) | collective-permute-done | bytes 65568 | tf_op jit(solution)/shard_map/ppermute | solution.py:174
  22.6 0.0 collective-permute-done.7.refs_2_
  22.6 0.1 collective-permute-done.8.refs_3_
  22.7 0.8 %shard_map.72 = f32[4,32,512]{2,1,0:T(8,128)} custom-call(f32[29,512]{1,0:T(8,128)S(1)} %get-tuple-element.12.table_ref, f32[8,128]{1,0:T(8,128)S(1)} %get-tuple-element.14.held_back_by, f32[4,32,512]{2,1,0:T(8,128)} %shard_map.70.settled_ref, f32[32,512]{1,0:T(8,128)S(1)} %get-tuple-element.18.refs_0_, ...), custom_call_target="tpu_custom_call", output_to_operand_aliasing={{}: (2, {})} | custom-call | bytes 849920 | tf_op jit(solution)/shard_map/pallas_call | solution.py:158
  (2 shorter events, 0.0 us)
Async XLA Ops:
  0.6 6.1 %copy-start = (f32[1,1,128,512]{3,2,1,0:T(8,128)S(1)}, f32[1,1,128,512]{3,2,1,0:T(8,128)}, u32[]{:S(2)}) copy-start(f32[1,1,128,512]{3,2,1,0:T(8,128)} %param.6) | copy-start | bytes 786436
  0.7 6.8 %copy-start.4 = (f32[1,1,128,512]{3,2,1,0:T(8,128)S(1)}, f32[1,1,128,512]{3,2,1,0:T(8,128)}, u32[]{:S(2)}) copy-start(f32[1,1,128,512]{3,2,1,0:T(8,128)} %param.5) | copy-start | bytes 786436
  1.6 10.9 %collective-permute-start.4 = (f32[32,512]{1,0:T(8,128)S(1)}, f32[32,512]{1,0:T(8,128)S(1)}, u32[]{:S(2)}, u32[]{:S(2)}) collective-permute-start(f32[32,512]{1,0:T(8,128)S(1)} %get-tuple-element.17), channel_id=1, source_target_pairs={{0,12},{4,8},{8,4},{12,0},{1,13},{5,9},{9,5},{13,1},{2,14},{6,10},... | collective-permute-start | bytes 196616 | tf_op jit(solution)/shard_map/ppermute | solution.py:174
  6.7 8.0 %collective-permute-start.5 = (f32[32,512]{1,0:T(8,128)S(1)}, f32[32,512]{1,0:T(8,128)S(1)}, u32[]{:S(2)}, u32[]{:S(2)}) collective-permute-start(f32[32,512]{1,0:T(8,128)S(1)} %get-tuple-element.22), channel_id=1, source_target_pairs={{0,8},{4,12},{8,0},{12,4},{1,9},{5,13},{9,1},{13,5},{2,10},{6,14},... | collective-permute-start | bytes 196616 | tf_op jit(solution)/shard_map/ppermute | solution.py:174
  6.7 7.9 %collective-permute-start.3 = (f32[32,512]{1,0:T(8,128)S(1)}, f32[32,512]{1,0:T(8,128)S(1)}, u32[]{:S(2)}, u32[]{:S(2)}) collective-permute-start(f32[32,512]{1,0:T(8,128)S(1)} %get-tuple-element.24), channel_id=1, source_target_pairs={{0,4},{4,0},{8,12},{12,8},{1,5},{5,1},{9,13},{13,9},{2,6},{6,2},{1... | collective-permute-start | bytes 196616 | tf_op jit(solution)/shard_map/ppermute | solution.py:174
  7.4 4.4 %copy-start.1 = (f32[1,32,2048]{2,1,0:T(8,128)S(1)}, f32[1,32,2048]{2,1,0:T(8,128)}, u32[]{:S(2)}) copy-start(f32[1,32,2048]{2,1,0:T(8,128)} %param.7) | copy-start | bytes 786436
  7.5 4.4 %copy-start.2 = (f32[4,4]{1,0:T(4,128)S(1)}, f32[4,4]{1,0:T(4,128)}, u32[]{:S(2)}) copy-start(f32[4,4]{1,0:T(4,128)} %generator_ref.1) | copy-start | bytes 196
  7.5 9.3 %collective-permute-start.2 = (f32[32,512]{1,0:T(8,128)S(1)}, f32[32,512]{1,0:T(8,128)S(1)}, u32[]{:S(2)}, u32[]{:S(2)}) collective-permute-start(f32[32,512]{1,0:T(8,128)S(1)} %get-tuple-element.26), channel_id=1, source_target_pairs={{0,4},{4,8},{8,12},{12,0},{1,5},{5,9},{9,13},{13,1},{2,6},{6,10},{... | collective-permute-start | bytes 196616 | tf_op jit(solution)/shard_map/ppermute | solution.py:174
  8.9 2.9 %copy-start.3 = (s32[1,2]{1,0:T(1,128)S(1)}, s32[1,2]{1,0:T(1,128)}, u32[]{:S(2)}) copy-start(s32[1,2]{1,0:T(1,128)} %ids_ref.1) | copy-start | bytes 28
  8.9 10.5 %collective-permute-start.1 = (f32[32,512]{1,0:T(8,128)S(1)}, f32[32,512]{1,0:T(8,128)S(1)}, u32[]{:S(2)}, u32[]{:S(2)}) collective-permute-start(f32[32,512]{1,0:T(8,128)S(1)} %get-tuple-element.27), channel_id=1, source_target_pairs={{0,8},{4,12},{8,0},{12,4},{1,9},{5,13},{9,1},{13,5},{2,10},{6,14},... | collective-permute-start | bytes 196616 | tf_op jit(solution)/shard_map/ppermute | solution.py:174
  12.5 6.9 %collective-permute-start = (f32[32,512]{1,0:T(8,128)S(1)}, f32[32,512]{1,0:T(8,128)S(1)}, u32[]{:S(2)}, u32[]{:S(2)}) collective-permute-start(f32[32,512]{1,0:T(8,128)S(1)} %get-tuple-element.28), channel_id=1, source_target_pairs={{0,12},{4,0},{8,4},{12,8},{1,13},{5,1},{9,5},{13,9},{2,14},{6,2},{... | collective-permute-start | bytes 196616 | tf_op jit(solution)/shard_map/ppermute | solution.py:174
  14.7 7.9 %collective-permute-start.6 = (f32[32,512]{1,0:T(8,128)S(1)}, f32[32,512]{1,0:T(8,128)S(1)}, u32[]{:S(2)}, u32[]{:S(2)}) collective-permute-start(f32[32,512]{1,0:T(8,128)S(1)} %get-tuple-element.19), channel_id=1, source_target_pairs={{0,8},{4,12},{8,0},{12,4},{1,9},{5,13},{9,1},{13,5},{2,10},{6,14},... | collective-permute-start | bytes 196616 | tf_op jit(solution)/shard_map/ppermute | solution.py:174
  14.8 7.8 %collective-permute-start.7 = (f32[32,512]{1,0:T(8,128)S(1)}, f32[32,512]{1,0:T(8,128)S(1)}, u32[]{:S(2)}, u32[]{:S(2)}) collective-permute-start(f32[32,512]{1,0:T(8,128)S(1)} %get-tuple-element.20), channel_id=1, source_target_pairs={{0,4},{4,8},{8,12},{12,0},{1,5},{5,9},{9,13},{13,1},{2,6},{6,10},{... | collective-permute-start | bytes 196616 | tf_op jit(solution)/shard_map/ppermute | solution.py:174
  16.8 6.0 %collective-permute-start.8 = (f32[32,512]{1,0:T(8,128)S(1)}, f32[32,512]{1,0:T(8,128)S(1)}, u32[]{:S(2)}, u32[]{:S(2)}) collective-permute-start(f32[32,512]{1,0:T(8,128)S(1)} %get-tuple-element.21), channel_id=1, source_target_pairs={{0,12},{4,0},{8,4},{12,8},{1,13},{5,1},{9,5},{13,9},{2,14},{6,2},{... | collective-permute-start | bytes 196616 | tf_op jit(solution)/shard_map/ppermute | solution.py:174

commit v29 on v26

--- a/solution.py
+++ b/solution.py
@@ -15,7 +15,7 @@
 KERNEL_VMEM = 8 * 2**20
 
 EARLIER_ROUNDS = (("xor", 1), ("xor", 2), ("xor", 3))
-CURRENT_ROUNDS = (("on", 3), ("on", 2), ("on", 1))
+CURRENT_ROUNDS = (("on", 3), ("on", 1), ("on", 2))
 REBUILT_ROUNDS = (("on", 1), ("on", 2), ("on", 3))
 
 

time: 22.7 us -> 22.9 us (level)
  starting transfers between devices: 16.4 us -> 17 us
  waiting for transfers between devices: 2.07 us -> 1.73 us
    ppermute x9, starting transfers between devices: 16.4 us -> 17 us  [pass_on(): lax.ppermute(piece, 'code', [(d, target(d, *way, members)) for d in range...]
    ppermute x9, waiting for transfers between devices: 2.07 us -> 1.73 us  [pass_on(): lax.ppermute(piece, 'code', [(d, target(d, *way, members)) for d in range...]
  transfers between devices with their start and end apart: 9 -> 9, of which waited for: 2 -> 3; matrix products, arithmetic and copies ran while one was open for 0% -> 0% of each run, Pallas kernels for 10% -> 10%
where the time goes in v29:
time: 22.9 us; the launch traced here: 22.8 us
  starting transfers between devices  17 us (74%)
  Pallas kernels  2.32 us (10%)
  waiting for transfers between devices  1.73 us (8%)
  local copies, waits for them, and re-layouts  0.99 us (4%)
  between operations  0.72 us (3%)
    ppermute x9, starting transfers between devices, pass_on(): lax.ppermute(piece, 'code', [(d, target(d, *way, members)) for d in range...  17 us
    pallas_call x5, Pallas kernels, call(): pl.pallas_call(kernel, in_specs=specs, out_shape=outs, compiler_params=pl...  2.32 us
    ppermute x9, waiting for transfers between devices, pass_on(): lax.ppermute(piece, 'code', [(d, target(d, *way, members)) for d in range...  1.73 us
    squeeze x3, local copies, waits for them, and re-layouts, cut(): lax.dynamic_index_in_dim(blocks, c, 0, keepdims=False)  0.96 us
  transfers between devices with their start and end apart: 9, of which 3 were waited for; matrix products, arithmetic and copies ran while one was open for 0% of the time, Pallas kernels for 10%

profile of v29, /device:TPU:0, one launch (start us, length us, event | category | flops | bytes accessed | tf_op | source)
XLA Modules:
  0.0 22.8 jit_solution(3278732749330779399)
XLA Ops:
  0.6 0.0 copy-start
  0.7 0.0 copy-start.4
  0.7 0.9 %dynamic-slice_bitcast_fusion = (f32[32,512]{1,0:T(8,128)S(1)}, f32[32,512]{1,0:T(8,128)S(1)}) fusion(f32[4,32,512]{2,1,0:T(8,128)} %bitcast.21, s32[]{:T(128)S(6)} %select_n.47, s32[]{:T(128)S(6)} %select_n.45), kind=kLoop, calls=%fused_computation | loop fusion | bytes 262152 | tf_op jit(solution)/shard_map/jit(dynamic_index_in_dim)/squeeze | solution.py:182
  1.6 4.1 %collective-permute-start.4 = (f32[32,512]{1,0:T(8,128)S(1)}, f32[32,512]{1,0:T(8,128)S(1)}, u32[]{:S(2)}, u32[]{:S(2)}) collective-permute-start(f32[32,512]{1,0:T(8,128)S(1)} %get-tuple-element.17), channel_id=1, source_target_pairs={{0,8},{4,12},{8,0},{12,4},{1,9},{5,13},{9,1},{13,5},{2,10},{6,14},... | collective-permute-start | bytes 196616 | tf_op jit(solution)/shard_map/ppermute | solution.py:174
  5.7 1.3 %collective-permute-start.5 = (f32[32,512]{1,0:T(8,128)S(1)}, f32[32,512]{1,0:T(8,128)S(1)}, u32[]{:S(2)}, u32[]{:S(2)}) collective-permute-start(f32[32,512]{1,0:T(8,128)S(1)} %get-tuple-element.22), channel_id=1, source_target_pairs={{0,12},{4,8},{8,4},{12,0},{1,13},{5,9},{9,5},{13,1},{2,14},{6,10},... | collective-permute-start | bytes 196616 | tf_op jit(solution)/shard_map/ppermute | solution.py:174
  7.1 0.0 copy-done
  7.1 0.3 %collective-permute-start.3 = (f32[32,512]{1,0:T(8,128)S(1)}, f32[32,512]{1,0:T(8,128)S(1)}, u32[]{:S(2)}, u32[]{:S(2)}) collective-permute-start(f32[32,512]{1,0:T(8,128)S(1)} %get-tuple-element.24), channel_id=1, source_target_pairs={{0,4},{4,0},{8,12},{12,8},{1,5},{5,1},{9,13},{13,9},{2,6},{6,2},{1... | collective-permute-start | bytes 196616 | tf_op jit(solution)/shard_map/ppermute | solution.py:174
  7.4 0.0 copy-done.4
  7.4 0.0 copy-start.1
  7.4 0.0 copy-start.2
  7.4 2.9 %collective-permute-start.2 = (f32[32,512]{1,0:T(8,128)S(1)}, f32[32,512]{1,0:T(8,128)S(1)}, u32[]{:S(2)}, u32[]{:S(2)}) collective-permute-start(f32[32,512]{1,0:T(8,128)S(1)} %get-tuple-element.26), channel_id=1, source_target_pairs={{0,8},{4,12},{8,0},{12,4},{1,9},{5,13},{9,1},{13,5},{2,10},{6,14},... | collective-permute-start | bytes 196616 | tf_op jit(solution)/shard_map/ppermute | solution.py:174
  10.3 0.0 copy-start.3
  10.3 0.7 %collective-permute-start.1 = (f32[32,512]{1,0:T(8,128)S(1)}, f32[32,512]{1,0:T(8,128)S(1)}, u32[]{:S(2)}, u32[]{:S(2)}) collective-permute-start(f32[32,512]{1,0:T(8,128)S(1)} %get-tuple-element.27), channel_id=1, source_target_pairs={{0,4},{4,8},{8,12},{12,0},{1,5},{5,9},{9,13},{13,1},{2,6},{6,10},{... | collective-permute-start | bytes 196616 | tf_op jit(solution)/shard_map/ppermute | solution.py:174
  11.0 0.0 copy-done.1
  11.0 0.0 copy-done.2
  11.0 0.0 copy-done.3
  11.0 0.7 %shard_map.68 = (f32[2,32,512]{2,1,0:T(8,128)S(1)}, f32[29,512]{1,0:T(8,128)S(1)}) custom-call(s32[1,2]{1,0:T(1,128)S(1)} %copy-done.3, f32[4,4]{1,0:T(4,128)S(1)} %copy-done.2, f32[32,2048]{1,0:T(8,128)S(1)} %bitcast.24), custom_call_target="tpu_custom_call" | custom-call | flops 262144 | bytes 452680 | tf_op jit(solution)/shard_map/pallas_call | solution.py:158
  11.6 0.0 collective-permute-done.4.refs_2_
  11.6 3.6 %collective-permute-start = (f32[32,512]{1,0:T(8,128)S(1)}, f32[32,512]{1,0:T(8,128)S(1)}, u32[]{:S(2)}, u32[]{:S(2)}) collective-permute-start(f32[32,512]{1,0:T(8,128)S(1)} %get-tuple-element.28), channel_id=1, source_target_pairs={{0,12},{4,0},{8,4},{12,8},{1,13},{5,1},{9,5},{13,9},{2,14},{6,2},{... | collective-permute-start | bytes 196616 | tf_op jit(solution)/shard_map/ppermute | solution.py:174
  15.3 0.0 collective-permute-done.5.refs_3_
  15.3 0.0 collective-permute-done.3.refs_1_
  15.3 0.1 shard_map.71
  15.4 0.1 collective-permute-start.6
  15.4 1.3 %collective-permute-start.7 = (f32[32,512]{1,0:T(8,128)S(1)}, f32[32,512]{1,0:T(8,128)S(1)}, u32[]{:S(2)}, u32[]{:S(2)}) collective-permute-start(f32[32,512]{1,0:T(8,128)S(1)} %get-tuple-element.20), channel_id=1, source_target_pairs={{0,8},{4,12},{8,0},{12,4},{1,9},{5,13},{9,1},{13,5},{2,10},{6,14},... | collective-permute-start | bytes 196616 | tf_op jit(solution)/shard_map/ppermute | solution.py:174
  16.7 0.1 collective-permute-done.2.refs_3_
  16.8 2.8 %collective-permute-start.8 = (f32[32,512]{1,0:T(8,128)S(1)}, f32[32,512]{1,0:T(8,128)S(1)}, u32[]{:S(2)}, u32[]{:S(2)}) collective-permute-start(f32[32,512]{1,0:T(8,128)S(1)} %get-tuple-element.21), channel_id=1, source_target_pairs={{0,12},{4,0},{8,4},{12,8},{1,13},{5,1},{9,5},{13,9},{2,14},{6,2},{... | collective-permute-start | bytes 196616 | tf_op jit(solution)/shard_map/ppermute | solution.py:174
  19.6 0.7 %shard_map.70.settled_ref = f32[4,32,512]{2,1,0:T(8,128)} custom-call(f32[4,32,512]{2,1,0:T(8,128)S(1)} %bitcast.23), custom_call_target="tpu_custom_call" | custom-call | bytes 524288 | tf_op jit(solution)/shard_map/pallas_call | solution.py:158
  20.3 0.0 collective-permute-done.1.refs_2_
  20.3 0.0 collective-permute-done.refs_1_
  20.3 0.8 %shard_map.69 = (f32[32,2048]{1,0:T(8,128)}, f32[8,128]{1,0:T(8,128)S(1)}) custom-call(f32[29,512]{1,0:T(8,128)S(1)} %get-tuple-element.12.table_ref, f32[32,512]{1,0:T(8,128)S(1)} %get-tuple-element.29.refs_0_, f32[32,512]{1,0:T(8,128)S(1)} %collective-permute-done.refs_1_, f32[32,512]{1,0:T(8,128)S(1)} %collective-permute-done.1.refs_2_, ...), custom_call_target="tpu_custom_call" | custom-call | flops 524288 | bytes 587776 | tf_op jit(solution)/shard_map/pallas_call | solution.py:158
  21.1 0.6 %collective-permute-done.6.refs_1_ = f32[32,512]{1,0:T(8,128)S(1)} collective-permute-done((f32[32,512]{1,0:T(8,128)S(1)}, f32[32,512]{1,0:T(8,128)S(1)}, u32[]{:S(2)}, u32[]{:S(2)}) %collective-permute-start.6) | collective-permute-done | bytes 65568 | tf_op jit(solution)/shard_map/ppermute | solution.py:174
  21.6 1.1 %collective-permute-done.7.refs_2_ = f32[32,512]{1,0:T(8,128)S(1)} collective-permute-done((f32[32,512]{1,0:T(8,128)S(1)}, f32[32,512]{1,0:T(8,128)S(1)}, u32[]{:S(2)}, u32[]{:S(2)}) %collective-permute-start.7) | collective-permute-done | bytes 65568 | tf_op jit(solution)/shard_map/ppermute | solution.py:174
  22.7 0.0 collective-permute-done.8.refs_3_
  22.7 0.1 shard_map.72
  (2 shorter events, 0.0 us)
Async XLA Ops:
  0.6 6.4 %copy-start = (f32[1,1,128,512]{3,2,1,0:T(8,128)S(1)}, f32[1,1,128,512]{3,2,1,0:T(8,128)}, u32[]{:S(2)}) copy-start(f32[1,1,128,512]{3,2,1,0:T(8,128)} %param.6) | copy-start | bytes 786436
  0.7 6.7 %copy-start.4 = (f32[1,1,128,512]{3,2,1,0:T(8,128)S(1)}, f32[1,1,128,512]{3,2,1,0:T(8,128)}, u32[]{:S(2)}) copy-start(f32[1,1,128,512]{3,2,1,0:T(8,128)} %param.5) | copy-start | bytes 786436
  1.6 10.0 %collective-permute-start.4 = (f32[32,512]{1,0:T(8,128)S(1)}, f32[32,512]{1,0:T(8,128)S(1)}, u32[]{:S(2)}, u32[]{:S(2)}) collective-permute-start(f32[32,512]{1,0:T(8,128)S(1)} %get-tuple-element.17), channel_id=1, source_target_pairs={{0,8},{4,12},{8,0},{12,4},{1,9},{5,13},{9,1},{13,5},{2,10},{6,14},... | collective-permute-start | bytes 196616 | tf_op jit(solution)/shard_map/ppermute | solution.py:174
  5.7 9.6 %collective-permute-start.5 = (f32[32,512]{1,0:T(8,128)S(1)}, f32[32,512]{1,0:T(8,128)S(1)}, u32[]{:S(2)}, u32[]{:S(2)}) collective-permute-start(f32[32,512]{1,0:T(8,128)S(1)} %get-tuple-element.22), channel_id=1, source_target_pairs={{0,12},{4,8},{8,4},{12,0},{1,13},{5,9},{9,5},{13,1},{2,14},{6,10},... | collective-permute-start | bytes 196616 | tf_op jit(solution)/shard_map/ppermute | solution.py:174
  7.1 8.2 %collective-permute-start.3 = (f32[32,512]{1,0:T(8,128)S(1)}, f32[32,512]{1,0:T(8,128)S(1)}, u32[]{:S(2)}, u32[]{:S(2)}) collective-permute-start(f32[32,512]{1,0:T(8,128)S(1)} %get-tuple-element.24), channel_id=1, source_target_pairs={{0,4},{4,0},{8,12},{12,8},{1,5},{5,1},{9,13},{13,9},{2,6},{6,2},{1... | collective-permute-start | bytes 196616 | tf_op jit(solution)/shard_map/ppermute | solution.py:174
  7.4 3.6 %copy-start.1 = (f32[1,32,2048]{2,1,0:T(8,128)S(1)}, f32[1,32,2048]{2,1,0:T(8,128)}, u32[]{:S(2)}) copy-start(f32[1,32,2048]{2,1,0:T(8,128)} %param.7) | copy-start | bytes 786436
  7.4 3.6 %copy-start.2 = (f32[4,4]{1,0:T(4,128)S(1)}, f32[4,4]{1,0:T(4,128)}, u32[]{:S(2)}) copy-start(f32[4,4]{1,0:T(4,128)} %generator_ref.1) | copy-start | bytes 196
  7.4 9.4 %collective-permute-start.2 = (f32[32,512]{1,0:T(8,128)S(1)}, f32[32,512]{1,0:T(8,128)S(1)}, u32[]{:S(2)}, u32[]{:S(2)}) collective-permute-start(f32[32,512]{1,0:T(8,128)S(1)} %get-tuple-element.26), channel_id=1, source_target_pairs={{0,8},{4,12},{8,0},{12,4},{1,9},{5,13},{9,1},{13,5},{2,10},{6,14},... | collective-permute-start | bytes 196616 | tf_op jit(solution)/shard_map/ppermute | solution.py:174
  10.3 0.7 %copy-start.3 = (s32[1,2]{1,0:T(1,128)S(1)}, s32[1,2]{1,0:T(1,128)}, u32[]{:S(2)}) copy-start(s32[1,2]{1,0:T(1,128)} %ids_ref.1) | copy-start | bytes 28
  10.3 10.0 %collective-permute-start.1 = (f32[32,512]{1,0:T(8,128)S(1)}, f32[32,512]{1,0:T(8,128)S(1)}, u32[]{:S(2)}, u32[]{:S(2)}) collective-permute-start(f32[32,512]{1,0:T(8,128)S(1)} %get-tuple-element.27), channel_id=1, source_target_pairs={{0,4},{4,8},{8,12},{12,0},{1,5},{5,9},{9,13},{13,1},{2,6},{6,10},{... | collective-permute-start | bytes 196616 | tf_op jit(solution)/shard_map/ppermute | solution.py:174
  11.6 8.6 %collective-permute-start = (f32[32,512]{1,0:T(8,128)S(1)}, f32[32,512]{1,0:T(8,128)S(1)}, u32[]{:S(2)}, u32[]{:S(2)}) collective-permute-start(f32[32,512]{1,0:T(8,128)S(1)} %get-tuple-element.28), channel_id=1, source_target_pairs={{0,12},{4,0},{8,4},{12,8},{1,13},{5,1},{9,5},{13,9},{2,14},{6,2},{... | collective-permute-start | bytes 196616 | tf_op jit(solution)/shard_map/ppermute | solution.py:174
  15.4 6.2 %collective-permute-start.6 = (f32[32,512]{1,0:T(8,128)S(1)}, f32[32,512]{1,0:T(8,128)S(1)}, u32[]{:S(2)}, u32[]{:S(2)}) collective-permute-start(f32[32,512]{1,0:T(8,128)S(1)} %get-tuple-element.19), channel_id=1, source_target_pairs={{0,4},{4,8},{8,12},{12,0},{1,5},{5,9},{9,13},{13,1},{2,6},{6,10},{... | collective-permute-start | bytes 196616 | tf_op jit(solution)/shard_map/ppermute | solution.py:174
  15.4 7.3 %collective-permute-start.7 = (f32[32,512]{1,0:T(8,128)S(1)}, f32[32,512]{1,0:T(8,128)S(1)}, u32[]{:S(2)}, u32[]{:S(2)}) collective-permute-start(f32[32,512]{1,0:T(8,128)S(1)} %get-tuple-element.20), channel_id=1, source_target_pairs={{0,8},{4,12},{8,0},{12,4},{1,9},{5,13},{9,1},{13,5},{2,10},{6,14},... | collective-permute-start | bytes 196616 | tf_op jit(solution)/shard_map/ppermute | solution.py:174
  16.8 5.9 %collective-permute-start.8 = (f32[32,512]{1,0:T(8,128)S(1)}, f32[32,512]{1,0:T(8,128)S(1)}, u32[]{:S(2)}, u32[]{:S(2)}) collective-permute-start(f32[32,512]{1,0:T(8,128)S(1)} %get-tuple-element.21), channel_id=1, source_target_pairs={{0,12},{4,0},{8,4},{12,8},{1,13},{5,1},{9,5},{13,9},{2,14},{6,2},{... | collective-permute-start | bytes 196616 | tf_op jit(solution)/shard_map/ppermute | solution.py:174
